TPU v7x, 32 devices: a whole 2x2x4 slice. The times are simulated.
32 devices in a mesh: copies: 2 (over x), rollout: 2 (over core), tensor: 8 (over z, y).
Axes of the slice: x: 2, y: 2, z: 4, core: 2. Of those that a mesh axis runs over, the one named last changes fastest.
Arguments:
- owners: int32 [4, 3], P('copies'), parts along dimension 0, may hold values from 0 to 1
- base_query: bfloat16 [4, 5120, 5120], P('copies', 'tensor'), parts along dimension 0, may hold values from -6 to 6
- base_key: bfloat16 [4, 1024, 5120], P('copies', 'tensor'), parts along dimension 0, may hold values from -6 to 6
- base_value: bfloat16 [4, 1024, 5120], P('copies', 'tensor'), parts along dimension 0, may hold values from -6 to 6
- left_shared_matrix: bfloat16 [2, 4, 3, 64, 5120], P('rollout', 'copies', None, None, 'tensor'), parts along dimension 1, may hold values from -6 to 6
- right_queries_matrix: bfloat16 [2, 4, 5120, 64], P('rollout', 'copies', 'tensor'), parts along dimension 1, may hold values from -6 to 6
- right_keys_matrix: bfloat16 [2, 4, 1024, 64], P('rollout', 'copies', 'tensor'), parts along dimension 1, may hold values from -6 to 6
- right_values_matrix: bfloat16 [2, 4, 1024, 64], P('rollout', 'copies', 'tensor'), parts along dimension 1, may hold values from -6 to 6
Outputs:
- merged_query: bfloat16 [4, 5120, 5120], P('copies', 'tensor'), parts along dimension 0
- merged_key: bfloat16 [4, 1024, 5120], P('copies', 'tensor'), parts along dimension 0
- merged_value: bfloat16 [4, 1024, 5120], P('copies', 'tensor'), parts along dimension 0
There are 2 independent parts, one for each index of `copies`. A program takes and returns all parts, laid end to end along the dimension named above; each array names one. Nothing has to cross between parts.
All inputs are finite; a program needn't handle non-finite values.
Results may differ from a plain program's by a relative error of at most 0.001.
Values may be sent and summed in bfloat16 or wider, within the bound.
No kernel may reach another device: no remote copies, remote signals or barrier semaphores. Data moves between devices by JAX's collectives and lax.ppermute only.
A program may use at most 128 MiB of HBM per device.

v0:
```python
import jax
import jax.numpy as jnp
from jax import lax
from jax.sharding import PartitionSpec as P

numerator_gain = 16.0


def from_root(array, axis, root):
    mine = lax.axis_index(axis) == root
    return lax.psum(jnp.where(mine, array, jnp.zeros_like(array)), axis)


def from_owner(inside, rows_b, owner):
    return (from_root(inside, "rollout", owner), from_root(rows_b, "rollout", owner))


def fetch_pairs(list_a, list_b, owner_list):
    fetched_a = []
    received_up_factor = []
    for index in range(len(list_a)):
        inside, rows_b = from_owner(list_a[index], list_b[index], owner_list[index])
        fetched_a.append(inside)
        received_up_factor.append(rows_b)
    return (fetched_a, received_up_factor)


def merge_into(base_rows, delta, update_multiplier):
    return (base_rows.astype(jnp.float32) + update_multiplier * delta).astype(jnp.bfloat16)


def per_device(
    owners,
    base_query,
    base_key,
    base_value,
    left_shared_matrix,
    right_queries_matrix,
    right_keys_matrix,
    right_values_matrix,
):
    adapter_rank = left_shared_matrix.shape[3]
    update_multiplier = numerator_gain / adapter_rank
    layers = base_query.shape[0]
    projs = left_shared_matrix.shape[2]
    bases = (base_query, base_key, base_value)
    outside = (right_queries_matrix, right_keys_matrix, right_values_matrix)
    merged_outputs = [[None] * layers for proj in range(projs)]
    owner_list = []
    own_b = []
    for layer in range(layers):
        for proj in range(projs):
            owner_list.append(owners[layer, proj])
            own_b.append(outside[proj][0, layer])
    own_a = [left_shared_matrix[0, layer, proj] for layer in range(layers) for proj in range(projs)]
    fetched_a, received_up_factor = fetch_pairs(own_a, own_b, owner_list)
    for layer in range(layers):
        for proj in range(projs):
            index = layer * projs + proj
            rows_b = received_up_factor[index]

            def expand(piece, start, rows_b=rows_b):
                return jnp.dot(rows_b, piece, preferred_element_type=jnp.float32)

            delta = expand(
                lax.all_gather(fetched_a[index], "tensor", axis=1, tiled=True), jnp.int32(0)
            )
            merged_outputs[proj][layer] = merge_into(bases[proj][layer], delta, update_multiplier)
    return (
        jnp.stack(merged_outputs[0], axis=0),
        jnp.stack(merged_outputs[1], axis=0),
        jnp.stack(merged_outputs[2], axis=0),
    )


def solution(mesh):
    return jax.shard_map(
        per_device,
        mesh=mesh,
        in_specs=(
            P("copies", None),
            P("copies", "tensor", None),
            P("copies", "tensor", None),
            P("copies", "tensor", None),
            P("rollout", "copies", None, None, "tensor"),
            P("rollout", "copies", "tensor", None),
            P("rollout", "copies", "tensor", None),
            P("rollout", "copies", "tensor", None),
        ),
        out_specs=(
            P("copies", "tensor", None),
            P("copies", "tensor", None),
            P("copies", "tensor", None),
        ),
        check_vma=False,
    )
```

profile of v0, /device:TPU:0, one launch (start us, length us, event | category | flops | bytes accessed | tf_op | source)
XLA Modules:
  0.0 265.0 jit_solution(15795586306177511583)
XLA Ops:
  7.2 0.0 all-reduce.7.cloned.1.call-start
  7.2 1.5 fusion.16
  12.5 1.6 select_bitcast_fusion.7
  14.1 1.9 select_bitcast_fusion.1
  16.0 0.0 all-reduce.7.cloned.1.call-update
  16.0 0.0 all-reduce.5.cloned.1.call-start
  16.1 1.4 select_bitcast_fusion.9
  17.4 0.0 all-reduce.5.cloned.1.call-update
  17.5 20.7 %all-reduce.7.cloned.1.call-done = (bf16[640,64]{0,1:T(8,128)(2,1)}, bf16[64,640]{1,0:T(8,128)(2,1)}, bf16[640,64]{0,1:T(8,128)(2,1)}, bf16[64,640]{1,0:T(8,128)...) async-done(((bf16[640,64]{0,1:T(8,128)(2,1)}, bf16[64,640]{1,0:T(8,128)(2,1)}, ...) | async-done | bytes 655376 | tf_op jit(solution)/shard_map/psum | solution.py:11
  38.2 32.4 %all_gather.18 = bf16[64,5120]{1,0:T(8,128)(2,1)S(1)} all-gather(bf16[64,640]{1,0:T(8,128)(2,1)} %get-tuple-element.10), channel_id=1, replica_groups=mesh['copies'=2,'rollout'=2,'tensor'=8] {'tensor'}, dimensions={1}, use_global_device_ids=true | all-gather | bytes 737280 | tf_op jit(solution)/shard_map/all_gather | solution.py:66
  70.6 32.3 %all_gather.19 = bf16[64,5120]{1,0:T(8,128)(2,1)S(1)} all-gather(bf16[64,640]{1,0:T(8,128)(2,1)} %get-tuple-element.8), channel_id=1, replica_groups=mesh['copies'=2,'rollout'=2,'tensor'=8] {'tensor'}, dimensions={1}, use_global_device_ids=true | all-gather | bytes 737280 | tf_op jit(solution)/shard_map/all_gather | solution.py:66
  102.9 34.1 %all_gather.21 = bf16[64,5120]{1,0:T(8,128)(2,1)} all-gather(bf16[64,640]{1,0:T(8,128)(2,1)} %get-tuple-element.11), channel_id=1, replica_groups=mesh['copies'=2,'rollout'=2,'tensor'=8] {'tensor'}, dimensions={1}, use_global_device_ids=true | all-gather | bytes 737280 | tf_op jit(solution)/shard_map/all_gather | solution.py:66
  137.0 33.9 %all_gather.20 = bf16[64,5120]{1,0:T(8,128)(2,1)} all-gather(bf16[64,640]{1,0:T(8,128)(2,1)} %get-tuple-element.12), channel_id=1, replica_groups=mesh['copies'=2,'rollout'=2,'tensor'=8] {'tensor'}, dimensions={1}, use_global_device_ids=true | all-gather | bytes 737280 | tf_op jit(solution)/shard_map/all_gather | solution.py:66
  170.9 0.0 copy-done.8
  170.9 31.8 %all_gather.23 = bf16[64,5120]{1,0:T(8,128)(2,1)S(1)} all-gather(bf16[64,640]{1,0:T(8,128)(2,1)S(1)} %copy-done.8), channel_id=1, replica_groups=mesh['copies'=2,'rollout'=2,'tensor'=8] {'tensor'}, dimensions={1}, use_global_device_ids=true | all-gather | bytes 737280 | tf_op jit(solution)/shard_map/all_gather | solution.py:66
  202.7 0.0 copy-done.6
  202.7 4.2 %fusion.2 = bf16[1,640,5120]{2,1,0:T(8,128)(2,1)S(1)} fusion(bf16[640,64]{0,1:T(8,128)(2,1)S(1)} %copy-done.6, bf16[64,5120]{1,0:T(8,128)(2,1)S(1)} %all_gather.18, bf16[2,640,5120]{2,1,0:T(8,128)(2,1)} %param.9), kind=kOutput, calls=%fused_computation.5 | convolution fusion | flops 432537600 | bytes 13844480 | tf_op jit(solution)/shard_map/dot_general | solution.py:63
  206.9 2.5 copy-done
  209.3 0.0 copy-done.5
  209.3 2.1 fusion.3
  211.4 0.0 copy-start.1
  211.4 5.5 %pad_maximum_fusion = bf16[2,640,5120]{2,1,0:T(8,128)(2,1)} fusion(bf16[1,640,5120]{2,1,0:T(8,128)(2,1)S(1)} %fusion.3, bf16[1,640,5120]{2,1,0:T(8,128)(2,1)S(1)} %fusion.2), kind=kLoop, calls=%fused_computation | loop fusion | flops 6553600 | bytes 26214400 | tf_op jit(solution)/shard_map/stack | solution.py:70
  216.9 33.5 %all_gather.22 = bf16[64,5120]{1,0:T(8,128)(2,1)} all-gather(bf16[64,640]{1,0:T(8,128)(2,1)S(1)} %copy-done.7), channel_id=1, replica_groups=mesh['copies'=2,'rollout'=2,'tensor'=8] {'tensor'}, dimensions={1}, use_global_device_ids=true | all-gather | bytes 737280 | tf_op jit(solution)/shard_map/all_gather | solution.py:66
  250.4 1.7 fusion.14
  252.1 0.5 fusion.15
  252.7 0.0 copy-start.2
  252.7 1.7 pad_maximum_fusion.1
  254.4 0.9 copy-done.2
  255.3 0.0 copy-done.10
  255.3 0.5 fusion.12
  255.9 0.5 fusion.13
  256.4 1.7 pad_maximum_fusion.2
  (17 shorter events, 0.0 us)
Async XLA Ops:
  7.2 31.0 %all-reduce.7.cloned.1.call-start = ((), (), s32[]{:S(2)}) async-start(), calls=%async_computation.1 | async-start | bytes 1310720 | tf_op jit(solution)/shard_map/psum | solution.py:11
  16.0 234.4 %all-reduce.5.cloned.1.call-start = ((), (), s32[]{:S(2)}) async-start(), calls=%async_computation | async-start | bytes 131072 | tf_op jit(solution)/shard_map/psum | solution.py:11
  38.2 132.7 %copy-start.8 = (bf16[64,640]{1,0:T(8,128)(2,1)S(1)}, bf16[64,640]{1,0:T(8,128)(2,1)}, u32[]{:S(2)}) copy-start(bf16[64,640]{1,0:T(8,128)(2,1)} %get-tuple-element.13) | copy-start | bytes 245764
  38.2 164.5 %copy-start.6 = (bf16[640,64]{0,1:T(8,128)(2,1)S(1)}, bf16[640,64]{0,1:T(8,128)(2,1)}, u32[]{:S(2)}) copy-start(bf16[640,64]{0,1:T(8,128)(2,1)} %get-tuple-element.9) | copy-start | bytes 245764
  202.7 6.7 %copy-start = (bf16[2,640,5120]{2,1,0:T(8,128)(2,1)S(1)}, bf16[2,640,5120]{2,1,0:T(8,128)(2,1)}, u32[]{:S(2)}) copy-start(bf16[2,640,5120]{2,1,0:T(8,128)(2,1)} %param.9) | copy-start | bytes 39321604
  202.7 6.7 %copy-start.5 = (bf16[640,64]{0,1:T(8,128)(2,1)S(1)}, bf16[640,64]{0,1:T(8,128)(2,1)}, u32[]{:S(2)}) copy-start(bf16[640,64]{0,1:T(8,128)(2,1)} %get-tuple-element.7) | copy-start | bytes 245764
  211.4 5.5 %copy-start.7 = (bf16[64,640]{1,0:T(8,128)(2,1)S(1)}, bf16[64,640]{1,0:T(8,128)(2,1)}, u32[]{:S(2)}) copy-start(bf16[64,640]{1,0:T(8,128)(2,1)} %get-tuple-element.14) | copy-start | bytes 245764
  211.4 39.0 %copy-start.1 = (bf16[2,128,5120]{2,1,0:T(8,128)(2,1)S(1)}, bf16[2,128,5120]{2,1,0:T(8,128)(2,1)}, u32[]{:S(2)}) copy-start(bf16[2,128,5120]{2,1,0:T(8,128)(2,1)} %param.10) | copy-start | bytes 7864324
  250.4 1.7 copy-start.3
  250.4 1.7 copy-start.11
  252.7 2.7 %copy-start.2 = (bf16[2,128,5120]{2,1,0:T(8,128)(2,1)S(1)}, bf16[2,128,5120]{2,1,0:T(8,128)(2,1)}, u32[]{:S(2)}) copy-start(bf16[2,128,5120]{2,1,0:T(8,128)(2,1)} %param.11) | copy-start | bytes 7864324
  252.7 2.7 %copy-start.10 = (bf16[128,64]{0,1:T(8,128)(2,1)S(1)}, bf16[128,64]{0,1:T(8,128)(2,1)}, u32[]{:S(2)}) copy-start(bf16[128,64]{0,1:T(8,128)(2,1)} %get-tuple-element.5) | copy-start | bytes 49156
  254.4 1.5 copy-start.4
  254.4 1.5 copy-start.9
Sparse Core Ops, SparseCore 0:
  16.1 21.9 all-reduce.6
  40.8 19.1 all-reduce.4
where the time goes:
time: 265 us
  blocking collectives  198 us (75%)
  waiting for transfers between devices  20.7 us (8%)
  between operations  17.9 us (7%)
  other arithmetic  13.8 us (5%)
  matrix products  9.56 us (4%)
  local copies, waits for them, and re-layouts  4.97 us (2%)
    all_gather x6, blocking collectives, per_device(): lax.all_gather(fetched_a[index], 'tensor', axis=1, tiled=True)  198 us
    psum x2, waiting for transfers between devices, from_root(): return lax.psum(jnp.where(mine, array, jnp.zeros_like(array)), axis)  20.7 us
    dot_general x6, matrix products, expand(): return jnp.dot(rows_b, piece, preferred_element_type=jnp.float32)  9.56 us
    another operation x1, other arithmetic, per_device(): jnp.stack(merged_outputs[0], axis=0)  5.47 us
  transfers between devices with their start and end apart: 2, of which 1 were waited for; matrix products, arithmetic and copies ran while one was open for 5% of the time, Pallas kernels for 0%

commit v1 on v0

v1 whole, which is shorter than its diff:
```python
import functools

import jax
import jax.numpy as jnp
from jax import lax
from jax.experimental import pallas as pl
from jax.experimental.pallas import tpu as pltpu
from jax.sharding import PartitionSpec as P

numerator_gain = 16.0
LANES = 128


def ring_order(n):
    return list(range(0, n, 2)) + list(range(n - 1, 0, -2))


def ring_perm(n):
    order = ring_order(n)
    pairs = []
    for k in range(n):
        pairs.append((order[k], order[(k + 1) % n]))
        pairs.append((n + order[k], n + order[(k - 1) % n]))
    return pairs


def ring_pass(array, n):
    return lax.ppermute(array, ("rollout", "tensor"), ring_perm(n))


def swap_cores(array):
    return lax.ppermute(array, "rollout", [(0, 1), (1, 0)])


def chunk_places(n, core, tensor):
    position = jnp.where(tensor % 2 == 0, tensor // 2, n - 1 - tensor // 2)
    slot = jnp.arange(n, dtype=jnp.int32)
    step = (slot + 1) // 2
    backward = (slot + core) % 2 == 1
    k = jnp.where(slot == 0, position, position + jnp.where(backward, -step, step))
    k = (k + n) % n
    return jnp.where(k < n // 2, 2 * k, 2 * n - 1 - 2 * k).astype(jnp.int32)


def merge_kernel(pieces, scale, cols, n_a, fresh, places, *refs):
    b_refs = refs[:3]
    a_refs = refs[3 : 3 + n_a]
    bases = refs[3 + n_a : 6 + n_a]
    at = 6 + n_a + (0 if fresh else 3)
    outs = refs[at : at + 3]
    buf, load_sem, store_sem = refs[at + 3 : at + 6]
    core = places[places.shape[0] - 1]
    tasks = []
    for slot, a_index, a_layer, layer in pieces:
        out_layer = layer if isinstance(layer, int) else layer[0] + (1 - 2 * layer[0]) * core
        columns = pl.ds(pl.multiple_of(places[slot] * cols, LANES), cols)
        for proj in range(3):
            rows = bases[proj].shape[1]
            for row in range(0, rows, min(rows, LANES)):
                tasks.append((proj, out_layer, row, min(rows, LANES), columns, a_index, a_layer))

    def load(j):
        proj, layer, row, size, columns, _, _ = tasks[j]
        return pltpu.make_async_copy(
            bases[proj].at[layer, pl.ds(row, size), columns], buf.at[j, pl.ds(0, size)], load_sem.at[j]
        )

    def store(j):
        proj, layer, row, size, columns, _, _ = tasks[j]
        return pltpu.make_async_copy(
            buf.at[j, pl.ds(0, size)], outs[proj].at[layer, pl.ds(row, size), columns], store_sem.at[j]
        )

    for j in range(len(tasks)):
        load(j).start()
    for j in range(len(tasks)):
        proj, layer, row, size, _, a_index, a_layer = tasks[j]
        load(j).wait()
        delta = lax.dot_general(
            b_refs[proj][layer, :, row : row + size],
            a_refs[a_index][a_layer, proj],
            (((0,), (0,)), ((), ())),
            preferred_element_type=jnp.float32,
        )
        merged = buf[j, :size].astype(jnp.float32) + scale * delta
        buf[j, :size] = merged.astype(jnp.bfloat16)
        store(j).start()
    for j in range(len(tasks)):
        store(j).wait()


def merge(places, b, a_list, bases, outs, pieces, scale, cols):
    fresh = outs is None
    n_a = len(a_list)
    tasks = len(pieces) * sum(-(-base.shape[1] // LANES) for base in bases)
    vmem = pl.BlockSpec(memory_space=pltpu.VMEM)
    hbm = pl.BlockSpec(memory_space=pl.ANY)
    operands = [places, *b, *a_list, *bases] + ([] if fresh else list(outs))
    rows = sum(base.shape[1] for base in bases)
    rank = a_list[0].shape[2]
    return pl.pallas_call(
        functools.partial(merge_kernel, pieces, scale, cols, n_a, fresh),
        in_specs=[pl.BlockSpec(memory_space=pltpu.SMEM)] + [vmem] * (3 + n_a) + [hbm] * (3 if fresh else 6),
        out_specs=[hbm] * 3,
        out_shape=[jax.ShapeDtypeStruct(base.shape, base.dtype) for base in bases],
        scratch_shapes=[
            pltpu.VMEM((tasks, min(LANES, max(base.shape[1] for base in bases)), cols), jnp.bfloat16),
            pltpu.SemaphoreType.DMA((tasks,)),
            pltpu.SemaphoreType.DMA((tasks,)),
        ],
        input_output_aliases={} if fresh else {7 + n_a + i: i for i in range(3)},
        compiler_params=pltpu.CompilerParams(vmem_limit_bytes=16 * 1024 * 1024),
        cost_estimate=pl.CostEstimate(
            flops=2 * len(pieces) * rows * cols * rank,
            bytes_accessed=4 * len(pieces) * rows * cols,
            transcendentals=0,
        ),
    )(*operands)


def per_device(
    n,
    owners,
    base_query,
    base_key,
    base_value,
    left_shared_matrix,
    right_queries_matrix,
    right_keys_matrix,
    right_values_matrix,
):
    layers, projs, rank, cols = left_shared_matrix.shape[1:]
    scale = numerator_gain / rank
    bases = (base_query, base_key, base_value)
    core = lax.axis_index("rollout")
    tensor = lax.axis_index("tensor")
    mine = owners == core

    own_a = left_shared_matrix[0]
    a = jnp.where(mine[:, :, None, None], own_a, swap_cores(own_a))
    b = []
    for proj, right in enumerate((right_queries_matrix, right_keys_matrix, right_values_matrix)):
        own_b = jnp.swapaxes(right[0], 1, 2)
        b.append(jnp.where(mine[:, proj, None, None], own_b, swap_cores(own_b)))

    half = layers // 2
    arrived = [(a,)]
    held = a
    for step in range(1, n // 2):
        held = ring_pass(held, n)
        arrived.append((held, swap_cores(held)))
    last = lax.dynamic_slice_in_dim(held, core * half, half, 0)
    last = ring_pass(last, n)
    arrived.append((last, swap_cores(last)))

    places = jnp.concatenate([chunk_places(n, core, tensor), core[None].astype(jnp.int32)])

    if cols % LANES == 0 and half == 1:
        outs = None
        for step, chunks in enumerate(arrived):
            if step == 0:
                pieces = [(0, 0, layer, layer) for layer in range(layers)]
            elif step < n // 2:
                pieces = [(2 * step - 1 + i, i, layer, layer) for i in range(2) for layer in range(layers)]
            else:
                pieces = [(n - 1, 0, 0, (0,)), (n - 1, 1, 0, (1,))]
            outs = merge(places, b, chunks, bases, outs, pieces, scale, cols)
        return tuple(outs)

    full = jnp.zeros((layers, projs, rank, n * cols), own_a.dtype)
    for step, chunks in enumerate(arrived[:-1]):
        for i, chunk in enumerate(chunks):
            start = places[max(0, 2 * step - 1) + i] * cols
            full = lax.dynamic_update_slice(full, chunk, (0, 0, 0, start))
    for i, chunk in enumerate(arrived[-1]):
        layer = half * jnp.where(core == i, 0, 1)
        full = lax.dynamic_update_slice(full, chunk, (layer, 0, 0, places[n - 1] * cols))
    merged = []
    for proj in range(projs):
        delta = jnp.einsum("lkr,lkc->lrc", b[proj], full[:, proj], preferred_element_type=jnp.float32)
        merged.append((bases[proj].astype(jnp.float32) + scale * delta).astype(jnp.bfloat16))
    return tuple(merged)


def solution(mesh):
    return jax.shard_map(
        functools.partial(per_device, mesh.shape["tensor"]),
        mesh=mesh,
        in_specs=(
            P("copies", None),
            P("copies", "tensor", None),
            P("copies", "tensor", None),
            P("copies", "tensor", None),
            P("rollout", "copies", None, None, "tensor"),
            P("rollout", "copies", "tensor", None),
            P("rollout", "copies", "tensor", None),
            P("rollout", "copies", "tensor", None),
        ),
        out_specs=(
            P("copies", "tensor", None),
            P("copies", "tensor", None),
            P("copies", "tensor", None),
        ),
        check_vma=False,
    )
```

time: 265 us -> 86.9 us (0.33)
  blocking collectives: 198 us -> 0 us
  Pallas kernels: 0 us -> 38.1 us
  between operations: 17.9 us -> 0.76 us
  starting transfers between devices: 0.08 us -> 11.4 us
  matrix products: 9.56 us -> 0 us
  other arithmetic: 13.8 us -> 5.01 us
  local copies, waits for them, and re-layouts: 4.97 us -> 8.94 us
    all_gather x6 -> x0, blocking collectives: 198 us -> none  [per_device(): lax.all_gather(fetched_a[index], 'tensor', axis=1, tiled=True)]
    pallas_call x0 -> x5, Pallas kernels: none -> 38.1 us  [merge(): pl.pallas_call(functools.partial(merge_kernel, pieces, scale, cols, n_a,...]
    ppermute x0 -> x12, waiting for transfers between devices: none -> 22.1 us  [the longest x4 21.2 us: ring_pass(): return lax.ppermute(array, ('rollout', 'tensor'), ring_perm(n))]
    psum x2 -> x0, waiting for transfers between devices: 20.7 us -> none  [from_root(): return lax.psum(jnp.where(mine, array, jnp.zeros_like(array)), axis)]
    ppermute x0 -> x12, starting transfers between devices: none -> 11.4 us  [the longest x4 9.28 us: ring_pass(): return lax.ppermute(array, ('rollout', 'tensor'), ring_perm(n))]
    dot_general x6 -> x0, matrix products: 9.56 us -> none  [expand(): return jnp.dot(rows_b, piece, preferred_element_type=jnp.float32)]
    another operation x3 -> x0, other arithmetic: 8.91 us -> none  [the longest x1 5.47 us: per_device(): jnp.stack(merged_outputs[0], axis=0)]
    unnamed x24 -> x12, local copies, waits for them, and re-layouts: 3.44 us -> 7.76 us
  transfers between devices with their start and end apart: 2 -> 12, of which waited for: 1 -> 5; matrix products, arithmetic and copies ran while one was open for 5% -> 6% of each run, Pallas kernels for 0% -> 38%
where the time goes in v1:
time: 86.9 us; the launch traced here: 86.3 us
  Pallas kernels  38.1 us (44%)
  waiting for transfers between devices  22.1 us (25%)
  starting transfers between devices  11.4 us (13%)
  local copies, waits for them, and re-layouts  8.94 us (10%)
  other arithmetic  5.01 us (6%)
    pallas_call x5, Pallas kernels, merge(): pl.pallas_call(functools.partial(merge_kernel, pieces, scale, cols, n_a,...  38.1 us
    ppermute x4, waiting for transfers between devices, ring_pass(): return lax.ppermute(array, ('rollout', 'tensor'), ring_perm(n))  21.2 us
    ppermute x4, starting transfers between devices, ring_pass(): return lax.ppermute(array, ('rollout', 'tensor'), ring_perm(n))  9.28 us
    unnamed x12, local copies, waits for them, and re-layouts  7.76 us
    select_n x3, other arithmetic, per_device(): b.append(jnp.where(mine[:, proj, None, None], own_b, swap_cores(own_b)))  2.67 us
    ppermute x8, starting transfers between devices, swap_cores(): return lax.ppermute(array, 'rollout', [(0, 1), (1, 0)])  2.1 us
  transfers between devices with their start and end apart: 12, of which 5 were waited for; matrix products, arithmetic and copies ran while one was open for 6% of the time, Pallas kernels for 38%

profile of v1, /device:TPU:0, one launch (start us, length us, event | category | flops | bytes accessed | tf_op | source)
XLA Modules:
  0.0 86.3 jit_solution(6463555051086783382)
XLA Ops:
  0.6 0.5 collective-permute-start.3
  1.2 0.9 %broadcast_compare_fusion = pred[2,3]{1,0:T(4,128)(4,1)S(1)} fusion(s32[2,3]{1,0:T(2,128)} %param.8, s32[]{:T(128)} %axis_index.25), kind=kLoop, calls=%fused_computation.24 | loop fusion | flops 6 | bytes 34 | tf_op jit(solution)/shard_map/eq | solution.py:137
  2.1 0.9 %collective-permute-done.3 = bf16[2,3,64,640]{3,2,1,0:T(8,128)(2,1)} collective-permute-done((bf16[2,3,64,640]{3,2,1,0:T(8,128)(2,1)}, bf16[2,3,64,640]{3,2,1,0:T(8,128)(2,1)}, u32[]{:S(2)}, u32[]{:S(2)}) %collective-permute-start.3) | collective-permute-done | bytes 491552 | tf_op jit(solution)/shard_map/ppermute | solution.py:32
  3.0 1.3 %broadcast_select_fusion.refs_3_ = bf16[2,3,64,640]{3,2,1,0:T(8,128)(2,1)S(1)} fusion(bf16[2,3,64,640]{3,2,1,0:T(8,128)(2,1)} %collective-permute-done.3, pred[2,3]{1,0:T(4,128)(4,1)S(1)} %broadcast_compare_fusion, bf16[1,2,3,64,640]{4,3,2,1,0:T(8,128)(2,1)} %param.12), kind=kLoop, calls=%fused_computation | loop fusion | flops 245760 | bytes 1474566 | tf_op jit(solution)/shard_map/jit(_where)/select_n | solution.py:140
  4.3 3.0 %collective-permute-start.4 = (bf16[2,3,64,640]{3,2,1,0:T(8,128)(2,1)S(1)}, bf16[2,3,64,640]{3,2,1,0:T(8,128)(2,1)S(1)}, u32[]{:S(2)}, u32[]{:S(2)}) collective-permute-start(bf16[2,3,64,640]{3,2,1,0:T(8,128)(2,1)S(1)} %broadcast_select_fusion.refs_3_), channel_id=1, source_target_pairs={{0,2},{8,9},{2,4},{10,8},{4,6},{12,10},{6,7},{14,12},{7,5},{15,14}... | collective-permute-start | bytes 1474568 | tf_op jit(solution)/shard_map/ppermute | solution.py:28
  7.3 6.8 %collective-permute-done.4.refs_3_ = bf16[2,3,64,640]{3,2,1,0:T(8,128)(2,1)S(1)} collective-permute-done((bf16[2,3,64,640]{3,2,1,0:T(8,128)(2,1)S(1)}, bf16[2,3,64,640]{3,2,1,0:T(8,128)(2,1)S(1)}, u32[]{:S(2)}, u32[]{:S(2)}) %collective-permute-start.4) | collective-permute-done | bytes 491552 | tf_op jit(solution)/shard_map/ppermute | solution.py:28
  14.0 0.8 copy-done.4
  14.8 2.1 %collective-permute-start.5 = (bf16[2,3,64,640]{3,2,1,0:T(8,128)(2,1)S(1)}, bf16[2,3,64,640]{3,2,1,0:T(8,128)(2,1)}, u32[]{:S(2)}, u32[]{:S(2)}) collective-permute-start(bf16[2,3,64,640]{3,2,1,0:T(8,128)(2,1)S(1)} %collective-permute-done.4.refs_3_), channel_id=1, source_target_pairs={{0,2},{8,9},{2,4},{10,8},{4,6},{12,10},{6,7},{14,12},{7,5},{15,14}... | collective-permute-start | bytes 1474568 | tf_op jit(solution)/shard_map/ppermute | solution.py:28
  16.9 6.9 %collective-permute-done.5.refs_3_ = bf16[2,3,64,640]{3,2,1,0:T(8,128)(2,1)} collective-permute-done((bf16[2,3,64,640]{3,2,1,0:T(8,128)(2,1)S(1)}, bf16[2,3,64,640]{3,2,1,0:T(8,128)(2,1)}, u32[]{:S(2)}, u32[]{:S(2)}) %collective-permute-start.5) | collective-permute-done | bytes 491552 | tf_op jit(solution)/shard_map/ppermute | solution.py:28
  23.8 2.1 %collective-permute-start.6 = (bf16[2,3,64,640]{3,2,1,0:T(8,128)(2,1)}, bf16[2,3,64,640]{3,2,1,0:T(8,128)(2,1)}, u32[]{:S(2)}, u32[]{:S(2)}) collective-permute-start(bf16[2,3,64,640]{3,2,1,0:T(8,128)(2,1)} %collective-permute-done.5.refs_3_), channel_id=1, source_target_pairs={{0,2},{8,9},{2,4},{10,8},{4,6},{12,10},{6,7},{14,12},{7,5},{15,14}... | collective-permute-start | bytes 1474568 | tf_op jit(solution)/shard_map/ppermute | solution.py:28
  25.9 0.5 collective-permute-start.2
  26.4 0.1 pad_add_fusion.places
  26.5 0.2 slice_reduce_fusion
  26.7 0.6 collective-permute-start.11
  27.3 5.7 %collective-permute-done.6.refs_3_ = bf16[2,3,64,640]{3,2,1,0:T(8,128)(2,1)} collective-permute-done((bf16[2,3,64,640]{3,2,1,0:T(8,128)(2,1)}, bf16[2,3,64,640]{3,2,1,0:T(8,128)(2,1)}, u32[]{:S(2)}, u32[]{:S(2)}) %collective-permute-start.6) | collective-permute-done | bytes 491552 | tf_op jit(solution)/shard_map/ppermute | solution.py:28
  32.9 1.0 %constant_dynamic-slice_fusion = bf16[1,3,64,640]{3,2,1,0:T(8,128)(2,1)S(1)} fusion(bf16[2,3,64,640]{3,2,1,0:T(8,128)(2,1)} %collective-permute-done.6.refs_3_, s32[]{:T(128)S(6)} %select_n.73), kind=kLoop, calls=%fused_computation.25 | loop fusion | bytes 491524 | tf_op jit(solution)/shard_map/dynamic_slice | solution.py:152
  33.9 2.1 %collective-permute-start.7 = (bf16[1,3,64,640]{3,2,1,0:T(8,128)(2,1)S(1)}, bf16[1,3,64,640]{3,2,1,0:T(8,128)(2,1)S(1)}, u32[]{:S(2)}, u32[]{:S(2)}) collective-permute-start(bf16[1,3,64,640]{3,2,1,0:T(8,128)(2,1)S(1)} %constant_dynamic-slice_fusion), channel_id=1, source_target_pairs={{0,2},{8,9},{2,4},{10,8},{4,6},{12,10},{6,7},{14,12},{7,5},{15,14}... | collective-permute-start | bytes 737288 | tf_op jit(solution)/shard_map/ppermute | solution.py:28
  36.0 0.8 broadcast_select_fusion.2.refs_2_
  36.9 0.0 collective-permute-start.10
  36.9 0.5 collective-permute-start.9
  37.4 0.8 broadcast_select_fusion.3.refs_1_
  38.2 1.9 %collective-permute-done.7.refs_3_ = bf16[1,3,64,640]{3,2,1,0:T(8,128)(2,1)S(1)} collective-permute-done((bf16[1,3,64,640]{3,2,1,0:T(8,128)(2,1)S(1)}, bf16[1,3,64,640]{3,2,1,0:T(8,128)(2,1)S(1)}, u32[]{:S(2)}, u32[]{:S(2)}) %collective-permute-start.7) | collective-permute-done | bytes 245792 | tf_op jit(solution)/shard_map/ppermute | solution.py:28
  40.2 1.0 %broadcast_select_fusion.1.refs_0_ = bf16[2,64,640]{2,1,0:T(8,128)(2,1)S(1)} fusion(bf16[2,64,640]{2,1,0:T(8,128)(2,1)S(1)} %collective-permute-done, pred[2]{0:T(512)(128)(4,1)S(1)} %get-tuple-element.29, bf16[1,2,640,64]{2,3,1,0:T(8,128)(2,1)} %param.13), kind=kLoop, calls=%fused_computation.1 | loop fusion | flops 81920 | bytes 491522 | tf_op jit(solution)/shard_map/jit(_where)/select_n | solution.py:144
  41.2 4.7 %copy-done = bf16[2,640,5120]{2,1,0:T(8,128)(2,1)S(1)} copy-done((bf16[2,640,5120]{2,1,0:T(8,128)(2,1)S(1)}, bf16[2,640,5120]{2,1,0:T(8,128)(2,1)}, u32[]{:S(2)}) %copy-start) | copy-done | bytes 13107224
  45.9 1.7 %copy-done.3 = bf16[2,128,5120]{2,1,0:T(8,128)(2,1)S(1)} copy-done((bf16[2,128,5120]{2,1,0:T(8,128)(2,1)S(1)}, bf16[2,128,5120]{2,1,0:T(8,128)(2,1)}, u32[]{:S(2)}) %copy-start.3) | copy-done | bytes 2621464
  47.6 5.1 %shard_map.103 = (bf16[2,640,5120]{2,1,0:T(8,128)(2,1)}, bf16[2,128,5120]{2,1,0:T(8,128)(2,1)}, bf16[2,128,5120]{2,1,0:T(8,128)(2,1)}) custom-call(s32[9]{0:T(128)S(1)} %pad_add_fusion.places, bf16[2,64,640]{2,1,0:T(8,128)(2,1)S(1)} %broadcast_select_fusion.1.refs_0_, bf16[2,64,128]{2,1,0:T(8,128)(2,1)S(1)} %broadcast_select_fusion.3.refs_1_, ...), custom_call_target="tpu_custom_call" | custom-call | flops 146800640 | bytes 4587520 | tf_op jit(solution)/shard_map/pallas_call | solution.py:101
  52.7 0.5 copy-done.1
  53.2 0.0 copy-done.5
  53.2 9.0 %shard_map.104 = (bf16[2,640,5120]{2,1,0:T(8,128)(2,1)}, bf16[2,128,5120]{2,1,0:T(8,128)(2,1)}, bf16[2,128,5120]{2,1,0:T(8,128)(2,1)}) custom-call(s32[9]{0:T(128)S(1)} %pad_add_fusion.places, bf16[2,64,640]{2,1,0:T(8,128)(2,1)S(1)} %broadcast_select_fusion.1.refs_0_, ...), custom_call_target="tpu_custom_call", output_to_operand_aliasing={{0}: (9, {}), {1}: (10, {}), {2}: (11, {})} | custom-call | flops 293601280 | bytes 9175040 | tf_op jit(solution)/shard_map/pallas_call | solution.py:101
  62.2 9.5 %shard_map.105 = (bf16[2,640,5120]{2,1,0:T(8,128)(2,1)}, bf16[2,128,5120]{2,1,0:T(8,128)(2,1)}, bf16[2,128,5120]{2,1,0:T(8,128)(2,1)}) custom-call(s32[9]{0:T(128)S(1)} %pad_add_fusion.places, bf16[2,64,640]{2,1,0:T(8,128)(2,1)S(1)} %broadcast_select_fusion.1.refs_0_, ...), custom_call_target="tpu_custom_call", output_to_operand_aliasing={{0}: (9, {}), {1}: (10, {}), {2}: (11, {})} | custom-call | flops 293601280 | bytes 9175040 | tf_op jit(solution)/shard_map/pallas_call | solution.py:101
  71.7 9.5 %shard_map.106 = (bf16[2,640,5120]{2,1,0:T(8,128)(2,1)}, bf16[2,128,5120]{2,1,0:T(8,128)(2,1)}, bf16[2,128,5120]{2,1,0:T(8,128)(2,1)}) custom-call(s32[9]{0:T(128)S(1)} %pad_add_fusion.places, bf16[2,64,640]{2,1,0:T(8,128)(2,1)S(1)} %broadcast_select_fusion.1.refs_0_, ...), custom_call_target="tpu_custom_call", output_to_operand_aliasing={{0}: (9, {}), {1}: (10, {}), {2}: (11, {})} | custom-call | flops 293601280 | bytes 9175040 | tf_op jit(solution)/shard_map/pallas_call | solution.py:101
  81.2 5.1 %shard_map.107 = (bf16[2,640,5120]{2,1,0:T(8,128)(2,1)}, bf16[2,128,5120]{2,1,0:T(8,128)(2,1)}, bf16[2,128,5120]{2,1,0:T(8,128)(2,1)}) custom-call(s32[9]{0:T(128)S(1)} %pad_add_fusion.places, bf16[2,64,640]{2,1,0:T(8,128)(2,1)S(1)} %broadcast_select_fusion.1.refs_0_, ...), custom_call_target="tpu_custom_call", output_to_operand_aliasing={{0}: (9, {}), {1}: (10, {}), {2}: (11, {})} | custom-call | flops 146800640 | bytes 4587520 | tf_op jit(solution)/shard_map/pallas_call | solution.py:101
  (18 shorter events, 0.1 us)
Async XLA Ops:
  0.6 40.5 %copy-start.2 = (bf16[2,128,5120]{2,1,0:T(8,128)(2,1)S(1)}, bf16[2,128,5120]{2,1,0:T(8,128)(2,1)}, u32[]{:S(2)}) copy-start(bf16[2,128,5120]{2,1,0:T(8,128)(2,1)} %refs_6_.9) | copy-start | bytes 7864324
  0.6 2.4 %collective-permute-start.3 = (bf16[2,3,64,640]{3,2,1,0:T(8,128)(2,1)}, bf16[2,3,64,640]{3,2,1,0:T(8,128)(2,1)}, u32[]{:S(2)}, u32[]{:S(2)}) collective-permute-start(bf16[2,3,64,640]{3,2,1,0:T(8,128)(2,1)} %bitcast.15), channel_id=1, source_target_pairs={{0,8},{8,0},{1,9},{9,1},{2,10},{10,2},{3,11},{11,3},{4,12},{12,4},... | collective-permute-start | bytes 1474568 | tf_op jit(solution)/shard_map/ppermute | solution.py:32
  4.3 9.8 %collective-permute-start.4 = (bf16[2,3,64,640]{3,2,1,0:T(8,128)(2,1)S(1)}, bf16[2,3,64,640]{3,2,1,0:T(8,128)(2,1)S(1)}, u32[]{:S(2)}, u32[]{:S(2)}) collective-permute-start(bf16[2,3,64,640]{3,2,1,0:T(8,128)(2,1)S(1)} %broadcast_select_fusion.refs_3_), channel_id=1, source_target_pairs={{0,2},{8,9},{2,4},{10,8},{4,6},{12,10},{6,7},{14,12},{7,5},{15,14}... | collective-permute-start | bytes 1474568 | tf_op jit(solution)/shard_map/ppermute | solution.py:28
  14.0 0.8 copy-start.4
  14.8 8.9 %collective-permute-start.5 = (bf16[2,3,64,640]{3,2,1,0:T(8,128)(2,1)S(1)}, bf16[2,3,64,640]{3,2,1,0:T(8,128)(2,1)}, u32[]{:S(2)}, u32[]{:S(2)}) collective-permute-start(bf16[2,3,64,640]{3,2,1,0:T(8,128)(2,1)S(1)} %collective-permute-done.4.refs_3_), channel_id=1, source_target_pairs={{0,2},{8,9},{2,4},{10,8},{4,6},{12,10},{6,7},{14,12},{7,5},{15,14}... | collective-permute-start | bytes 1474568 | tf_op jit(solution)/shard_map/ppermute | solution.py:28
  23.8 9.1 %collective-permute-start.6 = (bf16[2,3,64,640]{3,2,1,0:T(8,128)(2,1)}, bf16[2,3,64,640]{3,2,1,0:T(8,128)(2,1)}, u32[]{:S(2)}, u32[]{:S(2)}) collective-permute-start(bf16[2,3,64,640]{3,2,1,0:T(8,128)(2,1)} %collective-permute-done.5.refs_3_), channel_id=1, source_target_pairs={{0,2},{8,9},{2,4},{10,8},{4,6},{12,10},{6,7},{14,12},{7,5},{15,14}... | collective-permute-start | bytes 1474568 | tf_op jit(solution)/shard_map/ppermute | solution.py:28
  25.9 14.3 %collective-permute-start = (bf16[2,64,640]{2,1,0:T(8,128)(2,1)}, bf16[2,64,640]{2,1,0:T(8,128)(2,1)S(1)}, u32[]{:S(2)}, u32[]{:S(2)}) collective-permute-start(bf16[2,64,640]{2,1,0:T(8,128)(2,1)} %bitcast.16), channel_id=1, source_target_pairs={{0,8},{8,0},{1,9},{9,1},{2,10},{10,2},{3,11},{11,3},{4,12},{12,4},... | collective-permute-start | bytes 491528 | tf_op jit(solution)/shard_map/ppermute | solution.py:32
  25.9 10.2 %collective-permute-start.2 = (bf16[2,64,128]{2,1,0:T(8,128)(2,1)}, bf16[2,64,128]{2,1,0:T(8,128)(2,1)S(1)}, u32[]{:S(2)}, u32[]{:S(2)}) collective-permute-start(bf16[2,64,128]{2,1,0:T(8,128)(2,1)} %bitcast.17), channel_id=1, source_target_pairs={{0,8},{8,0},{1,9},{9,1},{2,10},{10,2},{3,11},{11,3},{4,12},{12,4},... | collective-permute-start | bytes 98312 | tf_op jit(solution)/shard_map/ppermute | solution.py:32
  26.4 10.5 %collective-permute-start.1 = (bf16[2,64,128]{2,1,0:T(8,128)(2,1)}, bf16[2,64,128]{2,1,0:T(8,128)(2,1)S(1)}, u32[]{:S(2)}, u32[]{:S(2)}) collective-permute-start(bf16[2,64,128]{2,1,0:T(8,128)(2,1)} %bitcast.18), channel_id=1, source_target_pairs={{0,8},{8,0},{1,9},{9,1},{2,10},{10,2},{3,11},{11,3},{4,12},{12,4},... | collective-permute-start | bytes 98312 | tf_op jit(solution)/shard_map/ppermute | solution.py:32
  26.7 26.1 %collective-permute-start.11 = (bf16[2,3,64,640]{3,2,1,0:T(8,128)(2,1)}, bf16[2,3,64,640]{3,2,1,0:T(8,128)(2,1)S(1)}, u32[]{:S(2)}, u32[]{:S(2)}) collective-permute-start(bf16[2,3,64,640]{3,2,1,0:T(8,128)(2,1)} %copy-done.4), channel_id=1, source_target_pairs={{0,8},{8,0},{1,9},{9,1},{2,10},{10,2},{3,11},{11,3},{4,12},{12,4},... | collective-permute-start | bytes 1474568 | tf_op jit(solution)/shard_map/ppermute | solution.py:32
  33.9 6.2 %collective-permute-start.7 = (bf16[1,3,64,640]{3,2,1,0:T(8,128)(2,1)S(1)}, bf16[1,3,64,640]{3,2,1,0:T(8,128)(2,1)S(1)}, u32[]{:S(2)}, u32[]{:S(2)}) collective-permute-start(bf16[1,3,64,640]{3,2,1,0:T(8,128)(2,1)S(1)} %constant_dynamic-slice_fusion), channel_id=1, source_target_pairs={{0,2},{8,9},{2,4},{10,8},{4,6},{12,10},{6,7},{14,12},{7,5},{15,14}... | collective-permute-start | bytes 737288 | tf_op jit(solution)/shard_map/ppermute | solution.py:28
  36.9 25.3 %collective-permute-start.10 = (bf16[2,3,64,640]{3,2,1,0:T(8,128)(2,1)}, bf16[2,3,64,640]{3,2,1,0:T(8,128)(2,1)S(1)}, u32[]{:S(2)}, u32[]{:S(2)}) collective-permute-start(bf16[2,3,64,640]{3,2,1,0:T(8,128)(2,1)} %collective-permute-done.5.refs_3_), channel_id=1, source_target_pairs={{0,8},{8,0},{1,9},{9,1},{2,10},{10,2},{3,11},{11,3},{4,12},{12,4},... | collective-permute-start | bytes 1474568 | tf_op jit(solution)/shard_map/ppermute | solution.py:32
  36.9 34.8 %collective-permute-start.9 = (bf16[2,3,64,640]{3,2,1,0:T(8,128)(2,1)}, bf16[2,3,64,640]{3,2,1,0:T(8,128)(2,1)S(1)}, u32[]{:S(2)}, u32[]{:S(2)}) collective-permute-start(bf16[2,3,64,640]{3,2,1,0:T(8,128)(2,1)} %collective-permute-done.6.refs_3_), channel_id=1, source_target_pairs={{0,8},{8,0},{1,9},{9,1},{2,10},{10,2},{3,11},{11,3},{4,12},{12,4},... | collective-permute-start | bytes 1474568 | tf_op jit(solution)/shard_map/ppermute | solution.py:32
  40.1 41.0 %collective-permute-start.8 = (bf16[1,3,64,640]{3,2,1,0:T(8,128)(2,1)S(1)}, bf16[1,3,64,640]{3,2,1,0:T(8,128)(2,1)S(1)}, u32[]{:S(2)}, u32[]{:S(2)}) collective-permute-start(bf16[1,3,64,640]{3,2,1,0:T(8,128)(2,1)S(1)} %collective-permute-done.7.refs_3_), channel_id=1, source_target_pairs={{0,8},{8,0},{1,9},{9,1},{2,10},{10,2},{3,11},{11,3},{4,12},{12,4},... | collective-permute-start | bytes 737288 | tf_op jit(solution)/shard_map/ppermute | solution.py:32
  41.2 4.7 %copy-start = (bf16[2,640,5120]{2,1,0:T(8,128)(2,1)S(1)}, bf16[2,640,5120]{2,1,0:T(8,128)(2,1)}, u32[]{:S(2)}) copy-start(bf16[2,640,5120]{2,1,0:T(8,128)(2,1)} %refs_5_.9) | copy-start | bytes 39321604
  45.9 1.7 %copy-start.3 = (bf16[2,128,5120]{2,1,0:T(8,128)(2,1)S(1)}, bf16[2,128,5120]{2,1,0:T(8,128)(2,1)}, u32[]{:S(2)}) copy-start(bf16[2,128,5120]{2,1,0:T(8,128)(2,1)} %refs_7_.7) | copy-start | bytes 7864324
  47.6 5.6 %copy-start.1 = (bf16[2,640,5120]{2,1,0:T(8,128)(2,1)S(1)}, bf16[2,640,5120]{2,1,0:T(8,128)(2,1)}, u32[]{:S(2)}) copy-start(bf16[2,640,5120]{2,1,0:T(8,128)(2,1)} %refs_5_.9) | copy-start | bytes 39321604
  47.6 5.6 %copy-start.5 = (bf16[2,3,64,640]{3,2,1,0:T(8,128)(2,1)S(1)}, bf16[2,3,64,640]{3,2,1,0:T(8,128)(2,1)}, u32[]{:S(2)}) copy-start(bf16[2,3,64,640]{3,2,1,0:T(8,128)(2,1)} %copy-done.4) | copy-start | bytes 1474564

commit v2 on v1

v2 whole, which is shorter than its diff:
```python
import functools

import jax
import jax.numpy as jnp
from jax import lax
from jax.experimental import pallas as pl
from jax.experimental.pallas import tpu as pltpu
from jax.sharding import PartitionSpec as P

numerator_gain = 16.0
LANES = 128


def ring_order(n):
    return list(range(0, n, 2)) + list(range(n - 1, 0, -2))


def ring_pass(array, n):
    order = ring_order(n)
    pairs = []
    for k in range(n):
        pairs.append((order[k], order[(k + 1) % n]))
        pairs.append((n + order[k], n + order[(k - 1) % n]))
    return lax.ppermute(array, ("rollout", "tensor"), pairs)


def swap_cores(array):
    return lax.ppermute(array, "rollout", [(0, 1), (1, 0)])


def chunk_places(n, core, tensor):
    position = jnp.where(tensor % 2 == 0, tensor // 2, n - 1 - tensor // 2)
    slot = jnp.arange(n, dtype=jnp.int32)
    step = (slot + 1) // 2
    backward = (slot + core) % 2 == 1
    k = jnp.where(slot == 0, position, position + jnp.where(backward, -step, step))
    k = (k + n) % n
    return jnp.where(k < n // 2, 2 * k, 2 * n - 1 - 2 * k).astype(jnp.int32)


def start_chosen(mine, own, other, target, sem):
    copy = pltpu.make_async_copy(own, target, sem)
    pl.when(mine)(copy.start)
    pl.when(jnp.logical_not(mine))(pltpu.make_async_copy(other, target, sem).start)
    return copy


def choose_a_kernel(n, places, own, other, first, second, sems):
    core = places[n]
    projs = own.shape[1]
    copies = []
    for i, (out, layer) in enumerate(((first, core), (second, 1 - core))):
        for proj in range(projs):
            mine = places[n + 1 + layer * 3 + proj] == core
            target = out.at[proj]
            copies.append(
                start_chosen(mine, own.at[layer, proj], other.at[layer, proj], target, sems.at[i * projs + proj])
            )
    for copy in copies:
        copy.wait()


def choose_a(places, n, own, other):
    smem = pl.BlockSpec(memory_space=pltpu.SMEM)
    vmem = pl.BlockSpec(memory_space=pltpu.VMEM)
    anywhere = pl.BlockSpec(memory_space=pl.ANY)
    piece = jax.ShapeDtypeStruct(own.shape[1:], own.dtype)
    return pl.pallas_call(
        functools.partial(choose_a_kernel, n),
        in_specs=[smem, anywhere, anywhere],
        out_specs=[vmem, vmem],
        out_shape=[piece, piece],
        scratch_shapes=[pltpu.SemaphoreType.DMA((own.shape[0] * own.shape[1],))],
    )(places, pltpu.with_memory_space_constraint(own, pltpu.HBM), other)


def choose_b_kernel(n, places, *refs):
    core = places[n]
    sems = refs[12]
    copies = []
    for proj in range(3):
        own, other, held = refs[proj], refs[3 + proj], refs[9 + proj]
        for layer in range(own.shape[0]):
            mine = places[n + 1 + layer * 3 + proj] == core
            copies.append(
                start_chosen(mine, own.at[layer], other.at[layer], held.at[layer], sems.at[layer * 3 + proj])
            )
    for proj in range(3):
        out, held = refs[6 + proj], refs[9 + proj]
        for layer in range(held.shape[0]):
            copies.pop(0).wait()
            out[layer] = held[layer].T


def choose_b(places, n, own, other):
    smem = pl.BlockSpec(memory_space=pltpu.SMEM)
    vmem = pl.BlockSpec(memory_space=pltpu.VMEM)
    anywhere = pl.BlockSpec(memory_space=pl.ANY)
    shapes = [jax.ShapeDtypeStruct((x.shape[0], x.shape[2], x.shape[1]), x.dtype) for x in own]
    return pl.pallas_call(
        functools.partial(choose_b_kernel, n),
        in_specs=[smem] + [anywhere] * 6,
        out_specs=[vmem] * 3,
        out_shape=shapes,
        scratch_shapes=[pltpu.VMEM(x.shape, x.dtype) for x in own] + [pltpu.SemaphoreType.DMA((3 * own[0].shape[0],))],
    )(places, *[pltpu.with_memory_space_constraint(x, pltpu.HBM) for x in own], *other)


def merge_kernel(n, pieces, scale, cols, n_a, fresh, places, *refs):
    b_refs = refs[:3]
    a_refs = refs[3 : 3 + n_a]
    bases = refs[3 + n_a : 6 + n_a]
    at = 6 + n_a + (0 if fresh else 3)
    outs = refs[at : at + 3]
    bufs = refs[at + 3 : at + 6]
    load_sem, store_sem = refs[at + 6 : at + 8]
    core = places[n]
    tasks = []
    for i, (slot, a_index, own) in enumerate(pieces):
        layer = core if own else 1 - core
        columns = pl.ds(pl.multiple_of(places[slot] * cols, LANES), cols)
        for proj in range(3):
            tasks.append((i, proj, layer, columns, a_index))

    def load(j):
        i, proj, layer, columns, _ = tasks[j]
        return pltpu.make_async_copy(bases[proj].at[layer, :, columns], bufs[proj].at[i], load_sem.at[j])

    def store(j):
        i, proj, layer, columns, _ = tasks[j]
        return pltpu.make_async_copy(bufs[proj].at[i], outs[proj].at[layer, :, columns], store_sem.at[j])

    for j in range(len(tasks)):
        load(j).start()
    for j in range(len(tasks)):
        i, proj, layer, _, a_index = tasks[j]
        load(j).wait()
        delta = jnp.dot(b_refs[proj][layer], a_refs[a_index][proj], preferred_element_type=jnp.float32)
        merged = bufs[proj][i].astype(jnp.float32) + scale * delta
        bufs[proj][i] = merged.astype(jnp.bfloat16)
        store(j).start()
    for j in range(len(tasks)):
        store(j).wait()


def merge(n, places, b, a_list, bases, outs, pieces, scale, cols):
    fresh = outs is None
    n_a = len(a_list)
    tasks = 3 * len(pieces)
    vmem = pl.BlockSpec(memory_space=pltpu.VMEM)
    hbm = pl.BlockSpec(memory_space=pltpu.HBM)
    held = [pltpu.with_memory_space_constraint(base, pltpu.HBM) for base in bases]
    operands = [places, *b, *a_list, *held] + ([] if fresh else list(outs))
    rows = sum(base.shape[1] for base in bases)
    rank = a_list[0].shape[1]
    return pl.pallas_call(
        functools.partial(merge_kernel, n, pieces, scale, cols, n_a, fresh),
        in_specs=[pl.BlockSpec(memory_space=pltpu.SMEM)] + [vmem] * (3 + n_a) + [hbm] * (3 if fresh else 6),
        out_specs=[hbm] * 3,
        out_shape=[jax.ShapeDtypeStruct(base.shape, base.dtype) for base in bases],
        scratch_shapes=[pltpu.VMEM((len(pieces), base.shape[1], cols), base.dtype) for base in bases]
        + [pltpu.SemaphoreType.DMA((tasks,)), pltpu.SemaphoreType.DMA((tasks,))],
        input_output_aliases={} if fresh else {7 + n_a + i: i for i in range(3)},
        compiler_params=pltpu.CompilerParams(vmem_limit_bytes=16 * 1024 * 1024),
        cost_estimate=pl.CostEstimate(
            flops=2 * len(pieces) * rows * cols * rank,
            bytes_accessed=4 * len(pieces) * rows * cols,
            transcendentals=0,
        ),
    )(*operands)


def after(array, outs):
    array, outs = lax.optimization_barrier((array, outs))
    return array, outs


def per_device(
    n,
    owners,
    base_query,
    base_key,
    base_value,
    left_shared_matrix,
    right_queries_matrix,
    right_keys_matrix,
    right_values_matrix,
):
    layers, projs, rank, cols = left_shared_matrix.shape[1:]
    scale = numerator_gain / rank
    bases = (base_query, base_key, base_value)
    core = lax.axis_index("rollout")
    tensor = lax.axis_index("tensor")
    places = jnp.concatenate([chunk_places(n, core, tensor), core[None].astype(jnp.int32), owners.reshape(-1)])

    own_a = left_shared_matrix[0]
    first, second = choose_a(places, n, own_a, swap_cores(own_a))
    own_b = [jnp.swapaxes(right[0], 1, 2) for right in (right_queries_matrix, right_keys_matrix, right_values_matrix)]
    b = choose_b(places, n, own_b, [swap_cores(x) for x in own_b])

    if cols % LANES == 0:
        held = [first, second]
        last = n // 2
        ready = []
        first = ring_pass(first, n)
        second = ring_pass(second, n)
        first, b = lax.optimization_barrier((first, b))
        go = functools.partial(merge, n, places, b, bases=bases, scale=scale, cols=cols)
        outs = go(held, outs=None, pieces=[(0, 0, True), (0, 1, False)])
        for step in range(1, last + 1):
            slot = 2 * step - 1
            if step > 1:
                chunks, pieces = ready.pop(0)
                outs = go(chunks, outs=outs, pieces=pieces)
            ready.append(([first, swap_cores(first)], [(slot, 0, True), (min(slot + 1, n - 1), 1, False)]))
            if step < last:
                first = ring_pass(first, n)
                second, outs = after(second, outs)
                ready.append(([second, swap_cores(second)], [(slot, 0, False), (slot + 1, 1, True)]))
                chunks, pieces = ready.pop(0)
                outs = go(chunks, outs=outs, pieces=pieces)
                first, outs = after(first, outs)
                if step < last - 1:
                    second = ring_pass(second, n)
        for chunks, pieces in ready:
            outs = go(chunks, outs=outs, pieces=pieces)
        return tuple(outs)

    full = jnp.zeros((layers, projs, rank, n * cols), own_a.dtype)

    def put(full, piece, layer, slot):
        return lax.dynamic_update_slice(full, piece[None], (layer, 0, 0, places[slot] * cols))

    full = put(full, first, core, 0)
    full = put(full, second, 1 - core, 0)
    for step in range(1, n // 2 + 1):
        slot = 2 * step - 1
        first = ring_pass(first, n)
        full = put(full, first, core, slot)
        full = put(full, swap_cores(first), 1 - core, min(slot + 1, n - 1))
        if step < n // 2:
            second = ring_pass(second, n)
            full = put(full, second, 1 - core, slot)
            full = put(full, swap_cores(second), core, slot + 1)
    merged = []
    for proj in range(projs):
        delta = jnp.einsum("lrk,lkc->lrc", b[proj], full[:, proj], preferred_element_type=jnp.float32)
        merged.append((bases[proj].astype(jnp.float32) + scale * delta).astype(jnp.bfloat16))
    return tuple(merged)


def solution(mesh):
    return jax.shard_map(
        functools.partial(per_device, mesh.shape["tensor"]),
        mesh=mesh,
        in_specs=(
            P("copies", None),
            P("copies", "tensor", None),
            P("copies", "tensor", None),
            P("copies", "tensor", None),
            P("rollout", "copies", None, None, "tensor"),
            P("rollout", "copies", "tensor", None),
            P("rollout", "copies", "tensor", None),
            P("rollout", "copies", "tensor", None),
        ),
        out_specs=(
            P("copies", "tensor", None),
            P("copies", "tensor", None),
            P("copies", "tensor", None),
        ),
        check_vma=False,
    )
```

time: 86.9 us -> 61.9 us (0.71)
  waiting for transfers between devices: 22.1 us -> 0.3 us
  other arithmetic: 5.01 us -> 0.69 us
  starting transfers between devices: 11.4 us -> 13.6 us
  local copies, waits for them, and re-layouts: 8.94 us -> 8.02 us
    ppermute x4 -> x7, waiting for transfers between devices: 21.2 us -> 0.02 us  [ring_pass(): return lax.ppermute(array, ('rollout', 'tensor'), pairs)]
    select_n x4 -> x0, other arithmetic: 3.97 us -> none  [the longest x3 2.67 us: per_device(): b.append(jnp.where(mine[:, proj, None, None], own_b, swap_cores(own_b)))]
    ppermute x4 -> x7, starting transfers between devices: 9.28 us -> 11.5 us  [ring_pass(): return lax.ppermute(array, ('rollout', 'tensor'), pairs)]
    dynamic_slice x1 -> x0, local copies, waits for them, and re-layouts: 0.97 us -> none  [per_device(): last = lax.dynamic_slice_in_dim(held, core * half, half, 0)]
    eq x1 -> x0, other arithmetic: 0.94 us -> none  [per_device(): mine = owners == core]
    unnamed x12 -> x20, local copies, waits for them, and re-layouts: 7.76 us -> 7.26 us
    pallas_call x5 -> x10, Pallas kernels: 38.1 us -> 37.8 us  [the longest x8 32.5 us: merge(): pl.pallas_call(functools.partial(merge_kernel, n, pieces, scale, cols, n_...]
    ppermute x8 -> x11, starting transfers between devices: 2.1 us -> 2.02 us  [swap_cores(): return lax.ppermute(array, 'rollout', [(0, 1), (1, 0)])]
  transfers between devices with their start and end apart: 12 -> 18, of which waited for: 5 -> 1; matrix products, arithmetic and copies ran while one was open for 6% -> 2% of each run, Pallas kernels for 38% -> 51%
where the time goes in v2:
time: 61.9 us; the launch traced here: 61.2 us
  Pallas kernels  37.8 us (61%)
  starting transfers between devices  13.6 us (22%)
  local copies, waits for them, and re-layouts  8.02 us (13%)
  between operations  0.84 us (1%)
  other arithmetic  0.69 us (1%)
    pallas_call x8, Pallas kernels, merge(): pl.pallas_call(functools.partial(merge_kernel, n, pieces, scale, cols, n_...  32.5 us
    ppermute x7, starting transfers between devices, ring_pass(): return lax.ppermute(array, ('rollout', 'tensor'), pairs)  11.5 us
    unnamed x20, local copies, waits for them, and re-layouts  7.26 us
    pallas_call x1, Pallas kernels, choose_b(): pl.pallas_call(functools.partial(choose_b_kernel, n), in_specs=[smem] + [...  2.78 us
    pallas_call x1, Pallas kernels, choose_a(): pl.pallas_call(functools.partial(choose_a_kernel, n), in_specs=[smem, any...  2.58 us
    ppermute x11, starting transfers between devices, swap_cores(): return lax.ppermute(array, 'rollout', [(0, 1), (1, 0)])  2.02 us
  transfers between devices with their start and end apart: 18, of which 1 were waited for; matrix products, arithmetic and copies ran while one was open for 2% of the time, Pallas kernels for 51%

profile of v2, /device:TPU:0, one launch (start us, length us, event | category | flops | bytes accessed | tf_op | source)
XLA Modules:
  0.0 61.2 jit_solution(8529510218451595402)
XLA Ops:
  0.6 0.5 collective-permute-start
  1.1 0.8 %reshape.9 = s32[6]{0:T(128)S(1)} reshape(s32[2,3]{1,0:T(2,128)} %param.8) | data formatting | bytes 48 | tf_op jit(solution)/shard_map/reshape | solution.py:194
  1.9 0.7 %pad_add_fusion.places = s32[15]{0:T(128)} fusion(s32[6]{0:T(128)S(1)} %reshape.9, s32[1]{0:T(128)} %bitcast, s32[8]{0:T(128)S(1)} %compare_select_fusion.4), kind=kLoop, calls=%fused_computation.16 | loop fusion | flops 30 | bytes 120 | tf_op jit(solution)/shard_map/concatenate | solution.py:194
  2.6 0.3 collective-permute-done.other
  2.9 0.8 %copy-done.6 = bf16[2,3,64,640]{3,2,1,0:T(8,128)(2,1)} copy-done((bf16[2,3,64,640]{3,2,1,0:T(8,128)(2,1)}, bf16[2,3,64,640]{3,2,1,0:T(8,128)(2,1)S(1)}, u32[]{:S(2)}) %copy-start.6) | copy-done | bytes 491544
  3.6 2.6 %shard_map.103 = (bf16[3,64,640]{2,1,0:T(8,128)(2,1)}, bf16[3,64,640]{2,1,0:T(8,128)(2,1)}) custom-call(s32[15]{0:T(128)} %pad_add_fusion.places, bf16[2,3,64,640]{3,2,1,0:T(8,128)(2,1)} %bitcast.12, bf16[2,3,64,640]{3,2,1,0:T(8,128)(2,1)} %copy-done.6), custom_call_target="tpu_custom_call" | custom-call | tf_op jit(solution)/shard_map/pallas_call | solution.py:68
  6.2 3.0 %collective-permute-start.1 = (bf16[3,64,640]{2,1,0:T(8,128)(2,1)}, bf16[3,64,640]{2,1,0:T(8,128)(2,1)S(1)}, u32[]{:S(2)}, u32[]{:S(2)}) collective-permute-start(bf16[3,64,640]{2,1,0:T(8,128)(2,1)} %get-tuple-element.57.refs_3_), channel_id=1, source_target_pairs={{0,2},{8,9},{2,4},{10,8},{4,6},{12,10},{6,7},{14,12},{7,5},{15,14}... | collective-permute-start | bytes 737288 | tf_op jit(solution)/shard_map/ppermute | solution.py:24
  9.2 0.5 collective-permute-start.3
  9.7 1.6 %collective-permute-start.7 = (bf16[3,64,640]{2,1,0:T(8,128)(2,1)}, bf16[3,64,640]{2,1,0:T(8,128)(2,1)S(1)}, u32[]{:S(2)}, u32[]{:S(2)}) collective-permute-start(bf16[3,64,640]{2,1,0:T(8,128)(2,1)} %get-tuple-element.65.refs_4_), channel_id=1, source_target_pairs={{0,2},{8,9},{2,4},{10,8},{4,6},{12,10},{6,7},{14,12},{7,5},{15,14}... | collective-permute-start | bytes 737288 | tf_op jit(solution)/shard_map/ppermute | solution.py:24
  11.3 0.6 copy-done.8
  11.9 0.7 %copy-done.7 = bf16[2,64,640]{2,1,0:T(8,128)(2,1)} copy-done((bf16[2,64,640]{2,1,0:T(8,128)(2,1)}, bf16[2,64,640]{2,1,0:T(8,128)(2,1)S(1)}, u32[]{:S(2)}) %copy-start.7) | copy-done | bytes 163864
  12.6 2.8 %shard_map.104 = (bf16[2,640,64]{2,1,0:T(8,128)(2,1)}, bf16[2,128,64]{2,1,0:T(8,128)(2,1)}, bf16[2,128,64]{2,1,0:T(8,128)(2,1)}) custom-call(s32[15]{0:T(128)} %pad_add_fusion.places, bf16[2,64,640]{2,1,0:T(8,128)(2,1)} %bitcast.14, bf16[2,64,128]{2,1,0:T(8,128)(2,1)} %bitcast.16, bf16[2,64,128]{2,1,0:T(8,128)(2,1)} %bitcast.18, ...), custom_call_target="tpu_custom_call" | custom-call | tf_op jit(solution)/shard_map/pallas_call | solution.py:100
  15.5 1.6 %collective-permute-start.5 = (bf16[3,64,640]{2,1,0:T(8,128)(2,1)S(1)}, bf16[3,64,640]{2,1,0:T(8,128)(2,1)S(1)}, u32[]{:S(2)}, u32[]{:S(2)}) collective-permute-start(bf16[3,64,640]{2,1,0:T(8,128)(2,1)S(1)} %collective-permute-done.1.refs_3_), channel_id=1, source_target_pairs={{0,2},{8,9},{2,4},{10,8},{4,6},{12,10},{6,7},{14,12},{7,5},{15,14}... | collective-permute-start | bytes 737288 | tf_op jit(solution)/shard_map/ppermute | solution.py:24
  17.1 1.0 %copy-done = bf16[2,640,64]{2,1,0:T(8,128)(2,1)S(1)} copy-done((bf16[2,640,64]{2,1,0:T(8,128)(2,1)S(1)}, bf16[2,640,64]{2,1,0:T(8,128)(2,1)}, u32[]{:S(2)}) %copy-start) | copy-done | bytes 163864
  18.1 0.8 %copy-done.1 = bf16[2,128,64]{2,1,0:T(8,128)(2,1)S(1)} copy-done((bf16[2,128,64]{2,1,0:T(8,128)(2,1)S(1)}, bf16[2,128,64]{2,1,0:T(8,128)(2,1)}, u32[]{:S(2)}) %copy-start.1) | copy-done | bytes 32792
  18.9 0.8 %copy-done.2 = bf16[2,128,64]{2,1,0:T(8,128)(2,1)S(1)} copy-done((bf16[2,128,64]{2,1,0:T(8,128)(2,1)S(1)}, bf16[2,128,64]{2,1,0:T(8,128)(2,1)}, u32[]{:S(2)}) %copy-start.2) | copy-done | bytes 32792
  19.8 0.9 %copy-done.3 = bf16[3,64,640]{2,1,0:T(8,128)(2,1)S(1)} copy-done((bf16[3,64,640]{2,1,0:T(8,128)(2,1)S(1)}, bf16[3,64,640]{2,1,0:T(8,128)(2,1)}, u32[]{:S(2)}) %copy-start.3) | copy-done | bytes 245784
  20.7 0.9 %copy-done.4 = bf16[3,64,640]{2,1,0:T(8,128)(2,1)S(1)} copy-done((bf16[3,64,640]{2,1,0:T(8,128)(2,1)S(1)}, bf16[3,64,640]{2,1,0:T(8,128)(2,1)}, u32[]{:S(2)}) %copy-start.4) | copy-done | bytes 245784
  21.7 0.7 %copy-done.5 = s32[15]{0:T(128)S(1)} copy-done((s32[15]{0:T(128)S(1)}, s32[15]{0:T(128)}, u32[]{:S(2)}) %copy-start.5) | copy-done | bytes 84
  22.3 4.1 %shard_map.105 = (bf16[2,640,5120]{2,1,0:T(8,128)(2,1)}, bf16[2,128,5120]{2,1,0:T(8,128)(2,1)}, bf16[2,128,5120]{2,1,0:T(8,128)(2,1)}) custom-call(s32[15]{0:T(128)S(1)} %copy-done.5, bf16[2,640,64]{2,1,0:T(8,128)(2,1)S(1)} %copy-done, bf16[2,128,64]{2,1,0:T(8,128)(2,1)S(1)} %copy-done.1, bf16[2,128,64]{2,1,0:T(8,128)(2,1)S(1)} %copy-done.2, ...), custom_call_target="tpu_custom_call" | custom-call | flops 146800640 | bytes 4587520 | tf_op jit(solution)/shard_map/pallas_call | solution.py:156
  26.5 1.6 %collective-permute-start.10 = (bf16[3,64,640]{2,1,0:T(8,128)(2,1)S(1)}, bf16[3,64,640]{2,1,0:T(8,128)(2,1)S(1)}, u32[]{:S(2)}, u32[]{:S(2)}) collective-permute-start(bf16[3,64,640]{2,1,0:T(8,128)(2,1)S(1)} %collective-permute-done.7.refs_3_), channel_id=1, source_target_pairs={{0,2},{8,9},{2,4},{10,8},{4,6},{12,10},{6,7},{14,12},{7,5},{15,14}... | collective-permute-start | bytes 737288 | tf_op jit(solution)/shard_map/ppermute | solution.py:24
  28.1 4.1 %shard_map.106 = (bf16[2,640,5120]{2,1,0:T(8,128)(2,1)}, bf16[2,128,5120]{2,1,0:T(8,128)(2,1)}, bf16[2,128,5120]{2,1,0:T(8,128)(2,1)}) custom-call(s32[15]{0:T(128)S(1)} %copy-done.5, bf16[2,640,64]{2,1,0:T(8,128)(2,1)S(1)} %copy-done, bf16[2,128,64]{2,1,0:T(8,128)(2,1)S(1)} %copy-done.1, ...), custom_call_target="tpu_custom_call", output_to_operand_aliasing={{0}: (9, {}), {1}: (10, {}), {2}: (11, {})} | custom-call | flops 146800640 | bytes 4587520 | tf_op jit(solution)/shard_map/pallas_call | solution.py:156
  32.2 1.5 %collective-permute-start.8 = (bf16[3,64,640]{2,1,0:T(8,128)(2,1)S(1)}, bf16[3,64,640]{2,1,0:T(8,128)(2,1)S(1)}, u32[]{:S(2)}, u32[]{:S(2)}) collective-permute-start(bf16[3,64,640]{2,1,0:T(8,128)(2,1)S(1)} %collective-permute-done.5.refs_3_), channel_id=1, source_target_pairs={{0,2},{8,9},{2,4},{10,8},{4,6},{12,10},{6,7},{14,12},{7,5},{15,14}... | collective-permute-start | bytes 737288 | tf_op jit(solution)/shard_map/ppermute | solution.py:24
  33.8 4.1 %shard_map.107 = (bf16[2,640,5120]{2,1,0:T(8,128)(2,1)}, bf16[2,128,5120]{2,1,0:T(8,128)(2,1)}, bf16[2,128,5120]{2,1,0:T(8,128)(2,1)}) custom-call(s32[15]{0:T(128)S(1)} %copy-done.5, bf16[2,640,64]{2,1,0:T(8,128)(2,1)S(1)} %copy-done, bf16[2,128,64]{2,1,0:T(8,128)(2,1)S(1)} %copy-done.1, ...), custom_call_target="tpu_custom_call", output_to_operand_aliasing={{0}: (9, {}), {1}: (10, {}), {2}: (11, {})} | custom-call | flops 146800640 | bytes 4587520 | tf_op jit(solution)/shard_map/pallas_call | solution.py:156
  37.9 0.7 %collective-permute-start.14 = (bf16[3,64,640]{2,1,0:T(8,128)(2,1)S(1)}, bf16[3,64,640]{2,1,0:T(8,128)(2,1)S(1)}, u32[]{:S(2)}, u32[]{:S(2)}) collective-permute-start(bf16[3,64,640]{2,1,0:T(8,128)(2,1)S(1)} %collective-permute-done.10.refs_3_), channel_id=1, source_target_pairs={{0,2},{8,9},{2,4},{10,8},{4,6},{12,10},{6,7},{14,12},{7,5},{15,14}... | collective-permute-start | bytes 737288 | tf_op jit(solution)/shard_map/ppermute | solution.py:24
  38.7 4.1 %shard_map.108 = (bf16[2,640,5120]{2,1,0:T(8,128)(2,1)}, bf16[2,128,5120]{2,1,0:T(8,128)(2,1)}, bf16[2,128,5120]{2,1,0:T(8,128)(2,1)}) custom-call(s32[15]{0:T(128)S(1)} %copy-done.5, bf16[2,640,64]{2,1,0:T(8,128)(2,1)S(1)} %copy-done, bf16[2,128,64]{2,1,0:T(8,128)(2,1)S(1)} %copy-done.1, ...), custom_call_target="tpu_custom_call", output_to_operand_aliasing={{0}: (9, {}), {1}: (10, {}), {2}: (11, {})} | custom-call | flops 146800640 | bytes 4587520 | tf_op jit(solution)/shard_map/pallas_call | solution.py:156
  42.8 1.5 %collective-permute-start.12 = (bf16[3,64,640]{2,1,0:T(8,128)(2,1)S(1)}, bf16[3,64,640]{2,1,0:T(8,128)(2,1)S(1)}, u32[]{:S(2)}, u32[]{:S(2)}) collective-permute-start(bf16[3,64,640]{2,1,0:T(8,128)(2,1)S(1)} %collective-permute-done.8.refs_3_), channel_id=1, source_target_pairs={{0,2},{8,9},{2,4},{10,8},{4,6},{12,10},{6,7},{14,12},{7,5},{15,14}... | collective-permute-start | bytes 737288 | tf_op jit(solution)/shard_map/ppermute | solution.py:24
  44.3 4.1 %shard_map.109 = (bf16[2,640,5120]{2,1,0:T(8,128)(2,1)}, bf16[2,128,5120]{2,1,0:T(8,128)(2,1)}, bf16[2,128,5120]{2,1,0:T(8,128)(2,1)}) custom-call(s32[15]{0:T(128)S(1)} %copy-done.5, bf16[2,640,64]{2,1,0:T(8,128)(2,1)S(1)} %copy-done, bf16[2,128,64]{2,1,0:T(8,128)(2,1)S(1)} %copy-done.1, ...), custom_call_target="tpu_custom_call", output_to_operand_aliasing={{0}: (9, {}), {1}: (10, {}), {2}: (11, {})} | custom-call | flops 146800640 | bytes 4587520 | tf_op jit(solution)/shard_map/pallas_call | solution.py:156
  48.5 4.1 %shard_map.110 = (bf16[2,640,5120]{2,1,0:T(8,128)(2,1)}, bf16[2,128,5120]{2,1,0:T(8,128)(2,1)}, bf16[2,128,5120]{2,1,0:T(8,128)(2,1)}) custom-call(s32[15]{0:T(128)S(1)} %copy-done.5, bf16[2,640,64]{2,1,0:T(8,128)(2,1)S(1)} %copy-done, bf16[2,128,64]{2,1,0:T(8,128)(2,1)S(1)} %copy-done.1, ...), custom_call_target="tpu_custom_call", output_to_operand_aliasing={{0}: (9, {}), {1}: (10, {}), {2}: (11, {})} | custom-call | flops 146800640 | bytes 4587520 | tf_op jit(solution)/shard_map/pallas_call | solution.py:156
  52.6 0.5 collective-permute-start.16
  53.1 4.1 %shard_map.111 = (bf16[2,640,5120]{2,1,0:T(8,128)(2,1)}, bf16[2,128,5120]{2,1,0:T(8,128)(2,1)}, bf16[2,128,5120]{2,1,0:T(8,128)(2,1)}) custom-call(s32[15]{0:T(128)S(1)} %copy-done.5, bf16[2,640,64]{2,1,0:T(8,128)(2,1)S(1)} %copy-done, bf16[2,128,64]{2,1,0:T(8,128)(2,1)S(1)} %copy-done.1, ...), custom_call_target="tpu_custom_call", output_to_operand_aliasing={{0}: (9, {}), {1}: (10, {}), {2}: (11, {})} | custom-call | flops 146800640 | bytes 4587520 | tf_op jit(solution)/shard_map/pallas_call | solution.py:156
  57.2 4.1 %shard_map.112 = (bf16[2,640,5120]{2,1,0:T(8,128)(2,1)}, bf16[2,128,5120]{2,1,0:T(8,128)(2,1)}, bf16[2,128,5120]{2,1,0:T(8,128)(2,1)}) custom-call(s32[15]{0:T(128)S(1)} %copy-done.5, bf16[2,640,64]{2,1,0:T(8,128)(2,1)S(1)} %copy-done, bf16[2,128,64]{2,1,0:T(8,128)(2,1)S(1)} %copy-done.1, ...), custom_call_target="tpu_custom_call", output_to_operand_aliasing={{0}: (9, {}), {1}: (10, {}), {2}: (11, {})} | custom-call | flops 146800640 | bytes 4587520 | tf_op jit(solution)/shard_map/pallas_call | solution.py:156
  (37 shorter events, 0.6 us)
Async XLA Ops:
  0.6 2.2 %collective-permute-start = (bf16[2,3,64,640]{3,2,1,0:T(8,128)(2,1)}, bf16[2,3,64,640]{3,2,1,0:T(8,128)(2,1)S(1)}, u32[]{:S(2)}, u32[]{:S(2)}) collective-permute-start(bf16[2,3,64,640]{3,2,1,0:T(8,128)(2,1)} %bitcast.11), channel_id=1, source_target_pairs={{0,8},{8,0},{1,9},{9,1},{2,10},{10,2},{3,11},{11,3},{4,12},{12,4},... | collective-permute-start | bytes 1474568 | tf_op jit(solution)/shard_map/ppermute | solution.py:28
  2.8 0.8 %copy-start.6 = (bf16[2,3,64,640]{3,2,1,0:T(8,128)(2,1)}, bf16[2,3,64,640]{3,2,1,0:T(8,128)(2,1)S(1)}, u32[]{:S(2)}) copy-start(bf16[2,3,64,640]{3,2,1,0:T(8,128)(2,1)S(1)} %collective-permute-done.other) | copy-start | bytes 1474564
  6.2 9.2 %collective-permute-start.1 = (bf16[3,64,640]{2,1,0:T(8,128)(2,1)}, bf16[3,64,640]{2,1,0:T(8,128)(2,1)S(1)}, u32[]{:S(2)}, u32[]{:S(2)}) collective-permute-start(bf16[3,64,640]{2,1,0:T(8,128)(2,1)} %get-tuple-element.57.refs_3_), channel_id=1, source_target_pairs={{0,2},{8,9},{2,4},{10,8},{4,6},{12,10},{6,7},{14,12},{7,5},{15,14}... | collective-permute-start | bytes 737288 | tf_op jit(solution)/shard_map/ppermute | solution.py:24
  9.2 2.1 %collective-permute-start.2 = (bf16[2,64,640]{2,1,0:T(8,128)(2,1)}, bf16[2,64,640]{2,1,0:T(8,128)(2,1)S(1)}, u32[]{:S(2)}, u32[]{:S(2)}) collective-permute-start(bf16[2,64,640]{2,1,0:T(8,128)(2,1)} %bitcast.13), channel_id=1, source_target_pairs={{0,8},{8,0},{1,9},{9,1},{2,10},{10,2},{3,11},{11,3},{4,12},{12,4},... | collective-permute-start | bytes 491528 | tf_op jit(solution)/shard_map/ppermute | solution.py:28
  9.2 2.1 %collective-permute-start.3 = (bf16[2,64,128]{2,1,0:T(8,128)(2,1)}, bf16[2,64,128]{2,1,0:T(8,128)(2,1)S(1)}, u32[]{:S(2)}, u32[]{:S(2)}) collective-permute-start(bf16[2,64,128]{2,1,0:T(8,128)(2,1)} %bitcast.15), channel_id=1, source_target_pairs={{0,8},{8,0},{1,9},{9,1},{2,10},{10,2},{3,11},{11,3},{4,12},{12,4},... | collective-permute-start | bytes 98312 | tf_op jit(solution)/shard_map/ppermute | solution.py:28
  9.7 1.6 %collective-permute-start.4 = (bf16[2,64,128]{2,1,0:T(8,128)(2,1)}, bf16[2,64,128]{2,1,0:T(8,128)(2,1)S(1)}, u32[]{:S(2)}, u32[]{:S(2)}) collective-permute-start(bf16[2,64,128]{2,1,0:T(8,128)(2,1)} %bitcast.17), channel_id=1, source_target_pairs={{0,8},{8,0},{1,9},{9,1},{2,10},{10,2},{3,11},{11,3},{4,12},{12,4},... | collective-permute-start | bytes 98312 | tf_op jit(solution)/shard_map/ppermute | solution.py:28
  9.7 16.7 %collective-permute-start.7 = (bf16[3,64,640]{2,1,0:T(8,128)(2,1)}, bf16[3,64,640]{2,1,0:T(8,128)(2,1)S(1)}, u32[]{:S(2)}, u32[]{:S(2)}) collective-permute-start(bf16[3,64,640]{2,1,0:T(8,128)(2,1)} %get-tuple-element.65.refs_4_), channel_id=1, source_target_pairs={{0,2},{8,9},{2,4},{10,8},{4,6},{12,10},{6,7},{14,12},{7,5},{15,14}... | collective-permute-start | bytes 737288 | tf_op jit(solution)/shard_map/ppermute | solution.py:24
  11.3 0.6 %copy-start.8 = (bf16[2,64,128]{2,1,0:T(8,128)(2,1)}, bf16[2,64,128]{2,1,0:T(8,128)(2,1)S(1)}, u32[]{:S(2)}) copy-start(bf16[2,64,128]{2,1,0:T(8,128)(2,1)S(1)} %collective-permute-done.3.refs_4_) | copy-start | bytes 98308
  11.3 0.6 %copy-start.9 = (bf16[2,64,128]{2,1,0:T(8,128)(2,1)}, bf16[2,64,128]{2,1,0:T(8,128)(2,1)S(1)}, u32[]{:S(2)}) copy-start(bf16[2,64,128]{2,1,0:T(8,128)(2,1)S(1)} %collective-permute-done.4.refs_5_) | copy-start | bytes 98308
  11.9 0.7 %copy-start.7 = (bf16[2,64,640]{2,1,0:T(8,128)(2,1)}, bf16[2,64,640]{2,1,0:T(8,128)(2,1)S(1)}, u32[]{:S(2)}) copy-start(bf16[2,64,640]{2,1,0:T(8,128)(2,1)S(1)} %collective-permute-done.2.refs_3_) | copy-start | bytes 491524
  15.4 12.7 %collective-permute-start.6 = (bf16[3,64,640]{2,1,0:T(8,128)(2,1)S(1)}, bf16[3,64,640]{2,1,0:T(8,128)(2,1)S(1)}, u32[]{:S(2)}, u32[]{:S(2)}) collective-permute-start(bf16[3,64,640]{2,1,0:T(8,128)(2,1)S(1)} %collective-permute-done.1.refs_3_), channel_id=1, source_target_pairs={{0,8},{8,0},{1,9},{9,1},{2,10},{10,2},{3,11},{11,3},{4,12},{12,4},... | collective-permute-start | bytes 737288 | tf_op jit(solution)/shard_map/ppermute | solution.py:28
  15.5 16.6 %collective-permute-start.5 = (bf16[3,64,640]{2,1,0:T(8,128)(2,1)S(1)}, bf16[3,64,640]{2,1,0:T(8,128)(2,1)S(1)}, u32[]{:S(2)}, u32[]{:S(2)}) collective-permute-start(bf16[3,64,640]{2,1,0:T(8,128)(2,1)S(1)} %collective-permute-done.1.refs_3_), channel_id=1, source_target_pairs={{0,2},{8,9},{2,4},{10,8},{4,6},{12,10},{6,7},{14,12},{7,5},{15,14}... | collective-permute-start | bytes 737288 | tf_op jit(solution)/shard_map/ppermute | solution.py:24
  17.1 1.0 %copy-start = (bf16[2,640,64]{2,1,0:T(8,128)(2,1)S(1)}, bf16[2,640,64]{2,1,0:T(8,128)(2,1)}, u32[]{:S(2)}) copy-start(bf16[2,640,64]{2,1,0:T(8,128)(2,1)} %get-tuple-element.61.refs_0_) | copy-start | bytes 491524
  18.1 0.8 %copy-start.1 = (bf16[2,128,64]{2,1,0:T(8,128)(2,1)S(1)}, bf16[2,128,64]{2,1,0:T(8,128)(2,1)}, u32[]{:S(2)}) copy-start(bf16[2,128,64]{2,1,0:T(8,128)(2,1)} %get-tuple-element.62.refs_1_) | copy-start | bytes 98308
  18.9 0.8 %copy-start.2 = (bf16[2,128,64]{2,1,0:T(8,128)(2,1)S(1)}, bf16[2,128,64]{2,1,0:T(8,128)(2,1)}, u32[]{:S(2)}) copy-start(bf16[2,128,64]{2,1,0:T(8,128)(2,1)} %get-tuple-element.63.refs_2_) | copy-start | bytes 98308
  19.8 0.9 %copy-start.3 = (bf16[3,64,640]{2,1,0:T(8,128)(2,1)S(1)}, bf16[3,64,640]{2,1,0:T(8,128)(2,1)}, u32[]{:S(2)}) copy-start(bf16[3,64,640]{2,1,0:T(8,128)(2,1)} %get-tuple-element.57.refs_3_) | copy-start | bytes 737284
  20.7 0.9 %copy-start.4 = (bf16[3,64,640]{2,1,0:T(8,128)(2,1)S(1)}, bf16[3,64,640]{2,1,0:T(8,128)(2,1)}, u32[]{:S(2)}) copy-start(bf16[3,64,640]{2,1,0:T(8,128)(2,1)} %get-tuple-element.65.refs_4_) | copy-start | bytes 737284
  21.7 0.7 %copy-start.5 = (s32[15]{0:T(128)S(1)}, s32[15]{0:T(128)}, u32[]{:S(2)}) copy-start(s32[15]{0:T(128)} %pad_add_fusion.places) | copy-start | bytes 184
  26.4 7.4 %collective-permute-start.11 = (bf16[3,64,640]{2,1,0:T(8,128)(2,1)S(1)}, bf16[3,64,640]{2,1,0:T(8,128)(2,1)S(1)}, u32[]{:S(2)}, u32[]{:S(2)}) collective-permute-start(bf16[3,64,640]{2,1,0:T(8,128)(2,1)S(1)} %collective-permute-done.7.refs_3_), channel_id=1, source_target_pairs={{0,8},{8,0},{1,9},{9,1},{2,10},{10,2},{3,11},{11,3},{4,12},{12,4},... | collective-permute-start | bytes 737288 | tf_op jit(solution)/shard_map/ppermute | solution.py:28
  26.5 11.3 %collective-permute-start.10 = (bf16[3,64,640]{2,1,0:T(8,128)(2,1)S(1)}, bf16[3,64,640]{2,1,0:T(8,128)(2,1)S(1)}, u32[]{:S(2)}, u32[]{:S(2)}) collective-permute-start(bf16[3,64,640]{2,1,0:T(8,128)(2,1)S(1)} %collective-permute-done.7.refs_3_), channel_id=1, source_target_pairs={{0,2},{8,9},{2,4},{10,8},{4,6},{12,10},{6,7},{14,12},{7,5},{15,14}... | collective-permute-start | bytes 737288 | tf_op jit(solution)/shard_map/ppermute | solution.py:24
  32.1 6.5 %collective-permute-start.9 = (bf16[3,64,640]{2,1,0:T(8,128)(2,1)S(1)}, bf16[3,64,640]{2,1,0:T(8,128)(2,1)S(1)}, u32[]{:S(2)}, u32[]{:S(2)}) collective-permute-start(bf16[3,64,640]{2,1,0:T(8,128)(2,1)S(1)} %collective-permute-done.5.refs_3_), channel_id=1, source_target_pairs={{0,8},{8,0},{1,9},{9,1},{2,10},{10,2},{3,11},{11,3},{4,12},{12,4},... | collective-permute-start | bytes 737288 | tf_op jit(solution)/shard_map/ppermute | solution.py:28
  32.2 10.5 %collective-permute-start.8 = (bf16[3,64,640]{2,1,0:T(8,128)(2,1)S(1)}, bf16[3,64,640]{2,1,0:T(8,128)(2,1)S(1)}, u32[]{:S(2)}, u32[]{:S(2)}) collective-permute-start(bf16[3,64,640]{2,1,0:T(8,128)(2,1)S(1)} %collective-permute-done.5.refs_3_), channel_id=1, source_target_pairs={{0,2},{8,9},{2,4},{10,8},{4,6},{12,10},{6,7},{14,12},{7,5},{15,14}... | collective-permute-start | bytes 737288 | tf_op jit(solution)/shard_map/ppermute | solution.py:24
  37.8 6.5 %collective-permute-start.15 = (bf16[3,64,640]{2,1,0:T(8,128)(2,1)S(1)}, bf16[3,64,640]{2,1,0:T(8,128)(2,1)S(1)}, u32[]{:S(2)}, u32[]{:S(2)}) collective-permute-start(bf16[3,64,640]{2,1,0:T(8,128)(2,1)S(1)} %collective-permute-done.10.refs_3_), channel_id=1, source_target_pairs={{0,8},{8,0},{1,9},{9,1},{2,10},{10,2},{3,11},{11,3},{4,12},{12,4},... | collective-permute-start | bytes 737288 | tf_op jit(solution)/shard_map/ppermute | solution.py:28
  37.9 10.5 %collective-permute-start.14 = (bf16[3,64,640]{2,1,0:T(8,128)(2,1)S(1)}, bf16[3,64,640]{2,1,0:T(8,128)(2,1)S(1)}, u32[]{:S(2)}, u32[]{:S(2)}) collective-permute-start(bf16[3,64,640]{2,1,0:T(8,128)(2,1)S(1)} %collective-permute-done.10.refs_3_), channel_id=1, source_target_pairs={{0,2},{8,9},{2,4},{10,8},{4,6},{12,10},{6,7},{14,12},{7,5},{15,14}... | collective-permute-start | bytes 737288 | tf_op jit(solution)/shard_map/ppermute | solution.py:24
  42.7 5.8 %collective-permute-start.13 = (bf16[3,64,640]{2,1,0:T(8,128)(2,1)S(1)}, bf16[3,64,640]{2,1,0:T(8,128)(2,1)S(1)}, u32[]{:S(2)}, u32[]{:S(2)}) collective-permute-start(bf16[3,64,640]{2,1,0:T(8,128)(2,1)S(1)} %collective-permute-done.8.refs_3_), channel_id=1, source_target_pairs={{0,8},{8,0},{1,9},{9,1},{2,10},{10,2},{3,11},{11,3},{4,12},{12,4},... | collective-permute-start | bytes 737288 | tf_op jit(solution)/shard_map/ppermute | solution.py:28
  42.8 9.8 %collective-permute-start.12 = (bf16[3,64,640]{2,1,0:T(8,128)(2,1)S(1)}, bf16[3,64,640]{2,1,0:T(8,128)(2,1)S(1)}, u32[]{:S(2)}, u32[]{:S(2)}) collective-permute-start(bf16[3,64,640]{2,1,0:T(8,128)(2,1)S(1)} %collective-permute-done.8.refs_3_), channel_id=1, source_target_pairs={{0,2},{8,9},{2,4},{10,8},{4,6},{12,10},{6,7},{14,12},{7,5},{15,14}... | collective-permute-start | bytes 737288 | tf_op jit(solution)/shard_map/ppermute | solution.py:24
  48.4 4.7 %collective-permute-start.17 = (bf16[3,64,640]{2,1,0:T(8,128)(2,1)S(1)}, bf16[3,64,640]{2,1,0:T(8,128)(2,1)S(1)}, u32[]{:S(2)}, u32[]{:S(2)}) collective-permute-start(bf16[3,64,640]{2,1,0:T(8,128)(2,1)S(1)} %collective-permute-done.14.refs_3_), channel_id=1, source_target_pairs={{0,8},{8,0},{1,9},{9,1},{2,10},{10,2},{3,11},{11,3},{4,12},{12,4},... | collective-permute-start | bytes 737288 | tf_op jit(solution)/shard_map/ppermute | solution.py:28
  52.6 4.6 %collective-permute-start.16 = (bf16[3,64,640]{2,1,0:T(8,128)(2,1)S(1)}, bf16[3,64,640]{2,1,0:T(8,128)(2,1)S(1)}, u32[]{:S(2)}, u32[]{:S(2)}) collective-permute-start(bf16[3,64,640]{2,1,0:T(8,128)(2,1)S(1)} %collective-permute-done.12.refs_3_), channel_id=1, source_target_pairs={{0,8},{8,0},{1,9},{9,1},{2,10},{10,2},{3,11},{11,3},{4,12},{12,4},... | collective-permute-start | bytes 737288 | tf_op jit(solution)/shard_map/ppermute | solution.py:28

commit v3 on v0

v3 whole, which is shorter than its diff:
```python
import functools

import jax
import jax.numpy as jnp
from jax import lax
from jax.experimental import pallas as pl
from jax.experimental.pallas import tpu as pltpu
from jax.sharding import PartitionSpec as P

numerator_gain = 16.0
LANES = 128
MIB = 1024 * 1024
SMEM = pl.BlockSpec(memory_space=pltpu.SMEM)
VMEM = pl.BlockSpec(memory_space=pltpu.VMEM)
HBM = pl.BlockSpec(memory_space=pltpu.HBM)
ANY = pl.BlockSpec(memory_space=pl.ANY)


def in_hbm(array):
    return pltpu.with_memory_space_constraint(array, pltpu.HBM)


def ring_order(n):
    return list(range(0, n, 2)) + list(range(n - 1, 0, -2))


def ring_pass(array, n):
    order = ring_order(n)
    pairs = []
    for k in range(n):
        pairs.append((order[k], order[(k + 1) % n]))
        pairs.append((n + order[k], n + order[(k - 1) % n]))
    return lax.ppermute(array, ("rollout", "tensor"), pairs)


def swap_cores(array):
    return lax.ppermute(array, "rollout", [(0, 1), (1, 0)])


def place_of(n, step, from_core, tensor):
    position = jnp.where(tensor % 2 == 0, tensor // 2, n - 1 - tensor // 2)
    k = position + jnp.where(from_core == 0, -step, step)
    k = jnp.where(k < 0, k + n, jnp.where(k >= n, k - n, k))
    return jnp.where(k < n // 2, 2 * k, 2 * n - 1 - 2 * k)


def base_copies(n, pieces, bases, targets, sems):
    core = lax.axis_index("rollout")
    tensor = lax.axis_index("tensor")
    cols = targets[0].shape[2]
    copies = []
    for i, (step, own_ring, own_layer) in enumerate(pieces):
        layer = core if own_layer else 1 - core
        place = place_of(n, step, core if own_ring else 1 - core, tensor)
        columns = pl.ds(pl.multiple_of(place * cols, LANES), cols)
        for proj in range(3):
            block = bases[proj].at[layer, :, columns]
            copies.append((block, targets[proj].at[i], sems.at[3 * i + proj]))
    return copies


def start_loads(n, pieces, bases, targets, sems):
    loads = [pltpu.make_async_copy(*copy) for copy in base_copies(n, pieces, bases, targets, sems)]
    for load in loads:
        load.start()
    return loads


def start_chosen(mine, own, other, target, sem):
    copy = pltpu.make_async_copy(own, target, sem)
    pl.when(mine)(copy.start)
    pl.when(jnp.logical_not(mine))(pltpu.make_async_copy(other, target, sem).start)
    return copy


def choose_a_kernel(owners, own, other, first, second, sems):
    core = lax.axis_index("rollout")
    projs = own.shape[1]
    copies = []
    for i, (out, layer) in enumerate(((first, core), (second, 1 - core))):
        for proj in range(projs):
            mine = owners[layer, proj] == core
            copies.append(
                start_chosen(
                    mine, own.at[layer, proj], other.at[layer, proj], out.at[proj], sems.at[i * projs + proj]
                )
            )
    for copy in copies:
        copy.wait()


def choose_a(owners, own, other):
    piece = jax.ShapeDtypeStruct(own.shape[1:], own.dtype)
    return pl.pallas_call(
        choose_a_kernel,
        in_specs=[SMEM, ANY, ANY],
        out_specs=[VMEM, VMEM],
        out_shape=[piece, piece],
        scratch_shapes=[pltpu.SemaphoreType.DMA((own.shape[0] * own.shape[1],))],
        compiler_params=pltpu.CompilerParams(vmem_limit_bytes=4 * MIB),
    )(owners, in_hbm(own), other)


def choose_b_kernel(n, pieces, owners, *refs):
    core = lax.axis_index("rollout")
    own, other, bases = refs[0:3], refs[3:6], refs[6:9]
    outs, nexts, held = refs[9:12], refs[12:15], refs[15:18]
    sems, load_sems = refs[18:20]
    copies = []
    for proj in range(3):
        for layer in range(own[proj].shape[0]):
            mine = owners[layer, proj] == core
            copies.append(
                start_chosen(
                    mine,
                    own[proj].at[layer],
                    other[proj].at[layer],
                    held[proj].at[layer],
                    sems.at[layer * 3 + proj],
                )
            )
    loads = start_loads(n, pieces, bases, nexts, load_sems)
    for proj in range(3):
        for layer in range(held[proj].shape[0]):
            copies.pop(0).wait()
            outs[proj][layer] = held[proj][layer].T
    for load in loads:
        load.wait()


def block_shapes(bases, pieces, cols):
    return [jax.ShapeDtypeStruct((len(pieces), base.shape[1], cols), base.dtype) for base in bases]


def choose_b(n, cols, owners, own, other, bases, pieces):
    shapes = [jax.ShapeDtypeStruct((x.shape[0], x.shape[2], x.shape[1]), x.dtype) for x in own]
    out = pl.pallas_call(
        functools.partial(choose_b_kernel, n, pieces),
        in_specs=[SMEM] + [ANY] * 6 + [HBM] * 3,
        out_specs=[VMEM] * 6,
        out_shape=shapes + block_shapes(bases, pieces, cols),
        scratch_shapes=[pltpu.VMEM(x.shape, x.dtype) for x in own]
        + [pltpu.SemaphoreType.DMA((3 * own[0].shape[0],)), pltpu.SemaphoreType.DMA((3 * len(pieces),))],
        compiler_params=pltpu.CompilerParams(vmem_limit_bytes=16 * MIB),
    )(owners, *[in_hbm(x) for x in own], *other, *[in_hbm(x) for x in bases])
    return out[:3], out[3:]


def merge_kernel(n, pieces, next_pieces, scale, fresh, *refs):
    b_refs, a_refs, blocks, bases = refs[0:3], refs[3:5], refs[5:8], refs[8:11]
    at = 11 if fresh else 14
    outs, at = refs[at : at + 3], at + 3
    nexts, at = (refs[at : at + 3], at + 3) if next_pieces else (None, at)
    bufs, load_sems, store_sems = refs[at : at + 3], refs[at + 3], refs[at + 4]
    core = lax.axis_index("rollout")
    loads = start_loads(n, next_pieces, bases, nexts, load_sems) if next_pieces else []
    stores = [
        pltpu.make_async_copy(buf, out, sem) for out, buf, sem in base_copies(n, pieces, outs, bufs, store_sems)
    ]
    for i, (_, _, own_layer) in enumerate(pieces):
        layer = core if own_layer else 1 - core
        for proj in range(3):
            delta = jnp.dot(b_refs[proj][layer], a_refs[i][proj], preferred_element_type=jnp.float32)
            merged = blocks[proj][i].astype(jnp.float32) + scale * delta
            bufs[proj][i] = merged.astype(jnp.bfloat16)
            stores[3 * i + proj].start()
    for copy in loads + stores:
        copy.wait()


def merge(n, scale, cols, b, a_list, blocks, bases, outs, pieces, next_pieces):
    fresh = outs is None
    rows = sum(base.shape[1] for base in bases)
    nexts = block_shapes(bases, next_pieces, cols) if next_pieces else []
    out = pl.pallas_call(
        functools.partial(merge_kernel, n, pieces, next_pieces, scale, fresh),
        in_specs=[VMEM] * (3 + len(a_list) + 3) + [HBM] * (3 if fresh else 6),
        out_specs=[HBM] * 3 + [VMEM] * len(nexts),
        out_shape=[jax.ShapeDtypeStruct(base.shape, base.dtype) for base in bases] + nexts,
        scratch_shapes=[pltpu.VMEM(x.shape, x.dtype) for x in block_shapes(bases, pieces, cols)]
        + [pltpu.SemaphoreType.DMA((3 * len(pieces),)), pltpu.SemaphoreType.DMA((3 * len(pieces),))],
        input_output_aliases={} if fresh else {9 + len(a_list) + i: i for i in range(3)},
        compiler_params=pltpu.CompilerParams(vmem_limit_bytes=16 * MIB),
        cost_estimate=pl.CostEstimate(
            flops=2 * len(pieces) * rows * cols * a_list[0].shape[1],
            bytes_accessed=4 * len(pieces) * rows * cols,
            transcendentals=0,
        ),
    )(*b, *a_list, *blocks, *[in_hbm(base) for base in bases], *([] if fresh else outs))
    return out[:3], out[3:]


def per_device(
    n,
    owners,
    base_query,
    base_key,
    base_value,
    left_shared_matrix,
    right_queries_matrix,
    right_keys_matrix,
    right_values_matrix,
):
    layers, projs, rank, cols = left_shared_matrix.shape[1:]
    scale = numerator_gain / rank
    bases = (base_query, base_key, base_value)
    rights = (right_queries_matrix, right_keys_matrix, right_values_matrix)
    last = n // 2

    own_a = left_shared_matrix[0]
    own_b = [jnp.swapaxes(right[0], 1, 2) for right in rights]

    if cols % LANES == 0:
        plan = [[(0, True, True), (0, True, False)]]
        for step in range(1, last + 1):
            plan.append([(step, True, True), (step, False, False)])
            if step < last:
                plan.append([(step, True, False), (step, False, True)])
        plan.append(None)

        first, second = choose_a(owners, own_a, swap_cores(own_a))
        held = [first, second]
        first = ring_pass(first, n)
        second = ring_pass(second, n)
        b, blocks = choose_b(n, cols, owners, own_b, [swap_cores(x) for x in own_b], bases, plan[0])
        first, b = lax.optimization_barrier((first, b))
        done = 0
        outs = None

        def advance(chunks, blocks, outs, done):
            outs, blocks = merge(
                n, scale, cols, b, chunks, blocks, bases, outs, plan[done], plan[done + 1]
            )
            return blocks, outs, done + 1

        blocks, outs, done = advance(held, blocks, outs, done)
        ready = []
        for step in range(1, last + 1):
            if step > 1:
                blocks, outs, done = advance(ready.pop(0), blocks, outs, done)
            ready.append([first, swap_cores(first)])
            if step < last:
                first = ring_pass(first, n)
                second, outs = lax.optimization_barrier((second, outs))
                ready.append([second, swap_cores(second)])
                blocks, outs, done = advance(ready.pop(0), blocks, outs, done)
                first, outs = lax.optimization_barrier((first, outs))
                if step < last - 1:
                    second = ring_pass(second, n)
        for chunks in ready:
            blocks, outs, done = advance(chunks, blocks, outs, done)
        return tuple(outs)

    core = lax.axis_index("rollout")
    tensor = lax.axis_index("tensor")
    mine = owners == core
    a = jnp.where(mine[:, :, None, None], own_a, swap_cores(own_a))
    b = [jnp.where(mine[:, proj, None, None], x, swap_cores(x)) for proj, x in enumerate(own_b)]
    full = jnp.zeros((layers, projs, rank, n * cols), own_a.dtype)

    def put(full, piece, layer, step, from_core):
        start = place_of(n, step, from_core, tensor) * cols
        return lax.dynamic_update_slice(full, piece[None], (layer, 0, 0, start))

    first = jnp.where(core == 0, a[0], a[1])
    second = jnp.where(core == 0, a[1], a[0])
    full = put(full, first, core, 0, core)
    full = put(full, second, 1 - core, 0, core)
    for step in range(1, last + 1):
        first = ring_pass(first, n)
        full = put(full, first, core, step, core)
        full = put(full, swap_cores(first), 1 - core, step, 1 - core)
        if step < last:
            second = ring_pass(second, n)
            full = put(full, second, 1 - core, step, core)
            full = put(full, swap_cores(second), core, step, 1 - core)
    merged = []
    for proj in range(projs):
        delta = jnp.einsum("lkr,lkc->lrc", b[proj], full[:, proj], preferred_element_type=jnp.float32)
        merged.append((bases[proj].astype(jnp.float32) + scale * delta).astype(jnp.bfloat16))
    return tuple(merged)


def solution(mesh):
    return jax.shard_map(
        functools.partial(per_device, mesh.shape["tensor"]),
        mesh=mesh,
        in_specs=(
            P("copies", None),
            P("copies", "tensor", None),
            P("copies", "tensor", None),
            P("copies", "tensor", None),
            P("rollout", "copies", None, None, "tensor"),
            P("rollout", "copies", "tensor", None),
            P("rollout", "copies", "tensor", None),
            P("rollout", "copies", "tensor", None),
        ),
        out_specs=(
            P("copies", "tensor", None),
            P("copies", "tensor", None),
            P("copies", "tensor", None),
        ),
        check_vma=False,
    )
```

time: 265 us -> 44.6 us (0.17)
  blocking collectives: 198 us -> 0 us
  Pallas kernels: 0 us -> 26.6 us
  waiting for transfers between devices: 20.7 us -> 1.75 us
  between operations: 17.9 us -> 0.83 us
  other arithmetic: 13.8 us -> 0 us
  starting transfers between devices: 0.08 us -> 13.6 us
  matrix products: 9.56 us -> 0 us
  local copies, waits for them, and re-layouts: 4.97 us -> 1.35 us
    all_gather x6 -> x0, blocking collectives: 198 us -> none  [per_device(): lax.all_gather(fetched_a[index], 'tensor', axis=1, tiled=True)]
    pallas_call x0 -> x10, Pallas kernels: none -> 26.6 us  [the longest x8 22.3 us: merge(): pl.pallas_call(functools.partial(merge_kernel, n, pieces, next_pieces, sc...]
    psum x2 -> x0, waiting for transfers between devices: 20.7 us -> none  [from_root(): return lax.psum(jnp.where(mine, array, jnp.zeros_like(array)), axis)]
    ppermute x0 -> x18, starting transfers between devices: none -> 13.6 us  [the longest x7 11.6 us: ring_pass(): return lax.ppermute(array, ('rollout', 'tensor'), pairs)]
    dot_general x6 -> x0, matrix products: 9.56 us -> none  [expand(): return jnp.dot(rows_b, piece, preferred_element_type=jnp.float32)]
    another operation x3 -> x0, other arithmetic: 8.91 us -> none  [the longest x1 5.47 us: per_device(): jnp.stack(merged_outputs[0], axis=0)]
    select_n x3 -> x0, other arithmetic: 4.87 us -> none  [from_root(): return lax.psum(jnp.where(mine, array, jnp.zeros_like(array)), axis)]
  transfers between devices with their start and end apart: 2 -> 18, of which waited for: 1 -> 1; matrix products, arithmetic and copies ran while one was open for 5% -> 0% of each run, Pallas kernels for 0% -> 52%
where the time goes in v3:
time: 44.6 us; the launch traced here: 44.1 us
  Pallas kernels  26.6 us (60%)
  starting transfers between devices  13.6 us (30%)
  waiting for transfers between devices  1.75 us (4%)
  local copies, waits for them, and re-layouts  1.35 us (3%)
  between operations  0.83 us (2%)
    pallas_call x8, Pallas kernels, merge(): pl.pallas_call(functools.partial(merge_kernel, n, pieces, next_pieces, sc...  22.3 us
    ppermute x7, starting transfers between devices, ring_pass(): return lax.ppermute(array, ('rollout', 'tensor'), pairs)  11.6 us
    pallas_call x1, Pallas kernels, choose_b(): pl.pallas_call(functools.partial(choose_b_kernel, n, pieces), in_specs=[S...  2.45 us
    ppermute x11, starting transfers between devices, swap_cores(): return lax.ppermute(array, 'rollout', [(0, 1), (1, 0)])  2.03 us
    pallas_call x1, Pallas kernels, choose_a(): pl.pallas_call(choose_a_kernel, in_specs=[SMEM, ANY, ANY], out_specs=[VME...  1.88 us
    ppermute x11, waiting for transfers between devices, swap_cores(): return lax.ppermute(array, 'rollout', [(0, 1), (1, 0)])  1.73 us
    unnamed x4, local copies, waits for them, and re-layouts  1.35 us
  transfers between devices with their start and end apart: 18, of which 1 were waited for; matrix products, arithmetic and copies ran while one was open for 0% of the time, Pallas kernels for 52%

profile of v3, /device:TPU:0, one launch (start us, length us, event | category | flops | bytes accessed | tf_op | source)
XLA Modules:
  0.0 44.1 jit_solution(778341005052760500)
XLA Ops:
  0.6 0.5 %collective-permute-start = (bf16[2,3,64,640]{3,2,1,0:T(8,128)(2,1)}, bf16[2,3,64,640]{3,2,1,0:T(8,128)(2,1)S(1)}, u32[]{:S(2)}, u32[]{:S(2)}) collective-permute-start(bf16[2,3,64,640]{3,2,1,0:T(8,128)(2,1)} %bitcast.10), channel_id=1, source_target_pairs={{0,8},{8,0},{1,9},{9,1},{2,10},{10,2},{3,11},{11,3},{4,12},{12,4},... | collective-permute-start | bytes 1474568 | tf_op jit(solution)/shard_map/ppermute | solution.py:37
  1.1 1.7 %collective-permute-done.other = bf16[2,3,64,640]{3,2,1,0:T(8,128)(2,1)S(1)} collective-permute-done((bf16[2,3,64,640]{3,2,1,0:T(8,128)(2,1)}, bf16[2,3,64,640]{3,2,1,0:T(8,128)(2,1)S(1)}, u32[]{:S(2)}, u32[]{:S(2)}) %collective-permute-start) | collective-permute-done | bytes 491552 | tf_op jit(solution)/shard_map/ppermute | solution.py:37
  2.9 0.7 %copy-done = s32[2,3]{1,0:T(2,128)S(1)} copy-done((s32[2,3]{1,0:T(2,128)S(1)}, s32[2,3]{1,0:T(2,128)}, u32[]{:S(2)}) %copy-start) | copy-done | bytes 48
  3.5 1.9 %shard_map.103 = (bf16[3,64,640]{2,1,0:T(8,128)(2,1)S(1)}, bf16[3,64,640]{2,1,0:T(8,128)(2,1)S(1)}) custom-call(s32[2,3]{1,0:T(2,128)S(1)} %copy-done, bf16[2,3,64,640]{3,2,1,0:T(8,128)(2,1)} %bitcast.11, bf16[2,3,64,640]{3,2,1,0:T(8,128)(2,1)S(1)} %collective-permute-done.other), custom_call_target="tpu_custom_call" | custom-call | tf_op jit(solution)/shard_map/pallas_call | solution.py:94
  5.4 3.0 %collective-permute-start.1 = (bf16[3,64,640]{2,1,0:T(8,128)(2,1)S(1)}, bf16[3,64,640]{2,1,0:T(8,128)(2,1)S(1)}, u32[]{:S(2)}, u32[]{:S(2)}) collective-permute-start(bf16[3,64,640]{2,1,0:T(8,128)(2,1)S(1)} %get-tuple-element.81.refs_3_), channel_id=1, source_target_pairs={{0,2},{8,9},{2,4},{10,8},{4,6},{12,10},{6,7},{14,12},{7,5},{15,14}... | collective-permute-start | bytes 737288 | tf_op jit(solution)/shard_map/ppermute | solution.py:33
  8.4 0.0 collective-permute-start.2
  8.4 0.5 %collective-permute-start.3 = (bf16[2,64,128]{2,1,0:T(8,128)(2,1)}, bf16[2,64,128]{2,1,0:T(8,128)(2,1)S(1)}, u32[]{:S(2)}, u32[]{:S(2)}) collective-permute-start(bf16[2,64,128]{2,1,0:T(8,128)(2,1)} %bitcast.14), channel_id=1, source_target_pairs={{0,8},{8,0},{1,9},{9,1},{2,10},{10,2},{3,11},{11,3},{4,12},{12,4},... | collective-permute-start | bytes 98312 | tf_op jit(solution)/shard_map/ppermute | solution.py:37
  8.9 0.0 collective-permute-start.4
  8.9 1.6 %collective-permute-start.7 = (bf16[3,64,640]{2,1,0:T(8,128)(2,1)S(1)}, bf16[3,64,640]{2,1,0:T(8,128)(2,1)S(1)}, u32[]{:S(2)}, u32[]{:S(2)}) collective-permute-start(bf16[3,64,640]{2,1,0:T(8,128)(2,1)S(1)} %get-tuple-element.89.refs_4_), channel_id=1, source_target_pairs={{0,2},{8,9},{2,4},{10,8},{4,6},{12,10},{6,7},{14,12},{7,5},{15,14}... | collective-permute-start | bytes 737288 | tf_op jit(solution)/shard_map/ppermute | solution.py:33
  10.5 0.0 copy-start.1
  10.5 0.7 %copy-done.1 = s32[2,3]{1,0:T(2,128)S(1)} copy-done((s32[2,3]{1,0:T(2,128)S(1)}, s32[2,3]{1,0:T(2,128)}, u32[]{:S(2)}) %copy-start.1) | copy-done | bytes 48
  11.2 2.5 %shard_map.104 = (bf16[2,640,64]{2,1,0:T(8,128)(2,1)S(1)}, bf16[2,128,64]{2,1,0:T(8,128)(2,1)S(1)}, bf16[2,128,64]{2,1,0:T(8,128)(2,1)S(1)}, bf16[2,640,640]{2,1...) custom-call(s32[2,3]{1,0:T(2,128)S(1)} %copy-done.1, ...), custom_call_target="tpu_custom_call" | custom-call | tf_op jit(solution)/shard_map/pallas_call | solution.py:137
  13.7 0.1 collective-permute-start.6
  13.7 1.6 %collective-permute-start.5 = (bf16[3,64,640]{2,1,0:T(8,128)(2,1)S(1)}, bf16[3,64,640]{2,1,0:T(8,128)(2,1)S(1)}, u32[]{:S(2)}, u32[]{:S(2)}) collective-permute-start(bf16[3,64,640]{2,1,0:T(8,128)(2,1)S(1)} %collective-permute-done.1.refs_3_), channel_id=1, source_target_pairs={{0,2},{8,9},{2,4},{10,8},{4,6},{12,10},{6,7},{14,12},{7,5},{15,14}... | collective-permute-start | bytes 737288 | tf_op jit(solution)/shard_map/ppermute | solution.py:33
  15.4 2.9 %shard_map.105 = (bf16[2,640,5120]{2,1,0:T(8,128)(2,1)}, bf16[2,128,5120]{2,1,0:T(8,128)(2,1)}, bf16[2,128,5120]{2,1,0:T(8,128)(2,1)}, bf16[2,640,640]{2,1,0:T(8...) custom-call(bf16[2,640,64]{2,1,0:T(8,128)(2,1)S(1)} %get-tuple-element.85.refs_0_, ...), custom_call_target="tpu_custom_call" | custom-call | flops 146800640 | bytes 4587520 | tf_op jit(solution)/shard_map/pallas_call | solution.py:175
  18.3 0.1 collective-permute-start.10
  18.4 1.6 %collective-permute-start.11 = (bf16[3,64,640]{2,1,0:T(8,128)(2,1)S(1)}, bf16[3,64,640]{2,1,0:T(8,128)(2,1)S(1)}, u32[]{:S(2)}, u32[]{:S(2)}) collective-permute-start(bf16[3,64,640]{2,1,0:T(8,128)(2,1)S(1)} %collective-permute-done.7.refs_3_), channel_id=1, source_target_pairs={{0,2},{8,9},{2,4},{10,8},{4,6},{12,10},{6,7},{14,12},{7,5},{15,14}... | collective-permute-start | bytes 737288 | tf_op jit(solution)/shard_map/ppermute | solution.py:33
  20.0 2.9 %shard_map.106 = (bf16[2,640,5120]{2,1,0:T(8,128)(2,1)}, bf16[2,128,5120]{2,1,0:T(8,128)(2,1)}, bf16[2,128,5120]{2,1,0:T(8,128)(2,1)}, bf16[2,640,640]{2,1,0:T(8...) custom-call(bf16[2,640,64]{2,1,0:T(8,128)(2,1)S(1)} %get-tuple-eleme, ...), custom_call_target="tpu_custom_call", output_to_operand_aliasing={{0}: (11, {}), {1}: (12, {}), {2}: (13, {})} | custom-call | flops 146800640 | bytes 4587520 | tf_op jit(solution)/shard_map/pallas_call | solution.py:175
  22.9 0.1 collective-permute-start.9
  23.0 1.6 %collective-permute-start.8 = (bf16[3,64,640]{2,1,0:T(8,128)(2,1)S(1)}, bf16[3,64,640]{2,1,0:T(8,128)(2,1)S(1)}, u32[]{:S(2)}, u32[]{:S(2)}) collective-permute-start(bf16[3,64,640]{2,1,0:T(8,128)(2,1)S(1)} %collective-permute-done.5.refs_3_), channel_id=1, source_target_pairs={{0,2},{8,9},{2,4},{10,8},{4,6},{12,10},{6,7},{14,12},{7,5},{15,14}... | collective-permute-start | bytes 737288 | tf_op jit(solution)/shard_map/ppermute | solution.py:33
  24.5 2.9 %shard_map.107 = (bf16[2,640,5120]{2,1,0:T(8,128)(2,1)}, bf16[2,128,5120]{2,1,0:T(8,128)(2,1)}, bf16[2,128,5120]{2,1,0:T(8,128)(2,1)}, bf16[2,640,640]{2,1,0:T(8...) custom-call(bf16[2,640,64]{2,1,0:T(8,128)(2,1)S(1)} %get-tuple-eleme, ...), custom_call_target="tpu_custom_call", output_to_operand_aliasing={{0}: (11, {}), {1}: (12, {}), {2}: (13, {})} | custom-call | flops 146800640 | bytes 4587520 | tf_op jit(solution)/shard_map/pallas_call | solution.py:175
  27.5 0.1 collective-permute-start.14
  27.5 0.9 %collective-permute-start.15 = (bf16[3,64,640]{2,1,0:T(8,128)(2,1)S(1)}, bf16[3,64,640]{2,1,0:T(8,128)(2,1)S(1)}, u32[]{:S(2)}, u32[]{:S(2)}) collective-permute-start(bf16[3,64,640]{2,1,0:T(8,128)(2,1)S(1)} %collective-permute-done.11.refs_3_), channel_id=1, source_target_pairs={{0,2},{8,9},{2,4},{10,8},{4,6},{12,10},{6,7},{14,12},{7,5},{15,14}... | collective-permute-start | bytes 737288 | tf_op jit(solution)/shard_map/ppermute | solution.py:33
  28.5 2.9 %shard_map.108 = (bf16[2,640,5120]{2,1,0:T(8,128)(2,1)}, bf16[2,128,5120]{2,1,0:T(8,128)(2,1)}, bf16[2,128,5120]{2,1,0:T(8,128)(2,1)}, bf16[2,640,640]{2,1,0:T(8...) custom-call(bf16[2,640,64]{2,1,0:T(8,128)(2,1)S(1)} %get-tuple-eleme, ...), custom_call_target="tpu_custom_call", output_to_operand_aliasing={{0}: (11, {}), {1}: (12, {}), {2}: (13, {})} | custom-call | flops 146800640 | bytes 4587520 | tf_op jit(solution)/shard_map/pallas_call | solution.py:175
  31.4 0.1 collective-permute-start.13
  31.5 1.3 %collective-permute-start.12 = (bf16[3,64,640]{2,1,0:T(8,128)(2,1)S(1)}, bf16[3,64,640]{2,1,0:T(8,128)(2,1)S(1)}, u32[]{:S(2)}, u32[]{:S(2)}) collective-permute-start(bf16[3,64,640]{2,1,0:T(8,128)(2,1)S(1)} %collective-permute-done.8.refs_3_), channel_id=1, source_target_pairs={{0,2},{8,9},{2,4},{10,8},{4,6},{12,10},{6,7},{14,12},{7,5},{15,14}... | collective-permute-start | bytes 737288 | tf_op jit(solution)/shard_map/ppermute | solution.py:33
  32.8 2.9 %shard_map.109 = (bf16[2,640,5120]{2,1,0:T(8,128)(2,1)}, bf16[2,128,5120]{2,1,0:T(8,128)(2,1)}, bf16[2,128,5120]{2,1,0:T(8,128)(2,1)}, bf16[2,640,640]{2,1,0:T(8...) custom-call(bf16[2,640,64]{2,1,0:T(8,128)(2,1)S(1)} %get-tuple-eleme, ...), custom_call_target="tpu_custom_call", output_to_operand_aliasing={{0}: (11, {}), {1}: (12, {}), {2}: (13, {})} | custom-call | flops 146800640 | bytes 4587520 | tf_op jit(solution)/shard_map/pallas_call | solution.py:175
  35.7 0.1 collective-permute-start.17
  35.9 2.9 %shard_map.110 = (bf16[2,640,5120]{2,1,0:T(8,128)(2,1)}, bf16[2,128,5120]{2,1,0:T(8,128)(2,1)}, bf16[2,128,5120]{2,1,0:T(8,128)(2,1)}, bf16[2,640,640]{2,1,0:T(8...) custom-call(bf16[2,640,64]{2,1,0:T(8,128)(2,1)S(1)} %get-tuple-eleme, ...), custom_call_target="tpu_custom_call", output_to_operand_aliasing={{0}: (11, {}), {1}: (12, {}), {2}: (13, {})} | custom-call | flops 146800640 | bytes 4587520 | tf_op jit(solution)/shard_map/pallas_call | solution.py:175
  38.8 0.5 %collective-permute-start.16 = (bf16[3,64,640]{2,1,0:T(8,128)(2,1)S(1)}, bf16[3,64,640]{2,1,0:T(8,128)(2,1)S(1)}, u32[]{:S(2)}, u32[]{:S(2)}) collective-permute-start(bf16[3,64,640]{2,1,0:T(8,128)(2,1)S(1)} %collective-permute-done.12.refs_3_), channel_id=1, source_target_pairs={{0,8},{8,0},{1,9},{9,1},{2,10},{10,2},{3,11},{11,3},{4,12},{12,4},... | collective-permute-start | bytes 737288 | tf_op jit(solution)/shard_map/ppermute | solution.py:37
  39.3 2.9 %shard_map.111 = (bf16[2,640,5120]{2,1,0:T(8,128)(2,1)}, bf16[2,128,5120]{2,1,0:T(8,128)(2,1)}, bf16[2,128,5120]{2,1,0:T(8,128)(2,1)}, bf16[2,640,640]{2,1,0:T(8...) custom-call(bf16[2,640,64]{2,1,0:T(8,128)(2,1)S(1)} %get-tuple-eleme, ...), custom_call_target="tpu_custom_call", output_to_operand_aliasing={{0}: (11, {}), {1}: (12, {}), {2}: (13, {})} | custom-call | flops 146800640 | bytes 4587520 | tf_op jit(solution)/shard_map/pallas_call | solution.py:175
  42.3 1.9 %shard_map.112 = (bf16[2,640,5120]{2,1,0:T(8,128)(2,1)}, bf16[2,128,5120]{2,1,0:T(8,128)(2,1)}, bf16[2,128,5120]{2,1,0:T(8,128)(2,1)}) custom-call(bf16[2,640,64]{2,1,0:T(8,128)(2,1)S(1)} %get-tuple-element.85.refs_0_, bf16[2,128,64]{2,1,0:T(8,128)(2,1)S(1)} %get-tuple-element.86.refs_1_, ...), custom_call_target="tpu_custom_call", output_to_operand_aliasing={{0}: (11, {}), {1}: (12, {}), {2}: (13, {})} | custom-call | flops 146800640 | bytes 4587520 | tf_op jit(solution)/shard_map/pallas_call | solution.py:175
  (18 shorter events, 0.0 us)
Async XLA Ops:
  0.6 2.2 %collective-permute-start = (bf16[2,3,64,640]{3,2,1,0:T(8,128)(2,1)}, bf16[2,3,64,640]{3,2,1,0:T(8,128)(2,1)S(1)}, u32[]{:S(2)}, u32[]{:S(2)}) collective-permute-start(bf16[2,3,64,640]{3,2,1,0:T(8,128)(2,1)} %bitcast.10), channel_id=1, source_target_pairs={{0,8},{8,0},{1,9},{9,1},{2,10},{10,2},{3,11},{11,3},{4,12},{12,4},... | collective-permute-start | bytes 1474568 | tf_op jit(solution)/shard_map/ppermute | solution.py:37
  2.8 0.7 %copy-start = (s32[2,3]{1,0:T(2,128)S(1)}, s32[2,3]{1,0:T(2,128)}, u32[]{:S(2)}) copy-start(s32[2,3]{1,0:T(2,128)} %owners.3) | copy-start | bytes 76
  5.4 8.2 %collective-permute-start.1 = (bf16[3,64,640]{2,1,0:T(8,128)(2,1)S(1)}, bf16[3,64,640]{2,1,0:T(8,128)(2,1)S(1)}, u32[]{:S(2)}, u32[]{:S(2)}) collective-permute-start(bf16[3,64,640]{2,1,0:T(8,128)(2,1)S(1)} %get-tuple-element.81.refs_3_), channel_id=1, source_target_pairs={{0,2},{8,9},{2,4},{10,8},{4,6},{12,10},{6,7},{14,12},{7,5},{15,14}... | collective-permute-start | bytes 737288 | tf_op jit(solution)/shard_map/ppermute | solution.py:33
  8.4 2.1 %collective-permute-start.2 = (bf16[2,64,640]{2,1,0:T(8,128)(2,1)}, bf16[2,64,640]{2,1,0:T(8,128)(2,1)S(1)}, u32[]{:S(2)}, u32[]{:S(2)}) collective-permute-start(bf16[2,64,640]{2,1,0:T(8,128)(2,1)} %bitcast.12), channel_id=1, source_target_pairs={{0,8},{8,0},{1,9},{9,1},{2,10},{10,2},{3,11},{11,3},{4,12},{12,4},... | collective-permute-start | bytes 491528 | tf_op jit(solution)/shard_map/ppermute | solution.py:37
  8.4 2.1 %collective-permute-start.3 = (bf16[2,64,128]{2,1,0:T(8,128)(2,1)}, bf16[2,64,128]{2,1,0:T(8,128)(2,1)S(1)}, u32[]{:S(2)}, u32[]{:S(2)}) collective-permute-start(bf16[2,64,128]{2,1,0:T(8,128)(2,1)} %bitcast.14), channel_id=1, source_target_pairs={{0,8},{8,0},{1,9},{9,1},{2,10},{10,2},{3,11},{11,3},{4,12},{12,4},... | collective-permute-start | bytes 98312 | tf_op jit(solution)/shard_map/ppermute | solution.py:37
  8.9 1.6 %collective-permute-start.4 = (bf16[2,64,128]{2,1,0:T(8,128)(2,1)}, bf16[2,64,128]{2,1,0:T(8,128)(2,1)S(1)}, u32[]{:S(2)}, u32[]{:S(2)}) collective-permute-start(bf16[2,64,128]{2,1,0:T(8,128)(2,1)} %bitcast.16), channel_id=1, source_target_pairs={{0,8},{8,0},{1,9},{9,1},{2,10},{10,2},{3,11},{11,3},{4,12},{12,4},... | collective-permute-start | bytes 98312 | tf_op jit(solution)/shard_map/ppermute | solution.py:37
  8.9 9.4 %collective-permute-start.7 = (bf16[3,64,640]{2,1,0:T(8,128)(2,1)S(1)}, bf16[3,64,640]{2,1,0:T(8,128)(2,1)S(1)}, u32[]{:S(2)}, u32[]{:S(2)}) collective-permute-start(bf16[3,64,640]{2,1,0:T(8,128)(2,1)S(1)} %get-tuple-element.89.refs_4_), channel_id=1, source_target_pairs={{0,2},{8,9},{2,4},{10,8},{4,6},{12,10},{6,7},{14,12},{7,5},{15,14}... | collective-permute-start | bytes 737288 | tf_op jit(solution)/shard_map/ppermute | solution.py:33
  10.5 0.7 %copy-start.1 = (s32[2,3]{1,0:T(2,128)S(1)}, s32[2,3]{1,0:T(2,128)}, u32[]{:S(2)}) copy-start(s32[2,3]{1,0:T(2,128)} %owners.3) | copy-start | bytes 76
  13.7 6.3 %collective-permute-start.6 = (bf16[3,64,640]{2,1,0:T(8,128)(2,1)S(1)}, bf16[3,64,640]{2,1,0:T(8,128)(2,1)S(1)}, u32[]{:S(2)}, u32[]{:S(2)}) collective-permute-start(bf16[3,64,640]{2,1,0:T(8,128)(2,1)S(1)} %collective-permute-done.1.refs_3_), channel_id=1, source_target_pairs={{0,8},{8,0},{1,9},{9,1},{2,10},{10,2},{3,11},{11,3},{4,12},{12,4},... | collective-permute-start | bytes 737288 | tf_op jit(solution)/shard_map/ppermute | solution.py:37
  13.7 9.1 %collective-permute-start.5 = (bf16[3,64,640]{2,1,0:T(8,128)(2,1)S(1)}, bf16[3,64,640]{2,1,0:T(8,128)(2,1)S(1)}, u32[]{:S(2)}, u32[]{:S(2)}) collective-permute-start(bf16[3,64,640]{2,1,0:T(8,128)(2,1)S(1)} %collective-permute-done.1.refs_3_), channel_id=1, source_target_pairs={{0,2},{8,9},{2,4},{10,8},{4,6},{12,10},{6,7},{14,12},{7,5},{15,14}... | collective-permute-start | bytes 737288 | tf_op jit(solution)/shard_map/ppermute | solution.py:33
  18.3 6.2 %collective-permute-start.10 = (bf16[3,64,640]{2,1,0:T(8,128)(2,1)S(1)}, bf16[3,64,640]{2,1,0:T(8,128)(2,1)S(1)}, u32[]{:S(2)}, u32[]{:S(2)}) collective-permute-start(bf16[3,64,640]{2,1,0:T(8,128)(2,1)S(1)} %collective-permute-done.7.refs_3_), channel_id=1, source_target_pairs={{0,8},{8,0},{1,9},{9,1},{2,10},{10,2},{3,11},{11,3},{4,12},{12,4},... | collective-permute-start | bytes 737288 | tf_op jit(solution)/shard_map/ppermute | solution.py:37
  18.4 9.1 %collective-permute-start.11 = (bf16[3,64,640]{2,1,0:T(8,128)(2,1)S(1)}, bf16[3,64,640]{2,1,0:T(8,128)(2,1)S(1)}, u32[]{:S(2)}, u32[]{:S(2)}) collective-permute-start(bf16[3,64,640]{2,1,0:T(8,128)(2,1)S(1)} %collective-permute-done.7.refs_3_), channel_id=1, source_target_pairs={{0,2},{8,9},{2,4},{10,8},{4,6},{12,10},{6,7},{14,12},{7,5},{15,14}... | collective-permute-start | bytes 737288 | tf_op jit(solution)/shard_map/ppermute | solution.py:33
  22.9 5.6 %collective-permute-start.9 = (bf16[3,64,640]{2,1,0:T(8,128)(2,1)S(1)}, bf16[3,64,640]{2,1,0:T(8,128)(2,1)S(1)}, u32[]{:S(2)}, u32[]{:S(2)}) collective-permute-start(bf16[3,64,640]{2,1,0:T(8,128)(2,1)S(1)} %collective-permute-done.5.refs_3_), channel_id=1, source_target_pairs={{0,8},{8,0},{1,9},{9,1},{2,10},{10,2},{3,11},{11,3},{4,12},{12,4},... | collective-permute-start | bytes 737288 | tf_op jit(solution)/shard_map/ppermute | solution.py:37
  23.0 8.4 %collective-permute-start.8 = (bf16[3,64,640]{2,1,0:T(8,128)(2,1)S(1)}, bf16[3,64,640]{2,1,0:T(8,128)(2,1)S(1)}, u32[]{:S(2)}, u32[]{:S(2)}) collective-permute-start(bf16[3,64,640]{2,1,0:T(8,128)(2,1)S(1)} %collective-permute-done.5.refs_3_), channel_id=1, source_target_pairs={{0,2},{8,9},{2,4},{10,8},{4,6},{12,10},{6,7},{14,12},{7,5},{15,14}... | collective-permute-start | bytes 737288 | tf_op jit(solution)/shard_map/ppermute | solution.py:33
  27.5 5.3 %collective-permute-start.14 = (bf16[3,64,640]{2,1,0:T(8,128)(2,1)S(1)}, bf16[3,64,640]{2,1,0:T(8,128)(2,1)S(1)}, u32[]{:S(2)}, u32[]{:S(2)}) collective-permute-start(bf16[3,64,640]{2,1,0:T(8,128)(2,1)S(1)} %collective-permute-done.11.refs_3_), channel_id=1, source_target_pairs={{0,8},{8,0},{1,9},{9,1},{2,10},{10,2},{3,11},{11,3},{4,12},{12,4},... | collective-permute-start | bytes 737288 | tf_op jit(solution)/shard_map/ppermute | solution.py:37
  27.5 8.2 %collective-permute-start.15 = (bf16[3,64,640]{2,1,0:T(8,128)(2,1)S(1)}, bf16[3,64,640]{2,1,0:T(8,128)(2,1)S(1)}, u32[]{:S(2)}, u32[]{:S(2)}) collective-permute-start(bf16[3,64,640]{2,1,0:T(8,128)(2,1)S(1)} %collective-permute-done.11.refs_3_), channel_id=1, source_target_pairs={{0,2},{8,9},{2,4},{10,8},{4,6},{12,10},{6,7},{14,12},{7,5},{15,14}... | collective-permute-start | bytes 737288 | tf_op jit(solution)/shard_map/ppermute | solution.py:33
  31.4 4.4 %collective-permute-start.13 = (bf16[3,64,640]{2,1,0:T(8,128)(2,1)S(1)}, bf16[3,64,640]{2,1,0:T(8,128)(2,1)S(1)}, u32[]{:S(2)}, u32[]{:S(2)}) collective-permute-start(bf16[3,64,640]{2,1,0:T(8,128)(2,1)S(1)} %collective-permute-done.8.refs_3_), channel_id=1, source_target_pairs={{0,8},{8,0},{1,9},{9,1},{2,10},{10,2},{3,11},{11,3},{4,12},{12,4},... | collective-permute-start | bytes 737288 | tf_op jit(solution)/shard_map/ppermute | solution.py:37
  31.5 7.3 %collective-permute-start.12 = (bf16[3,64,640]{2,1,0:T(8,128)(2,1)S(1)}, bf16[3,64,640]{2,1,0:T(8,128)(2,1)S(1)}, u32[]{:S(2)}, u32[]{:S(2)}) collective-permute-start(bf16[3,64,640]{2,1,0:T(8,128)(2,1)S(1)} %collective-permute-done.8.refs_3_), channel_id=1, source_target_pairs={{0,2},{8,9},{2,4},{10,8},{4,6},{12,10},{6,7},{14,12},{7,5},{15,14}... | collective-permute-start | bytes 737288 | tf_op jit(solution)/shard_map/ppermute | solution.py:33
  35.7 3.6 %collective-permute-start.17 = (bf16[3,64,640]{2,1,0:T(8,128)(2,1)S(1)}, bf16[3,64,640]{2,1,0:T(8,128)(2,1)S(1)}, u32[]{:S(2)}, u32[]{:S(2)}) collective-permute-start(bf16[3,64,640]{2,1,0:T(8,128)(2,1)S(1)} %collective-permute-done.15.refs_3_), channel_id=1, source_target_pairs={{0,8},{8,0},{1,9},{9,1},{2,10},{10,2},{3,11},{11,3},{4,12},{12,4},... | collective-permute-start | bytes 737288 | tf_op jit(solution)/shard_map/ppermute | solution.py:37
  38.8 3.5 %collective-permute-start.16 = (bf16[3,64,640]{2,1,0:T(8,128)(2,1)S(1)}, bf16[3,64,640]{2,1,0:T(8,128)(2,1)S(1)}, u32[]{:S(2)}, u32[]{:S(2)}) collective-permute-start(bf16[3,64,640]{2,1,0:T(8,128)(2,1)S(1)} %collective-permute-done.12.refs_3_), channel_id=1, source_target_pairs={{0,8},{8,0},{1,9},{9,1},{2,10},{10,2},{3,11},{11,3},{4,12},{12,4},... | collective-permute-start | bytes 737288 | tf_op jit(solution)/shard_map/ppermute | solution.py:37

commit v4 on v3

v4 whole, which is shorter than its diff:
```python
import functools

import jax
import jax.numpy as jnp
from jax import lax
from jax.experimental import pallas as pl
from jax.experimental.pallas import tpu as pltpu
from jax.sharding import PartitionSpec as P

numerator_gain = 16.0
LANES = 128
MIB = 1024 * 1024
SMEM = pl.BlockSpec(memory_space=pltpu.SMEM)
VMEM = pl.BlockSpec(memory_space=pltpu.VMEM)
HBM = pl.BlockSpec(memory_space=pltpu.HBM)
ANY = pl.BlockSpec(memory_space=pl.ANY)


def in_hbm(array):
    return pltpu.with_memory_space_constraint(array, pltpu.HBM)


def in_vmem(array):
    return pltpu.with_memory_space_constraint(array, pltpu.VMEM)


def ring_order(n):
    return list(range(0, n, 2)) + list(range(n - 1, 0, -2))


def ring_pass(array, n):
    order = ring_order(n)
    pairs = []
    for k in range(n):
        pairs.append((order[k], order[(k + 1) % n]))
        pairs.append((n + order[k], n + order[(k - 1) % n]))
    return lax.ppermute(array, ("rollout", "tensor"), pairs)


def swap_cores(array):
    return lax.ppermute(array, "rollout", [(0, 1), (1, 0)])


def place_of(n, step, from_core, tensor):
    position = jnp.where(tensor % 2 == 0, tensor // 2, n - 1 - tensor // 2)
    k = position + jnp.where(from_core == 0, -step, step)
    k = jnp.where(k < 0, k + n, jnp.where(k >= n, k - n, k))
    return jnp.where(k < n // 2, 2 * k, 2 * n - 1 - 2 * k)


def column_blocks(n, pieces, cols):
    core = lax.axis_index("rollout")
    tensor = lax.axis_index("tensor")
    blocks = []
    for step, own_ring, own_layer in pieces:
        place = place_of(n, step, core if own_ring else 1 - core, tensor)
        blocks.append((core if own_layer else 1 - core, pl.ds(pl.multiple_of(place * cols, LANES), cols)))
    return blocks


def fetch_kernel(n, pieces, *refs):
    bases, blocks, sems = refs[0:3], refs[3:6], refs[6]
    loads = []
    for i, (layer, columns) in enumerate(column_blocks(n, pieces, blocks[0].shape[2])):
        for proj in range(3):
            load = pltpu.make_async_copy(bases[proj].at[layer, :, columns], blocks[proj].at[i], sems.at[3 * i + proj])
            load.start()
            loads.append(load)
    for load in loads:
        load.wait()


def fetch(n, cols, bases, pieces):
    shapes = [jax.ShapeDtypeStruct((len(pieces), base.shape[1], cols), base.dtype) for base in bases]
    return pl.pallas_call(
        functools.partial(fetch_kernel, n, pieces),
        in_specs=[HBM] * 3,
        out_specs=[VMEM] * 3,
        out_shape=shapes,
        scratch_shapes=[pltpu.SemaphoreType.DMA((3 * len(pieces),))],
        compiler_params=pltpu.CompilerParams(vmem_limit_bytes=4 * MIB),
        cost_estimate=pl.CostEstimate(
            flops=0, bytes_accessed=2 * sum(x.size * x.dtype.itemsize for x in shapes), transcendentals=0
        ),
    )(*[in_hbm(base) for base in bases])


def choose_a_kernel(owners, own, other, first, second):
    core = lax.axis_index("rollout")
    for out, layer in ((first, core), (second, 1 - core)):
        for proj in range(own.shape[1]):
            mine = owners[layer, proj] == core
            out[proj] = jnp.where(mine, own[layer, proj], other[layer, proj])


def choose_a(owners, own, other):
    piece = jax.ShapeDtypeStruct(own.shape[1:], own.dtype)
    return pl.pallas_call(
        choose_a_kernel,
        in_specs=[SMEM, VMEM, VMEM],
        out_specs=[VMEM, VMEM],
        out_shape=[piece, piece],
        compiler_params=pltpu.CompilerParams(vmem_limit_bytes=4 * MIB),
    )(in_hbm(owners), in_vmem(own), other)


def choose_b_kernel(owners, *refs):
    core = lax.axis_index("rollout")
    for proj in range(3):
        own, other, out = refs[proj], refs[3 + proj], refs[6 + proj]
        for layer in range(own.shape[0]):
            mine = owners[layer, proj] == core
            out[layer] = jnp.where(mine, own[layer], other[layer]).T


def choose_b(owners, own, other):
    return pl.pallas_call(
        choose_b_kernel,
        in_specs=[SMEM] + [VMEM] * 6,
        out_specs=[VMEM] * 3,
        out_shape=[jax.ShapeDtypeStruct((x.shape[0], x.shape[2], x.shape[1]), x.dtype) for x in own],
        compiler_params=pltpu.CompilerParams(vmem_limit_bytes=4 * MIB),
    )(in_hbm(owners), *[in_vmem(x) for x in own], *other)


def merge_kernel(n, pieces, scale, fresh, *refs):
    b_refs, a_refs, bases = refs[0:3], refs[3:5], refs[5:8]
    at = 8 if fresh else 11
    outs, bufs, sems = refs[at : at + 3], refs[at + 3 : at + 6], refs[at + 6]
    cols = a_refs[0].shape[2]
    stores = []
    for i, (layer, columns) in enumerate(column_blocks(n, pieces, cols)):
        for proj in range(3):
            delta = jnp.dot(b_refs[proj][layer], a_refs[i][proj], preferred_element_type=jnp.float32)
            block = bases[proj][i] if fresh else bases[proj][layer, :, columns]
            merged = block.astype(jnp.float32) + scale * delta
            bufs[proj][i] = merged.astype(jnp.bfloat16)
            store = pltpu.make_async_copy(bufs[proj].at[i], outs[proj].at[layer, :, columns], sems.at[3 * i + proj])
            store.start()
            stores.append(store)
    for store in stores:
        store.wait()


def merge(n, scale, b, a_list, bases, shapes, outs, pieces):
    fresh = outs is None
    rank, cols = a_list[0].shape[1:]
    rows = sum(base.shape[1] for base in bases)
    return pl.pallas_call(
        functools.partial(merge_kernel, n, pieces, scale, fresh),
        in_specs=[VMEM] * (3 + len(a_list) + 3) + [HBM] * (0 if fresh else 3),
        out_specs=[HBM] * 3,
        out_shape=shapes,
        scratch_shapes=[pltpu.VMEM((len(pieces), base.shape[1], cols), base.dtype) for base in bases]
        + [pltpu.SemaphoreType.DMA((3 * len(pieces),))],
        input_output_aliases={} if fresh else {6 + len(a_list) + i: i for i in range(3)},
        compiler_params=pltpu.CompilerParams(vmem_limit_bytes=16 * MIB),
        cost_estimate=pl.CostEstimate(
            flops=2 * len(pieces) * rows * cols * rank,
            bytes_accessed=4 * len(pieces) * rows * cols,
            transcendentals=0,
        ),
    )(*b, *a_list, *(bases if fresh else [in_vmem(base) for base in bases]), *([] if fresh else outs))


def per_device(
    n,
    owners,
    base_query,
    base_key,
    base_value,
    left_shared_matrix,
    right_queries_matrix,
    right_keys_matrix,
    right_values_matrix,
):
    layers, projs, rank, cols = left_shared_matrix.shape[1:]
    scale = numerator_gain / rank
    bases = (base_query, base_key, base_value)
    rights = (right_queries_matrix, right_keys_matrix, right_values_matrix)
    last = n // 2

    own_a = left_shared_matrix[0]
    own_b = [jnp.swapaxes(right[0], 1, 2) for right in rights]

    if cols % LANES == 0:
        own_pieces = [(0, True, True), (0, True, False)]
        blocks = fetch(n, cols, bases, own_pieces)
        other_a, blocks = lax.optimization_barrier((swap_cores(own_a), blocks))
        first, second = choose_a(owners, own_a, other_a)
        held = [first, second]
        first = ring_pass(first, n)
        second = ring_pass(second, n)
        b = choose_b(owners, own_b, [swap_cores(x) for x in own_b])
        first, b = lax.optimization_barrier((first, b))

        def go(chunks, pieces, outs=None):
            return merge(n, scale, b, chunks, bases if outs else blocks, shapes, outs, pieces)

        shapes = [jax.ShapeDtypeStruct(base.shape, base.dtype) for base in bases]
        outs = go(held, own_pieces)
        ready = []
        for step in range(1, last + 1):
            if step > 1:
                outs = go(*ready.pop(0), outs)
            ready.append(([first, swap_cores(first)], [(step, True, True), (step, False, False)]))
            if step < last:
                first = ring_pass(first, n)
                second, outs = lax.optimization_barrier((second, outs))
                ready.append(([second, swap_cores(second)], [(step, True, False), (step, False, True)]))
                outs = go(*ready.pop(0), outs)
                first, outs = lax.optimization_barrier((first, outs))
                if step < last - 1:
                    second = ring_pass(second, n)
        for item in ready:
            outs = go(*item, outs)
        return tuple(outs)

    core = lax.axis_index("rollout")
    tensor = lax.axis_index("tensor")
    mine = owners == core
    a = jnp.where(mine[:, :, None, None], own_a, swap_cores(own_a))
    b = [jnp.where(mine[:, proj, None, None], x, swap_cores(x)) for proj, x in enumerate(own_b)]
    full = jnp.zeros((layers, projs, rank, n * cols), own_a.dtype)

    def put(full, piece, layer, step, from_core):
        start = place_of(n, step, from_core, tensor) * cols
        return lax.dynamic_update_slice(full, piece[None], (layer, 0, 0, start))

    first = jnp.where(core == 0, a[0], a[1])
    second = jnp.where(core == 0, a[1], a[0])
    full = put(full, first, core, 0, core)
    full = put(full, second, 1 - core, 0, core)
    for step in range(1, last + 1):
        first = ring_pass(first, n)
        full = put(full, first, core, step, core)
        full = put(full, swap_cores(first), 1 - core, step, 1 - core)
        if step < last:
            second = ring_pass(second, n)
            full = put(full, second, 1 - core, step, core)
            full = put(full, swap_cores(second), core, step, 1 - core)
    merged = []
    for proj in range(projs):
        delta = jnp.einsum("lkr,lkc->lrc", b[proj], full[:, proj], preferred_element_type=jnp.float32)
        merged.append((bases[proj].astype(jnp.float32) + scale * delta).astype(jnp.bfloat16))
    return tuple(merged)


def solution(mesh):
    return jax.shard_map(
        functools.partial(per_device, mesh.shape["tensor"]),
        mesh=mesh,
        in_specs=(
            P("copies", None),
            P("copies", "tensor", None),
            P("copies", "tensor", None),
            P("copies", "tensor", None),
            P("rollout", "copies", None, None, "tensor"),
            P("rollout", "copies", "tensor", None),
            P("rollout", "copies", "tensor", None),
            P("rollout", "copies", "tensor", None),
        ),
        out_specs=(
            P("copies", "tensor", None),
            P("copies", "tensor", None),
            P("copies", "tensor", None),
        ),
        check_vma=False,
    )
```

time: 44.6 us -> 35.7 us (0.80)
  Pallas kernels: 26.6 us -> 18.1 us
  local copies, waits for them, and re-layouts: 1.35 us -> 0.03 us
  waiting for transfers between devices: 1.75 us -> 2.89 us
    pallas_call x10 -> x11, Pallas kernels: 26.6 us -> 18.1 us  [the longest x8 14.6 us: merge(): pl.pallas_call(functools.partial(merge_kernel, n, pieces, scale, fresh),...]
    ppermute x7, waiting for transfers between devices: 0.02 us -> 2.87 us  [ring_pass(): return lax.ppermute(array, ('rollout', 'tensor'), pairs)]
    ppermute x11, waiting for transfers between devices: 1.73 us -> 0.03 us  [swap_cores(): return lax.ppermute(array, 'rollout', [(0, 1), (1, 0)])]
    unnamed x4 -> x14, local copies, waits for them, and re-layouts: 1.35 us -> 0.03 us
    ppermute x11, starting transfers between devices: 2.03 us -> 1.56 us  [swap_cores(): return lax.ppermute(array, 'rollout', [(0, 1), (1, 0)])]
  transfers between devices with their start and end apart: 18 -> 18, of which waited for: 1 -> 3; matrix products, arithmetic and copies ran while one was open for 0% -> 0% of each run, Pallas kernels for 52% -> 43%
where the time goes in v4:
time: 35.7 us; the launch traced here: 35.5 us
  Pallas kernels  18.1 us (51%)
  starting transfers between devices  13.5 us (38%)
  waiting for transfers between devices  2.89 us (8%)
  between operations  0.86 us (2%)
    pallas_call x8, Pallas kernels, merge(): pl.pallas_call(functools.partial(merge_kernel, n, pieces, scale, fresh),...  14.6 us
    ppermute x7, starting transfers between devices, ring_pass(): return lax.ppermute(array, ('rollout', 'tensor'), pairs)  12 us
    ppermute x7, waiting for transfers between devices, ring_pass(): return lax.ppermute(array, ('rollout', 'tensor'), pairs)  2.87 us
    pallas_call x1, Pallas kernels, fetch(): pl.pallas_call(functools.partial(fetch_kernel, n, pieces), in_specs=[HBM]...  1.77 us
    ppermute x11, starting transfers between devices, swap_cores(): return lax.ppermute(array, 'rollout', [(0, 1), (1, 0)])  1.56 us
    pallas_call x1, Pallas kernels, choose_a(): pl.pallas_call(choose_a_kernel, in_specs=[SMEM, VMEM, VMEM], out_specs=[V...  0.89 us
    pallas_call x1, Pallas kernels, choose_b(): pl.pallas_call(choose_b_kernel, in_specs=[SMEM] + [VMEM] * 6, out_specs=[...  0.88 us
  transfers between devices with their start and end apart: 18, of which 3 were waited for; matrix products, arithmetic and copies ran while one was open for 0% of the time, Pallas kernels for 43%

profile of v4, /device:TPU:0, one launch (start us, length us, event | category | flops | bytes accessed | tf_op | source)
XLA Modules:
  0.0 35.5 jit_solution(1444609319296165524)
XLA Ops:
  0.7 0.5 %collective-permute-start = (bf16[2,3,64,640]{3,2,1,0:T(8,128)(2,1)}, bf16[2,3,64,640]{3,2,1,0:T(8,128)(2,1)S(1)}, u32[]{:S(2)}, u32[]{:S(2)}) collective-permute-start(bf16[2,3,64,640]{3,2,1,0:T(8,128)(2,1)} %bitcast.10), channel_id=1, source_target_pairs={{0,8},{8,0},{1,9},{9,1},{2,10},{10,2},{3,11},{11,3},{4,12},{12,4},... | collective-permute-start | bytes 1474568 | tf_op jit(solution)/shard_map/ppermute | solution.py:41
  1.2 1.8 %shard_map.103 = (bf16[2,640,640]{2,1,0:T(8,128)(2,1)S(1)}, bf16[2,128,640]{2,1,0:T(8,128)(2,1)S(1)}, bf16[2,128,640]{2,1,0:T(8,128)(2,1)S(1)}) custom-call(bf16[2,640,5120]{2,1,0:T(8,128)(2,1)} %refs_5_.13, bf16[2,128,5120]{2,1,0:T(8,128)(2,1)} %refs_6_.13, bf16[2,128,5120]{2,1,0:T(8,128)(2,1)} %refs_7_.13), custom_call_target="tpu_custom_call" | custom-call | bytes 4587520 | tf_op jit(solution)/shard_map/pallas_call | solution.py:75
  3.0 0.0 copy-start.1
  3.0 0.0 collective-permute-done.other
  3.0 0.9 %shard_map.104 = (bf16[3,64,640]{2,1,0:T(8,128)(2,1)S(1)}, bf16[3,64,640]{2,1,0:T(8,128)(2,1)S(1)}) custom-call(s32[2,3]{1,0:T(2,128)} %owners.3, bf16[2,3,64,640]{3,2,1,0:T(8,128)(2,1)S(1)} %bitcast.11, bf16[2,3,64,640]{3,2,1,0:T(8,128)(2,1)S(1)} %collective-permute-done.other), custom_call_target="tpu_custom_call" | custom-call | tf_op jit(solution)/shard_map/pallas_call | solution.py:98
  3.9 2.9 %collective-permute-start.1 = (bf16[3,64,640]{2,1,0:T(8,128)(2,1)S(1)}, bf16[3,64,640]{2,1,0:T(8,128)(2,1)S(1)}, u32[]{:S(2)}, u32[]{:S(2)}) collective-permute-start(bf16[3,64,640]{2,1,0:T(8,128)(2,1)S(1)} %get-tuple-element.68.refs_3_), channel_id=1, source_target_pairs={{0,2},{8,9},{2,4},{10,8},{4,6},{12,10},{6,7},{14,12},{7,5},{15,14}... | collective-permute-start | bytes 737288 | tf_op jit(solution)/shard_map/ppermute | solution.py:37
  6.8 0.0 collective-permute-start.2
  6.8 0.5 %collective-permute-start.3 = (bf16[2,64,128]{2,1,0:T(8,128)(2,1)S(1)}, bf16[2,64,128]{2,1,0:T(8,128)(2,1)S(1)}, u32[]{:S(2)}, u32[]{:S(2)}) collective-permute-start(bf16[2,64,128]{2,1,0:T(8,128)(2,1)S(1)} %bitcast.14), channel_id=1, source_target_pairs={{0,8},{8,0},{1,9},{9,1},{2,10},{10,2},{3,11},{11,3},{4,12},{12,4},... | collective-permute-start | bytes 98312 | tf_op jit(solution)/shard_map/ppermute | solution.py:41
  7.3 0.1 collective-permute-start.4
  7.4 1.6 %collective-permute-start.7 = (bf16[3,64,640]{2,1,0:T(8,128)(2,1)S(1)}, bf16[3,64,640]{2,1,0:T(8,128)(2,1)S(1)}, u32[]{:S(2)}, u32[]{:S(2)}) collective-permute-start(bf16[3,64,640]{2,1,0:T(8,128)(2,1)S(1)} %get-tuple-element.76.refs_4_), channel_id=1, source_target_pairs={{0,2},{8,9},{2,4},{10,8},{4,6},{12,10},{6,7},{14,12},{7,5},{15,14}... | collective-permute-start | bytes 737288 | tf_op jit(solution)/shard_map/ppermute | solution.py:37
  9.0 0.0 collective-permute-done.3.refs_4_
  9.0 0.9 %shard_map.105 = (bf16[2,640,64]{2,1,0:T(8,128)(2,1)S(1)}, bf16[2,128,64]{2,1,0:T(8,128)(2,1)S(1)}, bf16[2,128,64]{2,1,0:T(8,128)(2,1)S(1)}) custom-call(s32[2,3]{1,0:T(2,128)} %owners.3, bf16[2,64,640]{2,1,0:T(8,128)(2,1)S(1)} %bitcast.13, bf16[2,64,128]{2,1,0:T(8,128)(2,1)S(1)} %bitcast.15, bf16[2,64,128]{2,1,0:T(8,128)(2,1)S(1)} %bitcast.17, ...), custom_call_target="tpu_custom_call" | custom-call | tf_op jit(solution)/shard_map/pallas_call | solution.py:117
  9.9 1.1 %collective-permute-done.1.refs_3_ = bf16[3,64,640]{2,1,0:T(8,128)(2,1)S(1)} collective-permute-done((bf16[3,64,640]{2,1,0:T(8,128)(2,1)S(1)}, bf16[3,64,640]{2,1,0:T(8,128)(2,1)S(1)}, u32[]{:S(2)}, u32[]{:S(2)}) %collective-permute-start.1) | collective-permute-done | bytes 245792 | tf_op jit(solution)/shard_map/ppermute | solution.py:37
  10.9 2.1 %collective-permute-start.5 = (bf16[3,64,640]{2,1,0:T(8,128)(2,1)S(1)}, bf16[3,64,640]{2,1,0:T(8,128)(2,1)S(1)}, u32[]{:S(2)}, u32[]{:S(2)}) collective-permute-start(bf16[3,64,640]{2,1,0:T(8,128)(2,1)S(1)} %collective-permute-done.1.refs_3_), channel_id=1, source_target_pairs={{0,2},{8,9},{2,4},{10,8},{4,6},{12,10},{6,7},{14,12},{7,5},{15,14}... | collective-permute-start | bytes 737288 | tf_op jit(solution)/shard_map/ppermute | solution.py:37
  13.0 1.8 %shard_map.106 = (bf16[2,640,5120]{2,1,0:T(8,128)(2,1)}, bf16[2,128,5120]{2,1,0:T(8,128)(2,1)}, bf16[2,128,5120]{2,1,0:T(8,128)(2,1)}) custom-call(bf16[2,640,64]{2,1,0:T(8,128)(2,1)S(1)} %get-tuple-element.72.refs_0_, bf16[2,128,64]{2,1,0:T(8,128)(2,1)S(1)} %get-tuple-element.73.refs_1_, bf16[2,128,64]{2,1,0:T(8,128)(2,1)S(1)} %get-tuple-element.74.refs_2_, ...), custom_call_target="tpu_custom_call" | custom-call | flops 146800640 | bytes 4587520 | tf_op jit(solution)/shard_map/pallas_call | solution.py:149
  14.8 0.2 collective-permute-start.11
  15.1 1.5 %collective-permute-start.10 = (bf16[3,64,640]{2,1,0:T(8,128)(2,1)S(1)}, bf16[3,64,640]{2,1,0:T(8,128)(2,1)S(1)}, u32[]{:S(2)}, u32[]{:S(2)}) collective-permute-start(bf16[3,64,640]{2,1,0:T(8,128)(2,1)S(1)} %collective-permute-done.7.refs_3_), channel_id=1, source_target_pairs={{0,2},{8,9},{2,4},{10,8},{4,6},{12,10},{6,7},{14,12},{7,5},{15,14}... | collective-permute-start | bytes 737288 | tf_op jit(solution)/shard_map/ppermute | solution.py:37
  16.5 1.8 %shard_map.107 = (bf16[2,640,5120]{2,1,0:T(8,128)(2,1)}, bf16[2,128,5120]{2,1,0:T(8,128)(2,1)}, bf16[2,128,5120]{2,1,0:T(8,128)(2,1)}) custom-call(bf16[2,640,64]{2,1,0:T(8,128)(2,1)S(1)} %get-tuple-element.72.refs_0_, bf16[2,128,64]{2,1,0:T(8,128)(2,1)S(1)} %get-tuple-element.73.refs_1_, ...), custom_call_target="tpu_custom_call", output_to_operand_aliasing={{0}: (8, {}), {1}: (9, {}), {2}: (10, {})} | custom-call | flops 146800640 | bytes 4587520 | tf_op jit(solution)/shard_map/pallas_call | solution.py:149
  18.4 0.1 collective-permute-start.9
  18.5 1.6 %collective-permute-start.8 = (bf16[3,64,640]{2,1,0:T(8,128)(2,1)S(1)}, bf16[3,64,640]{2,1,0:T(8,128)(2,1)S(1)}, u32[]{:S(2)}, u32[]{:S(2)}) collective-permute-start(bf16[3,64,640]{2,1,0:T(8,128)(2,1)S(1)} %collective-permute-done.5.refs_3_), channel_id=1, source_target_pairs={{0,2},{8,9},{2,4},{10,8},{4,6},{12,10},{6,7},{14,12},{7,5},{15,14}... | collective-permute-start | bytes 737288 | tf_op jit(solution)/shard_map/ppermute | solution.py:37
  20.1 1.8 %shard_map.108 = (bf16[2,640,5120]{2,1,0:T(8,128)(2,1)}, bf16[2,128,5120]{2,1,0:T(8,128)(2,1)}, bf16[2,128,5120]{2,1,0:T(8,128)(2,1)}) custom-call(bf16[2,640,64]{2,1,0:T(8,128)(2,1)S(1)} %get-tuple-element.72.refs_0_, bf16[2,128,64]{2,1,0:T(8,128)(2,1)S(1)} %get-tuple-element.73.refs_1_, ...), custom_call_target="tpu_custom_call", output_to_operand_aliasing={{0}: (8, {}), {1}: (9, {}), {2}: (10, {})} | custom-call | flops 146800640 | bytes 4587520 | tf_op jit(solution)/shard_map/pallas_call | solution.py:149
  21.9 0.1 collective-permute-start.15
  22.0 1.6 %collective-permute-start.14 = (bf16[3,64,640]{2,1,0:T(8,128)(2,1)S(1)}, bf16[3,64,640]{2,1,0:T(8,128)(2,1)S(1)}, u32[]{:S(2)}, u32[]{:S(2)}) collective-permute-start(bf16[3,64,640]{2,1,0:T(8,128)(2,1)S(1)} %collective-permute-done.10.refs_3_), channel_id=1, source_target_pairs={{0,2},{8,9},{2,4},{10,8},{4,6},{12,10},{6,7},{14,12},{7,5},{15,14}... | collective-permute-start | bytes 737288 | tf_op jit(solution)/shard_map/ppermute | solution.py:37
  23.6 1.8 %shard_map.109 = (bf16[2,640,5120]{2,1,0:T(8,128)(2,1)}, bf16[2,128,5120]{2,1,0:T(8,128)(2,1)}, bf16[2,128,5120]{2,1,0:T(8,128)(2,1)}) custom-call(bf16[2,640,64]{2,1,0:T(8,128)(2,1)S(1)} %get-tuple-element.72.refs_0_, bf16[2,128,64]{2,1,0:T(8,128)(2,1)S(1)} %get-tuple-element.73.refs_1_, ...), custom_call_target="tpu_custom_call", output_to_operand_aliasing={{0}: (8, {}), {1}: (9, {}), {2}: (10, {})} | custom-call | flops 146800640 | bytes 4587520 | tf_op jit(solution)/shard_map/pallas_call | solution.py:149
  25.4 0.1 collective-permute-start.13
  25.5 0.8 %collective-permute-start.12 = (bf16[3,64,640]{2,1,0:T(8,128)(2,1)S(1)}, bf16[3,64,640]{2,1,0:T(8,128)(2,1)S(1)}, u32[]{:S(2)}, u32[]{:S(2)}) collective-permute-start(bf16[3,64,640]{2,1,0:T(8,128)(2,1)S(1)} %collective-permute-done.8.refs_3_), channel_id=1, source_target_pairs={{0,2},{8,9},{2,4},{10,8},{4,6},{12,10},{6,7},{14,12},{7,5},{15,14}... | collective-permute-start | bytes 737288 | tf_op jit(solution)/shard_map/ppermute | solution.py:37
  26.3 1.8 %shard_map.110 = (bf16[2,640,5120]{2,1,0:T(8,128)(2,1)}, bf16[2,128,5120]{2,1,0:T(8,128)(2,1)}, bf16[2,128,5120]{2,1,0:T(8,128)(2,1)}) custom-call(bf16[2,640,64]{2,1,0:T(8,128)(2,1)S(1)} %get-tuple-element.72.refs_0_, bf16[2,128,64]{2,1,0:T(8,128)(2,1)S(1)} %get-tuple-element.73.refs_1_, ...), custom_call_target="tpu_custom_call", output_to_operand_aliasing={{0}: (8, {}), {1}: (9, {}), {2}: (10, {})} | custom-call | flops 146800640 | bytes 4587520 | tf_op jit(solution)/shard_map/pallas_call | solution.py:149
  28.1 0.1 collective-permute-done.14.refs_3_
  28.3 1.8 %shard_map.111 = (bf16[2,640,5120]{2,1,0:T(8,128)(2,1)}, bf16[2,128,5120]{2,1,0:T(8,128)(2,1)}, bf16[2,128,5120]{2,1,0:T(8,128)(2,1)}) custom-call(bf16[2,640,64]{2,1,0:T(8,128)(2,1)S(1)} %get-tuple-element.72.refs_0_, bf16[2,128,64]{2,1,0:T(8,128)(2,1)S(1)} %get-tuple-element.73.refs_1_, ...), custom_call_target="tpu_custom_call", output_to_operand_aliasing={{0}: (8, {}), {1}: (9, {}), {2}: (10, {})} | custom-call | flops 146800640 | bytes 4587520 | tf_op jit(solution)/shard_map/pallas_call | solution.py:149
  30.1 1.7 %collective-permute-done.12.refs_3_ = bf16[3,64,640]{2,1,0:T(8,128)(2,1)S(1)} collective-permute-done((bf16[3,64,640]{2,1,0:T(8,128)(2,1)S(1)}, bf16[3,64,640]{2,1,0:T(8,128)(2,1)S(1)}, u32[]{:S(2)}, u32[]{:S(2)}) %collective-permute-start.12) | collective-permute-done | bytes 245792 | tf_op jit(solution)/shard_map/ppermute | solution.py:37
  31.8 1.8 %shard_map.112 = (bf16[2,640,5120]{2,1,0:T(8,128)(2,1)}, bf16[2,128,5120]{2,1,0:T(8,128)(2,1)}, bf16[2,128,5120]{2,1,0:T(8,128)(2,1)}) custom-call(bf16[2,640,64]{2,1,0:T(8,128)(2,1)S(1)} %get-tuple-element.72.refs_0_, bf16[2,128,64]{2,1,0:T(8,128)(2,1)S(1)} %get-tuple-element.73.refs_1_, ...), custom_call_target="tpu_custom_call", output_to_operand_aliasing={{0}: (8, {}), {1}: (9, {}), {2}: (10, {})} | custom-call | flops 146800640 | bytes 4587520 | tf_op jit(solution)/shard_map/pallas_call | solution.py:149
  33.6 1.8 %shard_map.113 = (bf16[2,640,5120]{2,1,0:T(8,128)(2,1)}, bf16[2,128,5120]{2,1,0:T(8,128)(2,1)}, bf16[2,128,5120]{2,1,0:T(8,128)(2,1)}) custom-call(bf16[2,640,64]{2,1,0:T(8,128)(2,1)S(1)} %get-tuple-element.72.refs_0_, bf16[2,128,64]{2,1,0:T(8,128)(2,1)S(1)} %get-tuple-element.73.refs_1_, ...), custom_call_target="tpu_custom_call", output_to_operand_aliasing={{0}: (8, {}), {1}: (9, {}), {2}: (10, {})} | custom-call | flops 146800640 | bytes 4587520 | tf_op jit(solution)/shard_map/pallas_call | solution.py:149
  (29 shorter events, 0.1 us)
Async XLA Ops:
  0.6 2.4 %copy-start.3 = (bf16[1,2,3,64,640]{4,3,2,1,0:T(8,128)(2,1)S(1)}, bf16[1,2,3,64,640]{4,3,2,1,0:T(8,128)(2,1)}, u32[]{:S(2)}) copy-start(bf16[1,2,3,64,640]{4,3,2,1,0:T(8,128)(2,1)} %param.12) | copy-start | bytes 1474564
  0.6 6.2 %copy-start.4 = (bf16[1,2,640,64]{2,3,1,0:T(8,128)(2,1)S(1)}, bf16[1,2,640,64]{2,3,1,0:T(8,128)(2,1)}, u32[]{:S(2)}) copy-start(bf16[1,2,640,64]{2,3,1,0:T(8,128)(2,1)} %param.13) | copy-start | bytes 491524
  0.7 6.1 %copy-start.5 = (bf16[1,2,128,64]{2,3,1,0:T(8,128)(2,1)S(1)}, bf16[1,2,128,64]{2,3,1,0:T(8,128)(2,1)}, u32[]{:S(2)}) copy-start(bf16[1,2,128,64]{2,3,1,0:T(8,128)(2,1)} %param.14) | copy-start | bytes 98308
  0.7 6.6 %copy-start.6 = (bf16[1,2,128,64]{2,3,1,0:T(8,128)(2,1)S(1)}, bf16[1,2,128,64]{2,3,1,0:T(8,128)(2,1)}, u32[]{:S(2)}) copy-start(bf16[1,2,128,64]{2,3,1,0:T(8,128)(2,1)} %param.15) | copy-start | bytes 98308
  0.7 2.3 %collective-permute-start = (bf16[2,3,64,640]{3,2,1,0:T(8,128)(2,1)}, bf16[2,3,64,640]{3,2,1,0:T(8,128)(2,1)S(1)}, u32[]{:S(2)}, u32[]{:S(2)}) collective-permute-start(bf16[2,3,64,640]{3,2,1,0:T(8,128)(2,1)} %bitcast.10), channel_id=1, source_target_pairs={{0,8},{8,0},{1,9},{9,1},{2,10},{10,2},{3,11},{11,3},{4,12},{12,4},... | collective-permute-start | bytes 1474568 | tf_op jit(solution)/shard_map/ppermute | solution.py:41
  1.2 15.3 %copy-start = (bf16[2,640,5120]{2,1,0:T(8,128)(2,1)S(1)}, bf16[2,640,5120]{2,1,0:T(8,128)(2,1)}, u32[]{:S(2)}) copy-start(bf16[2,640,5120]{2,1,0:T(8,128)(2,1)} %refs_5_.13) | copy-start | bytes 39321604
  1.2 15.3 %copy-start.2 = (bf16[2,128,5120]{2,1,0:T(8,128)(2,1)S(1)}, bf16[2,128,5120]{2,1,0:T(8,128)(2,1)}, u32[]{:S(2)}) copy-start(bf16[2,128,5120]{2,1,0:T(8,128)(2,1)} %refs_7_.13) | copy-start | bytes 7864324
  3.0 13.6 %copy-start.1 = (bf16[2,128,5120]{2,1,0:T(8,128)(2,1)S(1)}, bf16[2,128,5120]{2,1,0:T(8,128)(2,1)}, u32[]{:S(2)}) copy-start(bf16[2,128,5120]{2,1,0:T(8,128)(2,1)} %refs_6_.13) | copy-start | bytes 7864324
  3.9 7.0 %collective-permute-start.1 = (bf16[3,64,640]{2,1,0:T(8,128)(2,1)S(1)}, bf16[3,64,640]{2,1,0:T(8,128)(2,1)S(1)}, u32[]{:S(2)}, u32[]{:S(2)}) collective-permute-start(bf16[3,64,640]{2,1,0:T(8,128)(2,1)S(1)} %get-tuple-element.68.refs_3_), channel_id=1, source_target_pairs={{0,2},{8,9},{2,4},{10,8},{4,6},{12,10},{6,7},{14,12},{7,5},{15,14}... | collective-permute-start | bytes 737288 | tf_op jit(solution)/shard_map/ppermute | solution.py:37
  6.8 2.2 %collective-permute-start.2 = (bf16[2,64,640]{2,1,0:T(8,128)(2,1)S(1)}, bf16[2,64,640]{2,1,0:T(8,128)(2,1)S(1)}, u32[]{:S(2)}, u32[]{:S(2)}) collective-permute-start(bf16[2,64,640]{2,1,0:T(8,128)(2,1)S(1)} %bitcast.12), channel_id=1, source_target_pairs={{0,8},{8,0},{1,9},{9,1},{2,10},{10,2},{3,11},{11,3},{4,12},{12,4},... | collective-permute-start | bytes 491528 | tf_op jit(solution)/shard_map/ppermute | solution.py:41
  6.8 2.2 %collective-permute-start.3 = (bf16[2,64,128]{2,1,0:T(8,128)(2,1)S(1)}, bf16[2,64,128]{2,1,0:T(8,128)(2,1)S(1)}, u32[]{:S(2)}, u32[]{:S(2)}) collective-permute-start(bf16[2,64,128]{2,1,0:T(8,128)(2,1)S(1)} %bitcast.14), channel_id=1, source_target_pairs={{0,8},{8,0},{1,9},{9,1},{2,10},{10,2},{3,11},{11,3},{4,12},{12,4},... | collective-permute-start | bytes 98312 | tf_op jit(solution)/shard_map/ppermute | solution.py:41
  7.3 1.7 %collective-permute-start.4 = (bf16[2,64,128]{2,1,0:T(8,128)(2,1)S(1)}, bf16[2,64,128]{2,1,0:T(8,128)(2,1)S(1)}, u32[]{:S(2)}, u32[]{:S(2)}) collective-permute-start(bf16[2,64,128]{2,1,0:T(8,128)(2,1)S(1)} %bitcast.16), channel_id=1, source_target_pairs={{0,8},{8,0},{1,9},{9,1},{2,10},{10,2},{3,11},{11,3},{4,12},{12,4},... | collective-permute-start | bytes 98312 | tf_op jit(solution)/shard_map/ppermute | solution.py:41
  7.4 7.4 %collective-permute-start.7 = (bf16[3,64,640]{2,1,0:T(8,128)(2,1)S(1)}, bf16[3,64,640]{2,1,0:T(8,128)(2,1)S(1)}, u32[]{:S(2)}, u32[]{:S(2)}) collective-permute-start(bf16[3,64,640]{2,1,0:T(8,128)(2,1)S(1)} %get-tuple-element.76.refs_4_), channel_id=1, source_target_pairs={{0,2},{8,9},{2,4},{10,8},{4,6},{12,10},{6,7},{14,12},{7,5},{15,14}... | collective-permute-start | bytes 737288 | tf_op jit(solution)/shard_map/ppermute | solution.py:37
  10.9 5.6 %collective-permute-start.6 = (bf16[3,64,640]{2,1,0:T(8,128)(2,1)S(1)}, bf16[3,64,640]{2,1,0:T(8,128)(2,1)S(1)}, u32[]{:S(2)}, u32[]{:S(2)}) collective-permute-start(bf16[3,64,640]{2,1,0:T(8,128)(2,1)S(1)} %collective-permute-done.1.refs_3_), channel_id=1, source_target_pairs={{0,8},{8,0},{1,9},{9,1},{2,10},{10,2},{3,11},{11,3},{4,12},{12,4},... | collective-permute-start | bytes 737288 | tf_op jit(solution)/shard_map/ppermute | solution.py:41
  10.9 7.5 %collective-permute-start.5 = (bf16[3,64,640]{2,1,0:T(8,128)(2,1)S(1)}, bf16[3,64,640]{2,1,0:T(8,128)(2,1)S(1)}, u32[]{:S(2)}, u32[]{:S(2)}) collective-permute-start(bf16[3,64,640]{2,1,0:T(8,128)(2,1)S(1)} %collective-permute-done.1.refs_3_), channel_id=1, source_target_pairs={{0,2},{8,9},{2,4},{10,8},{4,6},{12,10},{6,7},{14,12},{7,5},{15,14}... | collective-permute-start | bytes 737288 | tf_op jit(solution)/shard_map/ppermute | solution.py:37
  14.8 5.3 %collective-permute-start.11 = (bf16[3,64,640]{2,1,0:T(8,128)(2,1)S(1)}, bf16[3,64,640]{2,1,0:T(8,128)(2,1)S(1)}, u32[]{:S(2)}, u32[]{:S(2)}) collective-permute-start(bf16[3,64,640]{2,1,0:T(8,128)(2,1)S(1)} %collective-permute-done.7.refs_3_), channel_id=1, source_target_pairs={{0,8},{8,0},{1,9},{9,1},{2,10},{10,2},{3,11},{11,3},{4,12},{12,4},... | collective-permute-start | bytes 737288 | tf_op jit(solution)/shard_map/ppermute | solution.py:41
  15.1 6.9 %collective-permute-start.10 = (bf16[3,64,640]{2,1,0:T(8,128)(2,1)S(1)}, bf16[3,64,640]{2,1,0:T(8,128)(2,1)S(1)}, u32[]{:S(2)}, u32[]{:S(2)}) collective-permute-start(bf16[3,64,640]{2,1,0:T(8,128)(2,1)S(1)} %collective-permute-done.7.refs_3_), channel_id=1, source_target_pairs={{0,2},{8,9},{2,4},{10,8},{4,6},{12,10},{6,7},{14,12},{7,5},{15,14}... | collective-permute-start | bytes 737288 | tf_op jit(solution)/shard_map/ppermute | solution.py:37
  18.4 5.2 %collective-permute-start.9 = (bf16[3,64,640]{2,1,0:T(8,128)(2,1)S(1)}, bf16[3,64,640]{2,1,0:T(8,128)(2,1)S(1)}, u32[]{:S(2)}, u32[]{:S(2)}) collective-permute-start(bf16[3,64,640]{2,1,0:T(8,128)(2,1)S(1)} %collective-permute-done.5.refs_3_), channel_id=1, source_target_pairs={{0,8},{8,0},{1,9},{9,1},{2,10},{10,2},{3,11},{11,3},{4,12},{12,4},... | collective-permute-start | bytes 737288 | tf_op jit(solution)/shard_map/ppermute | solution.py:41
  18.5 7.0 %collective-permute-start.8 = (bf16[3,64,640]{2,1,0:T(8,128)(2,1)S(1)}, bf16[3,64,640]{2,1,0:T(8,128)(2,1)S(1)}, u32[]{:S(2)}, u32[]{:S(2)}) collective-permute-start(bf16[3,64,640]{2,1,0:T(8,128)(2,1)S(1)} %collective-permute-done.5.refs_3_), channel_id=1, source_target_pairs={{0,2},{8,9},{2,4},{10,8},{4,6},{12,10},{6,7},{14,12},{7,5},{15,14}... | collective-permute-start | bytes 737288 | tf_op jit(solution)/shard_map/ppermute | solution.py:37
  21.9 4.4 %collective-permute-start.15 = (bf16[3,64,640]{2,1,0:T(8,128)(2,1)S(1)}, bf16[3,64,640]{2,1,0:T(8,128)(2,1)S(1)}, u32[]{:S(2)}, u32[]{:S(2)}) collective-permute-start(bf16[3,64,640]{2,1,0:T(8,128)(2,1)S(1)} %collective-permute-done.10.refs_3_), channel_id=1, source_target_pairs={{0,8},{8,0},{1,9},{9,1},{2,10},{10,2},{3,11},{11,3},{4,12},{12,4},... | collective-permute-start | bytes 737288 | tf_op jit(solution)/shard_map/ppermute | solution.py:41
  22.0 6.2 %collective-permute-start.14 = (bf16[3,64,640]{2,1,0:T(8,128)(2,1)S(1)}, bf16[3,64,640]{2,1,0:T(8,128)(2,1)S(1)}, u32[]{:S(2)}, u32[]{:S(2)}) collective-permute-start(bf16[3,64,640]{2,1,0:T(8,128)(2,1)S(1)} %collective-permute-done.10.refs_3_), channel_id=1, source_target_pairs={{0,2},{8,9},{2,4},{10,8},{4,6},{12,10},{6,7},{14,12},{7,5},{15,14}... | collective-permute-start | bytes 737288 | tf_op jit(solution)/shard_map/ppermute | solution.py:37
  25.4 2.8 %collective-permute-start.13 = (bf16[3,64,640]{2,1,0:T(8,128)(2,1)S(1)}, bf16[3,64,640]{2,1,0:T(8,128)(2,1)S(1)}, u32[]{:S(2)}, u32[]{:S(2)}) collective-permute-start(bf16[3,64,640]{2,1,0:T(8,128)(2,1)S(1)} %collective-permute-done.8.refs_3_), channel_id=1, source_target_pairs={{0,8},{8,0},{1,9},{9,1},{2,10},{10,2},{3,11},{11,3},{4,12},{12,4},... | collective-permute-start | bytes 737288 | tf_op jit(solution)/shard_map/ppermute | solution.py:41
  25.5 6.2 %collective-permute-start.12 = (bf16[3,64,640]{2,1,0:T(8,128)(2,1)S(1)}, bf16[3,64,640]{2,1,0:T(8,128)(2,1)S(1)}, u32[]{:S(2)}, u32[]{:S(2)}) collective-permute-start(bf16[3,64,640]{2,1,0:T(8,128)(2,1)S(1)} %collective-permute-done.8.refs_3_), channel_id=1, source_target_pairs={{0,2},{8,9},{2,4},{10,8},{4,6},{12,10},{6,7},{14,12},{7,5},{15,14}... | collective-permute-start | bytes 737288 | tf_op jit(solution)/shard_map/ppermute | solution.py:37
  28.3 3.5 %collective-permute-start.17 = (bf16[3,64,640]{2,1,0:T(8,128)(2,1)S(1)}, bf16[3,64,640]{2,1,0:T(8,128)(2,1)S(1)}, u32[]{:S(2)}, u32[]{:S(2)}) collective-permute-start(bf16[3,64,640]{2,1,0:T(8,128)(2,1)S(1)} %collective-permute-done.14.refs_3_), channel_id=1, source_target_pairs={{0,8},{8,0},{1,9},{9,1},{2,10},{10,2},{3,11},{11,3},{4,12},{12,4},... | collective-permute-start | bytes 737288 | tf_op jit(solution)/shard_map/ppermute | solution.py:41
  31.8 1.8 %collective-permute-start.16 = (bf16[3,64,640]{2,1,0:T(8,128)(2,1)S(1)}, bf16[3,64,640]{2,1,0:T(8,128)(2,1)S(1)}, u32[]{:S(2)}, u32[]{:S(2)}) collective-permute-start(bf16[3,64,640]{2,1,0:T(8,128)(2,1)S(1)} %collective-permute-done.12.refs_3_), channel_id=1, source_target_pairs={{0,8},{8,0},{1,9},{9,1},{2,10},{10,2},{3,11},{11,3},{4,12},{12,4},... | collective-permute-start | bytes 737288 | tf_op jit(solution)/shard_map/ppermute | solution.py:41

commit v5 on v4

--- a/solution.py
+++ b/solution.py
@@ -10,6 +10,8 @@
 numerator_gain = 16.0
 LANES = 128
 MIB = 1024 * 1024
+TILE_ROWS = 128
+TILE_COLS = 256
 SMEM = pl.BlockSpec(memory_space=pltpu.SMEM)
 VMEM = pl.BlockSpec(memory_space=pltpu.VMEM)
 HBM = pl.BlockSpec(memory_space=pltpu.HBM)
@@ -48,20 +50,22 @@
     return jnp.where(k < n // 2, 2 * k, 2 * n - 1 - 2 * k)
 
 
-def column_blocks(n, pieces, cols):
+def column_starts(n, pieces, cols):
     core = lax.axis_index("rollout")
     tensor = lax.axis_index("tensor")
     blocks = []
     for step, own_ring, own_layer in pieces:
         place = place_of(n, step, core if own_ring else 1 - core, tensor)
-        blocks.append((core if own_layer else 1 - core, pl.ds(pl.multiple_of(place * cols, LANES), cols)))
+        blocks.append((core if own_layer else 1 - core, pl.multiple_of(place * cols, LANES)))
     return blocks
 
 
 def fetch_kernel(n, pieces, *refs):
     bases, blocks, sems = refs[0:3], refs[3:6], refs[6]
     loads = []
-    for i, (layer, columns) in enumerate(column_blocks(n, pieces, blocks[0].shape[2])):
+    cols = blocks[0].shape[2]
+    for i, (layer, start) in enumerate(column_starts(n, pieces, cols)):
+        columns = pl.ds(start, cols)
         for proj in range(3):
             load = pltpu.make_async_copy(bases[proj].at[layer, :, columns], blocks[proj].at[i], sems.at[3 * i + proj])
             load.start()
@@ -129,12 +133,22 @@
     outs, bufs, sems = refs[at : at + 3], refs[at + 3 : at + 6], refs[at + 6]
     cols = a_refs[0].shape[2]
     stores = []
-    for i, (layer, columns) in enumerate(column_blocks(n, pieces, cols)):
+    for i, (layer, start) in enumerate(column_starts(n, pieces, cols)):
+        columns = pl.ds(start, cols)
         for proj in range(3):
-            delta = jnp.dot(b_refs[proj][layer], a_refs[i][proj], preferred_element_type=jnp.float32)
-            block = bases[proj][i] if fresh else bases[proj][layer, :, columns]
-            merged = block.astype(jnp.float32) + scale * delta
-            bufs[proj][i] = merged.astype(jnp.bfloat16)
+            for col in range(0, cols, TILE_COLS):
+                width = min(TILE_COLS, cols - col)
+                tile = pl.ds(col, width) if fresh else pl.ds(pl.multiple_of(start + col, LANES), width)
+                for row in range(0, bufs[proj].shape[1], TILE_ROWS):
+                    rows = pl.ds(row, min(TILE_ROWS, bufs[proj].shape[1] - row))
+                    delta = jnp.dot(
+                        b_refs[proj][layer, rows],
+                        a_refs[i][proj, :, col : col + width],
+                        preferred_element_type=jnp.float32,
+                    )
+                    block = bases[proj][i if fresh else layer, rows, tile]
+                    merged = block.astype(jnp.float32) + scale * delta
+                    bufs[proj][i, rows, col : col + width] = merged.astype(jnp.bfloat16)
             store = pltpu.make_async_copy(bufs[proj].at[i], outs[proj].at[layer, :, columns], sems.at[3 * i + proj])
             store.start()
             stores.append(store)
@@ -186,19 +200,20 @@
     if cols % LANES == 0:
         own_pieces = [(0, True, True), (0, True, False)]
         blocks = fetch(n, cols, bases, own_pieces)
-        other_a, blocks = lax.optimization_barrier((swap_cores(own_a), blocks))
+        swapped = (swap_cores(own_a), [swap_cores(x) for x in own_b])
+        (other_a, other_b), blocks = lax.optimization_barrier((swapped, blocks))
         first, second = choose_a(owners, own_a, other_a)
         held = [first, second]
         first = ring_pass(first, n)
         second = ring_pass(second, n)
-        b = choose_b(owners, own_b, [swap_cores(x) for x in own_b])
-        first, b = lax.optimization_barrier((first, b))
+        b = choose_b(owners, own_b, other_b)
 
         def go(chunks, pieces, outs=None):
             return merge(n, scale, b, chunks, bases if outs else blocks, shapes, outs, pieces)
 
         shapes = [jax.ShapeDtypeStruct(base.shape, base.dtype) for base in bases]
         outs = go(held, own_pieces)
+        first, outs = lax.optimization_barrier((first, outs))
         ready = []
         for step in range(1, last + 1):
             if step > 1:

time: 35.7 us -> 35.6 us (level)
  starting transfers between devices: 13.5 us -> 15 us
  waiting for transfers between devices: 2.89 us -> 1.49 us
    ppermute x7, waiting for transfers between devices: 2.87 us -> 1.46 us  [ring_pass(): return lax.ppermute(array, ('rollout', 'tensor'), pairs)]
    ppermute x7, starting transfers between devices: 12 us -> 13.1 us  [ring_pass(): return lax.ppermute(array, ('rollout', 'tensor'), pairs)]
  transfers between devices with their start and end apart: 18 -> 18, of which waited for: 3 -> 2; matrix products, arithmetic and copies ran while one was open for 0% -> 0% of each run, Pallas kernels for 43% -> 43%
where the time goes in v5:
time: 35.6 us; the launch traced here: 35.3 us
  Pallas kernels  17.9 us (50%)
  starting transfers between devices  15 us (42%)
  waiting for transfers between devices  1.49 us (4%)
  between operations  0.87 us (2%)
    pallas_call x8, Pallas kernels, merge(): pl.pallas_call(functools.partial(merge_kernel, n, pieces, scale, fresh),...  14.4 us
    ppermute x7, starting transfers between devices, ring_pass(): return lax.ppermute(array, ('rollout', 'tensor'), pairs)  13.1 us
    ppermute x11, starting transfers between devices, swap_cores(): return lax.ppermute(array, 'rollout', [(0, 1), (1, 0)])  1.86 us
    pallas_call x1, Pallas kernels, fetch(): pl.pallas_call(functools.partial(fetch_kernel, n, pieces), in_specs=[HBM]...  1.77 us
    ppermute x7, waiting for transfers between devices, ring_pass(): return lax.ppermute(array, ('rollout', 'tensor'), pairs)  1.46 us
    pallas_call x1, Pallas kernels, choose_a(): pl.pallas_call(choose_a_kernel, in_specs=[SMEM, VMEM, VMEM], out_specs=[V...  0.89 us
    pallas_call x1, Pallas kernels, choose_b(): pl.pallas_call(choose_b_kernel, in_specs=[SMEM] + [VMEM] * 6, out_specs=[...  0.88 us
  transfers between devices with their start and end apart: 18, of which 2 were waited for; matrix products, arithmetic and copies ran while one was open for 0% of the time, Pallas kernels for 43%

profile of v5, /device:TPU:0, one launch (start us, length us, event | category | flops | bytes accessed | tf_op | source)
XLA Modules:
  0.0 35.3 jit_solution(1071249357449192026)
XLA Ops:
  0.6 0.5 %collective-permute-start = (bf16[2,3,64,640]{3,2,1,0:T(8,128)(2,1)}, bf16[2,3,64,640]{3,2,1,0:T(8,128)(2,1)S(1)}, u32[]{:S(2)}, u32[]{:S(2)}) collective-permute-start(bf16[2,3,64,640]{3,2,1,0:T(8,128)(2,1)} %bitcast.10), channel_id=1, source_target_pairs={{0,8},{8,0},{1,9},{9,1},{2,10},{10,2},{3,11},{11,3},{4,12},{12,4},... | collective-permute-start | bytes 1474568 | tf_op jit(solution)/shard_map/ppermute | solution.py:43
  1.2 0.1 collective-permute-start.1
  1.2 0.4 %collective-permute-start.2 = (bf16[2,64,128]{2,1,0:T(8,128)(2,1)}, bf16[2,64,128]{2,1,0:T(8,128)(2,1)S(1)}, u32[]{:S(2)}, u32[]{:S(2)}) collective-permute-start(bf16[2,64,128]{2,1,0:T(8,128)(2,1)} %bitcast.14), channel_id=1, source_target_pairs={{0,8},{8,0},{1,9},{9,1},{2,10},{10,2},{3,11},{11,3},{4,12},{12,4},... | collective-permute-start | bytes 98312 | tf_op jit(solution)/shard_map/ppermute | solution.py:43
  1.7 0.1 collective-permute-start.3
  1.8 1.8 %shard_map.103 = (bf16[2,640,640]{2,1,0:T(8,128)(2,1)S(1)}, bf16[2,128,640]{2,1,0:T(8,128)(2,1)S(1)}, bf16[2,128,640]{2,1,0:T(8,128)(2,1)S(1)}) custom-call(bf16[2,640,5120]{2,1,0:T(8,128)(2,1)} %refs_5_.13, bf16[2,128,5120]{2,1,0:T(8,128)(2,1)} %refs_6_.13, bf16[2,128,5120]{2,1,0:T(8,128)(2,1)} %refs_7_.13), custom_call_target="tpu_custom_call" | custom-call | bytes 4587520 | tf_op jit(solution)/shard_map/pallas_call | solution.py:79
  3.6 0.0 copy-start.1
  3.6 0.0 collective-permute-done.3.refs_5_
  3.6 0.0 collective-permute-done.1.refs_3_
  3.7 0.9 %shard_map.105 = (bf16[3,64,640]{2,1,0:T(8,128)(2,1)S(1)}, bf16[3,64,640]{2,1,0:T(8,128)(2,1)S(1)}) custom-call(s32[2,3]{1,0:T(2,128)} %owners.3, bf16[2,3,64,640]{3,2,1,0:T(8,128)(2,1)S(1)} %bitcast.11, bf16[2,3,64,640]{3,2,1,0:T(8,128)(2,1)S(1)} %collective-permute-done.other), custom_call_target="tpu_custom_call" | custom-call | tf_op jit(solution)/shard_map/pallas_call | solution.py:102
  4.6 3.1 %collective-permute-start.4 = (bf16[3,64,640]{2,1,0:T(8,128)(2,1)S(1)}, bf16[3,64,640]{2,1,0:T(8,128)(2,1)S(1)}, u32[]{:S(2)}, u32[]{:S(2)}) collective-permute-start(bf16[3,64,640]{2,1,0:T(8,128)(2,1)S(1)} %get-tuple-element.77.refs_3_), channel_id=1, source_target_pairs={{0,2},{8,9},{2,4},{10,8},{4,6},{12,10},{6,7},{14,12},{7,5},{15,14}... | collective-permute-start | bytes 737288 | tf_op jit(solution)/shard_map/ppermute | solution.py:39
  7.6 1.6 %collective-permute-start.7 = (bf16[3,64,640]{2,1,0:T(8,128)(2,1)S(1)}, bf16[3,64,640]{2,1,0:T(8,128)(2,1)S(1)}, u32[]{:S(2)}, u32[]{:S(2)}) collective-permute-start(bf16[3,64,640]{2,1,0:T(8,128)(2,1)S(1)} %get-tuple-element.78.refs_4_), channel_id=1, source_target_pairs={{0,2},{8,9},{2,4},{10,8},{4,6},{12,10},{6,7},{14,12},{7,5},{15,14}... | collective-permute-start | bytes 737288 | tf_op jit(solution)/shard_map/ppermute | solution.py:39
  9.2 0.9 %shard_map.104 = (bf16[2,640,64]{2,1,0:T(8,128)(2,1)S(1)}, bf16[2,128,64]{2,1,0:T(8,128)(2,1)S(1)}, bf16[2,128,64]{2,1,0:T(8,128)(2,1)S(1)}) custom-call(s32[2,3]{1,0:T(2,128)} %owners.3, bf16[2,64,640]{2,1,0:T(8,128)(2,1)S(1)} %bitcast.13, bf16[2,64,128]{2,1,0:T(8,128)(2,1)S(1)} %bitcast.15, bf16[2,64,128]{2,1,0:T(8,128)(2,1)S(1)} %bitcast.17, ...), custom_call_target="tpu_custom_call" | custom-call | tf_op jit(solution)/shard_map/pallas_call | solution.py:121
  10.1 1.8 %shard_map.106 = (bf16[2,640,5120]{2,1,0:T(8,128)(2,1)}, bf16[2,128,5120]{2,1,0:T(8,128)(2,1)}, bf16[2,128,5120]{2,1,0:T(8,128)(2,1)}) custom-call(bf16[2,640,64]{2,1,0:T(8,128)(2,1)S(1)} %get-tuple-element.73.refs_0_, bf16[2,128,64]{2,1,0:T(8,128)(2,1)S(1)} %get-tuple-element.74.refs_1_, bf16[2,128,64]{2,1,0:T(8,128)(2,1)S(1)} %get-tuple-element.75.refs_2_, ...), custom_call_target="tpu_custom_call" | custom-call | flops 146800640 | bytes 4587520 | tf_op jit(solution)/shard_map/pallas_call | solution.py:163
  11.9 0.1 collective-permute-start.6
  12.0 1.8 %collective-permute-start.5 = (bf16[3,64,640]{2,1,0:T(8,128)(2,1)S(1)}, bf16[3,64,640]{2,1,0:T(8,128)(2,1)S(1)}, u32[]{:S(2)}, u32[]{:S(2)}) collective-permute-start(bf16[3,64,640]{2,1,0:T(8,128)(2,1)S(1)} %collective-permute-done.4.refs_3_), channel_id=1, source_target_pairs={{0,2},{8,9},{2,4},{10,8},{4,6},{12,10},{6,7},{14,12},{7,5},{15,14}... | collective-permute-start | bytes 737288 | tf_op jit(solution)/shard_map/ppermute | solution.py:39
  13.8 0.6 %collective-permute-done.7.refs_3_ = bf16[3,64,640]{2,1,0:T(8,128)(2,1)S(1)} collective-permute-done((bf16[3,64,640]{2,1,0:T(8,128)(2,1)S(1)}, bf16[3,64,640]{2,1,0:T(8,128)(2,1)S(1)}, u32[]{:S(2)}, u32[]{:S(2)}) %collective-permute-start.7) | collective-permute-done | bytes 245792 | tf_op jit(solution)/shard_map/ppermute | solution.py:39
  14.4 2.1 %collective-permute-start.10 = (bf16[3,64,640]{2,1,0:T(8,128)(2,1)S(1)}, bf16[3,64,640]{2,1,0:T(8,128)(2,1)S(1)}, u32[]{:S(2)}, u32[]{:S(2)}) collective-permute-start(bf16[3,64,640]{2,1,0:T(8,128)(2,1)S(1)} %collective-permute-done.7.refs_3_), channel_id=1, source_target_pairs={{0,2},{8,9},{2,4},{10,8},{4,6},{12,10},{6,7},{14,12},{7,5},{15,14}... | collective-permute-start | bytes 737288 | tf_op jit(solution)/shard_map/ppermute | solution.py:39
  16.5 1.8 %shard_map.107 = (bf16[2,640,5120]{2,1,0:T(8,128)(2,1)}, bf16[2,128,5120]{2,1,0:T(8,128)(2,1)}, bf16[2,128,5120]{2,1,0:T(8,128)(2,1)}) custom-call(bf16[2,640,64]{2,1,0:T(8,128)(2,1)S(1)} %get-tuple-element.73.refs_0_, bf16[2,128,64]{2,1,0:T(8,128)(2,1)S(1)} %get-tuple-element.74.refs_1_, ...), custom_call_target="tpu_custom_call", output_to_operand_aliasing={{0}: (8, {}), {1}: (9, {}), {2}: (10, {})} | custom-call | flops 146800640 | bytes 4587520 | tf_op jit(solution)/shard_map/pallas_call | solution.py:163
  18.3 0.2 collective-permute-start.9
  18.5 1.5 %collective-permute-start.8 = (bf16[3,64,640]{2,1,0:T(8,128)(2,1)S(1)}, bf16[3,64,640]{2,1,0:T(8,128)(2,1)S(1)}, u32[]{:S(2)}, u32[]{:S(2)}) collective-permute-start(bf16[3,64,640]{2,1,0:T(8,128)(2,1)S(1)} %collective-permute-done.5.refs_3_), channel_id=1, source_target_pairs={{0,2},{8,9},{2,4},{10,8},{4,6},{12,10},{6,7},{14,12},{7,5},{15,14}... | collective-permute-start | bytes 737288 | tf_op jit(solution)/shard_map/ppermute | solution.py:39
  20.0 1.8 %shard_map.108 = (bf16[2,640,5120]{2,1,0:T(8,128)(2,1)}, bf16[2,128,5120]{2,1,0:T(8,128)(2,1)}, bf16[2,128,5120]{2,1,0:T(8,128)(2,1)}) custom-call(bf16[2,640,64]{2,1,0:T(8,128)(2,1)S(1)} %get-tuple-element.73.refs_0_, bf16[2,128,64]{2,1,0:T(8,128)(2,1)S(1)} %get-tuple-element.74.refs_1_, ...), custom_call_target="tpu_custom_call", output_to_operand_aliasing={{0}: (8, {}), {1}: (9, {}), {2}: (10, {})} | custom-call | flops 146800640 | bytes 4587520 | tf_op jit(solution)/shard_map/pallas_call | solution.py:163
  21.8 0.2 collective-permute-start.15
  22.1 1.5 %collective-permute-start.14 = (bf16[3,64,640]{2,1,0:T(8,128)(2,1)S(1)}, bf16[3,64,640]{2,1,0:T(8,128)(2,1)S(1)}, u32[]{:S(2)}, u32[]{:S(2)}) collective-permute-start(bf16[3,64,640]{2,1,0:T(8,128)(2,1)S(1)} %collective-permute-done.10.refs_3_), channel_id=1, source_target_pairs={{0,2},{8,9},{2,4},{10,8},{4,6},{12,10},{6,7},{14,12},{7,5},{15,14}... | collective-permute-start | bytes 737288 | tf_op jit(solution)/shard_map/ppermute | solution.py:39
  23.6 1.8 %shard_map.109 = (bf16[2,640,5120]{2,1,0:T(8,128)(2,1)}, bf16[2,128,5120]{2,1,0:T(8,128)(2,1)}, bf16[2,128,5120]{2,1,0:T(8,128)(2,1)}) custom-call(bf16[2,640,64]{2,1,0:T(8,128)(2,1)S(1)} %get-tuple-element.73.refs_0_, bf16[2,128,64]{2,1,0:T(8,128)(2,1)S(1)} %get-tuple-element.74.refs_1_, ...), custom_call_target="tpu_custom_call", output_to_operand_aliasing={{0}: (8, {}), {1}: (9, {}), {2}: (10, {})} | custom-call | flops 146800640 | bytes 4587520 | tf_op jit(solution)/shard_map/pallas_call | solution.py:163
  25.4 0.1 collective-permute-start.13
  25.4 1.6 %collective-permute-start.12 = (bf16[3,64,640]{2,1,0:T(8,128)(2,1)S(1)}, bf16[3,64,640]{2,1,0:T(8,128)(2,1)S(1)}, u32[]{:S(2)}, u32[]{:S(2)}) collective-permute-start(bf16[3,64,640]{2,1,0:T(8,128)(2,1)S(1)} %collective-permute-done.8.refs_3_), channel_id=1, source_target_pairs={{0,2},{8,9},{2,4},{10,8},{4,6},{12,10},{6,7},{14,12},{7,5},{15,14}... | collective-permute-start | bytes 737288 | tf_op jit(solution)/shard_map/ppermute | solution.py:39
  27.1 1.8 %shard_map.110 = (bf16[2,640,5120]{2,1,0:T(8,128)(2,1)}, bf16[2,128,5120]{2,1,0:T(8,128)(2,1)}, bf16[2,128,5120]{2,1,0:T(8,128)(2,1)}) custom-call(bf16[2,640,64]{2,1,0:T(8,128)(2,1)S(1)} %get-tuple-element.73.refs_0_, bf16[2,128,64]{2,1,0:T(8,128)(2,1)S(1)} %get-tuple-element.74.refs_1_, ...), custom_call_target="tpu_custom_call", output_to_operand_aliasing={{0}: (8, {}), {1}: (9, {}), {2}: (10, {})} | custom-call | flops 146800640 | bytes 4587520 | tf_op jit(solution)/shard_map/pallas_call | solution.py:163
  28.9 0.1 collective-permute-start.17
  29.0 1.8 %shard_map.111 = (bf16[2,640,5120]{2,1,0:T(8,128)(2,1)}, bf16[2,128,5120]{2,1,0:T(8,128)(2,1)}, bf16[2,128,5120]{2,1,0:T(8,128)(2,1)}) custom-call(bf16[2,640,64]{2,1,0:T(8,128)(2,1)S(1)} %get-tuple-element.73.refs_0_, bf16[2,128,64]{2,1,0:T(8,128)(2,1)S(1)} %get-tuple-element.74.refs_1_, ...), custom_call_target="tpu_custom_call", output_to_operand_aliasing={{0}: (8, {}), {1}: (9, {}), {2}: (10, {})} | custom-call | flops 146800640 | bytes 4587520 | tf_op jit(solution)/shard_map/pallas_call | solution.py:163
  30.8 0.9 %collective-permute-done.12.refs_3_ = bf16[3,64,640]{2,1,0:T(8,128)(2,1)S(1)} collective-permute-done((bf16[3,64,640]{2,1,0:T(8,128)(2,1)S(1)}, bf16[3,64,640]{2,1,0:T(8,128)(2,1)S(1)}, u32[]{:S(2)}, u32[]{:S(2)}) %collective-permute-start.12) | collective-permute-done | bytes 245792 | tf_op jit(solution)/shard_map/ppermute | solution.py:39
  31.7 1.8 %shard_map.112 = (bf16[2,640,5120]{2,1,0:T(8,128)(2,1)}, bf16[2,128,5120]{2,1,0:T(8,128)(2,1)}, bf16[2,128,5120]{2,1,0:T(8,128)(2,1)}) custom-call(bf16[2,640,64]{2,1,0:T(8,128)(2,1)S(1)} %get-tuple-element.73.refs_0_, bf16[2,128,64]{2,1,0:T(8,128)(2,1)S(1)} %get-tuple-element.74.refs_1_, ...), custom_call_target="tpu_custom_call", output_to_operand_aliasing={{0}: (8, {}), {1}: (9, {}), {2}: (10, {})} | custom-call | flops 146800640 | bytes 4587520 | tf_op jit(solution)/shard_map/pallas_call | solution.py:163
  33.5 1.8 %shard_map.113 = (bf16[2,640,5120]{2,1,0:T(8,128)(2,1)}, bf16[2,128,5120]{2,1,0:T(8,128)(2,1)}, bf16[2,128,5120]{2,1,0:T(8,128)(2,1)}) custom-call(bf16[2,640,64]{2,1,0:T(8,128)(2,1)S(1)} %get-tuple-element.73.refs_0_, bf16[2,128,64]{2,1,0:T(8,128)(2,1)S(1)} %get-tuple-element.74.refs_1_, ...), custom_call_target="tpu_custom_call", output_to_operand_aliasing={{0}: (8, {}), {1}: (9, {}), {2}: (10, {})} | custom-call | flops 146800640 | bytes 4587520 | tf_op jit(solution)/shard_map/pallas_call | solution.py:163
  (29 shorter events, 0.1 us)
Async XLA Ops:
  0.6 3.0 %collective-permute-start = (bf16[2,3,64,640]{3,2,1,0:T(8,128)(2,1)}, bf16[2,3,64,640]{3,2,1,0:T(8,128)(2,1)S(1)}, u32[]{:S(2)}, u32[]{:S(2)}) collective-permute-start(bf16[2,3,64,640]{3,2,1,0:T(8,128)(2,1)} %bitcast.10), channel_id=1, source_target_pairs={{0,8},{8,0},{1,9},{9,1},{2,10},{10,2},{3,11},{11,3},{4,12},{12,4},... | collective-permute-start | bytes 1474568 | tf_op jit(solution)/shard_map/ppermute | solution.py:43
  1.2 2.5 %collective-permute-start.1 = (bf16[2,64,640]{2,1,0:T(8,128)(2,1)}, bf16[2,64,640]{2,1,0:T(8,128)(2,1)S(1)}, u32[]{:S(2)}, u32[]{:S(2)}) collective-permute-start(bf16[2,64,640]{2,1,0:T(8,128)(2,1)} %bitcast.12), channel_id=1, source_target_pairs={{0,8},{8,0},{1,9},{9,1},{2,10},{10,2},{3,11},{11,3},{4,12},{12,4},... | collective-permute-start | bytes 491528 | tf_op jit(solution)/shard_map/ppermute | solution.py:43
  1.2 2.4 %collective-permute-start.2 = (bf16[2,64,128]{2,1,0:T(8,128)(2,1)}, bf16[2,64,128]{2,1,0:T(8,128)(2,1)S(1)}, u32[]{:S(2)}, u32[]{:S(2)}) collective-permute-start(bf16[2,64,128]{2,1,0:T(8,128)(2,1)} %bitcast.14), channel_id=1, source_target_pairs={{0,8},{8,0},{1,9},{9,1},{2,10},{10,2},{3,11},{11,3},{4,12},{12,4},... | collective-permute-start | bytes 98312 | tf_op jit(solution)/shard_map/ppermute | solution.py:43
  1.7 2.0 %copy-start.3 = (bf16[1,2,3,64,640]{4,3,2,1,0:T(8,128)(2,1)S(1)}, bf16[1,2,3,64,640]{4,3,2,1,0:T(8,128)(2,1)}, u32[]{:S(2)}) copy-start(bf16[1,2,3,64,640]{4,3,2,1,0:T(8,128)(2,1)} %param.12) | copy-start | bytes 1474564
  1.7 7.5 %copy-start.4 = (bf16[1,2,640,64]{2,3,1,0:T(8,128)(2,1)S(1)}, bf16[1,2,640,64]{2,3,1,0:T(8,128)(2,1)}, u32[]{:S(2)}) copy-start(bf16[1,2,640,64]{2,3,1,0:T(8,128)(2,1)} %param.13) | copy-start | bytes 491524
  1.7 7.5 %copy-start.5 = (bf16[1,2,128,64]{2,3,1,0:T(8,128)(2,1)S(1)}, bf16[1,2,128,64]{2,3,1,0:T(8,128)(2,1)}, u32[]{:S(2)}) copy-start(bf16[1,2,128,64]{2,3,1,0:T(8,128)(2,1)} %param.14) | copy-start | bytes 98308
  1.7 7.5 %copy-start.6 = (bf16[1,2,128,64]{2,3,1,0:T(8,128)(2,1)S(1)}, bf16[1,2,128,64]{2,3,1,0:T(8,128)(2,1)}, u32[]{:S(2)}) copy-start(bf16[1,2,128,64]{2,3,1,0:T(8,128)(2,1)} %param.15) | copy-start | bytes 98308
  1.7 2.0 %collective-permute-start.3 = (bf16[2,64,128]{2,1,0:T(8,128)(2,1)}, bf16[2,64,128]{2,1,0:T(8,128)(2,1)S(1)}, u32[]{:S(2)}, u32[]{:S(2)}) collective-permute-start(bf16[2,64,128]{2,1,0:T(8,128)(2,1)} %bitcast.16), channel_id=1, source_target_pairs={{0,8},{8,0},{1,9},{9,1},{2,10},{10,2},{3,11},{11,3},{4,12},{12,4},... | collective-permute-start | bytes 98312 | tf_op jit(solution)/shard_map/ppermute | solution.py:43
  1.8 14.6 %copy-start = (bf16[2,640,5120]{2,1,0:T(8,128)(2,1)S(1)}, bf16[2,640,5120]{2,1,0:T(8,128)(2,1)}, u32[]{:S(2)}) copy-start(bf16[2,640,5120]{2,1,0:T(8,128)(2,1)} %refs_5_.13) | copy-start | bytes 39321604
  1.8 14.6 %copy-start.2 = (bf16[2,128,5120]{2,1,0:T(8,128)(2,1)S(1)}, bf16[2,128,5120]{2,1,0:T(8,128)(2,1)}, u32[]{:S(2)}) copy-start(bf16[2,128,5120]{2,1,0:T(8,128)(2,1)} %refs_7_.13) | copy-start | bytes 7864324
  3.6 12.9 %copy-start.1 = (bf16[2,128,5120]{2,1,0:T(8,128)(2,1)S(1)}, bf16[2,128,5120]{2,1,0:T(8,128)(2,1)}, u32[]{:S(2)}) copy-start(bf16[2,128,5120]{2,1,0:T(8,128)(2,1)} %refs_6_.13) | copy-start | bytes 7864324
  4.6 7.3 %collective-permute-start.4 = (bf16[3,64,640]{2,1,0:T(8,128)(2,1)S(1)}, bf16[3,64,640]{2,1,0:T(8,128)(2,1)S(1)}, u32[]{:S(2)}, u32[]{:S(2)}) collective-permute-start(bf16[3,64,640]{2,1,0:T(8,128)(2,1)S(1)} %get-tuple-element.77.refs_3_), channel_id=1, source_target_pairs={{0,2},{8,9},{2,4},{10,8},{4,6},{12,10},{6,7},{14,12},{7,5},{15,14}... | collective-permute-start | bytes 737288 | tf_op jit(solution)/shard_map/ppermute | solution.py:39
  7.6 6.8 %collective-permute-start.7 = (bf16[3,64,640]{2,1,0:T(8,128)(2,1)S(1)}, bf16[3,64,640]{2,1,0:T(8,128)(2,1)S(1)}, u32[]{:S(2)}, u32[]{:S(2)}) collective-permute-start(bf16[3,64,640]{2,1,0:T(8,128)(2,1)S(1)} %get-tuple-element.78.refs_4_), channel_id=1, source_target_pairs={{0,2},{8,9},{2,4},{10,8},{4,6},{12,10},{6,7},{14,12},{7,5},{15,14}... | collective-permute-start | bytes 737288 | tf_op jit(solution)/shard_map/ppermute | solution.py:39
  11.9 4.6 %collective-permute-start.6 = (bf16[3,64,640]{2,1,0:T(8,128)(2,1)S(1)}, bf16[3,64,640]{2,1,0:T(8,128)(2,1)S(1)}, u32[]{:S(2)}, u32[]{:S(2)}) collective-permute-start(bf16[3,64,640]{2,1,0:T(8,128)(2,1)S(1)} %collective-permute-done.4.refs_3_), channel_id=1, source_target_pairs={{0,8},{8,0},{1,9},{9,1},{2,10},{10,2},{3,11},{11,3},{4,12},{12,4},... | collective-permute-start | bytes 737288 | tf_op jit(solution)/shard_map/ppermute | solution.py:43
  12.0 6.3 %collective-permute-start.5 = (bf16[3,64,640]{2,1,0:T(8,128)(2,1)S(1)}, bf16[3,64,640]{2,1,0:T(8,128)(2,1)S(1)}, u32[]{:S(2)}, u32[]{:S(2)}) collective-permute-start(bf16[3,64,640]{2,1,0:T(8,128)(2,1)S(1)} %collective-permute-done.4.refs_3_), channel_id=1, source_target_pairs={{0,2},{8,9},{2,4},{10,8},{4,6},{12,10},{6,7},{14,12},{7,5},{15,14}... | collective-permute-start | bytes 737288 | tf_op jit(solution)/shard_map/ppermute | solution.py:39
  14.4 5.7 %collective-permute-start.11 = (bf16[3,64,640]{2,1,0:T(8,128)(2,1)S(1)}, bf16[3,64,640]{2,1,0:T(8,128)(2,1)S(1)}, u32[]{:S(2)}, u32[]{:S(2)}) collective-permute-start(bf16[3,64,640]{2,1,0:T(8,128)(2,1)S(1)} %collective-permute-done.7.refs_3_), channel_id=1, source_target_pairs={{0,8},{8,0},{1,9},{9,1},{2,10},{10,2},{3,11},{11,3},{4,12},{12,4},... | collective-permute-start | bytes 737288 | tf_op jit(solution)/shard_map/ppermute | solution.py:43
  14.4 7.5 %collective-permute-start.10 = (bf16[3,64,640]{2,1,0:T(8,128)(2,1)S(1)}, bf16[3,64,640]{2,1,0:T(8,128)(2,1)S(1)}, u32[]{:S(2)}, u32[]{:S(2)}) collective-permute-start(bf16[3,64,640]{2,1,0:T(8,128)(2,1)S(1)} %collective-permute-done.7.refs_3_), channel_id=1, source_target_pairs={{0,2},{8,9},{2,4},{10,8},{4,6},{12,10},{6,7},{14,12},{7,5},{15,14}... | collective-permute-start | bytes 737288 | tf_op jit(solution)/shard_map/ppermute | solution.py:39
  18.3 5.2 %collective-permute-start.9 = (bf16[3,64,640]{2,1,0:T(8,128)(2,1)S(1)}, bf16[3,64,640]{2,1,0:T(8,128)(2,1)S(1)}, u32[]{:S(2)}, u32[]{:S(2)}) collective-permute-start(bf16[3,64,640]{2,1,0:T(8,128)(2,1)S(1)} %collective-permute-done.5.refs_3_), channel_id=1, source_target_pairs={{0,8},{8,0},{1,9},{9,1},{2,10},{10,2},{3,11},{11,3},{4,12},{12,4},... | collective-permute-start | bytes 737288 | tf_op jit(solution)/shard_map/ppermute | solution.py:43
  18.5 6.8 %collective-permute-start.8 = (bf16[3,64,640]{2,1,0:T(8,128)(2,1)S(1)}, bf16[3,64,640]{2,1,0:T(8,128)(2,1)S(1)}, u32[]{:S(2)}, u32[]{:S(2)}) collective-permute-start(bf16[3,64,640]{2,1,0:T(8,128)(2,1)S(1)} %collective-permute-done.5.refs_3_), channel_id=1, source_target_pairs={{0,2},{8,9},{2,4},{10,8},{4,6},{12,10},{6,7},{14,12},{7,5},{15,14}... | collective-permute-start | bytes 737288 | tf_op jit(solution)/shard_map/ppermute | solution.py:39
  21.8 5.2 %collective-permute-start.15 = (bf16[3,64,640]{2,1,0:T(8,128)(2,1)S(1)}, bf16[3,64,640]{2,1,0:T(8,128)(2,1)S(1)}, u32[]{:S(2)}, u32[]{:S(2)}) collective-permute-start(bf16[3,64,640]{2,1,0:T(8,128)(2,1)S(1)} %collective-permute-done.10.refs_3_), channel_id=1, source_target_pairs={{0,8},{8,0},{1,9},{9,1},{2,10},{10,2},{3,11},{11,3},{4,12},{12,4},... | collective-permute-start | bytes 737288 | tf_op jit(solution)/shard_map/ppermute | solution.py:43
  22.1 6.8 %collective-permute-start.14 = (bf16[3,64,640]{2,1,0:T(8,128)(2,1)S(1)}, bf16[3,64,640]{2,1,0:T(8,128)(2,1)S(1)}, u32[]{:S(2)}, u32[]{:S(2)}) collective-permute-start(bf16[3,64,640]{2,1,0:T(8,128)(2,1)S(1)} %collective-permute-done.10.refs_3_), channel_id=1, source_target_pairs={{0,2},{8,9},{2,4},{10,8},{4,6},{12,10},{6,7},{14,12},{7,5},{15,14}... | collective-permute-start | bytes 737288 | tf_op jit(solution)/shard_map/ppermute | solution.py:39
  25.4 3.6 %collective-permute-start.13 = (bf16[3,64,640]{2,1,0:T(8,128)(2,1)S(1)}, bf16[3,64,640]{2,1,0:T(8,128)(2,1)S(1)}, u32[]{:S(2)}, u32[]{:S(2)}) collective-permute-start(bf16[3,64,640]{2,1,0:T(8,128)(2,1)S(1)} %collective-permute-done.8.refs_3_), channel_id=1, source_target_pairs={{0,8},{8,0},{1,9},{9,1},{2,10},{10,2},{3,11},{11,3},{4,12},{12,4},... | collective-permute-start | bytes 737288 | tf_op jit(solution)/shard_map/ppermute | solution.py:43
  25.4 6.2 %collective-permute-start.12 = (bf16[3,64,640]{2,1,0:T(8,128)(2,1)S(1)}, bf16[3,64,640]{2,1,0:T(8,128)(2,1)S(1)}, u32[]{:S(2)}, u32[]{:S(2)}) collective-permute-start(bf16[3,64,640]{2,1,0:T(8,128)(2,1)S(1)} %collective-permute-done.8.refs_3_), channel_id=1, source_target_pairs={{0,2},{8,9},{2,4},{10,8},{4,6},{12,10},{6,7},{14,12},{7,5},{15,14}... | collective-permute-start | bytes 737288 | tf_op jit(solution)/shard_map/ppermute | solution.py:39
  28.9 2.8 %collective-permute-start.17 = (bf16[3,64,640]{2,1,0:T(8,128)(2,1)S(1)}, bf16[3,64,640]{2,1,0:T(8,128)(2,1)S(1)}, u32[]{:S(2)}, u32[]{:S(2)}) collective-permute-start(bf16[3,64,640]{2,1,0:T(8,128)(2,1)S(1)} %collective-permute-done.14.refs_3_), channel_id=1, source_target_pairs={{0,8},{8,0},{1,9},{9,1},{2,10},{10,2},{3,11},{11,3},{4,12},{12,4},... | collective-permute-start | bytes 737288 | tf_op jit(solution)/shard_map/ppermute | solution.py:43
  31.7 1.8 %collective-permute-start.16 = (bf16[3,64,640]{2,1,0:T(8,128)(2,1)S(1)}, bf16[3,64,640]{2,1,0:T(8,128)(2,1)S(1)}, u32[]{:S(2)}, u32[]{:S(2)}) collective-permute-start(bf16[3,64,640]{2,1,0:T(8,128)(2,1)S(1)} %collective-permute-done.12.refs_3_), channel_id=1, source_target_pairs={{0,8},{8,0},{1,9},{9,1},{2,10},{10,2},{3,11},{11,3},{4,12},{12,4},... | collective-permute-start | bytes 737288 | tf_op jit(solution)/shard_map/ppermute | solution.py:43

commit v6 on v5

--- a/solution.py
+++ b/solution.py
@@ -60,35 +60,6 @@
     return blocks
 
 
-def fetch_kernel(n, pieces, *refs):
-    bases, blocks, sems = refs[0:3], refs[3:6], refs[6]
-    loads = []
-    cols = blocks[0].shape[2]
-    for i, (layer, start) in enumerate(column_starts(n, pieces, cols)):
-        columns = pl.ds(start, cols)
-        for proj in range(3):
-            load = pltpu.make_async_copy(bases[proj].at[layer, :, columns], blocks[proj].at[i], sems.at[3 * i + proj])
-            load.start()
-            loads.append(load)
-    for load in loads:
-        load.wait()
-
-
-def fetch(n, cols, bases, pieces):
-    shapes = [jax.ShapeDtypeStruct((len(pieces), base.shape[1], cols), base.dtype) for base in bases]
-    return pl.pallas_call(
-        functools.partial(fetch_kernel, n, pieces),
-        in_specs=[HBM] * 3,
-        out_specs=[VMEM] * 3,
-        out_shape=shapes,
-        scratch_shapes=[pltpu.SemaphoreType.DMA((3 * len(pieces),))],
-        compiler_params=pltpu.CompilerParams(vmem_limit_bytes=4 * MIB),
-        cost_estimate=pl.CostEstimate(
-            flops=0, bytes_accessed=2 * sum(x.size * x.dtype.itemsize for x in shapes), transcendentals=0
-        ),
-    )(*[in_hbm(base) for base in bases])
-
-
 def choose_a_kernel(owners, own, other, first, second):
     core = lax.axis_index("rollout")
     for out, layer in ((first, core), (second, 1 - core)):
@@ -108,39 +79,85 @@
     )(in_hbm(owners), in_vmem(own), other)
 
 
-def choose_b_kernel(owners, *refs):
+def start_fetches(n, pieces, bases, blocks, sems):
+    cols = blocks[0].shape[2]
+    fetches = []
+    for i, (layer, start) in enumerate(column_starts(n, pieces, cols)):
+        for base, block in zip(bases, blocks):
+            source = base.at[layer, :, pl.ds(start, cols)]
+            fetches.append(pltpu.make_async_copy(source, block.at[i], sems.at[len(fetches)]))
+            fetches[-1].start()
+    return fetches
+
+
+def block_shapes(bases, pieces, cols):
+    return [jax.ShapeDtypeStruct((len(pieces), base.shape[1], cols), base.dtype) for base in bases]
+
+
+def moved(shapes):
+    size = sum(x.size * x.dtype.itemsize for x in shapes)
+    return pl.CostEstimate(flops=0, bytes_accessed=2 * size, transcendentals=0)
+
+
+def fetch_kernel(n, pieces, *refs):
+    count = len(refs) // 2
+    for fetch in start_fetches(n, pieces, refs[:count], refs[count:-1], refs[-1]):
+        fetch.wait()
+
+
+def fetch_blocks(n, cols, bases, pieces):
+    blocks = block_shapes(bases, pieces, cols)
+    return pl.pallas_call(
+        functools.partial(fetch_kernel, n, pieces),
+        in_specs=[HBM] * len(bases),
+        out_specs=[VMEM] * len(bases),
+        out_shape=blocks,
+        scratch_shapes=[pltpu.SemaphoreType.DMA((len(bases) * len(pieces),))],
+        compiler_params=pltpu.CompilerParams(vmem_limit_bytes=4 * MIB),
+        cost_estimate=moved(blocks),
+    )(*[in_hbm(base) for base in bases])
+
+
+def choose_b_kernel(n, pieces, owners, *refs):
     core = lax.axis_index("rollout")
+    own, other, base, outs, block, sems = refs[0:3], refs[3:6], refs[6], refs[7:10], refs[10], refs[11]
+    fetches = start_fetches(n, pieces, [base], [block], sems)
     for proj in range(3):
-        own, other, out = refs[proj], refs[3 + proj], refs[6 + proj]
-        for layer in range(own.shape[0]):
+        for layer in range(own[proj].shape[0]):
             mine = owners[layer, proj] == core
-            out[layer] = jnp.where(mine, own[layer], other[layer]).T
-
-
-def choose_b(owners, own, other):
-    return pl.pallas_call(
-        choose_b_kernel,
-        in_specs=[SMEM] + [VMEM] * 6,
-        out_specs=[VMEM] * 3,
-        out_shape=[jax.ShapeDtypeStruct((x.shape[0], x.shape[2], x.shape[1]), x.dtype) for x in own],
+            outs[proj][layer] = jnp.where(mine, own[proj][layer], other[proj][layer]).T
+    for fetch in fetches:
+        fetch.wait()
+
+
+def choose_b(n, cols, owners, own, other, base, pieces):
+    chosen = [jax.ShapeDtypeStruct((x.shape[0], x.shape[2], x.shape[1]), x.dtype) for x in own]
+    blocks = block_shapes([base], pieces, cols)
+    out = pl.pallas_call(
+        functools.partial(choose_b_kernel, n, pieces),
+        in_specs=[SMEM] + [VMEM] * 6 + [HBM],
+        out_specs=[VMEM] * 4,
+        out_shape=chosen + blocks,
+        scratch_shapes=[pltpu.SemaphoreType.DMA((len(pieces),))],
         compiler_params=pltpu.CompilerParams(vmem_limit_bytes=4 * MIB),
-    )(in_hbm(owners), *[in_vmem(x) for x in own], *other)
+        cost_estimate=moved(blocks),
+    )(in_hbm(owners), *[in_vmem(x) for x in own], *other, in_hbm(base))
+    return out[:3], out[3]
 
 
 def merge_kernel(n, pieces, scale, fresh, *refs):
     b_refs, a_refs, bases = refs[0:3], refs[3:5], refs[5:8]
     at = 8 if fresh else 11
-    outs, bufs, sems = refs[at : at + 3], refs[at + 3 : at + 6], refs[at + 6]
-    cols = a_refs[0].shape[2]
+    outs, bufs, sem = refs[at : at + 3], refs[at + 3 : at + 6], refs[at + 6]
+    cols = a_refs[0].shape[-1]
     stores = []
     for i, (layer, start) in enumerate(column_starts(n, pieces, cols)):
-        columns = pl.ds(start, cols)
-        for proj in range(3):
-            for col in range(0, cols, TILE_COLS):
-                width = min(TILE_COLS, cols - col)
-                tile = pl.ds(col, width) if fresh else pl.ds(pl.multiple_of(start + col, LANES), width)
-                for row in range(0, bufs[proj].shape[1], TILE_ROWS):
-                    rows = pl.ds(row, min(TILE_ROWS, bufs[proj].shape[1] - row))
+        for proj in (1, 2, 0):
+            for row in range(0, bufs[proj].shape[1], TILE_ROWS):
+                rows = pl.ds(row, min(TILE_ROWS, bufs[proj].shape[1] - row))
+                for col in range(0, cols, TILE_COLS):
+                    width = min(TILE_COLS, cols - col)
+                    tile = pl.ds(col, width) if fresh else pl.ds(pl.multiple_of(start + col, LANES), width)
                     delta = jnp.dot(
                         b_refs[proj][layer, rows],
                         a_refs[i][proj, :, col : col + width],
@@ -149,24 +166,27 @@
                     block = bases[proj][i if fresh else layer, rows, tile]
                     merged = block.astype(jnp.float32) + scale * delta
                     bufs[proj][i, rows, col : col + width] = merged.astype(jnp.bfloat16)
-            store = pltpu.make_async_copy(bufs[proj].at[i], outs[proj].at[layer, :, columns], sems.at[3 * i + proj])
-            store.start()
-            stores.append(store)
+                store = pltpu.make_async_copy(
+                    bufs[proj].at[i, rows], outs[proj].at[layer, rows, pl.ds(start, cols)], sem.at[len(stores)]
+                )
+                store.start()
+                stores.append(store)
     for store in stores:
         store.wait()
 
 
 def merge(n, scale, b, a_list, bases, shapes, outs, pieces):
     fresh = outs is None
-    rank, cols = a_list[0].shape[1:]
+    rank, cols = a_list[0].shape[-2:]
     rows = sum(base.shape[1] for base in bases)
+    stores = len(pieces) * sum(-(-base.shape[1] // TILE_ROWS) for base in bases)
     return pl.pallas_call(
         functools.partial(merge_kernel, n, pieces, scale, fresh),
         in_specs=[VMEM] * (3 + len(a_list) + 3) + [HBM] * (0 if fresh else 3),
         out_specs=[HBM] * 3,
         out_shape=shapes,
         scratch_shapes=[pltpu.VMEM((len(pieces), base.shape[1], cols), base.dtype) for base in bases]
-        + [pltpu.SemaphoreType.DMA((3 * len(pieces),))],
+        + [pltpu.SemaphoreType.DMA((stores,))],
         input_output_aliases={} if fresh else {6 + len(a_list) + i: i for i in range(3)},
         compiler_params=pltpu.CompilerParams(vmem_limit_bytes=16 * MIB),
         cost_estimate=pl.CostEstimate(
@@ -175,7 +195,6 @@
             transcendentals=0,
         ),
     )(*b, *a_list, *(bases if fresh else [in_vmem(base) for base in bases]), *([] if fresh else outs))
-
 
 def per_device(
     n,
@@ -198,38 +217,38 @@
     own_b = [jnp.swapaxes(right[0], 1, 2) for right in rights]
 
     if cols % LANES == 0:
-        own_pieces = [(0, True, True), (0, True, False)]
-        blocks = fetch(n, cols, bases, own_pieces)
+        tie = lax.optimization_barrier
+        shapes = [jax.ShapeDtypeStruct(base.shape, base.dtype) for base in bases]
         swapped = (swap_cores(own_a), [swap_cores(x) for x in own_b])
-        (other_a, other_b), blocks = lax.optimization_barrier((swapped, blocks))
+        pieces = [(0, True, True), (0, True, False)]
+        small_blocks = fetch_blocks(n, cols, bases[1:], pieces)
+        (other_a, other_b), small_blocks = tie((swapped, small_blocks))
         first, second = choose_a(owners, own_a, other_a)
         held = [first, second]
         first = ring_pass(first, n)
         second = ring_pass(second, n)
-        b = choose_b(owners, own_b, other_b)
-
-        def go(chunks, pieces, outs=None):
-            return merge(n, scale, b, chunks, bases if outs else blocks, shapes, outs, pieces)
-
-        shapes = [jax.ShapeDtypeStruct(base.shape, base.dtype) for base in bases]
-        outs = go(held, own_pieces)
-        first, outs = lax.optimization_barrier((first, outs))
-        ready = []
-        for step in range(1, last + 1):
+        b, block = choose_b(n, cols, owners, own_b, other_b, base_query, pieces)
+        outs = merge(n, scale, b, held, [block, *small_blocks], shapes, None, pieces)
+        first, _ = tie((first, outs))
+
+        def go(pieces, chunks, outs):
+            return merge(n, scale, b, chunks, bases, shapes, outs, pieces)
+
+        def later(array, *others):
+            return tie((array, others))[0]
+
+        others = None
+        for step in range(1, last):
+            onward = ring_pass(first, n)
             if step > 1:
-                outs = go(*ready.pop(0), outs)
-            ready.append(([first, swap_cores(first)], [(step, True, True), (step, False, False)]))
-            if step < last:
-                first = ring_pass(first, n)
-                second, outs = lax.optimization_barrier((second, outs))
-                ready.append(([second, swap_cores(second)], [(step, True, False), (step, False, True)]))
-                outs = go(*ready.pop(0), outs)
-                first, outs = lax.optimization_barrier((first, outs))
-                if step < last - 1:
-                    second = ring_pass(second, n)
-        for item in ready:
-            outs = go(*item, outs)
-        return tuple(outs)
+                outs = go([(step - 1, False, False), (step - 1, False, True)], others, outs)
+            onward_second = ring_pass(later(second, outs), n) if step < last - 1 else None
+            others = [swap_cores(later(first, second)), swap_cores(second)]
+            outs = go([(step, True, True), (step, True, False)], [first, second], outs)
+            first, second = later(onward, outs), onward_second
+        outs = go([(last - 1, False, False), (last - 1, False, True)], others, outs)
+        first = later(first, outs)
+        return tuple(go([(last, True, True), (last, False, False)], [first, swap_cores(first)], outs))
 
     core = lax.axis_index("rollout")
     tensor = lax.axis_index("tensor")

time: 35.6 us -> 38 us (1.067)
  waiting for transfers between devices: 1.49 us -> 3.95 us
  Pallas kernels: 17.9 us -> 18.4 us
  starting transfers between devices: 15 us -> 14.6 us
    ppermute x11, waiting for transfers between devices: 0.03 us -> 1.52 us  [swap_cores(): return lax.ppermute(array, 'rollout', [(0, 1), (1, 0)])]
    pallas_call x2, Pallas kernels: 2.65 us -> 4.07 us  [the longest x1 2.73 us: choose_b(): pl.pallas_call(functools.partial(choose_b_kernel, n, pieces), in_specs=[S...]
    ppermute x7, starting transfers between devices: 13.1 us -> 11.8 us  [ring_pass(): return lax.ppermute(array, ('rollout', 'tensor'), pairs)]
    ppermute x7, waiting for transfers between devices: 1.46 us -> 2.43 us  [ring_pass(): return lax.ppermute(array, ('rollout', 'tensor'), pairs)]
    ppermute x11, starting transfers between devices: 1.86 us -> 2.79 us  [swap_cores(): return lax.ppermute(array, 'rollout', [(0, 1), (1, 0)])]
    pallas_call x8, Pallas kernels: 14.4 us -> 13.5 us  [merge(): pl.pallas_call(functools.partial(merge_kernel, n, pieces, scale, fresh),...]
  transfers between devices with their start and end apart: 18 -> 18, of which waited for: 2 -> 3; matrix products, arithmetic and copies ran while one was open for 0% -> 0% of each run, Pallas kernels for 43% -> 38%
where the time goes in v6:
time: 38 us; the launch traced here: 37.8 us
  Pallas kernels  18.4 us (48%)
  starting transfers between devices  14.6 us (38%)
  waiting for transfers between devices  3.95 us (10%)
  between operations  0.83 us (2%)
    pallas_call x8, Pallas kernels, merge(): pl.pallas_call(functools.partial(merge_kernel, n, pieces, scale, fresh),...  13.5 us
    ppermute x7, starting transfers between devices, ring_pass(): return lax.ppermute(array, ('rollout', 'tensor'), pairs)  11.8 us
    ppermute x11, starting transfers between devices, swap_cores(): return lax.ppermute(array, 'rollout', [(0, 1), (1, 0)])  2.79 us
    pallas_call x1, Pallas kernels, choose_b(): pl.pallas_call(functools.partial(choose_b_kernel, n, pieces), in_specs=[S...  2.73 us
    ppermute x7, waiting for transfers between devices, ring_pass(): return lax.ppermute(array, ('rollout', 'tensor'), pairs)  2.43 us
    ppermute x11, waiting for transfers between devices, swap_cores(): return lax.ppermute(array, 'rollout', [(0, 1), (1, 0)])  1.52 us
    pallas_call x1, Pallas kernels, fetch_blocks(): pl.pallas_call(functools.partial(fetch_kernel, n, pieces), in_specs=[HBM]...  1.34 us
    pallas_call x1, Pallas kernels, choose_a(): pl.pallas_call(choose_a_kernel, in_specs=[SMEM, VMEM, VMEM], out_specs=[V...  0.76 us
  transfers between devices with their start and end apart: 18, of which 3 were waited for; matrix products, arithmetic and copies ran while one was open for 0% of the time, Pallas kernels for 38%

profile of v6, /device:TPU:0, one launch (start us, length us, event | category | flops | bytes accessed | tf_op | source)
XLA Modules:
  0.0 37.8 jit_solution(531477293902175152)
XLA Ops:
  0.6 0.5 %collective-permute-start = (bf16[2,3,64,640]{3,2,1,0:T(8,128)(2,1)}, bf16[2,3,64,640]{3,2,1,0:T(8,128)(2,1)S(1)}, u32[]{:S(2)}, u32[]{:S(2)}) collective-permute-start(bf16[2,3,64,640]{3,2,1,0:T(8,128)(2,1)} %bitcast.10), channel_id=1, source_target_pairs={{0,8},{8,0},{1,9},{9,1},{2,10},{10,2},{3,11},{11,3},{4,12},{12,4},... | collective-permute-start | bytes 1474568 | tf_op jit(solution)/shard_map/ppermute | solution.py:43
  1.1 0.1 collective-permute-start.1
  1.2 0.4 %collective-permute-start.2 = (bf16[2,64,128]{2,1,0:T(8,128)(2,1)}, bf16[2,64,128]{2,1,0:T(8,128)(2,1)S(1)}, u32[]{:S(2)}, u32[]{:S(2)}) collective-permute-start(bf16[2,64,128]{2,1,0:T(8,128)(2,1)} %bitcast.14), channel_id=1, source_target_pairs={{0,8},{8,0},{1,9},{9,1},{2,10},{10,2},{3,11},{11,3},{4,12},{12,4},... | collective-permute-start | bytes 98312 | tf_op jit(solution)/shard_map/ppermute | solution.py:43
  1.7 0.1 collective-permute-start.3
  1.8 1.3 %shard_map.103 = (bf16[2,128,640]{2,1,0:T(8,128)(2,1)S(1)}, bf16[2,128,640]{2,1,0:T(8,128)(2,1)S(1)}) custom-call(bf16[2,128,5120]{2,1,0:T(8,128)(2,1)} %refs_6_.15, bf16[2,128,5120]{2,1,0:T(8,128)(2,1)} %refs_7_.13), custom_call_target="tpu_custom_call" | custom-call | bytes 1310720 | tf_op jit(solution)/shard_map/pallas_call | solution.py:110
  3.2 0.0 collective-permute-done.2.refs_4_
  3.2 0.0 collective-permute-done.3.refs_5_
  3.2 0.8 %shard_map.105 = (bf16[3,64,640]{2,1,0:T(8,128)(2,1)S(1)}, bf16[3,64,640]{2,1,0:T(8,128)(2,1)S(1)}) custom-call(s32[2,3]{1,0:T(2,128)} %owners.3, bf16[2,3,64,640]{3,2,1,0:T(8,128)(2,1)S(1)} %bitcast.11, bf16[2,3,64,640]{3,2,1,0:T(8,128)(2,1)S(1)} %collective-permute-done.other), custom_call_target="tpu_custom_call" | custom-call | tf_op jit(solution)/shard_map/pallas_call | solution.py:73
  4.0 3.1 %collective-permute-start.4 = (bf16[3,64,640]{2,1,0:T(8,128)(2,1)S(1)}, bf16[3,64,640]{2,1,0:T(8,128)(2,1)S(1)}, u32[]{:S(2)}, u32[]{:S(2)}) collective-permute-start(bf16[3,64,640]{2,1,0:T(8,128)(2,1)S(1)} %get-tuple-element.57.refs_3_), channel_id=1, source_target_pairs={{0,2},{8,9},{2,4},{10,8},{4,6},{12,10},{6,7},{14,12},{7,5},{15,14}... | collective-permute-start | bytes 737288 | tf_op jit(solution)/shard_map/ppermute | solution.py:39
  7.0 1.6 %collective-permute-start.6 = (bf16[3,64,640]{2,1,0:T(8,128)(2,1)S(1)}, bf16[3,64,640]{2,1,0:T(8,128)(2,1)S(1)}, u32[]{:S(2)}, u32[]{:S(2)}) collective-permute-start(bf16[3,64,640]{2,1,0:T(8,128)(2,1)S(1)} %get-tuple-element.58.refs_4_), channel_id=1, source_target_pairs={{0,2},{8,9},{2,4},{10,8},{4,6},{12,10},{6,7},{14,12},{7,5},{15,14}... | collective-permute-start | bytes 737288 | tf_op jit(solution)/shard_map/ppermute | solution.py:39
  8.6 2.7 %shard_map.104 = (bf16[2,640,64]{2,1,0:T(8,128)(2,1)S(1)}, bf16[2,128,64]{2,1,0:T(8,128)(2,1)S(1)}, bf16[2,128,64]{2,1,0:T(8,128)(2,1)S(1)}, bf16[2,640,640]{2,1,0:T(8,128)(2,1)S(1)}) custom-call(s32[2,3]{1,0:T(2,128)} %owners.3, bf16[2,64,640]{2,1,0:T(8,128)(2,1)S(1)} %bitcast.13, bf16[2,64,128]{2,1,0:T(8,128)(2,1)S(1)} %bitcast.15, ...), custom_call_target="tpu_custom_call" | custom-call | bytes 3276800 | tf_op jit(solution)/shard_map/pallas_call | solution.py:136
  11.4 0.0 copy-start.1
  11.4 1.7 %shard_map.106 = (bf16[2,640,5120]{2,1,0:T(8,128)(2,1)}, bf16[2,128,5120]{2,1,0:T(8,128)(2,1)}, bf16[2,128,5120]{2,1,0:T(8,128)(2,1)}) custom-call(bf16[2,640,64]{2,1,0:T(8,128)(2,1)S(1)} %get-tuple-element.53.refs_0_, bf16[2,128,64]{2,1,0:T(8,128)(2,1)S(1)} %get-tuple-element.54.refs_1_, bf16[2,128,64]{2,1,0:T(8,128)(2,1)S(1)} %get-tuple-element.55.refs_2_, ...), custom_call_target="tpu_custom_call" | custom-call | flops 146800640 | bytes 4587520 | tf_op jit(solution)/shard_map/pallas_call | solution.py:183
  13.1 1.6 %collective-permute-start.5 = (bf16[3,64,640]{2,1,0:T(8,128)(2,1)S(1)}, bf16[3,64,640]{2,1,0:T(8,128)(2,1)S(1)}, u32[]{:S(2)}, u32[]{:S(2)}) collective-permute-start(bf16[3,64,640]{2,1,0:T(8,128)(2,1)S(1)} %collective-permute-done.4.refs_3_), channel_id=1, source_target_pairs={{0,2},{8,9},{2,4},{10,8},{4,6},{12,10},{6,7},{14,12},{7,5},{15,14}... | collective-permute-start | bytes 737288 | tf_op jit(solution)/shard_map/ppermute | solution.py:39
  14.7 0.5 %collective-permute-start.10 = (bf16[3,64,640]{2,1,0:T(8,128)(2,1)S(1)}, bf16[3,64,640]{2,1,0:T(8,128)(2,1)S(1)}, u32[]{:S(2)}, u32[]{:S(2)}) collective-permute-start(bf16[3,64,640]{2,1,0:T(8,128)(2,1)S(1)} %collective-permute-done.6.refs_4_), channel_id=1, source_target_pairs={{0,8},{8,0},{1,9},{9,1},{2,10},{10,2},{3,11},{11,3},{4,12},{12,4},... | collective-permute-start | bytes 737288 | tf_op jit(solution)/shard_map/ppermute | solution.py:43
  15.2 1.5 %collective-permute-start.8 = (bf16[3,64,640]{2,1,0:T(8,128)(2,1)S(1)}, bf16[3,64,640]{2,1,0:T(8,128)(2,1)S(1)}, u32[]{:S(2)}, u32[]{:S(2)}) collective-permute-start(bf16[3,64,640]{2,1,0:T(8,128)(2,1)S(1)} %collective-permute-done.6.refs_4_), channel_id=1, source_target_pairs={{0,2},{8,9},{2,4},{10,8},{4,6},{12,10},{6,7},{14,12},{7,5},{15,14}... | collective-permute-start | bytes 737288 | tf_op jit(solution)/shard_map/ppermute | solution.py:39
  16.8 1.7 %shard_map.107 = (bf16[2,640,5120]{2,1,0:T(8,128)(2,1)}, bf16[2,128,5120]{2,1,0:T(8,128)(2,1)}, bf16[2,128,5120]{2,1,0:T(8,128)(2,1)}) custom-call(bf16[2,640,64]{2,1,0:T(8,128)(2,1)S(1)} %get-tuple-element.53.refs_0_, bf16[2,128,64]{2,1,0:T(8,128)(2,1)S(1)} %get-tuple-element.54.refs_1_, ...), custom_call_target="tpu_custom_call", output_to_operand_aliasing={{0}: (8, {}), {1}: (9, {}), {2}: (10, {})} | custom-call | flops 146800640 | bytes 4587520 | tf_op jit(solution)/shard_map/pallas_call | solution.py:183
  18.5 0.9 %collective-permute-done.5.refs_3_ = bf16[3,64,640]{2,1,0:T(8,128)(2,1)S(1)} collective-permute-done((bf16[3,64,640]{2,1,0:T(8,128)(2,1)S(1)}, bf16[3,64,640]{2,1,0:T(8,128)(2,1)S(1)}, u32[]{:S(2)}, u32[]{:S(2)}) %collective-permute-start.5) | collective-permute-done | bytes 245792 | tf_op jit(solution)/shard_map/ppermute | solution.py:39
  19.3 1.6 %collective-permute-start.7 = (bf16[3,64,640]{2,1,0:T(8,128)(2,1)S(1)}, bf16[3,64,640]{2,1,0:T(8,128)(2,1)S(1)}, u32[]{:S(2)}, u32[]{:S(2)}) collective-permute-start(bf16[3,64,640]{2,1,0:T(8,128)(2,1)S(1)} %collective-permute-done.5.refs_3_), channel_id=1, source_target_pairs={{0,2},{8,9},{2,4},{10,8},{4,6},{12,10},{6,7},{14,12},{7,5},{15,14}... | collective-permute-start | bytes 737288 | tf_op jit(solution)/shard_map/ppermute | solution.py:39
  20.9 1.7 %shard_map.108 = (bf16[2,640,5120]{2,1,0:T(8,128)(2,1)}, bf16[2,128,5120]{2,1,0:T(8,128)(2,1)}, bf16[2,128,5120]{2,1,0:T(8,128)(2,1)}) custom-call(bf16[2,640,64]{2,1,0:T(8,128)(2,1)S(1)} %get-tuple-element.53.refs_0_, bf16[2,128,64]{2,1,0:T(8,128)(2,1)S(1)} %get-tuple-element.54.refs_1_, ...), custom_call_target="tpu_custom_call", output_to_operand_aliasing={{0}: (8, {}), {1}: (9, {}), {2}: (10, {})} | custom-call | flops 146800640 | bytes 4587520 | tf_op jit(solution)/shard_map/pallas_call | solution.py:183
  22.6 1.6 %collective-permute-start.12 = (bf16[3,64,640]{2,1,0:T(8,128)(2,1)S(1)}, bf16[3,64,640]{2,1,0:T(8,128)(2,1)S(1)}, u32[]{:S(2)}, u32[]{:S(2)}) collective-permute-start(bf16[3,64,640]{2,1,0:T(8,128)(2,1)S(1)} %collective-permute-done.8.refs_4_), channel_id=1, source_target_pairs={{0,2},{8,9},{2,4},{10,8},{4,6},{12,10},{6,7},{14,12},{7,5},{15,14}... | collective-permute-start | bytes 737288 | tf_op jit(solution)/shard_map/ppermute | solution.py:39
  24.2 0.5 %collective-permute-start.14 = (bf16[3,64,640]{2,1,0:T(8,128)(2,1)S(1)}, bf16[3,64,640]{2,1,0:T(8,128)(2,1)S(1)}, u32[]{:S(2)}, u32[]{:S(2)}) collective-permute-start(bf16[3,64,640]{2,1,0:T(8,128)(2,1)S(1)} %collective-permute-done.8.refs_4_), channel_id=1, source_target_pairs={{0,8},{8,0},{1,9},{9,1},{2,10},{10,2},{3,11},{11,3},{4,12},{12,4},... | collective-permute-start | bytes 737288 | tf_op jit(solution)/shard_map/ppermute | solution.py:43
  24.7 1.7 %shard_map.109 = (bf16[2,640,5120]{2,1,0:T(8,128)(2,1)}, bf16[2,128,5120]{2,1,0:T(8,128)(2,1)}, bf16[2,128,5120]{2,1,0:T(8,128)(2,1)}) custom-call(bf16[2,640,64]{2,1,0:T(8,128)(2,1)S(1)} %get-tuple-element.53.refs_0_, bf16[2,128,64]{2,1,0:T(8,128)(2,1)S(1)} %get-tuple-element.54.refs_1_, ...), custom_call_target="tpu_custom_call", output_to_operand_aliasing={{0}: (8, {}), {1}: (9, {}), {2}: (10, {})} | custom-call | flops 146800640 | bytes 4587520 | tf_op jit(solution)/shard_map/pallas_call | solution.py:183
  26.4 0.9 %collective-permute-start.11 = (bf16[3,64,640]{2,1,0:T(8,128)(2,1)S(1)}, bf16[3,64,640]{2,1,0:T(8,128)(2,1)S(1)}, u32[]{:S(2)}, u32[]{:S(2)}) collective-permute-start(bf16[3,64,640]{2,1,0:T(8,128)(2,1)S(1)} %collective-permute-done.7.refs_3_), channel_id=1, source_target_pairs={{0,2},{8,9},{2,4},{10,8},{4,6},{12,10},{6,7},{14,12},{7,5},{15,14}... | collective-permute-start | bytes 737288 | tf_op jit(solution)/shard_map/ppermute | solution.py:39
  27.4 1.5 %collective-permute-done.12.refs_4_ = bf16[3,64,640]{2,1,0:T(8,128)(2,1)S(1)} collective-permute-done((bf16[3,64,640]{2,1,0:T(8,128)(2,1)S(1)}, bf16[3,64,640]{2,1,0:T(8,128)(2,1)S(1)}, u32[]{:S(2)}, u32[]{:S(2)}) %collective-permute-start.12) | collective-permute-done | bytes 245792 | tf_op jit(solution)/shard_map/ppermute | solution.py:39
  28.9 0.5 %collective-permute-start.16 = (bf16[3,64,640]{2,1,0:T(8,128)(2,1)S(1)}, bf16[3,64,640]{2,1,0:T(8,128)(2,1)S(1)}, u32[]{:S(2)}, u32[]{:S(2)}) collective-permute-start(bf16[3,64,640]{2,1,0:T(8,128)(2,1)S(1)} %collective-permute-done.12.refs_4_), channel_id=1, source_target_pairs={{0,8},{8,0},{1,9},{9,1},{2,10},{10,2},{3,11},{11,3},{4,12},{12,4},... | collective-permute-start | bytes 737288 | tf_op jit(solution)/shard_map/ppermute | solution.py:43
  29.4 1.7 %shard_map.110 = (bf16[2,640,5120]{2,1,0:T(8,128)(2,1)}, bf16[2,128,5120]{2,1,0:T(8,128)(2,1)}, bf16[2,128,5120]{2,1,0:T(8,128)(2,1)}) custom-call(bf16[2,640,64]{2,1,0:T(8,128)(2,1)S(1)} %get-tuple-element.53.refs_0_, bf16[2,128,64]{2,1,0:T(8,128)(2,1)S(1)} %get-tuple-element.54.refs_1_, ...), custom_call_target="tpu_custom_call", output_to_operand_aliasing={{0}: (8, {}), {1}: (9, {}), {2}: (10, {})} | custom-call | flops 146800640 | bytes 4587520 | tf_op jit(solution)/shard_map/pallas_call | solution.py:183
  31.1 1.7 %shard_map.111 = (bf16[2,640,5120]{2,1,0:T(8,128)(2,1)}, bf16[2,128,5120]{2,1,0:T(8,128)(2,1)}, bf16[2,128,5120]{2,1,0:T(8,128)(2,1)}) custom-call(bf16[2,640,64]{2,1,0:T(8,128)(2,1)S(1)} %get-tuple-element.53.refs_0_, bf16[2,128,64]{2,1,0:T(8,128)(2,1)S(1)} %get-tuple-element.54.refs_1_, ...), custom_call_target="tpu_custom_call", output_to_operand_aliasing={{0}: (8, {}), {1}: (9, {}), {2}: (10, {})} | custom-call | flops 146800640 | bytes 4587520 | tf_op jit(solution)/shard_map/pallas_call | solution.py:183
  32.9 1.7 %shard_map.112 = (bf16[2,640,5120]{2,1,0:T(8,128)(2,1)}, bf16[2,128,5120]{2,1,0:T(8,128)(2,1)}, bf16[2,128,5120]{2,1,0:T(8,128)(2,1)}) custom-call(bf16[2,640,64]{2,1,0:T(8,128)(2,1)S(1)} %get-tuple-element.53.refs_0_, bf16[2,128,64]{2,1,0:T(8,128)(2,1)S(1)} %get-tuple-element.54.refs_1_, ...), custom_call_target="tpu_custom_call", output_to_operand_aliasing={{0}: (8, {}), {1}: (9, {}), {2}: (10, {})} | custom-call | flops 146800640 | bytes 4587520 | tf_op jit(solution)/shard_map/pallas_call | solution.py:183
  34.6 0.1 collective-permute-start.17
  34.6 1.5 %collective-permute-done.17.refs_4_ = bf16[3,64,640]{2,1,0:T(8,128)(2,1)S(1)} collective-permute-done((bf16[3,64,640]{2,1,0:T(8,128)(2,1)S(1)}, bf16[3,64,640]{2,1,0:T(8,128)(2,1)S(1)}, u32[]{:S(2)}, u32[]{:S(2)}) %collective-permute-start.17) | collective-permute-done | bytes 245792 | tf_op jit(solution)/shard_map/ppermute | solution.py:43
  36.1 1.7 %shard_map.113 = (bf16[2,640,5120]{2,1,0:T(8,128)(2,1)}, bf16[2,128,5120]{2,1,0:T(8,128)(2,1)}, bf16[2,128,5120]{2,1,0:T(8,128)(2,1)}) custom-call(bf16[2,640,64]{2,1,0:T(8,128)(2,1)S(1)} %get-tuple-element.53.refs_0_, bf16[2,128,64]{2,1,0:T(8,128)(2,1)S(1)} %get-tuple-element.54.refs_1_, ...), custom_call_target="tpu_custom_call", output_to_operand_aliasing={{0}: (8, {}), {1}: (9, {}), {2}: (10, {})} | custom-call | flops 146800640 | bytes 4587520 | tf_op jit(solution)/shard_map/pallas_call | solution.py:183
  (29 shorter events, 0.1 us)
Async XLA Ops:
  0.6 2.6 %collective-permute-start = (bf16[2,3,64,640]{3,2,1,0:T(8,128)(2,1)}, bf16[2,3,64,640]{3,2,1,0:T(8,128)(2,1)S(1)}, u32[]{:S(2)}, u32[]{:S(2)}) collective-permute-start(bf16[2,3,64,640]{3,2,1,0:T(8,128)(2,1)} %bitcast.10), channel_id=1, source_target_pairs={{0,8},{8,0},{1,9},{9,1},{2,10},{10,2},{3,11},{11,3},{4,12},{12,4},... | collective-permute-start | bytes 1474568 | tf_op jit(solution)/shard_map/ppermute | solution.py:43
  1.1 2.0 %collective-permute-start.1 = (bf16[2,64,640]{2,1,0:T(8,128)(2,1)}, bf16[2,64,640]{2,1,0:T(8,128)(2,1)S(1)}, u32[]{:S(2)}, u32[]{:S(2)}) collective-permute-start(bf16[2,64,640]{2,1,0:T(8,128)(2,1)} %bitcast.12), channel_id=1, source_target_pairs={{0,8},{8,0},{1,9},{9,1},{2,10},{10,2},{3,11},{11,3},{4,12},{12,4},... | collective-permute-start | bytes 491528 | tf_op jit(solution)/shard_map/ppermute | solution.py:43
  1.2 1.9 %collective-permute-start.2 = (bf16[2,64,128]{2,1,0:T(8,128)(2,1)}, bf16[2,64,128]{2,1,0:T(8,128)(2,1)S(1)}, u32[]{:S(2)}, u32[]{:S(2)}) collective-permute-start(bf16[2,64,128]{2,1,0:T(8,128)(2,1)} %bitcast.14), channel_id=1, source_target_pairs={{0,8},{8,0},{1,9},{9,1},{2,10},{10,2},{3,11},{11,3},{4,12},{12,4},... | collective-permute-start | bytes 98312 | tf_op jit(solution)/shard_map/ppermute | solution.py:43
  1.7 1.5 %copy-start.3 = (bf16[1,2,3,64,640]{4,3,2,1,0:T(8,128)(2,1)S(1)}, bf16[1,2,3,64,640]{4,3,2,1,0:T(8,128)(2,1)}, u32[]{:S(2)}) copy-start(bf16[1,2,3,64,640]{4,3,2,1,0:T(8,128)(2,1)} %param.12) | copy-start | bytes 1474564
  1.7 7.0 %copy-start.4 = (bf16[1,2,640,64]{2,3,1,0:T(8,128)(2,1)S(1)}, bf16[1,2,640,64]{2,3,1,0:T(8,128)(2,1)}, u32[]{:S(2)}) copy-start(bf16[1,2,640,64]{2,3,1,0:T(8,128)(2,1)} %param.13) | copy-start | bytes 491524
  1.7 7.0 %copy-start.5 = (bf16[1,2,128,64]{2,3,1,0:T(8,128)(2,1)S(1)}, bf16[1,2,128,64]{2,3,1,0:T(8,128)(2,1)}, u32[]{:S(2)}) copy-start(bf16[1,2,128,64]{2,3,1,0:T(8,128)(2,1)} %param.14) | copy-start | bytes 98308
  1.7 7.0 %copy-start.6 = (bf16[1,2,128,64]{2,3,1,0:T(8,128)(2,1)S(1)}, bf16[1,2,128,64]{2,3,1,0:T(8,128)(2,1)}, u32[]{:S(2)}) copy-start(bf16[1,2,128,64]{2,3,1,0:T(8,128)(2,1)} %param.15) | copy-start | bytes 98308
  1.7 1.5 %collective-permute-start.3 = (bf16[2,64,128]{2,1,0:T(8,128)(2,1)}, bf16[2,64,128]{2,1,0:T(8,128)(2,1)S(1)}, u32[]{:S(2)}, u32[]{:S(2)}) collective-permute-start(bf16[2,64,128]{2,1,0:T(8,128)(2,1)} %bitcast.16), channel_id=1, source_target_pairs={{0,8},{8,0},{1,9},{9,1},{2,10},{10,2},{3,11},{11,3},{4,12},{12,4},... | collective-permute-start | bytes 98312 | tf_op jit(solution)/shard_map/ppermute | solution.py:43
  1.8 14.9 %copy-start.2 = (bf16[2,128,5120]{2,1,0:T(8,128)(2,1)S(1)}, bf16[2,128,5120]{2,1,0:T(8,128)(2,1)}, u32[]{:S(2)}) copy-start(bf16[2,128,5120]{2,1,0:T(8,128)(2,1)} %refs_7_.13) | copy-start | bytes 7864324
  4.0 9.1 %collective-permute-start.4 = (bf16[3,64,640]{2,1,0:T(8,128)(2,1)S(1)}, bf16[3,64,640]{2,1,0:T(8,128)(2,1)S(1)}, u32[]{:S(2)}, u32[]{:S(2)}) collective-permute-start(bf16[3,64,640]{2,1,0:T(8,128)(2,1)S(1)} %get-tuple-element.57.refs_3_), channel_id=1, source_target_pairs={{0,2},{8,9},{2,4},{10,8},{4,6},{12,10},{6,7},{14,12},{7,5},{15,14}... | collective-permute-start | bytes 737288 | tf_op jit(solution)/shard_map/ppermute | solution.py:39
  7.0 7.7 %collective-permute-start.6 = (bf16[3,64,640]{2,1,0:T(8,128)(2,1)S(1)}, bf16[3,64,640]{2,1,0:T(8,128)(2,1)S(1)}, u32[]{:S(2)}, u32[]{:S(2)}) collective-permute-start(bf16[3,64,640]{2,1,0:T(8,128)(2,1)S(1)} %get-tuple-element.58.refs_4_), channel_id=1, source_target_pairs={{0,2},{8,9},{2,4},{10,8},{4,6},{12,10},{6,7},{14,12},{7,5},{15,14}... | collective-permute-start | bytes 737288 | tf_op jit(solution)/shard_map/ppermute | solution.py:39
  8.6 8.1 %copy-start = (bf16[2,640,5120]{2,1,0:T(8,128)(2,1)S(1)}, bf16[2,640,5120]{2,1,0:T(8,128)(2,1)}, u32[]{:S(2)}) copy-start(bf16[2,640,5120]{2,1,0:T(8,128)(2,1)} %refs_5_.13) | copy-start | bytes 39321604
  11.4 5.4 %copy-start.1 = (bf16[2,128,5120]{2,1,0:T(8,128)(2,1)S(1)}, bf16[2,128,5120]{2,1,0:T(8,128)(2,1)}, u32[]{:S(2)}) copy-start(bf16[2,128,5120]{2,1,0:T(8,128)(2,1)} %refs_6_.15) | copy-start | bytes 7864324
  13.1 6.2 %collective-permute-start.5 = (bf16[3,64,640]{2,1,0:T(8,128)(2,1)S(1)}, bf16[3,64,640]{2,1,0:T(8,128)(2,1)S(1)}, u32[]{:S(2)}, u32[]{:S(2)}) collective-permute-start(bf16[3,64,640]{2,1,0:T(8,128)(2,1)S(1)} %collective-permute-done.4.refs_3_), channel_id=1, source_target_pairs={{0,2},{8,9},{2,4},{10,8},{4,6},{12,10},{6,7},{14,12},{7,5},{15,14}... | collective-permute-start | bytes 737288 | tf_op jit(solution)/shard_map/ppermute | solution.py:39
  14.7 6.2 %collective-permute-start.9 = (bf16[3,64,640]{2,1,0:T(8,128)(2,1)S(1)}, bf16[3,64,640]{2,1,0:T(8,128)(2,1)S(1)}, u32[]{:S(2)}, u32[]{:S(2)}) collective-permute-start(bf16[3,64,640]{2,1,0:T(8,128)(2,1)S(1)} %collective-permute-done.4.refs_3_), channel_id=1, source_target_pairs={{0,8},{8,0},{1,9},{9,1},{2,10},{10,2},{3,11},{11,3},{4,12},{12,4},... | collective-permute-start | bytes 737288 | tf_op jit(solution)/shard_map/ppermute | solution.py:43
  14.7 6.2 %collective-permute-start.10 = (bf16[3,64,640]{2,1,0:T(8,128)(2,1)S(1)}, bf16[3,64,640]{2,1,0:T(8,128)(2,1)S(1)}, u32[]{:S(2)}, u32[]{:S(2)}) collective-permute-start(bf16[3,64,640]{2,1,0:T(8,128)(2,1)S(1)} %collective-permute-done.6.refs_4_), channel_id=1, source_target_pairs={{0,8},{8,0},{1,9},{9,1},{2,10},{10,2},{3,11},{11,3},{4,12},{12,4},... | collective-permute-start | bytes 737288 | tf_op jit(solution)/shard_map/ppermute | solution.py:43
  15.2 7.4 %collective-permute-start.8 = (bf16[3,64,640]{2,1,0:T(8,128)(2,1)S(1)}, bf16[3,64,640]{2,1,0:T(8,128)(2,1)S(1)}, u32[]{:S(2)}, u32[]{:S(2)}) collective-permute-start(bf16[3,64,640]{2,1,0:T(8,128)(2,1)S(1)} %collective-permute-done.6.refs_4_), channel_id=1, source_target_pairs={{0,2},{8,9},{2,4},{10,8},{4,6},{12,10},{6,7},{14,12},{7,5},{15,14}... | collective-permute-start | bytes 737288 | tf_op jit(solution)/shard_map/ppermute | solution.py:39
  19.3 7.1 %collective-permute-start.7 = (bf16[3,64,640]{2,1,0:T(8,128)(2,1)S(1)}, bf16[3,64,640]{2,1,0:T(8,128)(2,1)S(1)}, u32[]{:S(2)}, u32[]{:S(2)}) collective-permute-start(bf16[3,64,640]{2,1,0:T(8,128)(2,1)S(1)} %collective-permute-done.5.refs_3_), channel_id=1, source_target_pairs={{0,2},{8,9},{2,4},{10,8},{4,6},{12,10},{6,7},{14,12},{7,5},{15,14}... | collective-permute-start | bytes 737288 | tf_op jit(solution)/shard_map/ppermute | solution.py:39
  22.6 6.2 %collective-permute-start.12 = (bf16[3,64,640]{2,1,0:T(8,128)(2,1)S(1)}, bf16[3,64,640]{2,1,0:T(8,128)(2,1)S(1)}, u32[]{:S(2)}, u32[]{:S(2)}) collective-permute-start(bf16[3,64,640]{2,1,0:T(8,128)(2,1)S(1)} %collective-permute-done.8.refs_4_), channel_id=1, source_target_pairs={{0,2},{8,9},{2,4},{10,8},{4,6},{12,10},{6,7},{14,12},{7,5},{15,14}... | collective-permute-start | bytes 737288 | tf_op jit(solution)/shard_map/ppermute | solution.py:39
  24.2 5.2 %collective-permute-start.13 = (bf16[3,64,640]{2,1,0:T(8,128)(2,1)S(1)}, bf16[3,64,640]{2,1,0:T(8,128)(2,1)S(1)}, u32[]{:S(2)}, u32[]{:S(2)}) collective-permute-start(bf16[3,64,640]{2,1,0:T(8,128)(2,1)S(1)} %collective-permute-done.5.refs_3_), channel_id=1, source_target_pairs={{0,8},{8,0},{1,9},{9,1},{2,10},{10,2},{3,11},{11,3},{4,12},{12,4},... | collective-permute-start | bytes 737288 | tf_op jit(solution)/shard_map/ppermute | solution.py:43
  24.2 5.2 %collective-permute-start.14 = (bf16[3,64,640]{2,1,0:T(8,128)(2,1)S(1)}, bf16[3,64,640]{2,1,0:T(8,128)(2,1)S(1)}, u32[]{:S(2)}, u32[]{:S(2)}) collective-permute-start(bf16[3,64,640]{2,1,0:T(8,128)(2,1)S(1)} %collective-permute-done.8.refs_4_), channel_id=1, source_target_pairs={{0,8},{8,0},{1,9},{9,1},{2,10},{10,2},{3,11},{11,3},{4,12},{12,4},... | collective-permute-start | bytes 737288 | tf_op jit(solution)/shard_map/ppermute | solution.py:43
  26.4 6.4 %collective-permute-start.11 = (bf16[3,64,640]{2,1,0:T(8,128)(2,1)S(1)}, bf16[3,64,640]{2,1,0:T(8,128)(2,1)S(1)}, u32[]{:S(2)}, u32[]{:S(2)}) collective-permute-start(bf16[3,64,640]{2,1,0:T(8,128)(2,1)S(1)} %collective-permute-done.7.refs_3_), channel_id=1, source_target_pairs={{0,2},{8,9},{2,4},{10,8},{4,6},{12,10},{6,7},{14,12},{7,5},{15,14}... | collective-permute-start | bytes 737288 | tf_op jit(solution)/shard_map/ppermute | solution.py:39
  28.9 3.9 %collective-permute-start.15 = (bf16[3,64,640]{2,1,0:T(8,128)(2,1)S(1)}, bf16[3,64,640]{2,1,0:T(8,128)(2,1)S(1)}, u32[]{:S(2)}, u32[]{:S(2)}) collective-permute-start(bf16[3,64,640]{2,1,0:T(8,128)(2,1)S(1)} %collective-permute-done.7.refs_3_), channel_id=1, source_target_pairs={{0,8},{8,0},{1,9},{9,1},{2,10},{10,2},{3,11},{11,3},{4,12},{12,4},... | collective-permute-start | bytes 737288 | tf_op jit(solution)/shard_map/ppermute | solution.py:43
  28.9 3.9 %collective-permute-start.16 = (bf16[3,64,640]{2,1,0:T(8,128)(2,1)S(1)}, bf16[3,64,640]{2,1,0:T(8,128)(2,1)S(1)}, u32[]{:S(2)}, u32[]{:S(2)}) collective-permute-start(bf16[3,64,640]{2,1,0:T(8,128)(2,1)S(1)} %collective-permute-done.12.refs_4_), channel_id=1, source_target_pairs={{0,8},{8,0},{1,9},{9,1},{2,10},{10,2},{3,11},{11,3},{4,12},{12,4},... | collective-permute-start | bytes 737288 | tf_op jit(solution)/shard_map/ppermute | solution.py:43
  34.6 1.6 %collective-permute-start.17 = (bf16[3,64,640]{2,1,0:T(8,128)(2,1)S(1)}, bf16[3,64,640]{2,1,0:T(8,128)(2,1)S(1)}, u32[]{:S(2)}, u32[]{:S(2)}) collective-permute-start(bf16[3,64,640]{2,1,0:T(8,128)(2,1)S(1)} %collective-permute-done.11.refs_3_), channel_id=1, source_target_pairs={{0,8},{8,0},{1,9},{9,1},{2,10},{10,2},{3,11},{11,3},{4,12},{12,4},... | collective-permute-start | bytes 737288 | tf_op jit(solution)/shard_map/ppermute | solution.py:43

commit v7 on v6

--- a/solution.py
+++ b/solution.py
@@ -229,26 +229,27 @@
         second = ring_pass(second, n)
         b, block = choose_b(n, cols, owners, own_b, other_b, base_query, pieces)
         outs = merge(n, scale, b, held, [block, *small_blocks], shapes, None, pieces)
-        first, _ = tie((first, outs))
+        first, outs = tie((first, outs))
 
         def go(pieces, chunks, outs):
             return merge(n, scale, b, chunks, bases, shapes, outs, pieces)
 
-        def later(array, *others):
-            return tie((array, others))[0]
-
-        others = None
-        for step in range(1, last):
-            onward = ring_pass(first, n)
+        ready = []
+        for step in range(1, last + 1):
             if step > 1:
-                outs = go([(step - 1, False, False), (step - 1, False, True)], others, outs)
-            onward_second = ring_pass(later(second, outs), n) if step < last - 1 else None
-            others = [swap_cores(later(first, second)), swap_cores(second)]
-            outs = go([(step, True, True), (step, True, False)], [first, second], outs)
-            first, second = later(onward, outs), onward_second
-        outs = go([(last - 1, False, False), (last - 1, False, True)], others, outs)
-        first = later(first, outs)
-        return tuple(go([(last, True, True), (last, False, False)], [first, swap_cores(first)], outs))
+                outs = go(*ready.pop(0), outs)
+            ready.append(([(step, True, True), (step, False, False)], [first, swap_cores(first)]))
+            if step < last:
+                first = ring_pass(first, n)
+                second, outs = tie((second, outs))
+                ready.append(([(step, True, False), (step, False, True)], [second, swap_cores(second)]))
+                outs = go(*ready.pop(0), outs)
+                first, outs = tie((first, outs))
+                if step < last - 1:
+                    second = ring_pass(second, n)
+        for item in ready:
+            outs = go(*item, outs)
+        return tuple(outs)
 
     core = lax.axis_index("rollout")
     tensor = lax.axis_index("tensor")

time: 38 us -> 36.1 us (0.950)
  starting transfers between devices: 14.6 us -> 13.4 us
  waiting for transfers between devices: 3.95 us -> 3.21 us
    ppermute x11, waiting for transfers between devices: 1.52 us -> 0.03 us  [swap_cores(): return lax.ppermute(array, 'rollout', [(0, 1), (1, 0)])]
    ppermute x11, starting transfers between devices: 2.79 us -> 1.39 us  [swap_cores(): return lax.ppermute(array, 'rollout', [(0, 1), (1, 0)])]
    ppermute x7, waiting for transfers between devices: 2.43 us -> 3.18 us  [ring_pass(): return lax.ppermute(array, ('rollout', 'tensor'), pairs)]
  transfers between devices with their start and end apart: 18 -> 18, of which waited for: 3 -> 3; matrix products, arithmetic and copies ran while one was open for 0% -> 0% of each run, Pallas kernels for 38% -> 44%
where the time goes in v7:
time: 36.1 us; the launch traced here: 35.8 us
  Pallas kernels  18.4 us (51%)
  starting transfers between devices  13.4 us (37%)
  waiting for transfers between devices  3.21 us (9%)
  between operations  0.85 us (2%)
    pallas_call x8, Pallas kernels, merge(): pl.pallas_call(functools.partial(merge_kernel, n, pieces, scale, fresh),...  13.5 us
    ppermute x7, starting transfers between devices, ring_pass(): return lax.ppermute(array, ('rollout', 'tensor'), pairs)  12 us
    ppermute x7, waiting for transfers between devices, ring_pass(): return lax.ppermute(array, ('rollout', 'tensor'), pairs)  3.18 us
    pallas_call x1, Pallas kernels, choose_b(): pl.pallas_call(functools.partial(choose_b_kernel, n, pieces), in_specs=[S...  2.73 us
    ppermute x11, starting transfers between devices, swap_cores(): return lax.ppermute(array, 'rollout', [(0, 1), (1, 0)])  1.39 us
    pallas_call x1, Pallas kernels, fetch_blocks(): pl.pallas_call(functools.partial(fetch_kernel, n, pieces), in_specs=[HBM]...  1.34 us
    pallas_call x1, Pallas kernels, choose_a(): pl.pallas_call(choose_a_kernel, in_specs=[SMEM, VMEM, VMEM], out_specs=[V...  0.76 us
  transfers between devices with their start and end apart: 18, of which 3 were waited for; matrix products, arithmetic and copies ran while one was open for 0% of the time, Pallas kernels for 44%

profile of v7, /device:TPU:0, one launch (start us, length us, event | category | flops | bytes accessed | tf_op | source)
XLA Modules:
  0.0 35.8 jit_solution(3781914627496420395)
XLA Ops:
  0.6 0.5 %collective-permute-start = (bf16[2,3,64,640]{3,2,1,0:T(8,128)(2,1)}, bf16[2,3,64,640]{3,2,1,0:T(8,128)(2,1)S(1)}, u32[]{:S(2)}, u32[]{:S(2)}) collective-permute-start(bf16[2,3,64,640]{3,2,1,0:T(8,128)(2,1)} %bitcast.10), channel_id=1, source_target_pairs={{0,8},{8,0},{1,9},{9,1},{2,10},{10,2},{3,11},{11,3},{4,12},{12,4},... | collective-permute-start | bytes 1474568 | tf_op jit(solution)/shard_map/ppermute | solution.py:43
  1.1 0.1 collective-permute-start.1
  1.2 0.4 %collective-permute-start.2 = (bf16[2,64,128]{2,1,0:T(8,128)(2,1)}, bf16[2,64,128]{2,1,0:T(8,128)(2,1)S(1)}, u32[]{:S(2)}, u32[]{:S(2)}) collective-permute-start(bf16[2,64,128]{2,1,0:T(8,128)(2,1)} %bitcast.14), channel_id=1, source_target_pairs={{0,8},{8,0},{1,9},{9,1},{2,10},{10,2},{3,11},{11,3},{4,12},{12,4},... | collective-permute-start | bytes 98312 | tf_op jit(solution)/shard_map/ppermute | solution.py:43
  1.7 0.1 collective-permute-start.3
  1.8 1.3 %shard_map.103 = (bf16[2,128,640]{2,1,0:T(8,128)(2,1)S(1)}, bf16[2,128,640]{2,1,0:T(8,128)(2,1)S(1)}) custom-call(bf16[2,128,5120]{2,1,0:T(8,128)(2,1)} %refs_6_.15, bf16[2,128,5120]{2,1,0:T(8,128)(2,1)} %refs_7_.13), custom_call_target="tpu_custom_call" | custom-call | bytes 1310720 | tf_op jit(solution)/shard_map/pallas_call | solution.py:110
  3.2 0.0 collective-permute-done.2.refs_4_
  3.2 0.0 collective-permute-done.3.refs_5_
  3.2 0.0 collective-permute-done.1.refs_3_
  3.2 0.8 %shard_map.105 = (bf16[3,64,640]{2,1,0:T(8,128)(2,1)S(1)}, bf16[3,64,640]{2,1,0:T(8,128)(2,1)S(1)}) custom-call(s32[2,3]{1,0:T(2,128)} %owners.3, bf16[2,3,64,640]{3,2,1,0:T(8,128)(2,1)S(1)} %bitcast.11, bf16[2,3,64,640]{3,2,1,0:T(8,128)(2,1)S(1)} %collective-permute-done.other), custom_call_target="tpu_custom_call" | custom-call | tf_op jit(solution)/shard_map/pallas_call | solution.py:73
  4.0 3.1 %collective-permute-start.4 = (bf16[3,64,640]{2,1,0:T(8,128)(2,1)S(1)}, bf16[3,64,640]{2,1,0:T(8,128)(2,1)S(1)}, u32[]{:S(2)}, u32[]{:S(2)}) collective-permute-start(bf16[3,64,640]{2,1,0:T(8,128)(2,1)S(1)} %get-tuple-element.75.refs_3_), channel_id=1, source_target_pairs={{0,2},{8,9},{2,4},{10,8},{4,6},{12,10},{6,7},{14,12},{7,5},{15,14}... | collective-permute-start | bytes 737288 | tf_op jit(solution)/shard_map/ppermute | solution.py:39
  7.0 1.6 %collective-permute-start.7 = (bf16[3,64,640]{2,1,0:T(8,128)(2,1)S(1)}, bf16[3,64,640]{2,1,0:T(8,128)(2,1)S(1)}, u32[]{:S(2)}, u32[]{:S(2)}) collective-permute-start(bf16[3,64,640]{2,1,0:T(8,128)(2,1)S(1)} %get-tuple-element.76.refs_4_), channel_id=1, source_target_pairs={{0,2},{8,9},{2,4},{10,8},{4,6},{12,10},{6,7},{14,12},{7,5},{15,14}... | collective-permute-start | bytes 737288 | tf_op jit(solution)/shard_map/ppermute | solution.py:39
  8.6 2.7 %shard_map.104 = (bf16[2,640,64]{2,1,0:T(8,128)(2,1)S(1)}, bf16[2,128,64]{2,1,0:T(8,128)(2,1)S(1)}, bf16[2,128,64]{2,1,0:T(8,128)(2,1)S(1)}, bf16[2,640,640]{2,1,0:T(8,128)(2,1)S(1)}) custom-call(s32[2,3]{1,0:T(2,128)} %owners.3, bf16[2,64,640]{2,1,0:T(8,128)(2,1)S(1)} %bitcast.13, bf16[2,64,128]{2,1,0:T(8,128)(2,1)S(1)} %bitcast.15, ...), custom_call_target="tpu_custom_call" | custom-call | bytes 3276800 | tf_op jit(solution)/shard_map/pallas_call | solution.py:136
  11.4 0.0 copy-start.1
  11.4 1.7 %shard_map.106 = (bf16[2,640,5120]{2,1,0:T(8,128)(2,1)}, bf16[2,128,5120]{2,1,0:T(8,128)(2,1)}, bf16[2,128,5120]{2,1,0:T(8,128)(2,1)}) custom-call(bf16[2,640,64]{2,1,0:T(8,128)(2,1)S(1)} %get-tuple-element.71.refs_0_, bf16[2,128,64]{2,1,0:T(8,128)(2,1)S(1)} %get-tuple-element.72.refs_1_, bf16[2,128,64]{2,1,0:T(8,128)(2,1)S(1)} %get-tuple-element.73.refs_2_, ...), custom_call_target="tpu_custom_call" | custom-call | flops 146800640 | bytes 4587520 | tf_op jit(solution)/shard_map/pallas_call | solution.py:183
  13.1 0.1 collective-permute-start.6
  13.2 1.6 %collective-permute-start.5 = (bf16[3,64,640]{2,1,0:T(8,128)(2,1)S(1)}, bf16[3,64,640]{2,1,0:T(8,128)(2,1)S(1)}, u32[]{:S(2)}, u32[]{:S(2)}) collective-permute-start(bf16[3,64,640]{2,1,0:T(8,128)(2,1)S(1)} %collective-permute-done.4.refs_3_), channel_id=1, source_target_pairs={{0,2},{8,9},{2,4},{10,8},{4,6},{12,10},{6,7},{14,12},{7,5},{15,14}... | collective-permute-start | bytes 737288 | tf_op jit(solution)/shard_map/ppermute | solution.py:39
  14.8 1.5 %collective-permute-start.10 = (bf16[3,64,640]{2,1,0:T(8,128)(2,1)S(1)}, bf16[3,64,640]{2,1,0:T(8,128)(2,1)S(1)}, u32[]{:S(2)}, u32[]{:S(2)}) collective-permute-start(bf16[3,64,640]{2,1,0:T(8,128)(2,1)S(1)} %collective-permute-done.7.refs_3_), channel_id=1, source_target_pairs={{0,2},{8,9},{2,4},{10,8},{4,6},{12,10},{6,7},{14,12},{7,5},{15,14}... | collective-permute-start | bytes 737288 | tf_op jit(solution)/shard_map/ppermute | solution.py:39
  16.4 1.7 %shard_map.107 = (bf16[2,640,5120]{2,1,0:T(8,128)(2,1)}, bf16[2,128,5120]{2,1,0:T(8,128)(2,1)}, bf16[2,128,5120]{2,1,0:T(8,128)(2,1)}) custom-call(bf16[2,640,64]{2,1,0:T(8,128)(2,1)S(1)} %get-tuple-element.71.refs_0_, bf16[2,128,64]{2,1,0:T(8,128)(2,1)S(1)} %get-tuple-element.72.refs_1_, ...), custom_call_target="tpu_custom_call", output_to_operand_aliasing={{0}: (8, {}), {1}: (9, {}), {2}: (10, {})} | custom-call | flops 146800640 | bytes 4587520 | tf_op jit(solution)/shard_map/pallas_call | solution.py:183
  18.1 1.4 %collective-permute-done.5.refs_3_ = bf16[3,64,640]{2,1,0:T(8,128)(2,1)S(1)} collective-permute-done((bf16[3,64,640]{2,1,0:T(8,128)(2,1)S(1)}, bf16[3,64,640]{2,1,0:T(8,128)(2,1)S(1)}, u32[]{:S(2)}, u32[]{:S(2)}) %collective-permute-start.5) | collective-permute-done | bytes 245792 | tf_op jit(solution)/shard_map/ppermute | solution.py:39
  19.4 1.6 %collective-permute-start.8 = (bf16[3,64,640]{2,1,0:T(8,128)(2,1)S(1)}, bf16[3,64,640]{2,1,0:T(8,128)(2,1)S(1)}, u32[]{:S(2)}, u32[]{:S(2)}) collective-permute-start(bf16[3,64,640]{2,1,0:T(8,128)(2,1)S(1)} %collective-permute-done.5.refs_3_), channel_id=1, source_target_pairs={{0,2},{8,9},{2,4},{10,8},{4,6},{12,10},{6,7},{14,12},{7,5},{15,14}... | collective-permute-start | bytes 737288 | tf_op jit(solution)/shard_map/ppermute | solution.py:39
  21.0 1.7 %shard_map.108 = (bf16[2,640,5120]{2,1,0:T(8,128)(2,1)}, bf16[2,128,5120]{2,1,0:T(8,128)(2,1)}, bf16[2,128,5120]{2,1,0:T(8,128)(2,1)}) custom-call(bf16[2,640,64]{2,1,0:T(8,128)(2,1)S(1)} %get-tuple-element.71.refs_0_, bf16[2,128,64]{2,1,0:T(8,128)(2,1)S(1)} %get-tuple-element.72.refs_1_, ...), custom_call_target="tpu_custom_call", output_to_operand_aliasing={{0}: (8, {}), {1}: (9, {}), {2}: (10, {})} | custom-call | flops 146800640 | bytes 4587520 | tf_op jit(solution)/shard_map/pallas_call | solution.py:183
  22.7 0.1 collective-permute-start.15
  22.8 1.6 %collective-permute-start.14 = (bf16[3,64,640]{2,1,0:T(8,128)(2,1)S(1)}, bf16[3,64,640]{2,1,0:T(8,128)(2,1)S(1)}, u32[]{:S(2)}, u32[]{:S(2)}) collective-permute-start(bf16[3,64,640]{2,1,0:T(8,128)(2,1)S(1)} %collective-permute-done.10.refs_3_), channel_id=1, source_target_pairs={{0,2},{8,9},{2,4},{10,8},{4,6},{12,10},{6,7},{14,12},{7,5},{15,14}... | collective-permute-start | bytes 737288 | tf_op jit(solution)/shard_map/ppermute | solution.py:39
  24.4 1.7 %shard_map.109 = (bf16[2,640,5120]{2,1,0:T(8,128)(2,1)}, bf16[2,128,5120]{2,1,0:T(8,128)(2,1)}, bf16[2,128,5120]{2,1,0:T(8,128)(2,1)}) custom-call(bf16[2,640,64]{2,1,0:T(8,128)(2,1)S(1)} %get-tuple-element.71.refs_0_, bf16[2,128,64]{2,1,0:T(8,128)(2,1)S(1)} %get-tuple-element.72.refs_1_, ...), custom_call_target="tpu_custom_call", output_to_operand_aliasing={{0}: (8, {}), {1}: (9, {}), {2}: (10, {})} | custom-call | flops 146800640 | bytes 4587520 | tf_op jit(solution)/shard_map/pallas_call | solution.py:183
  26.1 0.1 collective-permute-start.13
  26.2 1.0 %collective-permute-start.12 = (bf16[3,64,640]{2,1,0:T(8,128)(2,1)S(1)}, bf16[3,64,640]{2,1,0:T(8,128)(2,1)S(1)}, u32[]{:S(2)}, u32[]{:S(2)}) collective-permute-start(bf16[3,64,640]{2,1,0:T(8,128)(2,1)S(1)} %collective-permute-done.8.refs_3_), channel_id=1, source_target_pairs={{0,2},{8,9},{2,4},{10,8},{4,6},{12,10},{6,7},{14,12},{7,5},{15,14}... | collective-permute-start | bytes 737288 | tf_op jit(solution)/shard_map/ppermute | solution.py:39
  27.2 1.7 %shard_map.110 = (bf16[2,640,5120]{2,1,0:T(8,128)(2,1)}, bf16[2,128,5120]{2,1,0:T(8,128)(2,1)}, bf16[2,128,5120]{2,1,0:T(8,128)(2,1)}) custom-call(bf16[2,640,64]{2,1,0:T(8,128)(2,1)S(1)} %get-tuple-element.71.refs_0_, bf16[2,128,64]{2,1,0:T(8,128)(2,1)S(1)} %get-tuple-element.72.refs_1_, ...), custom_call_target="tpu_custom_call", output_to_operand_aliasing={{0}: (8, {}), {1}: (9, {}), {2}: (10, {})} | custom-call | flops 146800640 | bytes 4587520 | tf_op jit(solution)/shard_map/pallas_call | solution.py:183
  28.9 0.1 collective-permute-done.14.refs_3_
  29.1 1.7 %shard_map.111 = (bf16[2,640,5120]{2,1,0:T(8,128)(2,1)}, bf16[2,128,5120]{2,1,0:T(8,128)(2,1)}, bf16[2,128,5120]{2,1,0:T(8,128)(2,1)}) custom-call(bf16[2,640,64]{2,1,0:T(8,128)(2,1)S(1)} %get-tuple-element.71.refs_0_, bf16[2,128,64]{2,1,0:T(8,128)(2,1)S(1)} %get-tuple-element.72.refs_1_, ...), custom_call_target="tpu_custom_call", output_to_operand_aliasing={{0}: (8, {}), {1}: (9, {}), {2}: (10, {})} | custom-call | flops 146800640 | bytes 4587520 | tf_op jit(solution)/shard_map/pallas_call | solution.py:183
  30.8 1.7 %collective-permute-done.12.refs_3_ = bf16[3,64,640]{2,1,0:T(8,128)(2,1)S(1)} collective-permute-done((bf16[3,64,640]{2,1,0:T(8,128)(2,1)S(1)}, bf16[3,64,640]{2,1,0:T(8,128)(2,1)S(1)}, u32[]{:S(2)}, u32[]{:S(2)}) %collective-permute-start.12) | collective-permute-done | bytes 245792 | tf_op jit(solution)/shard_map/ppermute | solution.py:39
  32.4 1.7 %shard_map.112 = (bf16[2,640,5120]{2,1,0:T(8,128)(2,1)}, bf16[2,128,5120]{2,1,0:T(8,128)(2,1)}, bf16[2,128,5120]{2,1,0:T(8,128)(2,1)}) custom-call(bf16[2,640,64]{2,1,0:T(8,128)(2,1)S(1)} %get-tuple-element.71.refs_0_, bf16[2,128,64]{2,1,0:T(8,128)(2,1)S(1)} %get-tuple-element.72.refs_1_, ...), custom_call_target="tpu_custom_call", output_to_operand_aliasing={{0}: (8, {}), {1}: (9, {}), {2}: (10, {})} | custom-call | flops 146800640 | bytes 4587520 | tf_op jit(solution)/shard_map/pallas_call | solution.py:183
  34.1 1.7 %shard_map.113 = (bf16[2,640,5120]{2,1,0:T(8,128)(2,1)}, bf16[2,128,5120]{2,1,0:T(8,128)(2,1)}, bf16[2,128,5120]{2,1,0:T(8,128)(2,1)}) custom-call(bf16[2,640,64]{2,1,0:T(8,128)(2,1)S(1)} %get-tuple-element.71.refs_0_, bf16[2,128,64]{2,1,0:T(8,128)(2,1)S(1)} %get-tuple-element.72.refs_1_, ...), custom_call_target="tpu_custom_call", output_to_operand_aliasing={{0}: (8, {}), {1}: (9, {}), {2}: (10, {})} | custom-call | flops 146800640 | bytes 4587520 | tf_op jit(solution)/shard_map/pallas_call | solution.py:183
  (29 shorter events, 0.1 us)
Async XLA Ops:
  0.6 2.6 %collective-permute-start = (bf16[2,3,64,640]{3,2,1,0:T(8,128)(2,1)}, bf16[2,3,64,640]{3,2,1,0:T(8,128)(2,1)S(1)}, u32[]{:S(2)}, u32[]{:S(2)}) collective-permute-start(bf16[2,3,64,640]{3,2,1,0:T(8,128)(2,1)} %bitcast.10), channel_id=1, source_target_pairs={{0,8},{8,0},{1,9},{9,1},{2,10},{10,2},{3,11},{11,3},{4,12},{12,4},... | collective-permute-start | bytes 1474568 | tf_op jit(solution)/shard_map/ppermute | solution.py:43
  1.1 2.0 %collective-permute-start.1 = (bf16[2,64,640]{2,1,0:T(8,128)(2,1)}, bf16[2,64,640]{2,1,0:T(8,128)(2,1)S(1)}, u32[]{:S(2)}, u32[]{:S(2)}) collective-permute-start(bf16[2,64,640]{2,1,0:T(8,128)(2,1)} %bitcast.12), channel_id=1, source_target_pairs={{0,8},{8,0},{1,9},{9,1},{2,10},{10,2},{3,11},{11,3},{4,12},{12,4},... | collective-permute-start | bytes 491528 | tf_op jit(solution)/shard_map/ppermute | solution.py:43
  1.2 1.9 %collective-permute-start.2 = (bf16[2,64,128]{2,1,0:T(8,128)(2,1)}, bf16[2,64,128]{2,1,0:T(8,128)(2,1)S(1)}, u32[]{:S(2)}, u32[]{:S(2)}) collective-permute-start(bf16[2,64,128]{2,1,0:T(8,128)(2,1)} %bitcast.14), channel_id=1, source_target_pairs={{0,8},{8,0},{1,9},{9,1},{2,10},{10,2},{3,11},{11,3},{4,12},{12,4},... | collective-permute-start | bytes 98312 | tf_op jit(solution)/shard_map/ppermute | solution.py:43
  1.7 1.5 %copy-start.3 = (bf16[1,2,3,64,640]{4,3,2,1,0:T(8,128)(2,1)S(1)}, bf16[1,2,3,64,640]{4,3,2,1,0:T(8,128)(2,1)}, u32[]{:S(2)}) copy-start(bf16[1,2,3,64,640]{4,3,2,1,0:T(8,128)(2,1)} %param.12) | copy-start | bytes 1474564
  1.7 7.0 %copy-start.4 = (bf16[1,2,640,64]{2,3,1,0:T(8,128)(2,1)S(1)}, bf16[1,2,640,64]{2,3,1,0:T(8,128)(2,1)}, u32[]{:S(2)}) copy-start(bf16[1,2,640,64]{2,3,1,0:T(8,128)(2,1)} %param.13) | copy-start | bytes 491524
  1.7 7.0 %copy-start.5 = (bf16[1,2,128,64]{2,3,1,0:T(8,128)(2,1)S(1)}, bf16[1,2,128,64]{2,3,1,0:T(8,128)(2,1)}, u32[]{:S(2)}) copy-start(bf16[1,2,128,64]{2,3,1,0:T(8,128)(2,1)} %param.14) | copy-start | bytes 98308
  1.7 7.0 %copy-start.6 = (bf16[1,2,128,64]{2,3,1,0:T(8,128)(2,1)S(1)}, bf16[1,2,128,64]{2,3,1,0:T(8,128)(2,1)}, u32[]{:S(2)}) copy-start(bf16[1,2,128,64]{2,3,1,0:T(8,128)(2,1)} %param.15) | copy-start | bytes 98308
  1.7 1.5 %collective-permute-start.3 = (bf16[2,64,128]{2,1,0:T(8,128)(2,1)}, bf16[2,64,128]{2,1,0:T(8,128)(2,1)S(1)}, u32[]{:S(2)}, u32[]{:S(2)}) collective-permute-start(bf16[2,64,128]{2,1,0:T(8,128)(2,1)} %bitcast.16), channel_id=1, source_target_pairs={{0,8},{8,0},{1,9},{9,1},{2,10},{10,2},{3,11},{11,3},{4,12},{12,4},... | collective-permute-start | bytes 98312 | tf_op jit(solution)/shard_map/ppermute | solution.py:43
  1.8 14.5 %copy-start.2 = (bf16[2,128,5120]{2,1,0:T(8,128)(2,1)S(1)}, bf16[2,128,5120]{2,1,0:T(8,128)(2,1)}, u32[]{:S(2)}) copy-start(bf16[2,128,5120]{2,1,0:T(8,128)(2,1)} %refs_7_.13) | copy-start | bytes 7864324
  4.0 9.1 %collective-permute-start.4 = (bf16[3,64,640]{2,1,0:T(8,128)(2,1)S(1)}, bf16[3,64,640]{2,1,0:T(8,128)(2,1)S(1)}, u32[]{:S(2)}, u32[]{:S(2)}) collective-permute-start(bf16[3,64,640]{2,1,0:T(8,128)(2,1)S(1)} %get-tuple-element.75.refs_3_), channel_id=1, source_target_pairs={{0,2},{8,9},{2,4},{10,8},{4,6},{12,10},{6,7},{14,12},{7,5},{15,14}... | collective-permute-start | bytes 737288 | tf_op jit(solution)/shard_map/ppermute | solution.py:39
  7.0 7.8 %collective-permute-start.7 = (bf16[3,64,640]{2,1,0:T(8,128)(2,1)S(1)}, bf16[3,64,640]{2,1,0:T(8,128)(2,1)S(1)}, u32[]{:S(2)}, u32[]{:S(2)}) collective-permute-start(bf16[3,64,640]{2,1,0:T(8,128)(2,1)S(1)} %get-tuple-element.76.refs_4_), channel_id=1, source_target_pairs={{0,2},{8,9},{2,4},{10,8},{4,6},{12,10},{6,7},{14,12},{7,5},{15,14}... | collective-permute-start | bytes 737288 | tf_op jit(solution)/shard_map/ppermute | solution.py:39
  8.6 7.7 %copy-start = (bf16[2,640,5120]{2,1,0:T(8,128)(2,1)S(1)}, bf16[2,640,5120]{2,1,0:T(8,128)(2,1)}, u32[]{:S(2)}) copy-start(bf16[2,640,5120]{2,1,0:T(8,128)(2,1)} %refs_5_.13) | copy-start | bytes 39321604
  11.4 5.0 %copy-start.1 = (bf16[2,128,5120]{2,1,0:T(8,128)(2,1)S(1)}, bf16[2,128,5120]{2,1,0:T(8,128)(2,1)}, u32[]{:S(2)}) copy-start(bf16[2,128,5120]{2,1,0:T(8,128)(2,1)} %refs_6_.15) | copy-start | bytes 7864324
  13.1 3.2 %collective-permute-start.6 = (bf16[3,64,640]{2,1,0:T(8,128)(2,1)S(1)}, bf16[3,64,640]{2,1,0:T(8,128)(2,1)S(1)}, u32[]{:S(2)}, u32[]{:S(2)}) collective-permute-start(bf16[3,64,640]{2,1,0:T(8,128)(2,1)S(1)} %collective-permute-done.4.refs_3_), channel_id=1, source_target_pairs={{0,8},{8,0},{1,9},{9,1},{2,10},{10,2},{3,11},{11,3},{4,12},{12,4},... | collective-permute-start | bytes 737288 | tf_op jit(solution)/shard_map/ppermute | solution.py:43
  13.2 6.2 %collective-permute-start.5 = (bf16[3,64,640]{2,1,0:T(8,128)(2,1)S(1)}, bf16[3,64,640]{2,1,0:T(8,128)(2,1)S(1)}, u32[]{:S(2)}, u32[]{:S(2)}) collective-permute-start(bf16[3,64,640]{2,1,0:T(8,128)(2,1)S(1)} %collective-permute-done.4.refs_3_), channel_id=1, source_target_pairs={{0,2},{8,9},{2,4},{10,8},{4,6},{12,10},{6,7},{14,12},{7,5},{15,14}... | collective-permute-start | bytes 737288 | tf_op jit(solution)/shard_map/ppermute | solution.py:39
  14.8 6.2 %collective-permute-start.11 = (bf16[3,64,640]{2,1,0:T(8,128)(2,1)S(1)}, bf16[3,64,640]{2,1,0:T(8,128)(2,1)S(1)}, u32[]{:S(2)}, u32[]{:S(2)}) collective-permute-start(bf16[3,64,640]{2,1,0:T(8,128)(2,1)S(1)} %collective-permute-done.7.refs_3_), channel_id=1, source_target_pairs={{0,8},{8,0},{1,9},{9,1},{2,10},{10,2},{3,11},{11,3},{4,12},{12,4},... | collective-permute-start | bytes 737288 | tf_op jit(solution)/shard_map/ppermute | solution.py:43
  14.8 7.9 %collective-permute-start.10 = (bf16[3,64,640]{2,1,0:T(8,128)(2,1)S(1)}, bf16[3,64,640]{2,1,0:T(8,128)(2,1)S(1)}, u32[]{:S(2)}, u32[]{:S(2)}) collective-permute-start(bf16[3,64,640]{2,1,0:T(8,128)(2,1)S(1)} %collective-permute-done.7.refs_3_), channel_id=1, source_target_pairs={{0,2},{8,9},{2,4},{10,8},{4,6},{12,10},{6,7},{14,12},{7,5},{15,14}... | collective-permute-start | bytes 737288 | tf_op jit(solution)/shard_map/ppermute | solution.py:39
  19.4 5.0 %collective-permute-start.9 = (bf16[3,64,640]{2,1,0:T(8,128)(2,1)S(1)}, bf16[3,64,640]{2,1,0:T(8,128)(2,1)S(1)}, u32[]{:S(2)}, u32[]{:S(2)}) collective-permute-start(bf16[3,64,640]{2,1,0:T(8,128)(2,1)S(1)} %collective-permute-done.5.refs_3_), channel_id=1, source_target_pairs={{0,8},{8,0},{1,9},{9,1},{2,10},{10,2},{3,11},{11,3},{4,12},{12,4},... | collective-permute-start | bytes 737288 | tf_op jit(solution)/shard_map/ppermute | solution.py:43
  19.4 6.7 %collective-permute-start.8 = (bf16[3,64,640]{2,1,0:T(8,128)(2,1)S(1)}, bf16[3,64,640]{2,1,0:T(8,128)(2,1)S(1)}, u32[]{:S(2)}, u32[]{:S(2)}) collective-permute-start(bf16[3,64,640]{2,1,0:T(8,128)(2,1)S(1)} %collective-permute-done.5.refs_3_), channel_id=1, source_target_pairs={{0,2},{8,9},{2,4},{10,8},{4,6},{12,10},{6,7},{14,12},{7,5},{15,14}... | collective-permute-start | bytes 737288 | tf_op jit(solution)/shard_map/ppermute | solution.py:39
  22.7 4.5 %collective-permute-start.15 = (bf16[3,64,640]{2,1,0:T(8,128)(2,1)S(1)}, bf16[3,64,640]{2,1,0:T(8,128)(2,1)S(1)}, u32[]{:S(2)}, u32[]{:S(2)}) collective-permute-start(bf16[3,64,640]{2,1,0:T(8,128)(2,1)S(1)} %collective-permute-done.10.refs_3_), channel_id=1, source_target_pairs={{0,8},{8,0},{1,9},{9,1},{2,10},{10,2},{3,11},{11,3},{4,12},{12,4},... | collective-permute-start | bytes 737288 | tf_op jit(solution)/shard_map/ppermute | solution.py:43
  22.8 6.2 %collective-permute-start.14 = (bf16[3,64,640]{2,1,0:T(8,128)(2,1)S(1)}, bf16[3,64,640]{2,1,0:T(8,128)(2,1)S(1)}, u32[]{:S(2)}, u32[]{:S(2)}) collective-permute-start(bf16[3,64,640]{2,1,0:T(8,128)(2,1)S(1)} %collective-permute-done.10.refs_3_), channel_id=1, source_target_pairs={{0,2},{8,9},{2,4},{10,8},{4,6},{12,10},{6,7},{14,12},{7,5},{15,14}... | collective-permute-start | bytes 737288 | tf_op jit(solution)/shard_map/ppermute | solution.py:39
  26.1 3.0 %collective-permute-start.13 = (bf16[3,64,640]{2,1,0:T(8,128)(2,1)S(1)}, bf16[3,64,640]{2,1,0:T(8,128)(2,1)S(1)}, u32[]{:S(2)}, u32[]{:S(2)}) collective-permute-start(bf16[3,64,640]{2,1,0:T(8,128)(2,1)S(1)} %collective-permute-done.8.refs_3_), channel_id=1, source_target_pairs={{0,8},{8,0},{1,9},{9,1},{2,10},{10,2},{3,11},{11,3},{4,12},{12,4},... | collective-permute-start | bytes 737288 | tf_op jit(solution)/shard_map/ppermute | solution.py:43
  26.2 6.2 %collective-permute-start.12 = (bf16[3,64,640]{2,1,0:T(8,128)(2,1)S(1)}, bf16[3,64,640]{2,1,0:T(8,128)(2,1)S(1)}, u32[]{:S(2)}, u32[]{:S(2)}) collective-permute-start(bf16[3,64,640]{2,1,0:T(8,128)(2,1)S(1)} %collective-permute-done.8.refs_3_), channel_id=1, source_target_pairs={{0,2},{8,9},{2,4},{10,8},{4,6},{12,10},{6,7},{14,12},{7,5},{15,14}... | collective-permute-start | bytes 737288 | tf_op jit(solution)/shard_map/ppermute | solution.py:39
  29.1 3.4 %collective-permute-start.17 = (bf16[3,64,640]{2,1,0:T(8,128)(2,1)S(1)}, bf16[3,64,640]{2,1,0:T(8,128)(2,1)S(1)}, u32[]{:S(2)}, u32[]{:S(2)}) collective-permute-start(bf16[3,64,640]{2,1,0:T(8,128)(2,1)S(1)} %collective-permute-done.14.refs_3_), channel_id=1, source_target_pairs={{0,8},{8,0},{1,9},{9,1},{2,10},{10,2},{3,11},{11,3},{4,12},{12,4},... | collective-permute-start | bytes 737288 | tf_op jit(solution)/shard_map/ppermute | solution.py:43
  32.4 1.7 %collective-permute-start.16 = (bf16[3,64,640]{2,1,0:T(8,128)(2,1)S(1)}, bf16[3,64,640]{2,1,0:T(8,128)(2,1)S(1)}, u32[]{:S(2)}, u32[]{:S(2)}) collective-permute-start(bf16[3,64,640]{2,1,0:T(8,128)(2,1)S(1)} %collective-permute-done.12.refs_3_), channel_id=1, source_target_pairs={{0,8},{8,0},{1,9},{9,1},{2,10},{10,2},{3,11},{11,3},{4,12},{12,4},... | collective-permute-start | bytes 737288 | tf_op jit(solution)/shard_map/ppermute | solution.py:43

commit v8 on v6

--- a/solution.py
+++ b/solution.py
@@ -12,7 +12,6 @@
 MIB = 1024 * 1024
 TILE_ROWS = 128
 TILE_COLS = 256
-SMEM = pl.BlockSpec(memory_space=pltpu.SMEM)
 VMEM = pl.BlockSpec(memory_space=pltpu.VMEM)
 HBM = pl.BlockSpec(memory_space=pltpu.HBM)
 ANY = pl.BlockSpec(memory_space=pl.ANY)
@@ -60,11 +59,15 @@
     return blocks
 
 
+def owned(owners, layer, proj, core, shape):
+    return jnp.broadcast_to(owners[pl.ds(layer, 1), proj : proj + 1] == core, shape)
+
+
 def choose_a_kernel(owners, own, other, first, second):
     core = lax.axis_index("rollout")
     for out, layer in ((first, core), (second, 1 - core)):
         for proj in range(own.shape[1]):
-            mine = owners[layer, proj] == core
+            mine = owned(owners, layer, proj, core, out.shape[1:])
             out[proj] = jnp.where(mine, own[layer, proj], other[layer, proj])
 
 
@@ -72,11 +75,11 @@
     piece = jax.ShapeDtypeStruct(own.shape[1:], own.dtype)
     return pl.pallas_call(
         choose_a_kernel,
-        in_specs=[SMEM, VMEM, VMEM],
+        in_specs=[VMEM, VMEM, VMEM],
         out_specs=[VMEM, VMEM],
         out_shape=[piece, piece],
         compiler_params=pltpu.CompilerParams(vmem_limit_bytes=4 * MIB),
-    )(in_hbm(owners), in_vmem(own), other)
+    )(in_vmem(owners), in_vmem(own), other)
 
 
 def start_fetches(n, pieces, bases, blocks, sems):
@@ -120,34 +123,37 @@
 
 def choose_b_kernel(n, pieces, owners, *refs):
     core = lax.axis_index("rollout")
-    own, other, base, outs, block, sems = refs[0:3], refs[3:6], refs[6], refs[7:10], refs[10], refs[11]
-    fetches = start_fetches(n, pieces, [base], [block], sems)
+    own, other, refs, sems = refs[0:3], refs[3:6], refs[6:-1], refs[-1]
+    count = (len(refs) - 3) // 2
+    bases, outs, blocks = refs[:count], refs[count : count + 3], refs[count + 3 :]
+    fetches = start_fetches(n, pieces, bases, blocks, sems)
     for proj in range(3):
         for layer in range(own[proj].shape[0]):
-            mine = owners[layer, proj] == core
+            mine = owned(owners, layer, proj, core, own[proj].shape[1:])
             outs[proj][layer] = jnp.where(mine, own[proj][layer], other[proj][layer]).T
     for fetch in fetches:
         fetch.wait()
 
 
-def choose_b(n, cols, owners, own, other, base, pieces):
+def choose_b(n, cols, owners, own, other, bases, pieces):
     chosen = [jax.ShapeDtypeStruct((x.shape[0], x.shape[2], x.shape[1]), x.dtype) for x in own]
-    blocks = block_shapes([base], pieces, cols)
+    blocks = block_shapes(bases, pieces, cols)
     out = pl.pallas_call(
         functools.partial(choose_b_kernel, n, pieces),
-        in_specs=[SMEM] + [VMEM] * 6 + [HBM],
-        out_specs=[VMEM] * 4,
+        in_specs=[VMEM] * 7 + [HBM] * len(bases),
+        out_specs=[VMEM] * (3 + len(blocks)),
         out_shape=chosen + blocks,
-        scratch_shapes=[pltpu.SemaphoreType.DMA((len(pieces),))],
+        scratch_shapes=[pltpu.SemaphoreType.DMA((len(bases) * len(pieces),))],
         compiler_params=pltpu.CompilerParams(vmem_limit_bytes=4 * MIB),
         cost_estimate=moved(blocks),
-    )(in_hbm(owners), *[in_vmem(x) for x in own], *other, in_hbm(base))
-    return out[:3], out[3]
+    )(in_vmem(owners), *[in_vmem(x) for x in own], *other, *[in_hbm(base) for base in bases])
+    return out[:3], out[3:]
 
 
 def merge_kernel(n, pieces, scale, fresh, *refs):
-    b_refs, a_refs, bases = refs[0:3], refs[3:5], refs[5:8]
-    at = 8 if fresh else 11
+    count = len(pieces)
+    b_refs, a_refs, bases = refs[0:3], refs[3 : 3 + count], refs[3 + count : 6 + count]
+    at = 6 + count + (0 if fresh else 3)
     outs, bufs, sem = refs[at : at + 3], refs[at + 3 : at + 6], refs[at + 6]
     cols = a_refs[0].shape[-1]
     stores = []
@@ -221,34 +227,37 @@
         shapes = [jax.ShapeDtypeStruct(base.shape, base.dtype) for base in bases]
         swapped = (swap_cores(own_a), [swap_cores(x) for x in own_b])
         pieces = [(0, True, True), (0, True, False)]
-        small_blocks = fetch_blocks(n, cols, bases[1:], pieces)
-        (other_a, other_b), small_blocks = tie((swapped, small_blocks))
+        key_block = fetch_blocks(n, cols, [base_key], pieces)
+        (other_a, other_b), key_block = tie((swapped, key_block))
         first, second = choose_a(owners, own_a, other_a)
         held = [first, second]
         first = ring_pass(first, n)
         second = ring_pass(second, n)
-        b, block = choose_b(n, cols, owners, own_b, other_b, base_query, pieces)
-        outs = merge(n, scale, b, held, [block, *small_blocks], shapes, None, pieces)
-        first, _ = tie((first, outs))
+        b, blocks = choose_b(n, cols, owners, own_b, other_b, [base_query, base_value], pieces)
+        outs = merge(n, scale, b, held, [blocks[0], key_block[0], blocks[1]], shapes, None, pieces)
+        first, outs = tie((first, outs))
 
         def go(pieces, chunks, outs):
             return merge(n, scale, b, chunks, bases, shapes, outs, pieces)
 
-        def later(array, *others):
-            return tie((array, others))[0]
-
-        others = None
+        waiting = None
         for step in range(1, last):
-            onward = ring_pass(first, n)
             if step > 1:
-                outs = go([(step - 1, False, False), (step - 1, False, True)], others, outs)
-            onward_second = ring_pass(later(second, outs), n) if step < last - 1 else None
-            others = [swap_cores(later(first, second)), swap_cores(second)]
-            outs = go([(step, True, True), (step, True, False)], [first, second], outs)
-            first, second = later(onward, outs), onward_second
-        outs = go([(last - 1, False, False), (last - 1, False, True)], others, outs)
-        first = later(first, outs)
-        return tuple(go([(last, True, True), (last, False, False)], [first, swap_cores(first)], outs))
+                outs = go(*waiting, outs)
+            pieces = [(step, True, True), (step, False, False)]
+            chunks = [first, swap_cores(first)]
+            first = ring_pass(first, n)
+            second, outs = tie((second, outs))
+            waiting = [(step, True, False), (step, False, True)], [second, swap_cores(second)]
+            if step == last - 1:
+                pieces, chunks = pieces + waiting[0][:1], chunks + waiting[1][:1]
+            outs = go(pieces, chunks, outs)
+            first, outs = tie((first, outs))
+            if step < last - 1:
+                second = ring_pass(second, n)
+        swapped = swap_cores(first)
+        outs = go([waiting[0][1], (last, True, True)], [waiting[1][1], first], outs)
+        return tuple(go([(last, False, False)], [swapped], outs))
 
     core = lax.axis_index("rollout")
     tensor = lax.axis_index("tensor")

time: 38 us -> 34 us (0.89)
  Pallas kernels: 18.4 us -> 16.5 us
  waiting for transfers between devices: 3.95 us -> 2.11 us
  starting transfers between devices: 14.6 us -> 13.7 us
  local copies, waits for them, and re-layouts: 0.03 us -> 0.67 us
    pallas_call x2, Pallas kernels: 3.5 us -> 1.97 us  [the longest x1 1.81 us: choose_b(): pl.pallas_call(functools.partial(choose_b_kernel, n, pieces), in_specs=[V...]
    ppermute x11, starting transfers between devices: 2.79 us -> 1.33 us  [swap_cores(): return lax.ppermute(array, 'rollout', [(0, 1), (1, 0)])]
    ppermute x11, waiting for transfers between devices: 1.52 us -> 0.44 us  [swap_cores(): return lax.ppermute(array, 'rollout', [(0, 1), (1, 0)])]
    ppermute x7, waiting for transfers between devices: 2.43 us -> 1.67 us  [ring_pass(): return lax.ppermute(array, ('rollout', 'tensor'), pairs)]
    unnamed x14 -> x16, local copies, waits for them, and re-layouts: 0.03 us -> 0.67 us
    ppermute x7, starting transfers between devices: 11.8 us -> 12.4 us  [ring_pass(): return lax.ppermute(array, ('rollout', 'tensor'), pairs)]
  transfers between devices with their start and end apart: 18 -> 18, of which waited for: 3 -> 4; matrix products, arithmetic and copies ran while one was open for 0% -> 0% of each run, Pallas kernels for 38% -> 45%
where the time goes in v8:
time: 34 us; the launch traced here: 33.8 us
  Pallas kernels  16.5 us (49%)
  starting transfers between devices  13.7 us (40%)
  waiting for transfers between devices  2.11 us (6%)
  between operations  0.86 us (3%)
  local copies, waits for them, and re-layouts  0.67 us (2%)
    pallas_call x8, Pallas kernels, merge(): pl.pallas_call(functools.partial(merge_kernel, n, pieces, scale, fresh),...  13.5 us
    ppermute x7, starting transfers between devices, ring_pass(): return lax.ppermute(array, ('rollout', 'tensor'), pairs)  12.4 us
    pallas_call x1, Pallas kernels, choose_b(): pl.pallas_call(functools.partial(choose_b_kernel, n, pieces), in_specs=[V...  1.81 us
    ppermute x7, waiting for transfers between devices, ring_pass(): return lax.ppermute(array, ('rollout', 'tensor'), pairs)  1.67 us
    ppermute x11, starting transfers between devices, swap_cores(): return lax.ppermute(array, 'rollout', [(0, 1), (1, 0)])  1.33 us
    pallas_call x1, Pallas kernels, fetch_blocks(): pl.pallas_call(functools.partial(fetch_kernel, n, pieces), in_specs=[HBM]...  1.01 us
  transfers between devices with their start and end apart: 18, of which 4 were waited for; matrix products, arithmetic and copies ran while one was open for 0% of the time, Pallas kernels for 45%

profile of v8, /device:TPU:0, one launch (start us, length us, event | category | flops | bytes accessed | tf_op | source)
XLA Modules:
  0.0 33.8 jit_solution(185460103819019508)
XLA Ops:
  0.7 0.5 %collective-permute-start = (bf16[2,3,64,640]{3,2,1,0:T(8,128)(2,1)}, bf16[2,3,64,640]{3,2,1,0:T(8,128)(2,1)S(1)}, u32[]{:S(2)}, u32[]{:S(2)}) collective-permute-start(bf16[2,3,64,640]{3,2,1,0:T(8,128)(2,1)} %bitcast.10), channel_id=1, source_target_pairs={{0,8},{8,0},{1,9},{9,1},{2,10},{10,2},{3,11},{11,3},{4,12},{12,4},... | collective-permute-start | bytes 1474568 | tf_op jit(solution)/shard_map/ppermute | solution.py:42
  1.2 0.1 collective-permute-start.1
  1.3 0.4 %collective-permute-start.2 = (bf16[2,64,128]{2,1,0:T(8,128)(2,1)}, bf16[2,64,128]{2,1,0:T(8,128)(2,1)S(1)}, u32[]{:S(2)}, u32[]{:S(2)}) collective-permute-start(bf16[2,64,128]{2,1,0:T(8,128)(2,1)} %bitcast.14), channel_id=1, source_target_pairs={{0,8},{8,0},{1,9},{9,1},{2,10},{10,2},{3,11},{11,3},{4,12},{12,4},... | collective-permute-start | bytes 98312 | tf_op jit(solution)/shard_map/ppermute | solution.py:42
  1.7 0.1 collective-permute-start.3
  1.8 1.0 %shard_map.103.refs_6_ = bf16[2,128,640]{2,1,0:T(8,128)(2,1)S(1)} custom-call(bf16[2,128,5120]{2,1,0:T(8,128)(2,1)} %refs_5_.11), custom_call_target="tpu_custom_call" | custom-call | bytes 655360 | tf_op jit(solution)/shard_map/pallas_call | solution.py:113
  2.8 0.4 %collective-permute-done.2.refs_4_ = bf16[2,64,128]{2,1,0:T(8,128)(2,1)S(1)} collective-permute-done((bf16[2,64,128]{2,1,0:T(8,128)(2,1)}, bf16[2,64,128]{2,1,0:T(8,128)(2,1)S(1)}, u32[]{:S(2)}, u32[]{:S(2)}) %collective-permute-start.2) | collective-permute-done | bytes 32800 | tf_op jit(solution)/shard_map/ppermute | solution.py:42
  3.2 0.0 collective-permute-done.3.refs_5_
  3.2 0.2 shard_map.105
  3.4 3.0 %collective-permute-start.4 = (bf16[3,64,640]{2,1,0:T(8,128)(2,1)S(1)}, bf16[3,64,640]{2,1,0:T(8,128)(2,1)S(1)}, u32[]{:S(2)}, u32[]{:S(2)}) collective-permute-start(bf16[3,64,640]{2,1,0:T(8,128)(2,1)S(1)} %get-tuple-element.71.refs_3_), channel_id=1, source_target_pairs={{0,2},{8,9},{2,4},{10,8},{4,6},{12,10},{6,7},{14,12},{7,5},{15,14}... | collective-permute-start | bytes 737288 | tf_op jit(solution)/shard_map/ppermute | solution.py:38
  6.4 1.6 %collective-permute-start.7 = (bf16[3,64,640]{2,1,0:T(8,128)(2,1)S(1)}, bf16[3,64,640]{2,1,0:T(8,128)(2,1)S(1)}, u32[]{:S(2)}, u32[]{:S(2)}) collective-permute-start(bf16[3,64,640]{2,1,0:T(8,128)(2,1)S(1)} %get-tuple-element.72.refs_4_), channel_id=1, source_target_pairs={{0,2},{8,9},{2,4},{10,8},{4,6},{12,10},{6,7},{14,12},{7,5},{15,14}... | collective-permute-start | bytes 737288 | tf_op jit(solution)/shard_map/ppermute | solution.py:38
  8.0 0.0 copy-start.2
  8.0 1.8 %shard_map.104 = (bf16[2,640,64]{2,1,0:T(8,128)(2,1)S(1)}, bf16[2,128,64]{2,1,0:T(8,128)(2,1)S(1)}, bf16[2,128,64]{2,1,0:T(8,128)(2,1)S(1)}, bf16[2,640,640]{2,1,0:T(8,128)(2,1)S(1)}, bf16[2,128,640]{2,1,0:T(8,128)(2,1)S(1)}) custom-call(s32[2,3]{1,0:T(2,128)S(1)} %copy-done.7, bf16[2,64,640]{2,1,0:T(8,128)(2,1)S(1)} %bitcast.13, ...), custom_call_target="tpu_custom_call" | custom-call | bytes 3932160 | tf_op jit(solution)/shard_map/pallas_call | solution.py:141
  9.9 1.7 %shard_map.106 = (bf16[2,640,5120]{2,1,0:T(8,128)(2,1)}, bf16[2,128,5120]{2,1,0:T(8,128)(2,1)}, bf16[2,128,5120]{2,1,0:T(8,128)(2,1)}) custom-call(bf16[2,640,64]{2,1,0:T(8,128)(2,1)S(1)} %get-tuple-element.67.refs_0_, bf16[2,128,64]{2,1,0:T(8,128)(2,1)S(1)} %get-tuple-element.68.refs_1_, bf16[2,128,64]{2,1,0:T(8,128)(2,1)S(1)} %get-tuple-element.69.refs_2_, ...), custom_call_target="tpu_custom_call" | custom-call | flops 146800640 | bytes 4587520 | tf_op jit(solution)/shard_map/pallas_call | solution.py:189
  11.6 0.1 collective-permute-start.6
  11.6 1.6 %collective-permute-start.5 = (bf16[3,64,640]{2,1,0:T(8,128)(2,1)S(1)}, bf16[3,64,640]{2,1,0:T(8,128)(2,1)S(1)}, u32[]{:S(2)}, u32[]{:S(2)}) collective-permute-start(bf16[3,64,640]{2,1,0:T(8,128)(2,1)S(1)} %collective-permute-done.4.refs_3_), channel_id=1, source_target_pairs={{0,2},{8,9},{2,4},{10,8},{4,6},{12,10},{6,7},{14,12},{7,5},{15,14}... | collective-permute-start | bytes 737288 | tf_op jit(solution)/shard_map/ppermute | solution.py:38
  13.3 2.0 %collective-permute-start.10 = (bf16[3,64,640]{2,1,0:T(8,128)(2,1)S(1)}, bf16[3,64,640]{2,1,0:T(8,128)(2,1)S(1)}, u32[]{:S(2)}, u32[]{:S(2)}) collective-permute-start(bf16[3,64,640]{2,1,0:T(8,128)(2,1)S(1)} %collective-permute-done.7.refs_3_), channel_id=1, source_target_pairs={{0,2},{8,9},{2,4},{10,8},{4,6},{12,10},{6,7},{14,12},{7,5},{15,14}... | collective-permute-start | bytes 737288 | tf_op jit(solution)/shard_map/ppermute | solution.py:38
  15.3 0.6 %copy-done.1 = bf16[2,128,5120]{2,1,0:T(8,128)(2,1)S(1)} copy-done((bf16[2,128,5120]{2,1,0:T(8,128)(2,1)S(1)}, bf16[2,128,5120]{2,1,0:T(8,128)(2,1)}, u32[]{:S(2)}) %copy-start.1) | copy-done | bytes 2621464
  15.9 1.7 %shard_map.107 = (bf16[2,640,5120]{2,1,0:T(8,128)(2,1)}, bf16[2,128,5120]{2,1,0:T(8,128)(2,1)}, bf16[2,128,5120]{2,1,0:T(8,128)(2,1)}) custom-call(bf16[2,640,64]{2,1,0:T(8,128)(2,1)S(1)} %get-tuple-element.67.refs_0_, bf16[2,128,64]{2,1,0:T(8,128)(2,1)S(1)} %get-tuple-element.68.refs_1_, ...), custom_call_target="tpu_custom_call", output_to_operand_aliasing={{0}: (8, {}), {1}: (9, {}), {2}: (10, {})} | custom-call | flops 146800640 | bytes 4587520 | tf_op jit(solution)/shard_map/pallas_call | solution.py:189
  17.6 0.3 collective-permute-done.5.refs_3_
  17.9 1.6 %collective-permute-start.8 = (bf16[3,64,640]{2,1,0:T(8,128)(2,1)S(1)}, bf16[3,64,640]{2,1,0:T(8,128)(2,1)S(1)}, u32[]{:S(2)}, u32[]{:S(2)}) collective-permute-start(bf16[3,64,640]{2,1,0:T(8,128)(2,1)S(1)} %collective-permute-done.5.refs_3_), channel_id=1, source_target_pairs={{0,2},{8,9},{2,4},{10,8},{4,6},{12,10},{6,7},{14,12},{7,5},{15,14}... | collective-permute-start | bytes 737288 | tf_op jit(solution)/shard_map/ppermute | solution.py:38
  19.5 1.7 %shard_map.108 = (bf16[2,640,5120]{2,1,0:T(8,128)(2,1)}, bf16[2,128,5120]{2,1,0:T(8,128)(2,1)}, bf16[2,128,5120]{2,1,0:T(8,128)(2,1)}) custom-call(bf16[2,640,64]{2,1,0:T(8,128)(2,1)S(1)} %get-tuple-element.67.refs_0_, bf16[2,128,64]{2,1,0:T(8,128)(2,1)S(1)} %get-tuple-element.68.refs_1_, ...), custom_call_target="tpu_custom_call", output_to_operand_aliasing={{0}: (8, {}), {1}: (9, {}), {2}: (10, {})} | custom-call | flops 146800640 | bytes 4587520 | tf_op jit(solution)/shard_map/pallas_call | solution.py:189
  21.2 0.1 collective-permute-start.15
  21.3 1.6 %collective-permute-start.14 = (bf16[3,64,640]{2,1,0:T(8,128)(2,1)S(1)}, bf16[3,64,640]{2,1,0:T(8,128)(2,1)S(1)}, u32[]{:S(2)}, u32[]{:S(2)}) collective-permute-start(bf16[3,64,640]{2,1,0:T(8,128)(2,1)S(1)} %collective-permute-done.10.refs_3_), channel_id=1, source_target_pairs={{0,2},{8,9},{2,4},{10,8},{4,6},{12,10},{6,7},{14,12},{7,5},{15,14}... | collective-permute-start | bytes 737288 | tf_op jit(solution)/shard_map/ppermute | solution.py:38
  22.8 1.7 %shard_map.109 = (bf16[2,640,5120]{2,1,0:T(8,128)(2,1)}, bf16[2,128,5120]{2,1,0:T(8,128)(2,1)}, bf16[2,128,5120]{2,1,0:T(8,128)(2,1)}) custom-call(bf16[2,640,64]{2,1,0:T(8,128)(2,1)S(1)} %get-tuple-element.67.refs_0_, bf16[2,128,64]{2,1,0:T(8,128)(2,1)S(1)} %get-tuple-element.68.refs_1_, ...), custom_call_target="tpu_custom_call", output_to_operand_aliasing={{0}: (8, {}), {1}: (9, {}), {2}: (10, {})} | custom-call | flops 146800640 | bytes 4587520 | tf_op jit(solution)/shard_map/pallas_call | solution.py:189
  24.5 0.1 collective-permute-start.13
  24.6 1.0 %collective-permute-start.12 = (bf16[3,64,640]{2,1,0:T(8,128)(2,1)S(1)}, bf16[3,64,640]{2,1,0:T(8,128)(2,1)S(1)}, u32[]{:S(2)}, u32[]{:S(2)}) collective-permute-start(bf16[3,64,640]{2,1,0:T(8,128)(2,1)S(1)} %collective-permute-done.8.refs_3_), channel_id=1, source_target_pairs={{0,2},{8,9},{2,4},{10,8},{4,6},{12,10},{6,7},{14,12},{7,5},{15,14}... | collective-permute-start | bytes 737288 | tf_op jit(solution)/shard_map/ppermute | solution.py:38
  25.7 1.7 %shard_map.110 = (bf16[2,640,5120]{2,1,0:T(8,128)(2,1)}, bf16[2,128,5120]{2,1,0:T(8,128)(2,1)}, bf16[2,128,5120]{2,1,0:T(8,128)(2,1)}) custom-call(bf16[2,640,64]{2,1,0:T(8,128)(2,1)S(1)} %get-tuple-element.67.refs_0_, bf16[2,128,64]{2,1,0:T(8,128)(2,1)S(1)} %get-tuple-element.68.refs_1_, ...), custom_call_target="tpu_custom_call", output_to_operand_aliasing={{0}: (8, {}), {1}: (9, {}), {2}: (10, {})} | custom-call | flops 146800640 | bytes 4587520 | tf_op jit(solution)/shard_map/pallas_call | solution.py:189
  27.4 0.1 collective-permute-done.14.refs_5_
  27.5 2.1 %shard_map.111 = (bf16[2,640,5120]{2,1,0:T(8,128)(2,1)}, bf16[2,128,5120]{2,1,0:T(8,128)(2,1)}, bf16[2,128,5120]{2,1,0:T(8,128)(2,1)}) custom-call(bf16[2,640,64]{2,1,0:T(8,128)(2,1)S(1)} %get-tuple-element.67.refs_0_, bf16[2,128,64]{2,1,0:T(8,128)(2,1)S(1)} %get-tuple-element.68.refs_1_, ...), custom_call_target="tpu_custom_call", output_to_operand_aliasing={{0}: (9, {}), {1}: (10, {}), {2}: (11, {})} | custom-call | flops 220200960 | bytes 6881280 | tf_op jit(solution)/shard_map/pallas_call | solution.py:189
  29.6 1.2 %collective-permute-done.12.refs_4_ = bf16[3,64,640]{2,1,0:T(8,128)(2,1)S(1)} collective-permute-done((bf16[3,64,640]{2,1,0:T(8,128)(2,1)S(1)}, bf16[3,64,640]{2,1,0:T(8,128)(2,1)S(1)}, u32[]{:S(2)}, u32[]{:S(2)}) %collective-permute-start.12) | collective-permute-done | bytes 245792 | tf_op jit(solution)/shard_map/ppermute | solution.py:38
  30.9 1.7 %shard_map.112 = (bf16[2,640,5120]{2,1,0:T(8,128)(2,1)}, bf16[2,128,5120]{2,1,0:T(8,128)(2,1)}, bf16[2,128,5120]{2,1,0:T(8,128)(2,1)}) custom-call(bf16[2,640,64]{2,1,0:T(8,128)(2,1)S(1)} %get-tuple-element.67.refs_0_, bf16[2,128,64]{2,1,0:T(8,128)(2,1)S(1)} %get-tuple-element.68.refs_1_, ...), custom_call_target="tpu_custom_call", output_to_operand_aliasing={{0}: (8, {}), {1}: (9, {}), {2}: (10, {})} | custom-call | flops 146800640 | bytes 4587520 | tf_op jit(solution)/shard_map/pallas_call | solution.py:189
  32.6 1.2 %shard_map.113 = (bf16[2,640,5120]{2,1,0:T(8,128)(2,1)}, bf16[2,128,5120]{2,1,0:T(8,128)(2,1)}, bf16[2,128,5120]{2,1,0:T(8,128)(2,1)}) custom-call(bf16[2,640,64]{2,1,0:T(8,128)(2,1)S(1)} %get-tuple-element.67.refs_0_, bf16[2,128,64]{2,1,0:T(8,128)(2,1)S(1)} %get-tuple-element.68.refs_1_, ...), custom_call_target="tpu_custom_call", output_to_operand_aliasing={{0}: (7, {}), {1}: (8, {}), {2}: (9, {})} | custom-call | flops 73400320 | bytes 2293760 | tf_op jit(solution)/shard_map/pallas_call | solution.py:189
  (31 shorter events, 0.1 us)
Async XLA Ops:
  0.6 2.6 %copy-start.3 = (bf16[1,2,3,64,640]{4,3,2,1,0:T(8,128)(2,1)S(1)}, bf16[1,2,3,64,640]{4,3,2,1,0:T(8,128)(2,1)}, u32[]{:S(2)}) copy-start(bf16[1,2,3,64,640]{4,3,2,1,0:T(8,128)(2,1)} %param.12) | copy-start | bytes 1474564
  0.6 7.4 %copy-start.4 = (bf16[1,2,640,64]{2,3,1,0:T(8,128)(2,1)S(1)}, bf16[1,2,640,64]{2,3,1,0:T(8,128)(2,1)}, u32[]{:S(2)}) copy-start(bf16[1,2,640,64]{2,3,1,0:T(8,128)(2,1)} %param.13) | copy-start | bytes 491524
  0.7 7.3 %copy-start.5 = (bf16[1,2,128,64]{2,3,1,0:T(8,128)(2,1)S(1)}, bf16[1,2,128,64]{2,3,1,0:T(8,128)(2,1)}, u32[]{:S(2)}) copy-start(bf16[1,2,128,64]{2,3,1,0:T(8,128)(2,1)} %param.14) | copy-start | bytes 98308
  0.7 7.3 %copy-start.6 = (bf16[1,2,128,64]{2,3,1,0:T(8,128)(2,1)S(1)}, bf16[1,2,128,64]{2,3,1,0:T(8,128)(2,1)}, u32[]{:S(2)}) copy-start(bf16[1,2,128,64]{2,3,1,0:T(8,128)(2,1)} %param.15) | copy-start | bytes 98308
  0.7 2.6 %copy-start.7 = (s32[2,3]{1,0:T(2,128)S(1)}, s32[2,3]{1,0:T(2,128)}, u32[]{:S(2)}) copy-start(s32[2,3]{1,0:T(2,128)} %owners.3) | copy-start | bytes 76
  0.7 2.6 %collective-permute-start = (bf16[2,3,64,640]{3,2,1,0:T(8,128)(2,1)}, bf16[2,3,64,640]{3,2,1,0:T(8,128)(2,1)S(1)}, u32[]{:S(2)}, u32[]{:S(2)}) collective-permute-start(bf16[2,3,64,640]{3,2,1,0:T(8,128)(2,1)} %bitcast.10), channel_id=1, source_target_pairs={{0,8},{8,0},{1,9},{9,1},{2,10},{10,2},{3,11},{11,3},{4,12},{12,4},... | collective-permute-start | bytes 1474568 | tf_op jit(solution)/shard_map/ppermute | solution.py:42
  1.2 2.0 %collective-permute-start.1 = (bf16[2,64,640]{2,1,0:T(8,128)(2,1)}, bf16[2,64,640]{2,1,0:T(8,128)(2,1)S(1)}, u32[]{:S(2)}, u32[]{:S(2)}) collective-permute-start(bf16[2,64,640]{2,1,0:T(8,128)(2,1)} %bitcast.12), channel_id=1, source_target_pairs={{0,8},{8,0},{1,9},{9,1},{2,10},{10,2},{3,11},{11,3},{4,12},{12,4},... | collective-permute-start | bytes 491528 | tf_op jit(solution)/shard_map/ppermute | solution.py:42
  1.3 1.9 %collective-permute-start.2 = (bf16[2,64,128]{2,1,0:T(8,128)(2,1)}, bf16[2,64,128]{2,1,0:T(8,128)(2,1)S(1)}, u32[]{:S(2)}, u32[]{:S(2)}) collective-permute-start(bf16[2,64,128]{2,1,0:T(8,128)(2,1)} %bitcast.14), channel_id=1, source_target_pairs={{0,8},{8,0},{1,9},{9,1},{2,10},{10,2},{3,11},{11,3},{4,12},{12,4},... | collective-permute-start | bytes 98312 | tf_op jit(solution)/shard_map/ppermute | solution.py:42
  1.7 1.5 %collective-permute-start.3 = (bf16[2,64,128]{2,1,0:T(8,128)(2,1)}, bf16[2,64,128]{2,1,0:T(8,128)(2,1)S(1)}, u32[]{:S(2)}, u32[]{:S(2)}) collective-permute-start(bf16[2,64,128]{2,1,0:T(8,128)(2,1)} %bitcast.16), channel_id=1, source_target_pairs={{0,8},{8,0},{1,9},{9,1},{2,10},{10,2},{3,11},{11,3},{4,12},{12,4},... | collective-permute-start | bytes 98312 | tf_op jit(solution)/shard_map/ppermute | solution.py:42
  3.4 8.1 %collective-permute-start.4 = (bf16[3,64,640]{2,1,0:T(8,128)(2,1)S(1)}, bf16[3,64,640]{2,1,0:T(8,128)(2,1)S(1)}, u32[]{:S(2)}, u32[]{:S(2)}) collective-permute-start(bf16[3,64,640]{2,1,0:T(8,128)(2,1)S(1)} %get-tuple-element.71.refs_3_), channel_id=1, source_target_pairs={{0,2},{8,9},{2,4},{10,8},{4,6},{12,10},{6,7},{14,12},{7,5},{15,14}... | collective-permute-start | bytes 737288 | tf_op jit(solution)/shard_map/ppermute | solution.py:38
  6.4 6.9 %collective-permute-start.7 = (bf16[3,64,640]{2,1,0:T(8,128)(2,1)S(1)}, bf16[3,64,640]{2,1,0:T(8,128)(2,1)S(1)}, u32[]{:S(2)}, u32[]{:S(2)}) collective-permute-start(bf16[3,64,640]{2,1,0:T(8,128)(2,1)S(1)} %get-tuple-element.72.refs_4_), channel_id=1, source_target_pairs={{0,2},{8,9},{2,4},{10,8},{4,6},{12,10},{6,7},{14,12},{7,5},{15,14}... | collective-permute-start | bytes 737288 | tf_op jit(solution)/shard_map/ppermute | solution.py:38
  8.0 7.3 %copy-start = (bf16[2,640,5120]{2,1,0:T(8,128)(2,1)S(1)}, bf16[2,640,5120]{2,1,0:T(8,128)(2,1)}, u32[]{:S(2)}) copy-start(bf16[2,640,5120]{2,1,0:T(8,128)(2,1)} %refs_4_.1) | copy-start | bytes 39321604
  8.0 7.2 %copy-start.2 = (bf16[2,128,5120]{2,1,0:T(8,128)(2,1)S(1)}, bf16[2,128,5120]{2,1,0:T(8,128)(2,1)}, u32[]{:S(2)}) copy-start(bf16[2,128,5120]{2,1,0:T(8,128)(2,1)} %refs_5_.11) | copy-start | bytes 7864324
  9.8 6.1 %copy-start.1 = (bf16[2,128,5120]{2,1,0:T(8,128)(2,1)S(1)}, bf16[2,128,5120]{2,1,0:T(8,128)(2,1)}, u32[]{:S(2)}) copy-start(bf16[2,128,5120]{2,1,0:T(8,128)(2,1)} %refs_6_.15) | copy-start | bytes 7864324
  11.6 3.7 %collective-permute-start.6 = (bf16[3,64,640]{2,1,0:T(8,128)(2,1)S(1)}, bf16[3,64,640]{2,1,0:T(8,128)(2,1)S(1)}, u32[]{:S(2)}, u32[]{:S(2)}) collective-permute-start(bf16[3,64,640]{2,1,0:T(8,128)(2,1)S(1)} %collective-permute-done.4.refs_3_), channel_id=1, source_target_pairs={{0,8},{8,0},{1,9},{9,1},{2,10},{10,2},{3,11},{11,3},{4,12},{12,4},... | collective-permute-start | bytes 737288 | tf_op jit(solution)/shard_map/ppermute | solution.py:42
  11.6 6.2 %collective-permute-start.5 = (bf16[3,64,640]{2,1,0:T(8,128)(2,1)S(1)}, bf16[3,64,640]{2,1,0:T(8,128)(2,1)S(1)}, u32[]{:S(2)}, u32[]{:S(2)}) collective-permute-start(bf16[3,64,640]{2,1,0:T(8,128)(2,1)S(1)} %collective-permute-done.4.refs_3_), channel_id=1, source_target_pairs={{0,2},{8,9},{2,4},{10,8},{4,6},{12,10},{6,7},{14,12},{7,5},{15,14}... | collective-permute-start | bytes 737288 | tf_op jit(solution)/shard_map/ppermute | solution.py:38
  13.3 6.2 %collective-permute-start.11 = (bf16[3,64,640]{2,1,0:T(8,128)(2,1)S(1)}, bf16[3,64,640]{2,1,0:T(8,128)(2,1)S(1)}, u32[]{:S(2)}, u32[]{:S(2)}) collective-permute-start(bf16[3,64,640]{2,1,0:T(8,128)(2,1)S(1)} %collective-permute-done.7.refs_3_), channel_id=1, source_target_pairs={{0,8},{8,0},{1,9},{9,1},{2,10},{10,2},{3,11},{11,3},{4,12},{12,4},... | collective-permute-start | bytes 737288 | tf_op jit(solution)/shard_map/ppermute | solution.py:42
  13.3 7.9 %collective-permute-start.10 = (bf16[3,64,640]{2,1,0:T(8,128)(2,1)S(1)}, bf16[3,64,640]{2,1,0:T(8,128)(2,1)S(1)}, u32[]{:S(2)}, u32[]{:S(2)}) collective-permute-start(bf16[3,64,640]{2,1,0:T(8,128)(2,1)S(1)} %collective-permute-done.7.refs_3_), channel_id=1, source_target_pairs={{0,2},{8,9},{2,4},{10,8},{4,6},{12,10},{6,7},{14,12},{7,5},{15,14}... | collective-permute-start | bytes 737288 | tf_op jit(solution)/shard_map/ppermute | solution.py:38
  17.9 4.9 %collective-permute-start.9 = (bf16[3,64,640]{2,1,0:T(8,128)(2,1)S(1)}, bf16[3,64,640]{2,1,0:T(8,128)(2,1)S(1)}, u32[]{:S(2)}, u32[]{:S(2)}) collective-permute-start(bf16[3,64,640]{2,1,0:T(8,128)(2,1)S(1)} %collective-permute-done.5.refs_3_), channel_id=1, source_target_pairs={{0,8},{8,0},{1,9},{9,1},{2,10},{10,2},{3,11},{11,3},{4,12},{12,4},... | collective-permute-start | bytes 737288 | tf_op jit(solution)/shard_map/ppermute | solution.py:42
  17.9 6.6 %collective-permute-start.8 = (bf16[3,64,640]{2,1,0:T(8,128)(2,1)S(1)}, bf16[3,64,640]{2,1,0:T(8,128)(2,1)S(1)}, u32[]{:S(2)}, u32[]{:S(2)}) collective-permute-start(bf16[3,64,640]{2,1,0:T(8,128)(2,1)S(1)} %collective-permute-done.5.refs_3_), channel_id=1, source_target_pairs={{0,2},{8,9},{2,4},{10,8},{4,6},{12,10},{6,7},{14,12},{7,5},{15,14}... | collective-permute-start | bytes 737288 | tf_op jit(solution)/shard_map/ppermute | solution.py:38
  21.2 4.5 %collective-permute-start.15 = (bf16[3,64,640]{2,1,0:T(8,128)(2,1)S(1)}, bf16[3,64,640]{2,1,0:T(8,128)(2,1)S(1)}, u32[]{:S(2)}, u32[]{:S(2)}) collective-permute-start(bf16[3,64,640]{2,1,0:T(8,128)(2,1)S(1)} %collective-permute-done.10.refs_3_), channel_id=1, source_target_pairs={{0,8},{8,0},{1,9},{9,1},{2,10},{10,2},{3,11},{11,3},{4,12},{12,4},... | collective-permute-start | bytes 737288 | tf_op jit(solution)/shard_map/ppermute | solution.py:42
  21.3 6.2 %collective-permute-start.14 = (bf16[3,64,640]{2,1,0:T(8,128)(2,1)S(1)}, bf16[3,64,640]{2,1,0:T(8,128)(2,1)S(1)}, u32[]{:S(2)}, u32[]{:S(2)}) collective-permute-start(bf16[3,64,640]{2,1,0:T(8,128)(2,1)S(1)} %collective-permute-done.10.refs_3_), channel_id=1, source_target_pairs={{0,2},{8,9},{2,4},{10,8},{4,6},{12,10},{6,7},{14,12},{7,5},{15,14}... | collective-permute-start | bytes 737288 | tf_op jit(solution)/shard_map/ppermute | solution.py:38
  24.5 3.0 %collective-permute-start.13 = (bf16[3,64,640]{2,1,0:T(8,128)(2,1)S(1)}, bf16[3,64,640]{2,1,0:T(8,128)(2,1)S(1)}, u32[]{:S(2)}, u32[]{:S(2)}) collective-permute-start(bf16[3,64,640]{2,1,0:T(8,128)(2,1)S(1)} %collective-permute-done.8.refs_3_), channel_id=1, source_target_pairs={{0,8},{8,0},{1,9},{9,1},{2,10},{10,2},{3,11},{11,3},{4,12},{12,4},... | collective-permute-start | bytes 737288 | tf_op jit(solution)/shard_map/ppermute | solution.py:42
  24.6 6.2 %collective-permute-start.12 = (bf16[3,64,640]{2,1,0:T(8,128)(2,1)S(1)}, bf16[3,64,640]{2,1,0:T(8,128)(2,1)S(1)}, u32[]{:S(2)}, u32[]{:S(2)}) collective-permute-start(bf16[3,64,640]{2,1,0:T(8,128)(2,1)S(1)} %collective-permute-done.8.refs_3_), channel_id=1, source_target_pairs={{0,2},{8,9},{2,4},{10,8},{4,6},{12,10},{6,7},{14,12},{7,5},{15,14}... | collective-permute-start | bytes 737288 | tf_op jit(solution)/shard_map/ppermute | solution.py:38
  27.5 3.4 %collective-permute-start.17 = (bf16[3,64,640]{2,1,0:T(8,128)(2,1)S(1)}, bf16[3,64,640]{2,1,0:T(8,128)(2,1)S(1)}, u32[]{:S(2)}, u32[]{:S(2)}) collective-permute-start(bf16[3,64,640]{2,1,0:T(8,128)(2,1)S(1)} %collective-permute-done.14.refs_5_), channel_id=1, source_target_pairs={{0,8},{8,0},{1,9},{9,1},{2,10},{10,2},{3,11},{11,3},{4,12},{12,4},... | collective-permute-start | bytes 737288 | tf_op jit(solution)/shard_map/ppermute | solution.py:42
  30.9 1.7 %collective-permute-start.16 = (bf16[3,64,640]{2,1,0:T(8,128)(2,1)S(1)}, bf16[3,64,640]{2,1,0:T(8,128)(2,1)S(1)}, u32[]{:S(2)}, u32[]{:S(2)}) collective-permute-start(bf16[3,64,640]{2,1,0:T(8,128)(2,1)S(1)} %collective-permute-done.12.refs_4_), channel_id=1, source_target_pairs={{0,8},{8,0},{1,9},{9,1},{2,10},{10,2},{3,11},{11,3},{4,12},{12,4},... | collective-permute-start | bytes 737288 | tf_op jit(solution)/shard_map/ppermute | solution.py:42

commit v9 on v8

--- a/solution.py
+++ b/solution.py
@@ -29,12 +29,12 @@
     return list(range(0, n, 2)) + list(range(n - 1, 0, -2))
 
 
-def ring_pass(array, n):
+def ring_pass(array, n, places=1):
     order = ring_order(n)
     pairs = []
     for k in range(n):
-        pairs.append((order[k], order[(k + 1) % n]))
-        pairs.append((n + order[k], n + order[(k - 1) % n]))
+        pairs.append((order[k], order[(k + places) % n]))
+        pairs.append((n + order[k], n + order[(k - places) % n]))
     return lax.ppermute(array, ("rollout", "tensor"), pairs)
 
 
@@ -222,7 +222,7 @@
     own_a = left_shared_matrix[0]
     own_b = [jnp.swapaxes(right[0], 1, 2) for right in rights]
 
-    if cols % LANES == 0:
+    if cols % LANES == 0 and n == 8:
         tie = lax.optimization_barrier
         shapes = [jax.ShapeDtypeStruct(base.shape, base.dtype) for base in bases]
         swapped = (swap_cores(own_a), [swap_cores(x) for x in own_b])
@@ -230,34 +230,40 @@
         key_block = fetch_blocks(n, cols, [base_key], pieces)
         (other_a, other_b), key_block = tie((swapped, key_block))
         first, second = choose_a(owners, own_a, other_a)
-        held = [first, second]
-        first = ring_pass(first, n)
-        second = ring_pass(second, n)
+        a1 = ring_pass(first, n)
+        b1 = ring_pass(second, n)
         b, blocks = choose_b(n, cols, owners, own_b, other_b, [base_query, base_value], pieces)
-        outs = merge(n, scale, b, held, [blocks[0], key_block[0], blocks[1]], shapes, None, pieces)
-        first, outs = tie((first, outs))
-
-        def go(pieces, chunks, outs):
-            return merge(n, scale, b, chunks, bases, shapes, outs, pieces)
-
-        waiting = None
-        for step in range(1, last):
-            if step > 1:
-                outs = go(*waiting, outs)
-            pieces = [(step, True, True), (step, False, False)]
-            chunks = [first, swap_cores(first)]
-            first = ring_pass(first, n)
-            second, outs = tie((second, outs))
-            waiting = [(step, True, False), (step, False, True)], [second, swap_cores(second)]
-            if step == last - 1:
-                pieces, chunks = pieces + waiting[0][:1], chunks + waiting[1][:1]
-            outs = go(pieces, chunks, outs)
-            first, outs = tie((first, outs))
-            if step < last - 1:
-                second = ring_pass(second, n)
-        swapped = swap_cores(first)
-        outs = go([waiting[0][1], (last, True, True)], [waiting[1][1], first], outs)
-        return tuple(go([(last, False, False)], [swapped], outs))
+        own_blocks = [blocks[0], key_block[0], blocks[1]]
+        outs = merge(n, scale, b, [first, second], own_blocks, shapes, None, pieces)
+
+        def go(outs, **chunks):
+            pieces = []
+            for name in chunks:
+                swapped = name.startswith("x")
+                pieces.append((int(name[-1]), not swapped, (name[-2] == "a") != swapped))
+            return merge(n, scale, b, list(chunks.values()), bases, shapes, outs, pieces)
+
+        a1, outs = tie((a1, outs))
+        a2, a3, xa1 = ring_pass(a1, n), ring_pass(a1, n, 2), swap_cores(a1)
+        b1, outs = tie((b1, outs))
+        b2, xb1 = ring_pass(b1, n), swap_cores(b1)
+        outs = go(outs, a1=a1, xa1=xa1)
+        a2, outs = tie((a2, outs))
+        xa2 = swap_cores(a2)
+        outs = go(outs, b1=b1, xb1=xb1)
+        a3, outs = tie((a3, outs))
+        a4, xa3 = ring_pass(a3, n), swap_cores(a3)
+        b2, outs = tie((b2, outs))
+        b3, xb2 = ring_pass(b2, n), swap_cores(b2)
+        outs = go(outs, a2=a2, xa2=xa2)
+        outs = go(outs, b2=b2, xb2=xb2)
+        a4, outs = tie((a4, outs))
+        xa4 = swap_cores(a4)
+        outs = go(outs, a3=a3, xa3=xa3)
+        b3, outs = tie((b3, outs))
+        xb3 = swap_cores(b3)
+        outs = go(outs, a4=a4, xa4=xa4, b3=b3)
+        return tuple(go(outs, xb3=xb3))
 
     core = lax.axis_index("rollout")
     tensor = lax.axis_index("tensor")

time: 34 us -> 38.5 us (1.13)
  starting transfers between devices: 13.7 us -> 17 us
  waiting for transfers between devices: 2.11 us -> 3.97 us
  local copies, waits for them, and re-layouts: 0.67 us -> 0.04 us
    ppermute x7, starting transfers between devices: 12.4 us -> 14.5 us  [ring_pass(): return lax.ppermute(array, ('rollout', 'tensor'), pairs)]
    ppermute x7, waiting for transfers between devices: 1.67 us -> 3.53 us  [ring_pass(): return lax.ppermute(array, ('rollout', 'tensor'), pairs)]
    ppermute x11, starting transfers between devices: 1.33 us -> 2.45 us  [swap_cores(): return lax.ppermute(array, 'rollout', [(0, 1), (1, 0)])]
    unnamed x16, local copies, waits for them, and re-layouts: 0.67 us -> 0.04 us
  transfers between devices with their start and end apart: 18 -> 18, of which waited for: 4 -> 3; matrix products, arithmetic and copies ran while one was open for 0% -> 0% of each run, Pallas kernels for 45% -> 39%
where the time goes in v9:
time: 38.5 us; the launch traced here: 38.4 us
  starting transfers between devices  17 us (44%)
  Pallas kernels  16.5 us (43%)
  waiting for transfers between devices  3.97 us (10%)
  between operations  0.9 us (2%)
    ppermute x7, starting transfers between devices, ring_pass(): return lax.ppermute(array, ('rollout', 'tensor'), pairs)  14.5 us
    pallas_call x8, Pallas kernels, merge(): pl.pallas_call(functools.partial(merge_kernel, n, pieces, scale, fresh),...  13.5 us
    ppermute x7, waiting for transfers between devices, ring_pass(): return lax.ppermute(array, ('rollout', 'tensor'), pairs)  3.53 us
    ppermute x11, starting transfers between devices, swap_cores(): return lax.ppermute(array, 'rollout', [(0, 1), (1, 0)])  2.45 us
    pallas_call x1, Pallas kernels, choose_b(): pl.pallas_call(functools.partial(choose_b_kernel, n, pieces), in_specs=[V...  1.81 us
    pallas_call x1, Pallas kernels, fetch_blocks(): pl.pallas_call(functools.partial(fetch_kernel, n, pieces), in_specs=[HBM]...  1.01 us
  transfers between devices with their start and end apart: 18, of which 3 were waited for; matrix products, arithmetic and copies ran while one was open for 0% of the time, Pallas kernels for 39%

profile of v9, /device:TPU:0, one launch (start us, length us, event | category | flops | bytes accessed | tf_op | source)
XLA Modules:
  0.0 38.4 jit_solution(6240218970509153087)
XLA Ops:
  0.7 0.5 %collective-permute-start = (bf16[2,3,64,640]{3,2,1,0:T(8,128)(2,1)}, bf16[2,3,64,640]{3,2,1,0:T(8,128)(2,1)S(1)}, u32[]{:S(2)}, u32[]{:S(2)}) collective-permute-start(bf16[2,3,64,640]{3,2,1,0:T(8,128)(2,1)} %bitcast.10), channel_id=1, source_target_pairs={{0,8},{8,0},{1,9},{9,1},{2,10},{10,2},{3,11},{11,3},{4,12},{12,4},... | collective-permute-start | bytes 1474568 | tf_op jit(solution)/shard_map/ppermute | solution.py:42
  1.2 0.1 collective-permute-start.1
  1.3 0.4 %collective-permute-start.2 = (bf16[2,64,128]{2,1,0:T(8,128)(2,1)}, bf16[2,64,128]{2,1,0:T(8,128)(2,1)S(1)}, u32[]{:S(2)}, u32[]{:S(2)}) collective-permute-start(bf16[2,64,128]{2,1,0:T(8,128)(2,1)} %bitcast.14), channel_id=1, source_target_pairs={{0,8},{8,0},{1,9},{9,1},{2,10},{10,2},{3,11},{11,3},{4,12},{12,4},... | collective-permute-start | bytes 98312 | tf_op jit(solution)/shard_map/ppermute | solution.py:42
  1.7 0.1 collective-permute-start.3
  1.8 1.0 %shard_map.103.refs_6_ = bf16[2,128,640]{2,1,0:T(8,128)(2,1)S(1)} custom-call(bf16[2,128,5120]{2,1,0:T(8,128)(2,1)} %refs_5_.11), custom_call_target="tpu_custom_call" | custom-call | bytes 655360 | tf_op jit(solution)/shard_map/pallas_call | solution.py:113
  2.8 0.4 collective-permute-done.2.refs_4_
  3.2 0.0 collective-permute-done.3.refs_5_
  3.2 0.2 shard_map.105
  3.4 3.0 %collective-permute-start.5 = (bf16[3,64,640]{2,1,0:T(8,128)(2,1)S(1)}, bf16[3,64,640]{2,1,0:T(8,128)(2,1)S(1)}, u32[]{:S(2)}, u32[]{:S(2)}) collective-permute-start(bf16[3,64,640]{2,1,0:T(8,128)(2,1)S(1)} %get-tuple-element.72.refs_3_), channel_id=1, source_target_pairs={{0,2},{8,9},{2,4},{10,8},{4,6},{12,10},{6,7},{14,12},{7,5},{15,14}... | collective-permute-start | bytes 737288 | tf_op jit(solution)/shard_map/ppermute | solution.py:38
  6.4 1.6 %collective-permute-start.4 = (bf16[3,64,640]{2,1,0:T(8,128)(2,1)S(1)}, bf16[3,64,640]{2,1,0:T(8,128)(2,1)S(1)}, u32[]{:S(2)}, u32[]{:S(2)}) collective-permute-start(bf16[3,64,640]{2,1,0:T(8,128)(2,1)S(1)} %get-tuple-element.71.refs_4_), channel_id=1, source_target_pairs={{0,2},{8,9},{2,4},{10,8},{4,6},{12,10},{6,7},{14,12},{7,5},{15,14}... | collective-permute-start | bytes 737288 | tf_op jit(solution)/shard_map/ppermute | solution.py:38
  8.0 1.8 %shard_map.104 = (bf16[2,640,64]{2,1,0:T(8,128)(2,1)S(1)}, bf16[2,128,64]{2,1,0:T(8,128)(2,1)S(1)}, bf16[2,128,64]{2,1,0:T(8,128)(2,1)S(1)}, bf16[2,640,640]{2,1,0:T(8,128)(2,1)S(1)}, bf16[2,128,640]{2,1,0:T(8,128)(2,1)S(1)}) custom-call(s32[2,3]{1,0:T(2,128)S(1)} %copy-done.7, bf16[2,64,640]{2,1,0:T(8,128)(2,1)S(1)} %bitcast.13, ...), custom_call_target="tpu_custom_call" | custom-call | bytes 3932160 | tf_op jit(solution)/shard_map/pallas_call | solution.py:141
  9.8 0.0 copy-start.1
  9.9 1.7 %shard_map.106 = (bf16[2,640,5120]{2,1,0:T(8,128)(2,1)}, bf16[2,128,5120]{2,1,0:T(8,128)(2,1)}, bf16[2,128,5120]{2,1,0:T(8,128)(2,1)}) custom-call(bf16[2,640,64]{2,1,0:T(8,128)(2,1)S(1)} %get-tuple-element.67.refs_0_, bf16[2,128,64]{2,1,0:T(8,128)(2,1)S(1)} %get-tuple-element.68.refs_1_, bf16[2,128,64]{2,1,0:T(8,128)(2,1)S(1)} %get-tuple-element.69.refs_2_, ...), custom_call_target="tpu_custom_call" | custom-call | flops 146800640 | bytes 4587520 | tf_op jit(solution)/shard_map/pallas_call | solution.py:189
  11.6 0.1 collective-permute-start.10
  11.6 1.6 %collective-permute-start.9 = (bf16[3,64,640]{2,1,0:T(8,128)(2,1)S(1)}, bf16[3,64,640]{2,1,0:T(8,128)(2,1)S(1)}, u32[]{:S(2)}, u32[]{:S(2)}) collective-permute-start(bf16[3,64,640]{2,1,0:T(8,128)(2,1)S(1)} %collective-permute-done.5.refs_3_), channel_id=1, source_target_pairs={{0,2},{8,9},{2,4},{10,8},{4,6},{12,10},{6,7},{14,12},{7,5},{15,14}... | collective-permute-start | bytes 737288 | tf_op jit(solution)/shard_map/ppermute | solution.py:38
  13.3 3.0 %collective-permute-start.7 = (bf16[3,64,640]{2,1,0:T(8,128)(2,1)S(1)}, bf16[3,64,640]{2,1,0:T(8,128)(2,1)S(1)}, u32[]{:S(2)}, u32[]{:S(2)}) collective-permute-start(bf16[3,64,640]{2,1,0:T(8,128)(2,1)S(1)} %collective-permute-done.5.refs_3_), channel_id=1, source_target_pairs={{0,4},{8,11},{2,6},{10,9},{4,7},{12,8},{6,5},{14,10},{7,3},{15,12}... | collective-permute-start | bytes 737288 | tf_op jit(solution)/shard_map/ppermute | solution.py:38
  16.3 1.6 %collective-permute-start.6 = (bf16[3,64,640]{2,1,0:T(8,128)(2,1)S(1)}, bf16[3,64,640]{2,1,0:T(8,128)(2,1)S(1)}, u32[]{:S(2)}, u32[]{:S(2)}) collective-permute-start(bf16[3,64,640]{2,1,0:T(8,128)(2,1)S(1)} %collective-permute-done.4.refs_3_), channel_id=1, source_target_pairs={{0,2},{8,9},{2,4},{10,8},{4,6},{12,10},{6,7},{14,12},{7,5},{15,14}... | collective-permute-start | bytes 737288 | tf_op jit(solution)/shard_map/ppermute | solution.py:38
  17.9 1.7 %shard_map.107 = (bf16[2,640,5120]{2,1,0:T(8,128)(2,1)}, bf16[2,128,5120]{2,1,0:T(8,128)(2,1)}, bf16[2,128,5120]{2,1,0:T(8,128)(2,1)}) custom-call(bf16[2,640,64]{2,1,0:T(8,128)(2,1)S(1)} %get-tuple-element.67.refs_0_, bf16[2,128,64]{2,1,0:T(8,128)(2,1)S(1)} %get-tuple-element.68.refs_1_, ...), custom_call_target="tpu_custom_call", output_to_operand_aliasing={{0}: (8, {}), {1}: (9, {}), {2}: (10, {})} | custom-call | flops 146800640 | bytes 4587520 | tf_op jit(solution)/shard_map/pallas_call | solution.py:189
  19.6 0.1 collective-permute-start.15
  19.7 1.7 %shard_map.108 = (bf16[2,640,5120]{2,1,0:T(8,128)(2,1)}, bf16[2,128,5120]{2,1,0:T(8,128)(2,1)}, bf16[2,128,5120]{2,1,0:T(8,128)(2,1)}) custom-call(bf16[2,640,64]{2,1,0:T(8,128)(2,1)S(1)} %get-tuple-element.67.refs_0_, bf16[2,128,64]{2,1,0:T(8,128)(2,1)S(1)} %get-tuple-element.68.refs_1_, ...), custom_call_target="tpu_custom_call", output_to_operand_aliasing={{0}: (8, {}), {1}: (9, {}), {2}: (10, {})} | custom-call | flops 146800640 | bytes 4587520 | tf_op jit(solution)/shard_map/pallas_call | solution.py:189
  21.4 2.4 %collective-permute-done.7.refs_3_ = bf16[3,64,640]{2,1,0:T(8,128)(2,1)S(1)} collective-permute-done((bf16[3,64,640]{2,1,0:T(8,128)(2,1)S(1)}, bf16[3,64,640]{2,1,0:T(8,128)(2,1)S(1)}, u32[]{:S(2)}, u32[]{:S(2)}) %collective-permute-start.7) | collective-permute-done | bytes 245792 | tf_op jit(solution)/shard_map/ppermute | solution.py:38
  23.7 1.1 %collective-permute-done.6.refs_3_ = bf16[3,64,640]{2,1,0:T(8,128)(2,1)S(1)} collective-permute-done((bf16[3,64,640]{2,1,0:T(8,128)(2,1)S(1)}, bf16[3,64,640]{2,1,0:T(8,128)(2,1)S(1)}, u32[]{:S(2)}, u32[]{:S(2)}) %collective-permute-start.6) | collective-permute-done | bytes 245792 | tf_op jit(solution)/shard_map/ppermute | solution.py:38
  24.9 0.6 %collective-permute-start.14 = (bf16[3,64,640]{2,1,0:T(8,128)(2,1)S(1)}, bf16[3,64,640]{2,1,0:T(8,128)(2,1)S(1)}, u32[]{:S(2)}, u32[]{:S(2)}) collective-permute-start(bf16[3,64,640]{2,1,0:T(8,128)(2,1)S(1)} %collective-permute-done.6.refs_3_), channel_id=1, source_target_pairs={{0,8},{8,0},{1,9},{9,1},{2,10},{10,2},{3,11},{11,3},{4,12},{12,4},... | collective-permute-start | bytes 737288 | tf_op jit(solution)/shard_map/ppermute | solution.py:42
  25.5 1.9 %collective-permute-start.13 = (bf16[3,64,640]{2,1,0:T(8,128)(2,1)S(1)}, bf16[3,64,640]{2,1,0:T(8,128)(2,1)S(1)}, u32[]{:S(2)}, u32[]{:S(2)}) collective-permute-start(bf16[3,64,640]{2,1,0:T(8,128)(2,1)S(1)} %collective-permute-done.7.refs_3_), channel_id=1, source_target_pairs={{0,2},{8,9},{2,4},{10,8},{4,6},{12,10},{6,7},{14,12},{7,5},{15,14}... | collective-permute-start | bytes 737288 | tf_op jit(solution)/shard_map/ppermute | solution.py:38
  27.4 1.8 %collective-permute-start.11 = (bf16[3,64,640]{2,1,0:T(8,128)(2,1)S(1)}, bf16[3,64,640]{2,1,0:T(8,128)(2,1)S(1)}, u32[]{:S(2)}, u32[]{:S(2)}) collective-permute-start(bf16[3,64,640]{2,1,0:T(8,128)(2,1)S(1)} %collective-permute-done.6.refs_3_), channel_id=1, source_target_pairs={{0,2},{8,9},{2,4},{10,8},{4,6},{12,10},{6,7},{14,12},{7,5},{15,14}... | collective-permute-start | bytes 737288 | tf_op jit(solution)/shard_map/ppermute | solution.py:38
  29.2 1.7 %shard_map.109 = (bf16[2,640,5120]{2,1,0:T(8,128)(2,1)}, bf16[2,128,5120]{2,1,0:T(8,128)(2,1)}, bf16[2,128,5120]{2,1,0:T(8,128)(2,1)}) custom-call(bf16[2,640,64]{2,1,0:T(8,128)(2,1)S(1)} %get-tuple-element.67.refs_0_, bf16[2,128,64]{2,1,0:T(8,128)(2,1)S(1)} %get-tuple-element.68.refs_1_, ...), custom_call_target="tpu_custom_call", output_to_operand_aliasing={{0}: (8, {}), {1}: (9, {}), {2}: (10, {})} | custom-call | flops 146800640 | bytes 4587520 | tf_op jit(solution)/shard_map/pallas_call | solution.py:189
  30.9 1.7 %shard_map.110 = (bf16[2,640,5120]{2,1,0:T(8,128)(2,1)}, bf16[2,128,5120]{2,1,0:T(8,128)(2,1)}, bf16[2,128,5120]{2,1,0:T(8,128)(2,1)}) custom-call(bf16[2,640,64]{2,1,0:T(8,128)(2,1)S(1)} %get-tuple-element.67.refs_0_, bf16[2,128,64]{2,1,0:T(8,128)(2,1)S(1)} %get-tuple-element.68.refs_1_, ...), custom_call_target="tpu_custom_call", output_to_operand_aliasing={{0}: (8, {}), {1}: (9, {}), {2}: (10, {})} | custom-call | flops 146800640 | bytes 4587520 | tf_op jit(solution)/shard_map/pallas_call | solution.py:189
  32.6 0.1 collective-permute-start.17
  32.7 1.7 %shard_map.111 = (bf16[2,640,5120]{2,1,0:T(8,128)(2,1)}, bf16[2,128,5120]{2,1,0:T(8,128)(2,1)}, bf16[2,128,5120]{2,1,0:T(8,128)(2,1)}) custom-call(bf16[2,640,64]{2,1,0:T(8,128)(2,1)S(1)} %get-tuple-element.67.refs_0_, bf16[2,128,64]{2,1,0:T(8,128)(2,1)S(1)} %get-tuple-element.68.refs_1_, ...), custom_call_target="tpu_custom_call", output_to_operand_aliasing={{0}: (8, {}), {1}: (9, {}), {2}: (10, {})} | custom-call | flops 146800640 | bytes 4587520 | tf_op jit(solution)/shard_map/pallas_call | solution.py:189
  34.5 0.5 %collective-permute-start.16 = (bf16[3,64,640]{2,1,0:T(8,128)(2,1)S(1)}, bf16[3,64,640]{2,1,0:T(8,128)(2,1)S(1)}, u32[]{:S(2)}, u32[]{:S(2)}) collective-permute-start(bf16[3,64,640]{2,1,0:T(8,128)(2,1)S(1)} %collective-permute-done.11.refs_5_), channel_id=1, source_target_pairs={{0,8},{8,0},{1,9},{9,1},{2,10},{10,2},{3,11},{11,3},{4,12},{12,4},... | collective-permute-start | bytes 737288 | tf_op jit(solution)/shard_map/ppermute | solution.py:42
  35.0 2.1 %shard_map.112 = (bf16[2,640,5120]{2,1,0:T(8,128)(2,1)}, bf16[2,128,5120]{2,1,0:T(8,128)(2,1)}, bf16[2,128,5120]{2,1,0:T(8,128)(2,1)}) custom-call(bf16[2,640,64]{2,1,0:T(8,128)(2,1)S(1)} %get-tuple-element.67.refs_0_, bf16[2,128,64]{2,1,0:T(8,128)(2,1)S(1)} %get-tuple-element.68.refs_1_, ...), custom_call_target="tpu_custom_call", output_to_operand_aliasing={{0}: (9, {}), {1}: (10, {}), {2}: (11, {})} | custom-call | flops 220200960 | bytes 6881280 | tf_op jit(solution)/shard_map/pallas_call | solution.py:189
  37.1 1.2 %shard_map.113 = (bf16[2,640,5120]{2,1,0:T(8,128)(2,1)}, bf16[2,128,5120]{2,1,0:T(8,128)(2,1)}, bf16[2,128,5120]{2,1,0:T(8,128)(2,1)}) custom-call(bf16[2,640,64]{2,1,0:T(8,128)(2,1)S(1)} %get-tuple-element.67.refs_0_, bf16[2,128,64]{2,1,0:T(8,128)(2,1)S(1)} %get-tuple-element.68.refs_1_, ...), custom_call_target="tpu_custom_call", output_to_operand_aliasing={{0}: (7, {}), {1}: (8, {}), {2}: (9, {})} | custom-call | flops 73400320 | bytes 2293760 | tf_op jit(solution)/shard_map/pallas_call | solution.py:189
  (31 shorter events, 0.1 us)
Async XLA Ops:
  0.6 2.6 %copy-start.3 = (bf16[1,2,3,64,640]{4,3,2,1,0:T(8,128)(2,1)S(1)}, bf16[1,2,3,64,640]{4,3,2,1,0:T(8,128)(2,1)}, u32[]{:S(2)}) copy-start(bf16[1,2,3,64,640]{4,3,2,1,0:T(8,128)(2,1)} %param.12) | copy-start | bytes 1474564
  0.6 7.4 %copy-start.4 = (bf16[1,2,640,64]{2,3,1,0:T(8,128)(2,1)S(1)}, bf16[1,2,640,64]{2,3,1,0:T(8,128)(2,1)}, u32[]{:S(2)}) copy-start(bf16[1,2,640,64]{2,3,1,0:T(8,128)(2,1)} %param.13) | copy-start | bytes 491524
  0.7 7.3 %copy-start.5 = (bf16[1,2,128,64]{2,3,1,0:T(8,128)(2,1)S(1)}, bf16[1,2,128,64]{2,3,1,0:T(8,128)(2,1)}, u32[]{:S(2)}) copy-start(bf16[1,2,128,64]{2,3,1,0:T(8,128)(2,1)} %param.14) | copy-start | bytes 98308
  0.7 7.3 %copy-start.6 = (bf16[1,2,128,64]{2,3,1,0:T(8,128)(2,1)S(1)}, bf16[1,2,128,64]{2,3,1,0:T(8,128)(2,1)}, u32[]{:S(2)}) copy-start(bf16[1,2,128,64]{2,3,1,0:T(8,128)(2,1)} %param.15) | copy-start | bytes 98308
  0.7 2.6 %copy-start.7 = (s32[2,3]{1,0:T(2,128)S(1)}, s32[2,3]{1,0:T(2,128)}, u32[]{:S(2)}) copy-start(s32[2,3]{1,0:T(2,128)} %owners.3) | copy-start | bytes 76
  0.7 2.6 %collective-permute-start = (bf16[2,3,64,640]{3,2,1,0:T(8,128)(2,1)}, bf16[2,3,64,640]{3,2,1,0:T(8,128)(2,1)S(1)}, u32[]{:S(2)}, u32[]{:S(2)}) collective-permute-start(bf16[2,3,64,640]{3,2,1,0:T(8,128)(2,1)} %bitcast.10), channel_id=1, source_target_pairs={{0,8},{8,0},{1,9},{9,1},{2,10},{10,2},{3,11},{11,3},{4,12},{12,4},... | collective-permute-start | bytes 1474568 | tf_op jit(solution)/shard_map/ppermute | solution.py:42
  1.2 2.0 %collective-permute-start.1 = (bf16[2,64,640]{2,1,0:T(8,128)(2,1)}, bf16[2,64,640]{2,1,0:T(8,128)(2,1)S(1)}, u32[]{:S(2)}, u32[]{:S(2)}) collective-permute-start(bf16[2,64,640]{2,1,0:T(8,128)(2,1)} %bitcast.12), channel_id=1, source_target_pairs={{0,8},{8,0},{1,9},{9,1},{2,10},{10,2},{3,11},{11,3},{4,12},{12,4},... | collective-permute-start | bytes 491528 | tf_op jit(solution)/shard_map/ppermute | solution.py:42
  1.3 1.9 %collective-permute-start.2 = (bf16[2,64,128]{2,1,0:T(8,128)(2,1)}, bf16[2,64,128]{2,1,0:T(8,128)(2,1)S(1)}, u32[]{:S(2)}, u32[]{:S(2)}) collective-permute-start(bf16[2,64,128]{2,1,0:T(8,128)(2,1)} %bitcast.14), channel_id=1, source_target_pairs={{0,8},{8,0},{1,9},{9,1},{2,10},{10,2},{3,11},{11,3},{4,12},{12,4},... | collective-permute-start | bytes 98312 | tf_op jit(solution)/shard_map/ppermute | solution.py:42
  1.7 1.5 %collective-permute-start.3 = (bf16[2,64,128]{2,1,0:T(8,128)(2,1)}, bf16[2,64,128]{2,1,0:T(8,128)(2,1)S(1)}, u32[]{:S(2)}, u32[]{:S(2)}) collective-permute-start(bf16[2,64,128]{2,1,0:T(8,128)(2,1)} %bitcast.16), channel_id=1, source_target_pairs={{0,8},{8,0},{1,9},{9,1},{2,10},{10,2},{3,11},{11,3},{4,12},{12,4},... | collective-permute-start | bytes 98312 | tf_op jit(solution)/shard_map/ppermute | solution.py:42
  3.4 8.1 %collective-permute-start.5 = (bf16[3,64,640]{2,1,0:T(8,128)(2,1)S(1)}, bf16[3,64,640]{2,1,0:T(8,128)(2,1)S(1)}, u32[]{:S(2)}, u32[]{:S(2)}) collective-permute-start(bf16[3,64,640]{2,1,0:T(8,128)(2,1)S(1)} %get-tuple-element.72.refs_3_), channel_id=1, source_target_pairs={{0,2},{8,9},{2,4},{10,8},{4,6},{12,10},{6,7},{14,12},{7,5},{15,14}... | collective-permute-start | bytes 737288 | tf_op jit(solution)/shard_map/ppermute | solution.py:38
  6.4 6.9 %collective-permute-start.4 = (bf16[3,64,640]{2,1,0:T(8,128)(2,1)S(1)}, bf16[3,64,640]{2,1,0:T(8,128)(2,1)S(1)}, u32[]{:S(2)}, u32[]{:S(2)}) collective-permute-start(bf16[3,64,640]{2,1,0:T(8,128)(2,1)S(1)} %get-tuple-element.71.refs_4_), channel_id=1, source_target_pairs={{0,2},{8,9},{2,4},{10,8},{4,6},{12,10},{6,7},{14,12},{7,5},{15,14}... | collective-permute-start | bytes 737288 | tf_op jit(solution)/shard_map/ppermute | solution.py:38
  8.0 9.8 %copy-start = (bf16[2,640,5120]{2,1,0:T(8,128)(2,1)S(1)}, bf16[2,640,5120]{2,1,0:T(8,128)(2,1)}, u32[]{:S(2)}) copy-start(bf16[2,640,5120]{2,1,0:T(8,128)(2,1)} %refs_4_.1) | copy-start | bytes 39321604
  8.0 9.8 %copy-start.2 = (bf16[2,128,5120]{2,1,0:T(8,128)(2,1)S(1)}, bf16[2,128,5120]{2,1,0:T(8,128)(2,1)}, u32[]{:S(2)}) copy-start(bf16[2,128,5120]{2,1,0:T(8,128)(2,1)} %refs_5_.11) | copy-start | bytes 7864324
  9.8 8.0 %copy-start.1 = (bf16[2,128,5120]{2,1,0:T(8,128)(2,1)S(1)}, bf16[2,128,5120]{2,1,0:T(8,128)(2,1)}, u32[]{:S(2)}) copy-start(bf16[2,128,5120]{2,1,0:T(8,128)(2,1)} %refs_6_.15) | copy-start | bytes 7864324
  11.6 6.3 %collective-permute-start.10 = (bf16[3,64,640]{2,1,0:T(8,128)(2,1)S(1)}, bf16[3,64,640]{2,1,0:T(8,128)(2,1)S(1)}, u32[]{:S(2)}, u32[]{:S(2)}) collective-permute-start(bf16[3,64,640]{2,1,0:T(8,128)(2,1)S(1)} %collective-permute-done.5.refs_3_), channel_id=1, source_target_pairs={{0,8},{8,0},{1,9},{9,1},{2,10},{10,2},{3,11},{11,3},{4,12},{12,4},... | collective-permute-start | bytes 737288 | tf_op jit(solution)/shard_map/ppermute | solution.py:42
  11.6 7.9 %collective-permute-start.9 = (bf16[3,64,640]{2,1,0:T(8,128)(2,1)S(1)}, bf16[3,64,640]{2,1,0:T(8,128)(2,1)S(1)}, u32[]{:S(2)}, u32[]{:S(2)}) collective-permute-start(bf16[3,64,640]{2,1,0:T(8,128)(2,1)S(1)} %collective-permute-done.5.refs_3_), channel_id=1, source_target_pairs={{0,2},{8,9},{2,4},{10,8},{4,6},{12,10},{6,7},{14,12},{7,5},{15,14}... | collective-permute-start | bytes 737288 | tf_op jit(solution)/shard_map/ppermute | solution.py:38
  13.3 6.4 %collective-permute-start.8 = (bf16[3,64,640]{2,1,0:T(8,128)(2,1)S(1)}, bf16[3,64,640]{2,1,0:T(8,128)(2,1)S(1)}, u32[]{:S(2)}, u32[]{:S(2)}) collective-permute-start(bf16[3,64,640]{2,1,0:T(8,128)(2,1)S(1)} %collective-permute-done.4.refs_3_), channel_id=1, source_target_pairs={{0,8},{8,0},{1,9},{9,1},{2,10},{10,2},{3,11},{11,3},{4,12},{12,4},... | collective-permute-start | bytes 737288 | tf_op jit(solution)/shard_map/ppermute | solution.py:42
  13.3 10.5 %collective-permute-start.7 = (bf16[3,64,640]{2,1,0:T(8,128)(2,1)S(1)}, bf16[3,64,640]{2,1,0:T(8,128)(2,1)S(1)}, u32[]{:S(2)}, u32[]{:S(2)}) collective-permute-start(bf16[3,64,640]{2,1,0:T(8,128)(2,1)S(1)} %collective-permute-done.5.refs_3_), channel_id=1, source_target_pairs={{0,4},{8,11},{2,6},{10,9},{4,7},{12,8},{6,5},{14,10},{7,3},{15,12}... | collective-permute-start | bytes 737288 | tf_op jit(solution)/shard_map/ppermute | solution.py:38
  16.3 8.6 %collective-permute-start.6 = (bf16[3,64,640]{2,1,0:T(8,128)(2,1)S(1)}, bf16[3,64,640]{2,1,0:T(8,128)(2,1)S(1)}, u32[]{:S(2)}, u32[]{:S(2)}) collective-permute-start(bf16[3,64,640]{2,1,0:T(8,128)(2,1)S(1)} %collective-permute-done.4.refs_3_), channel_id=1, source_target_pairs={{0,2},{8,9},{2,4},{10,8},{4,6},{12,10},{6,7},{14,12},{7,5},{15,14}... | collective-permute-start | bytes 737288 | tf_op jit(solution)/shard_map/ppermute | solution.py:38
  19.6 9.6 %collective-permute-start.15 = (bf16[3,64,640]{2,1,0:T(8,128)(2,1)S(1)}, bf16[3,64,640]{2,1,0:T(8,128)(2,1)S(1)}, u32[]{:S(2)}, u32[]{:S(2)}) collective-permute-start(bf16[3,64,640]{2,1,0:T(8,128)(2,1)S(1)} %collective-permute-done.9.refs_3_), channel_id=1, source_target_pairs={{0,8},{8,0},{1,9},{9,1},{2,10},{10,2},{3,11},{11,3},{4,12},{12,4},... | collective-permute-start | bytes 737288 | tf_op jit(solution)/shard_map/ppermute | solution.py:42
  24.9 6.0 %collective-permute-start.14 = (bf16[3,64,640]{2,1,0:T(8,128)(2,1)S(1)}, bf16[3,64,640]{2,1,0:T(8,128)(2,1)S(1)}, u32[]{:S(2)}, u32[]{:S(2)}) collective-permute-start(bf16[3,64,640]{2,1,0:T(8,128)(2,1)S(1)} %collective-permute-done.6.refs_3_), channel_id=1, source_target_pairs={{0,8},{8,0},{1,9},{9,1},{2,10},{10,2},{3,11},{11,3},{4,12},{12,4},... | collective-permute-start | bytes 737288 | tf_op jit(solution)/shard_map/ppermute | solution.py:42
  25.5 7.2 %collective-permute-start.13 = (bf16[3,64,640]{2,1,0:T(8,128)(2,1)S(1)}, bf16[3,64,640]{2,1,0:T(8,128)(2,1)S(1)}, u32[]{:S(2)}, u32[]{:S(2)}) collective-permute-start(bf16[3,64,640]{2,1,0:T(8,128)(2,1)S(1)} %collective-permute-done.7.refs_3_), channel_id=1, source_target_pairs={{0,2},{8,9},{2,4},{10,8},{4,6},{12,10},{6,7},{14,12},{7,5},{15,14}... | collective-permute-start | bytes 737288 | tf_op jit(solution)/shard_map/ppermute | solution.py:38
  27.4 5.4 %collective-permute-start.12 = (bf16[3,64,640]{2,1,0:T(8,128)(2,1)S(1)}, bf16[3,64,640]{2,1,0:T(8,128)(2,1)S(1)}, u32[]{:S(2)}, u32[]{:S(2)}) collective-permute-start(bf16[3,64,640]{2,1,0:T(8,128)(2,1)S(1)} %collective-permute-done.7.refs_3_), channel_id=1, source_target_pairs={{0,8},{8,0},{1,9},{9,1},{2,10},{10,2},{3,11},{11,3},{4,12},{12,4},... | collective-permute-start | bytes 737288 | tf_op jit(solution)/shard_map/ppermute | solution.py:42
  27.4 7.1 %collective-permute-start.11 = (bf16[3,64,640]{2,1,0:T(8,128)(2,1)S(1)}, bf16[3,64,640]{2,1,0:T(8,128)(2,1)S(1)}, u32[]{:S(2)}, u32[]{:S(2)}) collective-permute-start(bf16[3,64,640]{2,1,0:T(8,128)(2,1)S(1)} %collective-permute-done.6.refs_3_), channel_id=1, source_target_pairs={{0,2},{8,9},{2,4},{10,8},{4,6},{12,10},{6,7},{14,12},{7,5},{15,14}... | collective-permute-start | bytes 737288 | tf_op jit(solution)/shard_map/ppermute | solution.py:38
  32.6 2.4 %collective-permute-start.17 = (bf16[3,64,640]{2,1,0:T(8,128)(2,1)S(1)}, bf16[3,64,640]{2,1,0:T(8,128)(2,1)S(1)}, u32[]{:S(2)}, u32[]{:S(2)}) collective-permute-start(bf16[3,64,640]{2,1,0:T(8,128)(2,1)S(1)} %collective-permute-done.13.refs_3_), channel_id=1, source_target_pairs={{0,8},{8,0},{1,9},{9,1},{2,10},{10,2},{3,11},{11,3},{4,12},{12,4},... | collective-permute-start | bytes 737288 | tf_op jit(solution)/shard_map/ppermute | solution.py:42
  34.5 2.7 %collective-permute-start.16 = (bf16[3,64,640]{2,1,0:T(8,128)(2,1)S(1)}, bf16[3,64,640]{2,1,0:T(8,128)(2,1)S(1)}, u32[]{:S(2)}, u32[]{:S(2)}) collective-permute-start(bf16[3,64,640]{2,1,0:T(8,128)(2,1)S(1)} %collective-permute-done.11.refs_5_), channel_id=1, source_target_pairs={{0,8},{8,0},{1,9},{9,1},{2,10},{10,2},{3,11},{11,3},{4,12},{12,4},... | collective-permute-start | bytes 737288 | tf_op jit(solution)/shard_map/ppermute | solution.py:42

commit v10 on v8

--- a/solution.py
+++ b/solution.py
@@ -225,17 +225,18 @@
     if cols % LANES == 0:
         tie = lax.optimization_barrier
         shapes = [jax.ShapeDtypeStruct(base.shape, base.dtype) for base in bases]
-        swapped = (swap_cores(own_a), [swap_cores(x) for x in own_b])
         pieces = [(0, True, True), (0, True, False)]
         key_block = fetch_blocks(n, cols, [base_key], pieces)
-        (other_a, other_b), key_block = tie((swapped, key_block))
+        other_a, key_block = tie((swap_cores(own_a), key_block))
         first, second = choose_a(owners, own_a, other_a)
+        other_b = [swap_cores(x) for x in own_b]
+        second, other_b[1] = tie((second, other_b[1]))
         held = [first, second]
         first = ring_pass(first, n)
         second = ring_pass(second, n)
         b, blocks = choose_b(n, cols, owners, own_b, other_b, [base_query, base_value], pieces)
+        first, b = tie((first, b))
         outs = merge(n, scale, b, held, [blocks[0], key_block[0], blocks[1]], shapes, None, pieces)
-        first, outs = tie((first, outs))
 
         def go(pieces, chunks, outs):
             return merge(n, scale, b, chunks, bases, shapes, outs, pieces)

time: 34 us -> 35 us (1.029)
  waiting for transfers between devices: 2.11 us -> 2.94 us
    ppermute x11, waiting for transfers between devices: 0.44 us -> 1.56 us  [swap_cores(): return lax.ppermute(array, 'rollout', [(0, 1), (1, 0)])]
    ppermute x7, starting transfers between devices: 12.4 us -> 12 us  [ring_pass(): return lax.ppermute(array, ('rollout', 'tensor'), pairs)]
  transfers between devices with their start and end apart: 18 -> 18, of which waited for: 4 -> 4; matrix products, arithmetic and copies ran while one was open for 0% -> 0% of each run, Pallas kernels for 45% -> 43%
where the time goes in v10:
time: 35 us; the launch traced here: 34.8 us
  Pallas kernels  16.5 us (47%)
  starting transfers between devices  13.5 us (39%)
  waiting for transfers between devices  2.94 us (8%)
  local copies, waits for them, and re-layouts  1 us (3%)
  between operations  0.88 us (3%)
    pallas_call x8, Pallas kernels, merge(): pl.pallas_call(functools.partial(merge_kernel, n, pieces, scale, fresh),...  13.5 us
    ppermute x7, starting transfers between devices, ring_pass(): return lax.ppermute(array, ('rollout', 'tensor'), pairs)  12 us
    pallas_call x1, Pallas kernels, choose_b(): pl.pallas_call(functools.partial(choose_b_kernel, n, pieces), in_specs=[V...  1.81 us
    ppermute x11, waiting for transfers between devices, swap_cores(): return lax.ppermute(array, 'rollout', [(0, 1), (1, 0)])  1.56 us
    ppermute x11, starting transfers between devices, swap_cores(): return lax.ppermute(array, 'rollout', [(0, 1), (1, 0)])  1.46 us
    ppermute x7, waiting for transfers between devices, ring_pass(): return lax.ppermute(array, ('rollout', 'tensor'), pairs)  1.38 us
    pallas_call x1, Pallas kernels, fetch_blocks(): pl.pallas_call(functools.partial(fetch_kernel, n, pieces), in_specs=[HBM]...  1.01 us
    unnamed x16, local copies, waits for them, and re-layouts  1 us
  transfers between devices with their start and end apart: 18, of which 4 were waited for; matrix products, arithmetic and copies ran while one was open for 0% of the time, Pallas kernels for 43%

profile of v10, /device:TPU:0, one launch (start us, length us, event | category | flops | bytes accessed | tf_op | source)
XLA Modules:
  0.0 34.8 jit_solution(6162653585617083625)
XLA Ops:
  0.7 0.5 %collective-permute-start = (bf16[2,3,64,640]{3,2,1,0:T(8,128)(2,1)}, bf16[2,3,64,640]{3,2,1,0:T(8,128)(2,1)S(1)}, u32[]{:S(2)}, u32[]{:S(2)}) collective-permute-start(bf16[2,3,64,640]{3,2,1,0:T(8,128)(2,1)} %bitcast.10), channel_id=1, source_target_pairs={{0,8},{8,0},{1,9},{9,1},{2,10},{10,2},{3,11},{11,3},{4,12},{12,4},... | collective-permute-start | bytes 1474568 | tf_op jit(solution)/shard_map/ppermute | solution.py:42
  1.2 1.0 %shard_map.103.refs_6_ = bf16[2,128,640]{2,1,0:T(8,128)(2,1)S(1)} custom-call(bf16[2,128,5120]{2,1,0:T(8,128)(2,1)} %refs_5_.11), custom_call_target="tpu_custom_call" | custom-call | bytes 655360 | tf_op jit(solution)/shard_map/pallas_call | solution.py:113
  2.2 0.7 %collective-permute-done.other = bf16[2,3,64,640]{3,2,1,0:T(8,128)(2,1)S(1)} collective-permute-done((bf16[2,3,64,640]{3,2,1,0:T(8,128)(2,1)}, bf16[2,3,64,640]{3,2,1,0:T(8,128)(2,1)S(1)}, u32[]{:S(2)}, u32[]{:S(2)}) %collective-permute-start) | collective-permute-done | bytes 491552 | tf_op jit(solution)/shard_map/ppermute | solution.py:42
  2.9 0.1 shard_map.104
  3.1 3.0 %collective-permute-start.1 = (bf16[3,64,640]{2,1,0:T(8,128)(2,1)S(1)}, bf16[3,64,640]{2,1,0:T(8,128)(2,1)S(1)}, u32[]{:S(2)}, u32[]{:S(2)}) collective-permute-start(bf16[3,64,640]{2,1,0:T(8,128)(2,1)S(1)} %get-tuple-element.64.refs_3_), channel_id=1, source_target_pairs={{0,2},{8,9},{2,4},{10,8},{4,6},{12,10},{6,7},{14,12},{7,5},{15,14}... | collective-permute-start | bytes 737288 | tf_op jit(solution)/shard_map/ppermute | solution.py:38
  6.1 0.5 %collective-permute-start.3 = (bf16[2,64,128]{2,1,0:T(8,128)(2,1)S(1)}, bf16[2,64,128]{2,1,0:T(8,128)(2,1)S(1)}, u32[]{:S(2)}, u32[]{:S(2)}) collective-permute-start(bf16[2,64,128]{2,1,0:T(8,128)(2,1)S(1)} %bitcast.14), channel_id=1, source_target_pairs={{0,8},{8,0},{1,9},{9,1},{2,10},{10,2},{3,11},{11,3},{4,12},{12,4},... | collective-permute-start | bytes 98312 | tf_op jit(solution)/shard_map/ppermute | solution.py:42
  6.6 0.1 collective-permute-start.4
  6.7 0.9 %collective-permute-done.3.refs_4_ = bf16[2,64,128]{2,1,0:T(8,128)(2,1)S(1)} collective-permute-done((bf16[2,64,128]{2,1,0:T(8,128)(2,1)S(1)}, bf16[2,64,128]{2,1,0:T(8,128)(2,1)S(1)}, u32[]{:S(2)}, u32[]{:S(2)}) %collective-permute-start.3) | collective-permute-done | bytes 32800 | tf_op jit(solution)/shard_map/ppermute | solution.py:42
  7.5 1.6 %collective-permute-start.7 = (bf16[3,64,640]{2,1,0:T(8,128)(2,1)S(1)}, bf16[3,64,640]{2,1,0:T(8,128)(2,1)S(1)}, u32[]{:S(2)}, u32[]{:S(2)}) collective-permute-start(bf16[3,64,640]{2,1,0:T(8,128)(2,1)S(1)} %get-tuple-element.74.refs_4_), channel_id=1, source_target_pairs={{0,2},{8,9},{2,4},{10,8},{4,6},{12,10},{6,7},{14,12},{7,5},{15,14}... | collective-permute-start | bytes 737288 | tf_op jit(solution)/shard_map/ppermute | solution.py:38
  9.1 0.0 copy-start.2
  9.1 1.8 %shard_map.105 = (bf16[2,640,64]{2,1,0:T(8,128)(2,1)S(1)}, bf16[2,128,64]{2,1,0:T(8,128)(2,1)S(1)}, bf16[2,128,64]{2,1,0:T(8,128)(2,1)S(1)}, bf16[2,640,640]{2,1,0:T(8,128)(2,1)S(1)}, bf16[2,128,640]{2,1,0:T(8,128)(2,1)S(1)}) custom-call(s32[2,3]{1,0:T(2,128)S(1)} %copy-done.7, bf16[2,64,640]{2,1,0:T(8,128)(2,1)S(1)} %bitcast.13, ...), custom_call_target="tpu_custom_call" | custom-call | bytes 3932160 | tf_op jit(solution)/shard_map/pallas_call | solution.py:141
  10.9 0.1 collective-permute-start.6
  11.0 1.6 %collective-permute-start.5 = (bf16[3,64,640]{2,1,0:T(8,128)(2,1)S(1)}, bf16[3,64,640]{2,1,0:T(8,128)(2,1)S(1)}, u32[]{:S(2)}, u32[]{:S(2)}) collective-permute-start(bf16[3,64,640]{2,1,0:T(8,128)(2,1)S(1)} %collective-permute-done.1.refs_3_), channel_id=1, source_target_pairs={{0,2},{8,9},{2,4},{10,8},{4,6},{12,10},{6,7},{14,12},{7,5},{15,14}... | collective-permute-start | bytes 737288 | tf_op jit(solution)/shard_map/ppermute | solution.py:38
  12.7 1.7 %shard_map.106 = (bf16[2,640,5120]{2,1,0:T(8,128)(2,1)}, bf16[2,128,5120]{2,1,0:T(8,128)(2,1)}, bf16[2,128,5120]{2,1,0:T(8,128)(2,1)}) custom-call(bf16[2,640,64]{2,1,0:T(8,128)(2,1)S(1)} %get-tuple-element.70.refs_0_, bf16[2,128,64]{2,1,0:T(8,128)(2,1)S(1)} %get-tuple-element.71.refs_1_, bf16[2,128,64]{2,1,0:T(8,128)(2,1)S(1)} %get-tuple-element.72.refs_2_, ...), custom_call_target="tpu_custom_call" | custom-call | flops 146800640 | bytes 4587520 | tf_op jit(solution)/shard_map/pallas_call | solution.py:189
  14.4 0.1 collective-permute-start.11
  14.4 1.6 %collective-permute-start.10 = (bf16[3,64,640]{2,1,0:T(8,128)(2,1)S(1)}, bf16[3,64,640]{2,1,0:T(8,128)(2,1)S(1)}, u32[]{:S(2)}, u32[]{:S(2)}) collective-permute-start(bf16[3,64,640]{2,1,0:T(8,128)(2,1)S(1)} %collective-permute-done.7.refs_3_), channel_id=1, source_target_pairs={{0,2},{8,9},{2,4},{10,8},{4,6},{12,10},{6,7},{14,12},{7,5},{15,14}... | collective-permute-start | bytes 737288 | tf_op jit(solution)/shard_map/ppermute | solution.py:38
  16.0 1.0 %copy-done.1 = bf16[2,128,5120]{2,1,0:T(8,128)(2,1)S(1)} copy-done((bf16[2,128,5120]{2,1,0:T(8,128)(2,1)S(1)}, bf16[2,128,5120]{2,1,0:T(8,128)(2,1)}, u32[]{:S(2)}) %copy-start.1) | copy-done | bytes 2621464
  17.0 1.7 %shard_map.107 = (bf16[2,640,5120]{2,1,0:T(8,128)(2,1)}, bf16[2,128,5120]{2,1,0:T(8,128)(2,1)}, bf16[2,128,5120]{2,1,0:T(8,128)(2,1)}) custom-call(bf16[2,640,64]{2,1,0:T(8,128)(2,1)S(1)} %get-tuple-element.70.refs_0_, bf16[2,128,64]{2,1,0:T(8,128)(2,1)S(1)} %get-tuple-element.71.refs_1_, ...), custom_call_target="tpu_custom_call", output_to_operand_aliasing={{0}: (8, {}), {1}: (9, {}), {2}: (10, {})} | custom-call | flops 146800640 | bytes 4587520 | tf_op jit(solution)/shard_map/pallas_call | solution.py:189
  18.7 0.1 collective-permute-start.9
  18.8 1.6 %collective-permute-start.8 = (bf16[3,64,640]{2,1,0:T(8,128)(2,1)S(1)}, bf16[3,64,640]{2,1,0:T(8,128)(2,1)S(1)}, u32[]{:S(2)}, u32[]{:S(2)}) collective-permute-start(bf16[3,64,640]{2,1,0:T(8,128)(2,1)S(1)} %collective-permute-done.5.refs_3_), channel_id=1, source_target_pairs={{0,2},{8,9},{2,4},{10,8},{4,6},{12,10},{6,7},{14,12},{7,5},{15,14}... | collective-permute-start | bytes 737288 | tf_op jit(solution)/shard_map/ppermute | solution.py:38
  20.4 1.7 %shard_map.108 = (bf16[2,640,5120]{2,1,0:T(8,128)(2,1)}, bf16[2,128,5120]{2,1,0:T(8,128)(2,1)}, bf16[2,128,5120]{2,1,0:T(8,128)(2,1)}) custom-call(bf16[2,640,64]{2,1,0:T(8,128)(2,1)S(1)} %get-tuple-element.70.refs_0_, bf16[2,128,64]{2,1,0:T(8,128)(2,1)S(1)} %get-tuple-element.71.refs_1_, ...), custom_call_target="tpu_custom_call", output_to_operand_aliasing={{0}: (8, {}), {1}: (9, {}), {2}: (10, {})} | custom-call | flops 146800640 | bytes 4587520 | tf_op jit(solution)/shard_map/pallas_call | solution.py:189
  22.1 0.1 collective-permute-start.15
  22.2 1.6 %collective-permute-start.14 = (bf16[3,64,640]{2,1,0:T(8,128)(2,1)S(1)}, bf16[3,64,640]{2,1,0:T(8,128)(2,1)S(1)}, u32[]{:S(2)}, u32[]{:S(2)}) collective-permute-start(bf16[3,64,640]{2,1,0:T(8,128)(2,1)S(1)} %collective-permute-done.10.refs_3_), channel_id=1, source_target_pairs={{0,2},{8,9},{2,4},{10,8},{4,6},{12,10},{6,7},{14,12},{7,5},{15,14}... | collective-permute-start | bytes 737288 | tf_op jit(solution)/shard_map/ppermute | solution.py:38
  23.8 1.7 %shard_map.109 = (bf16[2,640,5120]{2,1,0:T(8,128)(2,1)}, bf16[2,128,5120]{2,1,0:T(8,128)(2,1)}, bf16[2,128,5120]{2,1,0:T(8,128)(2,1)}) custom-call(bf16[2,640,64]{2,1,0:T(8,128)(2,1)S(1)} %get-tuple-element.70.refs_0_, bf16[2,128,64]{2,1,0:T(8,128)(2,1)S(1)} %get-tuple-element.71.refs_1_, ...), custom_call_target="tpu_custom_call", output_to_operand_aliasing={{0}: (8, {}), {1}: (9, {}), {2}: (10, {})} | custom-call | flops 146800640 | bytes 4587520 | tf_op jit(solution)/shard_map/pallas_call | solution.py:189
  25.5 0.1 collective-permute-start.13
  25.6 1.0 %collective-permute-start.12 = (bf16[3,64,640]{2,1,0:T(8,128)(2,1)S(1)}, bf16[3,64,640]{2,1,0:T(8,128)(2,1)S(1)}, u32[]{:S(2)}, u32[]{:S(2)}) collective-permute-start(bf16[3,64,640]{2,1,0:T(8,128)(2,1)S(1)} %collective-permute-done.8.refs_3_), channel_id=1, source_target_pairs={{0,2},{8,9},{2,4},{10,8},{4,6},{12,10},{6,7},{14,12},{7,5},{15,14}... | collective-permute-start | bytes 737288 | tf_op jit(solution)/shard_map/ppermute | solution.py:38
  26.6 1.7 %shard_map.110 = (bf16[2,640,5120]{2,1,0:T(8,128)(2,1)}, bf16[2,128,5120]{2,1,0:T(8,128)(2,1)}, bf16[2,128,5120]{2,1,0:T(8,128)(2,1)}) custom-call(bf16[2,640,64]{2,1,0:T(8,128)(2,1)S(1)} %get-tuple-element.70.refs_0_, bf16[2,128,64]{2,1,0:T(8,128)(2,1)S(1)} %get-tuple-element.71.refs_1_, ...), custom_call_target="tpu_custom_call", output_to_operand_aliasing={{0}: (8, {}), {1}: (9, {}), {2}: (10, {})} | custom-call | flops 146800640 | bytes 4587520 | tf_op jit(solution)/shard_map/pallas_call | solution.py:189
  28.3 0.1 collective-permute-done.14.refs_5_
  28.4 2.1 %shard_map.111 = (bf16[2,640,5120]{2,1,0:T(8,128)(2,1)}, bf16[2,128,5120]{2,1,0:T(8,128)(2,1)}, bf16[2,128,5120]{2,1,0:T(8,128)(2,1)}) custom-call(bf16[2,640,64]{2,1,0:T(8,128)(2,1)S(1)} %get-tuple-element.70.refs_0_, bf16[2,128,64]{2,1,0:T(8,128)(2,1)S(1)} %get-tuple-element.71.refs_1_, ...), custom_call_target="tpu_custom_call", output_to_operand_aliasing={{0}: (9, {}), {1}: (10, {}), {2}: (11, {})} | custom-call | flops 220200960 | bytes 6881280 | tf_op jit(solution)/shard_map/pallas_call | solution.py:189
  30.6 1.2 %collective-permute-done.12.refs_4_ = bf16[3,64,640]{2,1,0:T(8,128)(2,1)S(1)} collective-permute-done((bf16[3,64,640]{2,1,0:T(8,128)(2,1)S(1)}, bf16[3,64,640]{2,1,0:T(8,128)(2,1)S(1)}, u32[]{:S(2)}, u32[]{:S(2)}) %collective-permute-start.12) | collective-permute-done | bytes 245792 | tf_op jit(solution)/shard_map/ppermute | solution.py:38
  31.8 1.7 %shard_map.112 = (bf16[2,640,5120]{2,1,0:T(8,128)(2,1)}, bf16[2,128,5120]{2,1,0:T(8,128)(2,1)}, bf16[2,128,5120]{2,1,0:T(8,128)(2,1)}) custom-call(bf16[2,640,64]{2,1,0:T(8,128)(2,1)S(1)} %get-tuple-element.70.refs_0_, bf16[2,128,64]{2,1,0:T(8,128)(2,1)S(1)} %get-tuple-element.71.refs_1_, ...), custom_call_target="tpu_custom_call", output_to_operand_aliasing={{0}: (8, {}), {1}: (9, {}), {2}: (10, {})} | custom-call | flops 146800640 | bytes 4587520 | tf_op jit(solution)/shard_map/pallas_call | solution.py:189
  33.5 1.2 %shard_map.113 = (bf16[2,640,5120]{2,1,0:T(8,128)(2,1)}, bf16[2,128,5120]{2,1,0:T(8,128)(2,1)}, bf16[2,128,5120]{2,1,0:T(8,128)(2,1)}) custom-call(bf16[2,640,64]{2,1,0:T(8,128)(2,1)S(1)} %get-tuple-element.70.refs_0_, bf16[2,128,64]{2,1,0:T(8,128)(2,1)S(1)} %get-tuple-element.71.refs_1_, ...), custom_call_target="tpu_custom_call", output_to_operand_aliasing={{0}: (7, {}), {1}: (8, {}), {2}: (9, {})} | custom-call | flops 73400320 | bytes 2293760 | tf_op jit(solution)/shard_map/pallas_call | solution.py:189
  (31 shorter events, 0.1 us)
Async XLA Ops:
  0.6 2.3 %copy-start.3 = (bf16[1,2,3,64,640]{4,3,2,1,0:T(8,128)(2,1)S(1)}, bf16[1,2,3,64,640]{4,3,2,1,0:T(8,128)(2,1)}, u32[]{:S(2)}) copy-start(bf16[1,2,3,64,640]{4,3,2,1,0:T(8,128)(2,1)} %param.12) | copy-start | bytes 1474564
  0.6 2.3 %copy-start.7 = (s32[2,3]{1,0:T(2,128)S(1)}, s32[2,3]{1,0:T(2,128)}, u32[]{:S(2)}) copy-start(s32[2,3]{1,0:T(2,128)} %owners.3) | copy-start | bytes 76
  0.7 5.4 %copy-start.4 = (bf16[1,2,640,64]{2,3,1,0:T(8,128)(2,1)S(1)}, bf16[1,2,640,64]{2,3,1,0:T(8,128)(2,1)}, u32[]{:S(2)}) copy-start(bf16[1,2,640,64]{2,3,1,0:T(8,128)(2,1)} %param.13) | copy-start | bytes 491524
  0.7 5.4 %copy-start.5 = (bf16[1,2,128,64]{2,3,1,0:T(8,128)(2,1)S(1)}, bf16[1,2,128,64]{2,3,1,0:T(8,128)(2,1)}, u32[]{:S(2)}) copy-start(bf16[1,2,128,64]{2,3,1,0:T(8,128)(2,1)} %param.14) | copy-start | bytes 98308
  0.7 5.9 %copy-start.6 = (bf16[1,2,128,64]{2,3,1,0:T(8,128)(2,1)S(1)}, bf16[1,2,128,64]{2,3,1,0:T(8,128)(2,1)}, u32[]{:S(2)}) copy-start(bf16[1,2,128,64]{2,3,1,0:T(8,128)(2,1)} %param.15) | copy-start | bytes 98308
  0.7 2.2 %collective-permute-start = (bf16[2,3,64,640]{3,2,1,0:T(8,128)(2,1)}, bf16[2,3,64,640]{3,2,1,0:T(8,128)(2,1)S(1)}, u32[]{:S(2)}, u32[]{:S(2)}) collective-permute-start(bf16[2,3,64,640]{3,2,1,0:T(8,128)(2,1)} %bitcast.10), channel_id=1, source_target_pairs={{0,8},{8,0},{1,9},{9,1},{2,10},{10,2},{3,11},{11,3},{4,12},{12,4},... | collective-permute-start | bytes 1474568 | tf_op jit(solution)/shard_map/ppermute | solution.py:42
  3.1 7.9 %collective-permute-start.1 = (bf16[3,64,640]{2,1,0:T(8,128)(2,1)S(1)}, bf16[3,64,640]{2,1,0:T(8,128)(2,1)S(1)}, u32[]{:S(2)}, u32[]{:S(2)}) collective-permute-start(bf16[3,64,640]{2,1,0:T(8,128)(2,1)S(1)} %get-tuple-element.64.refs_3_), channel_id=1, source_target_pairs={{0,2},{8,9},{2,4},{10,8},{4,6},{12,10},{6,7},{14,12},{7,5},{15,14}... | collective-permute-start | bytes 737288 | tf_op jit(solution)/shard_map/ppermute | solution.py:38
  6.1 3.0 %collective-permute-start.2 = (bf16[2,64,640]{2,1,0:T(8,128)(2,1)S(1)}, bf16[2,64,640]{2,1,0:T(8,128)(2,1)S(1)}, u32[]{:S(2)}, u32[]{:S(2)}) collective-permute-start(bf16[2,64,640]{2,1,0:T(8,128)(2,1)S(1)} %bitcast.12), channel_id=1, source_target_pairs={{0,8},{8,0},{1,9},{9,1},{2,10},{10,2},{3,11},{11,3},{4,12},{12,4},... | collective-permute-start | bytes 491528 | tf_op jit(solution)/shard_map/ppermute | solution.py:42
  6.1 1.4 %collective-permute-start.3 = (bf16[2,64,128]{2,1,0:T(8,128)(2,1)S(1)}, bf16[2,64,128]{2,1,0:T(8,128)(2,1)S(1)}, u32[]{:S(2)}, u32[]{:S(2)}) collective-permute-start(bf16[2,64,128]{2,1,0:T(8,128)(2,1)S(1)} %bitcast.14), channel_id=1, source_target_pairs={{0,8},{8,0},{1,9},{9,1},{2,10},{10,2},{3,11},{11,3},{4,12},{12,4},... | collective-permute-start | bytes 98312 | tf_op jit(solution)/shard_map/ppermute | solution.py:42
  6.6 2.5 %collective-permute-start.4 = (bf16[2,64,128]{2,1,0:T(8,128)(2,1)S(1)}, bf16[2,64,128]{2,1,0:T(8,128)(2,1)S(1)}, u32[]{:S(2)}, u32[]{:S(2)}) collective-permute-start(bf16[2,64,128]{2,1,0:T(8,128)(2,1)S(1)} %bitcast.16), channel_id=1, source_target_pairs={{0,8},{8,0},{1,9},{9,1},{2,10},{10,2},{3,11},{11,3},{4,12},{12,4},... | collective-permute-start | bytes 98312 | tf_op jit(solution)/shard_map/ppermute | solution.py:42
  7.5 6.9 %collective-permute-start.7 = (bf16[3,64,640]{2,1,0:T(8,128)(2,1)S(1)}, bf16[3,64,640]{2,1,0:T(8,128)(2,1)S(1)}, u32[]{:S(2)}, u32[]{:S(2)}) collective-permute-start(bf16[3,64,640]{2,1,0:T(8,128)(2,1)S(1)} %get-tuple-element.74.refs_4_), channel_id=1, source_target_pairs={{0,2},{8,9},{2,4},{10,8},{4,6},{12,10},{6,7},{14,12},{7,5},{15,14}... | collective-permute-start | bytes 737288 | tf_op jit(solution)/shard_map/ppermute | solution.py:38
  9.1 6.9 %copy-start = (bf16[2,640,5120]{2,1,0:T(8,128)(2,1)S(1)}, bf16[2,640,5120]{2,1,0:T(8,128)(2,1)}, u32[]{:S(2)}) copy-start(bf16[2,640,5120]{2,1,0:T(8,128)(2,1)} %refs_4_.1) | copy-start | bytes 39321604
  9.1 6.9 %copy-start.2 = (bf16[2,128,5120]{2,1,0:T(8,128)(2,1)S(1)}, bf16[2,128,5120]{2,1,0:T(8,128)(2,1)}, u32[]{:S(2)}) copy-start(bf16[2,128,5120]{2,1,0:T(8,128)(2,1)} %refs_5_.11) | copy-start | bytes 7864324
  10.9 6.1 %copy-start.1 = (bf16[2,128,5120]{2,1,0:T(8,128)(2,1)S(1)}, bf16[2,128,5120]{2,1,0:T(8,128)(2,1)}, u32[]{:S(2)}) copy-start(bf16[2,128,5120]{2,1,0:T(8,128)(2,1)} %refs_6_.15) | copy-start | bytes 7864324
  10.9 5.1 %collective-permute-start.6 = (bf16[3,64,640]{2,1,0:T(8,128)(2,1)S(1)}, bf16[3,64,640]{2,1,0:T(8,128)(2,1)S(1)}, u32[]{:S(2)}, u32[]{:S(2)}) collective-permute-start(bf16[3,64,640]{2,1,0:T(8,128)(2,1)S(1)} %collective-permute-done.1.refs_3_), channel_id=1, source_target_pairs={{0,8},{8,0},{1,9},{9,1},{2,10},{10,2},{3,11},{11,3},{4,12},{12,4},... | collective-permute-start | bytes 737288 | tf_op jit(solution)/shard_map/ppermute | solution.py:42
  11.0 7.7 %collective-permute-start.5 = (bf16[3,64,640]{2,1,0:T(8,128)(2,1)S(1)}, bf16[3,64,640]{2,1,0:T(8,128)(2,1)S(1)}, u32[]{:S(2)}, u32[]{:S(2)}) collective-permute-start(bf16[3,64,640]{2,1,0:T(8,128)(2,1)S(1)} %collective-permute-done.1.refs_3_), channel_id=1, source_target_pairs={{0,2},{8,9},{2,4},{10,8},{4,6},{12,10},{6,7},{14,12},{7,5},{15,14}... | collective-permute-start | bytes 737288 | tf_op jit(solution)/shard_map/ppermute | solution.py:38
  14.4 6.0 %collective-permute-start.11 = (bf16[3,64,640]{2,1,0:T(8,128)(2,1)S(1)}, bf16[3,64,640]{2,1,0:T(8,128)(2,1)S(1)}, u32[]{:S(2)}, u32[]{:S(2)}) collective-permute-start(bf16[3,64,640]{2,1,0:T(8,128)(2,1)S(1)} %collective-permute-done.7.refs_3_), channel_id=1, source_target_pairs={{0,8},{8,0},{1,9},{9,1},{2,10},{10,2},{3,11},{11,3},{4,12},{12,4},... | collective-permute-start | bytes 737288 | tf_op jit(solution)/shard_map/ppermute | solution.py:42
  14.4 7.7 %collective-permute-start.10 = (bf16[3,64,640]{2,1,0:T(8,128)(2,1)S(1)}, bf16[3,64,640]{2,1,0:T(8,128)(2,1)S(1)}, u32[]{:S(2)}, u32[]{:S(2)}) collective-permute-start(bf16[3,64,640]{2,1,0:T(8,128)(2,1)S(1)} %collective-permute-done.7.refs_3_), channel_id=1, source_target_pairs={{0,2},{8,9},{2,4},{10,8},{4,6},{12,10},{6,7},{14,12},{7,5},{15,14}... | collective-permute-start | bytes 737288 | tf_op jit(solution)/shard_map/ppermute | solution.py:38
  18.7 5.1 %collective-permute-start.9 = (bf16[3,64,640]{2,1,0:T(8,128)(2,1)S(1)}, bf16[3,64,640]{2,1,0:T(8,128)(2,1)S(1)}, u32[]{:S(2)}, u32[]{:S(2)}) collective-permute-start(bf16[3,64,640]{2,1,0:T(8,128)(2,1)S(1)} %collective-permute-done.5.refs_3_), channel_id=1, source_target_pairs={{0,8},{8,0},{1,9},{9,1},{2,10},{10,2},{3,11},{11,3},{4,12},{12,4},... | collective-permute-start | bytes 737288 | tf_op jit(solution)/shard_map/ppermute | solution.py:42
  18.8 6.7 %collective-permute-start.8 = (bf16[3,64,640]{2,1,0:T(8,128)(2,1)S(1)}, bf16[3,64,640]{2,1,0:T(8,128)(2,1)S(1)}, u32[]{:S(2)}, u32[]{:S(2)}) collective-permute-start(bf16[3,64,640]{2,1,0:T(8,128)(2,1)S(1)} %collective-permute-done.5.refs_3_), channel_id=1, source_target_pairs={{0,2},{8,9},{2,4},{10,8},{4,6},{12,10},{6,7},{14,12},{7,5},{15,14}... | collective-permute-start | bytes 737288 | tf_op jit(solution)/shard_map/ppermute | solution.py:38
  22.1 4.5 %collective-permute-start.15 = (bf16[3,64,640]{2,1,0:T(8,128)(2,1)S(1)}, bf16[3,64,640]{2,1,0:T(8,128)(2,1)S(1)}, u32[]{:S(2)}, u32[]{:S(2)}) collective-permute-start(bf16[3,64,640]{2,1,0:T(8,128)(2,1)S(1)} %collective-permute-done.10.refs_3_), channel_id=1, source_target_pairs={{0,8},{8,0},{1,9},{9,1},{2,10},{10,2},{3,11},{11,3},{4,12},{12,4},... | collective-permute-start | bytes 737288 | tf_op jit(solution)/shard_map/ppermute | solution.py:42
  22.2 6.2 %collective-permute-start.14 = (bf16[3,64,640]{2,1,0:T(8,128)(2,1)S(1)}, bf16[3,64,640]{2,1,0:T(8,128)(2,1)S(1)}, u32[]{:S(2)}, u32[]{:S(2)}) collective-permute-start(bf16[3,64,640]{2,1,0:T(8,128)(2,1)S(1)} %collective-permute-done.10.refs_3_), channel_id=1, source_target_pairs={{0,2},{8,9},{2,4},{10,8},{4,6},{12,10},{6,7},{14,12},{7,5},{15,14}... | collective-permute-start | bytes 737288 | tf_op jit(solution)/shard_map/ppermute | solution.py:38
  25.5 3.0 %collective-permute-start.13 = (bf16[3,64,640]{2,1,0:T(8,128)(2,1)S(1)}, bf16[3,64,640]{2,1,0:T(8,128)(2,1)S(1)}, u32[]{:S(2)}, u32[]{:S(2)}) collective-permute-start(bf16[3,64,640]{2,1,0:T(8,128)(2,1)S(1)} %collective-permute-done.8.refs_3_), channel_id=1, source_target_pairs={{0,8},{8,0},{1,9},{9,1},{2,10},{10,2},{3,11},{11,3},{4,12},{12,4},... | collective-permute-start | bytes 737288 | tf_op jit(solution)/shard_map/ppermute | solution.py:42
  25.6 6.2 %collective-permute-start.12 = (bf16[3,64,640]{2,1,0:T(8,128)(2,1)S(1)}, bf16[3,64,640]{2,1,0:T(8,128)(2,1)S(1)}, u32[]{:S(2)}, u32[]{:S(2)}) collective-permute-start(bf16[3,64,640]{2,1,0:T(8,128)(2,1)S(1)} %collective-permute-done.8.refs_3_), channel_id=1, source_target_pairs={{0,2},{8,9},{2,4},{10,8},{4,6},{12,10},{6,7},{14,12},{7,5},{15,14}... | collective-permute-start | bytes 737288 | tf_op jit(solution)/shard_map/ppermute | solution.py:38
  28.4 3.4 %collective-permute-start.17 = (bf16[3,64,640]{2,1,0:T(8,128)(2,1)S(1)}, bf16[3,64,640]{2,1,0:T(8,128)(2,1)S(1)}, u32[]{:S(2)}, u32[]{:S(2)}) collective-permute-start(bf16[3,64,640]{2,1,0:T(8,128)(2,1)S(1)} %collective-permute-done.14.refs_5_), channel_id=1, source_target_pairs={{0,8},{8,0},{1,9},{9,1},{2,10},{10,2},{3,11},{11,3},{4,12},{12,4},... | collective-permute-start | bytes 737288 | tf_op jit(solution)/shard_map/ppermute | solution.py:42
  31.8 1.7 %collective-permute-start.16 = (bf16[3,64,640]{2,1,0:T(8,128)(2,1)S(1)}, bf16[3,64,640]{2,1,0:T(8,128)(2,1)S(1)}, u32[]{:S(2)}, u32[]{:S(2)}) collective-permute-start(bf16[3,64,640]{2,1,0:T(8,128)(2,1)S(1)} %collective-permute-done.12.refs_4_), channel_id=1, source_target_pairs={{0,8},{8,0},{1,9},{9,1},{2,10},{10,2},{3,11},{11,3},{4,12},{12,4},... | collective-permute-start | bytes 737288 | tf_op jit(solution)/shard_map/ppermute | solution.py:42

commit v11 on v10

--- a/solution.py
+++ b/solution.py
@@ -226,17 +226,17 @@
         tie = lax.optimization_barrier
         shapes = [jax.ShapeDtypeStruct(base.shape, base.dtype) for base in bases]
         pieces = [(0, True, True), (0, True, False)]
-        key_block = fetch_blocks(n, cols, [base_key], pieces)
-        other_a, key_block = tie((swap_cores(own_a), key_block))
+        query_block = fetch_blocks(n, cols, [base_query], pieces)
+        other_a, query_block = tie((swap_cores(own_a), query_block))
         first, second = choose_a(owners, own_a, other_a)
         other_b = [swap_cores(x) for x in own_b]
         second, other_b[1] = tie((second, other_b[1]))
         held = [first, second]
         first = ring_pass(first, n)
         second = ring_pass(second, n)
-        b, blocks = choose_b(n, cols, owners, own_b, other_b, [base_query, base_value], pieces)
+        b, blocks = choose_b(n, cols, owners, own_b, other_b, [base_key, base_value], pieces)
         first, b = tie((first, b))
-        outs = merge(n, scale, b, held, [blocks[0], key_block[0], blocks[1]], shapes, None, pieces)
+        outs = merge(n, scale, b, held, [*query_block, *blocks], shapes, None, pieces)
 
         def go(pieces, chunks, outs):
             return merge(n, scale, b, chunks, bases, shapes, outs, pieces)

time: 35 us -> 33.7 us (0.963)
  local copies, waits for them, and re-layouts: 1 us -> 0.05 us
  waiting for transfers between devices: 2.94 us -> 2.38 us
    unnamed x16 -> x22, local copies, waits for them, and re-layouts: 1 us -> 0.05 us
    ppermute x11, waiting for transfers between devices: 1.56 us -> 1 us  [swap_cores(): return lax.ppermute(array, 'rollout', [(0, 1), (1, 0)])]
    pallas_call x1, Pallas kernels: 1.01 us -> 1.56 us  [fetch_blocks(): pl.pallas_call(functools.partial(fetch_kernel, n, pieces), in_specs=[HBM]...]
  transfers between devices with their start and end apart: 18 -> 18, of which waited for: 4 -> 4; matrix products, arithmetic and copies ran while one was open for 0% -> 0% of each run, Pallas kernels for 43% -> 46%
where the time goes in v11:
time: 33.7 us; the launch traced here: 33.5 us
  Pallas kernels  16.7 us (50%)
  starting transfers between devices  13.5 us (40%)
  waiting for transfers between devices  2.38 us (7%)
  between operations  0.9 us (3%)
    pallas_call x8, Pallas kernels, merge(): pl.pallas_call(functools.partial(merge_kernel, n, pieces, scale, fresh),...  13.5 us
    ppermute x7, starting transfers between devices, ring_pass(): return lax.ppermute(array, ('rollout', 'tensor'), pairs)  11.9 us
    pallas_call x1, Pallas kernels, fetch_blocks(): pl.pallas_call(functools.partial(fetch_kernel, n, pieces), in_specs=[HBM]...  1.56 us
    ppermute x11, starting transfers between devices, swap_cores(): return lax.ppermute(array, 'rollout', [(0, 1), (1, 0)])  1.56 us
    pallas_call x1, Pallas kernels, choose_b(): pl.pallas_call(functools.partial(choose_b_kernel, n, pieces), in_specs=[V...  1.5 us
    ppermute x7, waiting for transfers between devices, ring_pass(): return lax.ppermute(array, ('rollout', 'tensor'), pairs)  1.38 us
    ppermute x11, waiting for transfers between devices, swap_cores(): return lax.ppermute(array, 'rollout', [(0, 1), (1, 0)])  1 us
  transfers between devices with their start and end apart: 18, of which 4 were waited for; matrix products, arithmetic and copies ran while one was open for 0% of the time, Pallas kernels for 46%

profile of v11, /device:TPU:0, one launch (start us, length us, event | category | flops | bytes accessed | tf_op | source)
XLA Modules:
  0.0 33.5 jit_solution(11289932249505690123)
XLA Ops:
  0.7 0.5 %collective-permute-start = (bf16[2,3,64,640]{3,2,1,0:T(8,128)(2,1)}, bf16[2,3,64,640]{3,2,1,0:T(8,128)(2,1)S(1)}, u32[]{:S(2)}, u32[]{:S(2)}) collective-permute-start(bf16[2,3,64,640]{3,2,1,0:T(8,128)(2,1)} %bitcast.12), channel_id=1, source_target_pairs={{0,8},{8,0},{1,9},{9,1},{2,10},{10,2},{3,11},{11,3},{4,12},{12,4},... | collective-permute-start | bytes 1474568 | tf_op jit(solution)/shard_map/ppermute | solution.py:42
  1.2 1.6 %shard_map.103.refs_5_ = bf16[2,640,640]{2,1,0:T(8,128)(2,1)S(1)} custom-call(bf16[2,640,5120]{2,1,0:T(8,128)(2,1)} %refs_4_.1), custom_call_target="tpu_custom_call" | custom-call | bytes 3276800 | tf_op jit(solution)/shard_map/pallas_call | solution.py:113
  2.8 0.1 collective-permute-done.other
  2.9 0.1 shard_map.104
  3.1 3.0 %collective-permute-start.1 = (bf16[3,64,640]{2,1,0:T(8,128)(2,1)S(1)}, bf16[3,64,640]{2,1,0:T(8,128)(2,1)S(1)}, u32[]{:S(2)}, u32[]{:S(2)}) collective-permute-start(bf16[3,64,640]{2,1,0:T(8,128)(2,1)S(1)} %get-tuple-element.64.refs_3_), channel_id=1, source_target_pairs={{0,2},{8,9},{2,4},{10,8},{4,6},{12,10},{6,7},{14,12},{7,5},{15,14}... | collective-permute-start | bytes 737288 | tf_op jit(solution)/shard_map/ppermute | solution.py:38
  6.1 0.0 collective-permute-start.2
  6.1 0.5 %collective-permute-start.3 = (bf16[2,64,128]{2,1,0:T(8,128)(2,1)S(1)}, bf16[2,64,128]{2,1,0:T(8,128)(2,1)S(1)}, u32[]{:S(2)}, u32[]{:S(2)}) collective-permute-start(bf16[2,64,128]{2,1,0:T(8,128)(2,1)S(1)} %bitcast.16), channel_id=1, source_target_pairs={{0,8},{8,0},{1,9},{9,1},{2,10},{10,2},{3,11},{11,3},{4,12},{12,4},... | collective-permute-start | bytes 98312 | tf_op jit(solution)/shard_map/ppermute | solution.py:42
  6.6 0.1 collective-permute-start.4
  6.7 0.9 %collective-permute-done.3.refs_4_ = bf16[2,64,128]{2,1,0:T(8,128)(2,1)S(1)} collective-permute-done((bf16[2,64,128]{2,1,0:T(8,128)(2,1)S(1)}, bf16[2,64,128]{2,1,0:T(8,128)(2,1)S(1)}, u32[]{:S(2)}, u32[]{:S(2)}) %collective-permute-start.3) | collective-permute-done | bytes 32800 | tf_op jit(solution)/shard_map/ppermute | solution.py:42
  7.5 1.6 %collective-permute-start.7 = (bf16[3,64,640]{2,1,0:T(8,128)(2,1)S(1)}, bf16[3,64,640]{2,1,0:T(8,128)(2,1)S(1)}, u32[]{:S(2)}, u32[]{:S(2)}) collective-permute-start(bf16[3,64,640]{2,1,0:T(8,128)(2,1)S(1)} %get-tuple-element.74.refs_4_), channel_id=1, source_target_pairs={{0,2},{8,9},{2,4},{10,8},{4,6},{12,10},{6,7},{14,12},{7,5},{15,14}... | collective-permute-start | bytes 737288 | tf_op jit(solution)/shard_map/ppermute | solution.py:38
  9.1 1.5 %shard_map.105 = (bf16[2,640,64]{2,1,0:T(8,128)(2,1)S(1)}, bf16[2,128,64]{2,1,0:T(8,128)(2,1)S(1)}, bf16[2,128,64]{2,1,0:T(8,128)(2,1)S(1)}, bf16[2,128,640]{2,1,0:T(8,128)(2,1)S(1)}, bf16[2,128,640]{2,1,0:T(8,128)(2,1)S(1)}) custom-call(s32[2,3]{1,0:T(2,128)S(1)} %copy-done.6, bf16[2,64,640]{2,1,0:T(8,128)(2,1)S(1)} %bitcast.15, ...), custom_call_target="tpu_custom_call" | custom-call | bytes 1310720 | tf_op jit(solution)/shard_map/pallas_call | solution.py:141
  10.6 0.0 copy-start
  10.6 0.1 collective-permute-start.6
  10.7 1.6 %collective-permute-start.5 = (bf16[3,64,640]{2,1,0:T(8,128)(2,1)S(1)}, bf16[3,64,640]{2,1,0:T(8,128)(2,1)S(1)}, u32[]{:S(2)}, u32[]{:S(2)}) collective-permute-start(bf16[3,64,640]{2,1,0:T(8,128)(2,1)S(1)} %collective-permute-done.1.refs_3_), channel_id=1, source_target_pairs={{0,2},{8,9},{2,4},{10,8},{4,6},{12,10},{6,7},{14,12},{7,5},{15,14}... | collective-permute-start | bytes 737288 | tf_op jit(solution)/shard_map/ppermute | solution.py:38
  12.3 1.7 %shard_map.106 = (bf16[2,640,5120]{2,1,0:T(8,128)(2,1)}, bf16[2,128,5120]{2,1,0:T(8,128)(2,1)}, bf16[2,128,5120]{2,1,0:T(8,128)(2,1)}) custom-call(bf16[2,640,64]{2,1,0:T(8,128)(2,1)S(1)} %get-tuple-element.70.refs_0_, bf16[2,128,64]{2,1,0:T(8,128)(2,1)S(1)} %get-tuple-element.71.refs_1_, bf16[2,128,64]{2,1,0:T(8,128)(2,1)S(1)} %get-tuple-element.72.refs_2_, ...), custom_call_target="tpu_custom_call" | custom-call | flops 146800640 | bytes 4587520 | tf_op jit(solution)/shard_map/pallas_call | solution.py:189
  14.0 0.2 collective-permute-start.11
  14.2 1.5 %collective-permute-start.10 = (bf16[3,64,640]{2,1,0:T(8,128)(2,1)S(1)}, bf16[3,64,640]{2,1,0:T(8,128)(2,1)S(1)}, u32[]{:S(2)}, u32[]{:S(2)}) collective-permute-start(bf16[3,64,640]{2,1,0:T(8,128)(2,1)S(1)} %collective-permute-done.7.refs_3_), channel_id=1, source_target_pairs={{0,2},{8,9},{2,4},{10,8},{4,6},{12,10},{6,7},{14,12},{7,5},{15,14}... | collective-permute-start | bytes 737288 | tf_op jit(solution)/shard_map/ppermute | solution.py:38
  15.7 1.7 %shard_map.107 = (bf16[2,640,5120]{2,1,0:T(8,128)(2,1)}, bf16[2,128,5120]{2,1,0:T(8,128)(2,1)}, bf16[2,128,5120]{2,1,0:T(8,128)(2,1)}) custom-call(bf16[2,640,64]{2,1,0:T(8,128)(2,1)S(1)} %get-tuple-element.70.refs_0_, bf16[2,128,64]{2,1,0:T(8,128)(2,1)S(1)} %get-tuple-element.71.refs_1_, ...), custom_call_target="tpu_custom_call", output_to_operand_aliasing={{0}: (8, {}), {1}: (9, {}), {2}: (10, {})} | custom-call | flops 146800640 | bytes 4587520 | tf_op jit(solution)/shard_map/pallas_call | solution.py:189
  17.5 0.1 collective-permute-start.9
  17.5 1.6 %collective-permute-start.8 = (bf16[3,64,640]{2,1,0:T(8,128)(2,1)S(1)}, bf16[3,64,640]{2,1,0:T(8,128)(2,1)S(1)}, u32[]{:S(2)}, u32[]{:S(2)}) collective-permute-start(bf16[3,64,640]{2,1,0:T(8,128)(2,1)S(1)} %collective-permute-done.5.refs_3_), channel_id=1, source_target_pairs={{0,2},{8,9},{2,4},{10,8},{4,6},{12,10},{6,7},{14,12},{7,5},{15,14}... | collective-permute-start | bytes 737288 | tf_op jit(solution)/shard_map/ppermute | solution.py:38
  19.2 1.7 %shard_map.108 = (bf16[2,640,5120]{2,1,0:T(8,128)(2,1)}, bf16[2,128,5120]{2,1,0:T(8,128)(2,1)}, bf16[2,128,5120]{2,1,0:T(8,128)(2,1)}) custom-call(bf16[2,640,64]{2,1,0:T(8,128)(2,1)S(1)} %get-tuple-element.70.refs_0_, bf16[2,128,64]{2,1,0:T(8,128)(2,1)S(1)} %get-tuple-element.71.refs_1_, ...), custom_call_target="tpu_custom_call", output_to_operand_aliasing={{0}: (8, {}), {1}: (9, {}), {2}: (10, {})} | custom-call | flops 146800640 | bytes 4587520 | tf_op jit(solution)/shard_map/pallas_call | solution.py:189
  20.9 0.1 collective-permute-start.15
  21.0 1.6 %collective-permute-start.14 = (bf16[3,64,640]{2,1,0:T(8,128)(2,1)S(1)}, bf16[3,64,640]{2,1,0:T(8,128)(2,1)S(1)}, u32[]{:S(2)}, u32[]{:S(2)}) collective-permute-start(bf16[3,64,640]{2,1,0:T(8,128)(2,1)S(1)} %collective-permute-done.10.refs_3_), channel_id=1, source_target_pairs={{0,2},{8,9},{2,4},{10,8},{4,6},{12,10},{6,7},{14,12},{7,5},{15,14}... | collective-permute-start | bytes 737288 | tf_op jit(solution)/shard_map/ppermute | solution.py:38
  22.5 1.7 %shard_map.109 = (bf16[2,640,5120]{2,1,0:T(8,128)(2,1)}, bf16[2,128,5120]{2,1,0:T(8,128)(2,1)}, bf16[2,128,5120]{2,1,0:T(8,128)(2,1)}) custom-call(bf16[2,640,64]{2,1,0:T(8,128)(2,1)S(1)} %get-tuple-element.70.refs_0_, bf16[2,128,64]{2,1,0:T(8,128)(2,1)S(1)} %get-tuple-element.71.refs_1_, ...), custom_call_target="tpu_custom_call", output_to_operand_aliasing={{0}: (8, {}), {1}: (9, {}), {2}: (10, {})} | custom-call | flops 146800640 | bytes 4587520 | tf_op jit(solution)/shard_map/pallas_call | solution.py:189
  24.2 0.1 collective-permute-start.13
  24.3 1.0 %collective-permute-start.12 = (bf16[3,64,640]{2,1,0:T(8,128)(2,1)S(1)}, bf16[3,64,640]{2,1,0:T(8,128)(2,1)S(1)}, u32[]{:S(2)}, u32[]{:S(2)}) collective-permute-start(bf16[3,64,640]{2,1,0:T(8,128)(2,1)S(1)} %collective-permute-done.8.refs_3_), channel_id=1, source_target_pairs={{0,2},{8,9},{2,4},{10,8},{4,6},{12,10},{6,7},{14,12},{7,5},{15,14}... | collective-permute-start | bytes 737288 | tf_op jit(solution)/shard_map/ppermute | solution.py:38
  25.4 1.7 %shard_map.110 = (bf16[2,640,5120]{2,1,0:T(8,128)(2,1)}, bf16[2,128,5120]{2,1,0:T(8,128)(2,1)}, bf16[2,128,5120]{2,1,0:T(8,128)(2,1)}) custom-call(bf16[2,640,64]{2,1,0:T(8,128)(2,1)S(1)} %get-tuple-element.70.refs_0_, bf16[2,128,64]{2,1,0:T(8,128)(2,1)S(1)} %get-tuple-element.71.refs_1_, ...), custom_call_target="tpu_custom_call", output_to_operand_aliasing={{0}: (8, {}), {1}: (9, {}), {2}: (10, {})} | custom-call | flops 146800640 | bytes 4587520 | tf_op jit(solution)/shard_map/pallas_call | solution.py:189
  27.1 0.1 collective-permute-done.14.refs_5_
  27.2 2.1 %shard_map.111 = (bf16[2,640,5120]{2,1,0:T(8,128)(2,1)}, bf16[2,128,5120]{2,1,0:T(8,128)(2,1)}, bf16[2,128,5120]{2,1,0:T(8,128)(2,1)}) custom-call(bf16[2,640,64]{2,1,0:T(8,128)(2,1)S(1)} %get-tuple-element.70.refs_0_, bf16[2,128,64]{2,1,0:T(8,128)(2,1)S(1)} %get-tuple-element.71.refs_1_, ...), custom_call_target="tpu_custom_call", output_to_operand_aliasing={{0}: (9, {}), {1}: (10, {}), {2}: (11, {})} | custom-call | flops 220200960 | bytes 6881280 | tf_op jit(solution)/shard_map/pallas_call | solution.py:189
  29.3 1.2 %collective-permute-done.12.refs_4_ = bf16[3,64,640]{2,1,0:T(8,128)(2,1)S(1)} collective-permute-done((bf16[3,64,640]{2,1,0:T(8,128)(2,1)S(1)}, bf16[3,64,640]{2,1,0:T(8,128)(2,1)S(1)}, u32[]{:S(2)}, u32[]{:S(2)}) %collective-permute-start.12) | collective-permute-done | bytes 245792 | tf_op jit(solution)/shard_map/ppermute | solution.py:38
  30.6 1.7 %shard_map.112 = (bf16[2,640,5120]{2,1,0:T(8,128)(2,1)}, bf16[2,128,5120]{2,1,0:T(8,128)(2,1)}, bf16[2,128,5120]{2,1,0:T(8,128)(2,1)}) custom-call(bf16[2,640,64]{2,1,0:T(8,128)(2,1)S(1)} %get-tuple-element.70.refs_0_, bf16[2,128,64]{2,1,0:T(8,128)(2,1)S(1)} %get-tuple-element.71.refs_1_, ...), custom_call_target="tpu_custom_call", output_to_operand_aliasing={{0}: (8, {}), {1}: (9, {}), {2}: (10, {})} | custom-call | flops 146800640 | bytes 4587520 | tf_op jit(solution)/shard_map/pallas_call | solution.py:189
  32.3 1.2 %shard_map.113 = (bf16[2,640,5120]{2,1,0:T(8,128)(2,1)}, bf16[2,128,5120]{2,1,0:T(8,128)(2,1)}, bf16[2,128,5120]{2,1,0:T(8,128)(2,1)}) custom-call(bf16[2,640,64]{2,1,0:T(8,128)(2,1)S(1)} %get-tuple-element.70.refs_0_, bf16[2,128,64]{2,1,0:T(8,128)(2,1)S(1)} %get-tuple-element.71.refs_1_, ...), custom_call_target="tpu_custom_call", output_to_operand_aliasing={{0}: (7, {}), {1}: (8, {}), {2}: (9, {})} | custom-call | flops 73400320 | bytes 2293760 | tf_op jit(solution)/shard_map/pallas_call | solution.py:189
  (38 shorter events, 0.1 us)
Async XLA Ops:
  0.6 2.3 %copy-start.2 = (bf16[1,2,3,64,640]{4,3,2,1,0:T(8,128)(2,1)S(1)}, bf16[1,2,3,64,640]{4,3,2,1,0:T(8,128)(2,1)}, u32[]{:S(2)}) copy-start(bf16[1,2,3,64,640]{4,3,2,1,0:T(8,128)(2,1)} %param.12) | copy-start | bytes 1474564
  0.6 2.3 %copy-start.6 = (s32[2,3]{1,0:T(2,128)S(1)}, s32[2,3]{1,0:T(2,128)}, u32[]{:S(2)}) copy-start(s32[2,3]{1,0:T(2,128)} %owners.3) | copy-start | bytes 76
  0.7 5.4 %copy-start.3 = (bf16[1,2,640,64]{2,3,1,0:T(8,128)(2,1)S(1)}, bf16[1,2,640,64]{2,3,1,0:T(8,128)(2,1)}, u32[]{:S(2)}) copy-start(bf16[1,2,640,64]{2,3,1,0:T(8,128)(2,1)} %param.13) | copy-start | bytes 491524
  0.7 5.4 %copy-start.4 = (bf16[1,2,128,64]{2,3,1,0:T(8,128)(2,1)S(1)}, bf16[1,2,128,64]{2,3,1,0:T(8,128)(2,1)}, u32[]{:S(2)}) copy-start(bf16[1,2,128,64]{2,3,1,0:T(8,128)(2,1)} %param.14) | copy-start | bytes 98308
  0.7 5.9 %copy-start.5 = (bf16[1,2,128,64]{2,3,1,0:T(8,128)(2,1)S(1)}, bf16[1,2,128,64]{2,3,1,0:T(8,128)(2,1)}, u32[]{:S(2)}) copy-start(bf16[1,2,128,64]{2,3,1,0:T(8,128)(2,1)} %param.15) | copy-start | bytes 98308
  0.7 2.2 %collective-permute-start = (bf16[2,3,64,640]{3,2,1,0:T(8,128)(2,1)}, bf16[2,3,64,640]{3,2,1,0:T(8,128)(2,1)S(1)}, u32[]{:S(2)}, u32[]{:S(2)}) collective-permute-start(bf16[2,3,64,640]{3,2,1,0:T(8,128)(2,1)} %bitcast.12), channel_id=1, source_target_pairs={{0,8},{8,0},{1,9},{9,1},{2,10},{10,2},{3,11},{11,3},{4,12},{12,4},... | collective-permute-start | bytes 1474568 | tf_op jit(solution)/shard_map/ppermute | solution.py:42
  1.2 14.5 %slice-start = ((s8[13107200]{0:T(1024)(128)(4,1)}), s8[4194304]{0:T(1024)(128)(4,1)S(1)}, s32[]{:S(2)}) async-start(s8[13107200]{0:T(1024)(128)(4,1)} %bitcast.10), calls=%async_computation | async-start | bytes 8388608
  1.2 14.5 %slice-start.1 = ((s8[13107200]{0:T(1024)(128)(4,1)}), s8[4194304]{0:T(1024)(128)(4,1)S(1)}, s32[]{:S(2)}) async-start(s8[13107200]{0:T(1024)(128)(4,1)} %bitcast.10), calls=%async_computation.1 | async-start | bytes 8388608
  1.2 14.5 %slice-start.2 = ((s8[13107200]{0:T(1024)(128)(4,1)}), s8[4194304]{0:T(1024)(128)(4,1)S(1)}, s32[]{:S(2)}) async-start(s8[13107200]{0:T(1024)(128)(4,1)} %bitcast.10), calls=%async_computation.2 | async-start | bytes 8388608
  3.1 7.6 %collective-permute-start.1 = (bf16[3,64,640]{2,1,0:T(8,128)(2,1)S(1)}, bf16[3,64,640]{2,1,0:T(8,128)(2,1)S(1)}, u32[]{:S(2)}, u32[]{:S(2)}) collective-permute-start(bf16[3,64,640]{2,1,0:T(8,128)(2,1)S(1)} %get-tuple-element.64.refs_3_), channel_id=1, source_target_pairs={{0,2},{8,9},{2,4},{10,8},{4,6},{12,10},{6,7},{14,12},{7,5},{15,14}... | collective-permute-start | bytes 737288 | tf_op jit(solution)/shard_map/ppermute | solution.py:38
  6.1 3.0 %collective-permute-start.2 = (bf16[2,64,640]{2,1,0:T(8,128)(2,1)S(1)}, bf16[2,64,640]{2,1,0:T(8,128)(2,1)S(1)}, u32[]{:S(2)}, u32[]{:S(2)}) collective-permute-start(bf16[2,64,640]{2,1,0:T(8,128)(2,1)S(1)} %bitcast.14), channel_id=1, source_target_pairs={{0,8},{8,0},{1,9},{9,1},{2,10},{10,2},{3,11},{11,3},{4,12},{12,4},... | collective-permute-start | bytes 491528 | tf_op jit(solution)/shard_map/ppermute | solution.py:42
  6.1 1.4 %collective-permute-start.3 = (bf16[2,64,128]{2,1,0:T(8,128)(2,1)S(1)}, bf16[2,64,128]{2,1,0:T(8,128)(2,1)S(1)}, u32[]{:S(2)}, u32[]{:S(2)}) collective-permute-start(bf16[2,64,128]{2,1,0:T(8,128)(2,1)S(1)} %bitcast.16), channel_id=1, source_target_pairs={{0,8},{8,0},{1,9},{9,1},{2,10},{10,2},{3,11},{11,3},{4,12},{12,4},... | collective-permute-start | bytes 98312 | tf_op jit(solution)/shard_map/ppermute | solution.py:42
  6.6 2.5 %collective-permute-start.4 = (bf16[2,64,128]{2,1,0:T(8,128)(2,1)S(1)}, bf16[2,64,128]{2,1,0:T(8,128)(2,1)S(1)}, u32[]{:S(2)}, u32[]{:S(2)}) collective-permute-start(bf16[2,64,128]{2,1,0:T(8,128)(2,1)S(1)} %bitcast.18), channel_id=1, source_target_pairs={{0,8},{8,0},{1,9},{9,1},{2,10},{10,2},{3,11},{11,3},{4,12},{12,4},... | collective-permute-start | bytes 98312 | tf_op jit(solution)/shard_map/ppermute | solution.py:42
  7.5 8.2 %slice-start.3 = ((s8[13107200]{0:T(1024)(128)(4,1)}), s8[524288]{0:T(1024)(128)(4,1)S(1)}, s32[]{:S(2)}) async-start(s8[13107200]{0:T(1024)(128)(4,1)} %bitcast.10), calls=%async_computation.3 | async-start | bytes 1048576
  7.5 6.5 %collective-permute-start.7 = (bf16[3,64,640]{2,1,0:T(8,128)(2,1)S(1)}, bf16[3,64,640]{2,1,0:T(8,128)(2,1)S(1)}, u32[]{:S(2)}, u32[]{:S(2)}) collective-permute-start(bf16[3,64,640]{2,1,0:T(8,128)(2,1)S(1)} %get-tuple-element.74.refs_4_), channel_id=1, source_target_pairs={{0,2},{8,9},{2,4},{10,8},{4,6},{12,10},{6,7},{14,12},{7,5},{15,14}... | collective-permute-start | bytes 737288 | tf_op jit(solution)/shard_map/ppermute | solution.py:38
  9.1 6.6 %copy-start.1 = (bf16[2,128,5120]{2,1,0:T(8,128)(2,1)S(1)}, bf16[2,128,5120]{2,1,0:T(8,128)(2,1)}, u32[]{:S(2)}) copy-start(bf16[2,128,5120]{2,1,0:T(8,128)(2,1)} %refs_6_.15) | copy-start | bytes 7864324
  10.6 5.1 %copy-start = (bf16[2,128,5120]{2,1,0:T(8,128)(2,1)S(1)}, bf16[2,128,5120]{2,1,0:T(8,128)(2,1)}, u32[]{:S(2)}) copy-start(bf16[2,128,5120]{2,1,0:T(8,128)(2,1)} %refs_5_.11) | copy-start | bytes 7864324
  10.6 5.1 %collective-permute-start.6 = (bf16[3,64,640]{2,1,0:T(8,128)(2,1)S(1)}, bf16[3,64,640]{2,1,0:T(8,128)(2,1)S(1)}, u32[]{:S(2)}, u32[]{:S(2)}) collective-permute-start(bf16[3,64,640]{2,1,0:T(8,128)(2,1)S(1)} %collective-permute-done.1.refs_3_), channel_id=1, source_target_pairs={{0,8},{8,0},{1,9},{9,1},{2,10},{10,2},{3,11},{11,3},{4,12},{12,4},... | collective-permute-start | bytes 737288 | tf_op jit(solution)/shard_map/ppermute | solution.py:42
  10.7 6.7 %collective-permute-start.5 = (bf16[3,64,640]{2,1,0:T(8,128)(2,1)S(1)}, bf16[3,64,640]{2,1,0:T(8,128)(2,1)S(1)}, u32[]{:S(2)}, u32[]{:S(2)}) collective-permute-start(bf16[3,64,640]{2,1,0:T(8,128)(2,1)S(1)} %collective-permute-done.1.refs_3_), channel_id=1, source_target_pairs={{0,2},{8,9},{2,4},{10,8},{4,6},{12,10},{6,7},{14,12},{7,5},{15,14}... | collective-permute-start | bytes 737288 | tf_op jit(solution)/shard_map/ppermute | solution.py:38
  14.0 5.1 %collective-permute-start.11 = (bf16[3,64,640]{2,1,0:T(8,128)(2,1)S(1)}, bf16[3,64,640]{2,1,0:T(8,128)(2,1)S(1)}, u32[]{:S(2)}, u32[]{:S(2)}) collective-permute-start(bf16[3,64,640]{2,1,0:T(8,128)(2,1)S(1)} %collective-permute-done.7.refs_3_), channel_id=1, source_target_pairs={{0,8},{8,0},{1,9},{9,1},{2,10},{10,2},{3,11},{11,3},{4,12},{12,4},... | collective-permute-start | bytes 737288 | tf_op jit(solution)/shard_map/ppermute | solution.py:42
  14.2 6.7 %collective-permute-start.10 = (bf16[3,64,640]{2,1,0:T(8,128)(2,1)S(1)}, bf16[3,64,640]{2,1,0:T(8,128)(2,1)S(1)}, u32[]{:S(2)}, u32[]{:S(2)}) collective-permute-start(bf16[3,64,640]{2,1,0:T(8,128)(2,1)S(1)} %collective-permute-done.7.refs_3_), channel_id=1, source_target_pairs={{0,2},{8,9},{2,4},{10,8},{4,6},{12,10},{6,7},{14,12},{7,5},{15,14}... | collective-permute-start | bytes 737288 | tf_op jit(solution)/shard_map/ppermute | solution.py:38
  17.5 5.1 %collective-permute-start.9 = (bf16[3,64,640]{2,1,0:T(8,128)(2,1)S(1)}, bf16[3,64,640]{2,1,0:T(8,128)(2,1)S(1)}, u32[]{:S(2)}, u32[]{:S(2)}) collective-permute-start(bf16[3,64,640]{2,1,0:T(8,128)(2,1)S(1)} %collective-permute-done.5.refs_3_), channel_id=1, source_target_pairs={{0,8},{8,0},{1,9},{9,1},{2,10},{10,2},{3,11},{11,3},{4,12},{12,4},... | collective-permute-start | bytes 737288 | tf_op jit(solution)/shard_map/ppermute | solution.py:42
  17.5 6.7 %collective-permute-start.8 = (bf16[3,64,640]{2,1,0:T(8,128)(2,1)S(1)}, bf16[3,64,640]{2,1,0:T(8,128)(2,1)S(1)}, u32[]{:S(2)}, u32[]{:S(2)}) collective-permute-start(bf16[3,64,640]{2,1,0:T(8,128)(2,1)S(1)} %collective-permute-done.5.refs_3_), channel_id=1, source_target_pairs={{0,2},{8,9},{2,4},{10,8},{4,6},{12,10},{6,7},{14,12},{7,5},{15,14}... | collective-permute-start | bytes 737288 | tf_op jit(solution)/shard_map/ppermute | solution.py:38
  20.9 4.5 %collective-permute-start.15 = (bf16[3,64,640]{2,1,0:T(8,128)(2,1)S(1)}, bf16[3,64,640]{2,1,0:T(8,128)(2,1)S(1)}, u32[]{:S(2)}, u32[]{:S(2)}) collective-permute-start(bf16[3,64,640]{2,1,0:T(8,128)(2,1)S(1)} %collective-permute-done.10.refs_3_), channel_id=1, source_target_pairs={{0,8},{8,0},{1,9},{9,1},{2,10},{10,2},{3,11},{11,3},{4,12},{12,4},... | collective-permute-start | bytes 737288 | tf_op jit(solution)/shard_map/ppermute | solution.py:42
  21.0 6.2 %collective-permute-start.14 = (bf16[3,64,640]{2,1,0:T(8,128)(2,1)S(1)}, bf16[3,64,640]{2,1,0:T(8,128)(2,1)S(1)}, u32[]{:S(2)}, u32[]{:S(2)}) collective-permute-start(bf16[3,64,640]{2,1,0:T(8,128)(2,1)S(1)} %collective-permute-done.10.refs_3_), channel_id=1, source_target_pairs={{0,2},{8,9},{2,4},{10,8},{4,6},{12,10},{6,7},{14,12},{7,5},{15,14}... | collective-permute-start | bytes 737288 | tf_op jit(solution)/shard_map/ppermute | solution.py:38
  24.2 3.0 %collective-permute-start.13 = (bf16[3,64,640]{2,1,0:T(8,128)(2,1)S(1)}, bf16[3,64,640]{2,1,0:T(8,128)(2,1)S(1)}, u32[]{:S(2)}, u32[]{:S(2)}) collective-permute-start(bf16[3,64,640]{2,1,0:T(8,128)(2,1)S(1)} %collective-permute-done.8.refs_3_), channel_id=1, source_target_pairs={{0,8},{8,0},{1,9},{9,1},{2,10},{10,2},{3,11},{11,3},{4,12},{12,4},... | collective-permute-start | bytes 737288 | tf_op jit(solution)/shard_map/ppermute | solution.py:42
  24.3 6.2 %collective-permute-start.12 = (bf16[3,64,640]{2,1,0:T(8,128)(2,1)S(1)}, bf16[3,64,640]{2,1,0:T(8,128)(2,1)S(1)}, u32[]{:S(2)}, u32[]{:S(2)}) collective-permute-start(bf16[3,64,640]{2,1,0:T(8,128)(2,1)S(1)} %collective-permute-done.8.refs_3_), channel_id=1, source_target_pairs={{0,2},{8,9},{2,4},{10,8},{4,6},{12,10},{6,7},{14,12},{7,5},{15,14}... | collective-permute-start | bytes 737288 | tf_op jit(solution)/shard_map/ppermute | solution.py:38
  27.2 3.4 %collective-permute-start.17 = (bf16[3,64,640]{2,1,0:T(8,128)(2,1)S(1)}, bf16[3,64,640]{2,1,0:T(8,128)(2,1)S(1)}, u32[]{:S(2)}, u32[]{:S(2)}) collective-permute-start(bf16[3,64,640]{2,1,0:T(8,128)(2,1)S(1)} %collective-permute-done.14.refs_5_), channel_id=1, source_target_pairs={{0,8},{8,0},{1,9},{9,1},{2,10},{10,2},{3,11},{11,3},{4,12},{12,4},... | collective-permute-start | bytes 737288 | tf_op jit(solution)/shard_map/ppermute | solution.py:42
  30.6 1.7 %collective-permute-start.16 = (bf16[3,64,640]{2,1,0:T(8,128)(2,1)S(1)}, bf16[3,64,640]{2,1,0:T(8,128)(2,1)S(1)}, u32[]{:S(2)}, u32[]{:S(2)}) collective-permute-start(bf16[3,64,640]{2,1,0:T(8,128)(2,1)S(1)} %collective-permute-done.12.refs_4_), channel_id=1, source_target_pairs={{0,8},{8,0},{1,9},{9,1},{2,10},{10,2},{3,11},{11,3},{4,12},{12,4},... | collective-permute-start | bytes 737288 | tf_op jit(solution)/shard_map/ppermute | solution.py:42

commit v12 on v11

--- a/solution.py
+++ b/solution.py
@@ -33,8 +33,9 @@
     order = ring_order(n)
     pairs = []
     for k in range(n):
-        pairs.append((order[k], order[(k + 1) % n]))
-        pairs.append((n + order[k], n + order[(k - 1) % n]))
+        up, down = k % 2, 1 - k % 2
+        pairs.append((up * n + order[k], (1 - up) * n + order[(k + 1) % n]))
+        pairs.append((down * n + order[k], (1 - down) * n + order[(k - 1) % n]))
     return lax.ppermute(array, ("rollout", "tensor"), pairs)
 
 
@@ -44,7 +45,7 @@
 
 def place_of(n, step, from_core, tensor):
     position = jnp.where(tensor % 2 == 0, tensor // 2, n - 1 - tensor // 2)
-    k = position + jnp.where(from_core == 0, -step, step)
+    k = position + jnp.where(from_core == position % 2, -step, step)
     k = jnp.where(k < 0, k + n, jnp.where(k >= n, k - n, k))
     return jnp.where(k < n // 2, 2 * k, 2 * n - 1 - 2 * k)
 
@@ -245,11 +246,12 @@
         for step in range(1, last):
             if step > 1:
                 outs = go(*waiting, outs)
-            pieces = [(step, True, True), (step, False, False)]
+            even = step % 2 == 0
+            pieces = [(step, True, even), (step, False, not even)]
             chunks = [first, swap_cores(first)]
             first = ring_pass(first, n)
             second, outs = tie((second, outs))
-            waiting = [(step, True, False), (step, False, True)], [second, swap_cores(second)]
+            waiting = [(step, True, not even), (step, False, even)], [second, swap_cores(second)]
             if step == last - 1:
                 pieces, chunks = pieces + waiting[0][:1], chunks + waiting[1][:1]
             outs = go(pieces, chunks, outs)
@@ -257,8 +259,9 @@
             if step < last - 1:
                 second = ring_pass(second, n)
         swapped = swap_cores(first)
-        outs = go([waiting[0][1], (last, True, True)], [waiting[1][1], first], outs)
-        return tuple(go([(last, False, False)], [swapped], outs))
+        even = last % 2 == 0
+        outs = go([waiting[0][1], (last, True, even)], [waiting[1][1], first], outs)
+        return tuple(go([(last, False, not even)], [swapped], outs))
 
     core = lax.axis_index("rollout")
     tensor = lax.axis_index("tensor")
@@ -276,13 +279,14 @@
     full = put(full, first, core, 0, core)
     full = put(full, second, 1 - core, 0, core)
     for step in range(1, last + 1):
+        layer = (core + step) % 2
         first = ring_pass(first, n)
-        full = put(full, first, core, step, core)
-        full = put(full, swap_cores(first), 1 - core, step, 1 - core)
+        full = put(full, first, layer, step, core)
+        full = put(full, swap_cores(first), 1 - layer, step, 1 - core)
         if step < last:
             second = ring_pass(second, n)
-            full = put(full, second, 1 - core, step, core)
-            full = put(full, swap_cores(second), core, step, 1 - core)
+            full = put(full, second, 1 - layer, step, core)
+            full = put(full, swap_cores(second), layer, step, 1 - core)
     merged = []
     for proj in range(projs):
         delta = jnp.einsum("lkr,lkc->lrc", b[proj], full[:, proj], preferred_element_type=jnp.float32)

time: 33.7 us -> 32.8 us (0.973)
  waiting for transfers between devices: 2.38 us -> 1.08 us
  starting transfers between devices: 13.5 us -> 14 us
    ppermute x11, starting transfers between devices: 1.56 us -> 3.78 us  [swap_cores(): return lax.ppermute(array, 'rollout', [(0, 1), (1, 0)])]
    ppermute x7, starting transfers between devices: 11.9 us -> 10.2 us  [ring_pass(): return lax.ppermute(array, ('rollout', 'tensor'), pairs)]
    ppermute x7, waiting for transfers between devices: 1.38 us -> 0.24 us  [ring_pass(): return lax.ppermute(array, ('rollout', 'tensor'), pairs)]
  transfers between devices with their start and end apart: 18 -> 18, of which waited for: 4 -> 3; matrix products, arithmetic and copies ran while one was open for 0% -> 0% of each run, Pallas kernels for 46% -> 47%
where the time goes in v12:
time: 32.8 us; the launch traced here: 32.7 us
  Pallas kernels  16.7 us (51%)
  starting transfers between devices  14 us (43%)
  waiting for transfers between devices  1.08 us (3%)
  between operations  0.88 us (3%)
    pallas_call x8, Pallas kernels, merge(): pl.pallas_call(functools.partial(merge_kernel, n, pieces, scale, fresh),...  13.5 us
    ppermute x7, starting transfers between devices, ring_pass(): return lax.ppermute(array, ('rollout', 'tensor'), pairs)  10.2 us
    ppermute x11, starting transfers between devices, swap_cores(): return lax.ppermute(array, 'rollout', [(0, 1), (1, 0)])  3.78 us
    pallas_call x1, Pallas kernels, fetch_blocks(): pl.pallas_call(functools.partial(fetch_kernel, n, pieces), in_specs=[HBM]...  1.56 us
    pallas_call x1, Pallas kernels, choose_b(): pl.pallas_call(functools.partial(choose_b_kernel, n, pieces), in_specs=[V...  1.5 us
    ppermute x11, waiting for transfers between devices, swap_cores(): return lax.ppermute(array, 'rollout', [(0, 1), (1, 0)])  0.84 us
  transfers between devices with their start and end apart: 18, of which 3 were waited for; matrix products, arithmetic and copies ran while one was open for 0% of the time, Pallas kernels for 47%

profile of v12, /device:TPU:0, one launch (start us, length us, event | category | flops | bytes accessed | tf_op | source)
XLA Modules:
  0.0 32.7 jit_solution(8040844950489546538)
XLA Ops:
  0.7 0.5 %collective-permute-start = (bf16[2,3,64,640]{3,2,1,0:T(8,128)(2,1)}, bf16[2,3,64,640]{3,2,1,0:T(8,128)(2,1)S(1)}, u32[]{:S(2)}, u32[]{:S(2)}) collective-permute-start(bf16[2,3,64,640]{3,2,1,0:T(8,128)(2,1)} %bitcast.12), channel_id=1, source_target_pairs={{0,8},{8,0},{1,9},{9,1},{2,10},{10,2},{3,11},{11,3},{4,12},{12,4},... | collective-permute-start | bytes 1474568 | tf_op jit(solution)/shard_map/ppermute | solution.py:43
  1.2 1.6 %shard_map.103.refs_5_ = bf16[2,640,640]{2,1,0:T(8,128)(2,1)S(1)} custom-call(bf16[2,640,5120]{2,1,0:T(8,128)(2,1)} %refs_4_.1), custom_call_target="tpu_custom_call" | custom-call | bytes 3276800 | tf_op jit(solution)/shard_map/pallas_call | solution.py:114
  2.8 0.1 collective-permute-done.other
  2.9 0.1 shard_map.104
  3.1 2.7 %collective-permute-start.1 = (bf16[3,64,640]{2,1,0:T(8,128)(2,1)S(1)}, bf16[3,64,640]{2,1,0:T(8,128)(2,1)S(1)}, u32[]{:S(2)}, u32[]{:S(2)}) collective-permute-start(bf16[3,64,640]{2,1,0:T(8,128)(2,1)S(1)} %get-tuple-element.64.refs_3_), channel_id=1, source_target_pairs={{0,10},{8,1},{10,4},{2,8},{4,14},{12,2},{14,7},{6,12},{7,13},{15,6... | collective-permute-start | bytes 737288 | tf_op jit(solution)/shard_map/ppermute | solution.py:39
  5.8 0.3 collective-permute-start.2
  6.1 0.2 collective-permute-start.3
  6.3 0.3 collective-permute-start.4
  6.6 0.7 %collective-permute-done.3.refs_4_ = bf16[2,64,128]{2,1,0:T(8,128)(2,1)S(1)} collective-permute-done((bf16[2,64,128]{2,1,0:T(8,128)(2,1)S(1)}, bf16[2,64,128]{2,1,0:T(8,128)(2,1)S(1)}, u32[]{:S(2)}, u32[]{:S(2)}) %collective-permute-start.3) | collective-permute-done | bytes 32800 | tf_op jit(solution)/shard_map/ppermute | solution.py:43
  7.3 1.5 %collective-permute-start.7 = (bf16[3,64,640]{2,1,0:T(8,128)(2,1)S(1)}, bf16[3,64,640]{2,1,0:T(8,128)(2,1)S(1)}, u32[]{:S(2)}, u32[]{:S(2)}) collective-permute-start(bf16[3,64,640]{2,1,0:T(8,128)(2,1)S(1)} %get-tuple-element.74.refs_4_), channel_id=1, source_target_pairs={{0,10},{8,1},{10,4},{2,8},{4,14},{12,2},{14,7},{6,12},{7,13},{15,6... | collective-permute-start | bytes 737288 | tf_op jit(solution)/shard_map/ppermute | solution.py:39
  8.8 1.5 %shard_map.105 = (bf16[2,640,64]{2,1,0:T(8,128)(2,1)S(1)}, bf16[2,128,64]{2,1,0:T(8,128)(2,1)S(1)}, bf16[2,128,64]{2,1,0:T(8,128)(2,1)S(1)}, bf16[2,128,640]{2,1,0:T(8,128)(2,1)S(1)}, bf16[2,128,640]{2,1,0:T(8,128)(2,1)S(1)}) custom-call(s32[2,3]{1,0:T(2,128)S(1)} %copy-done.6, bf16[2,64,640]{2,1,0:T(8,128)(2,1)S(1)} %bitcast.15, ...), custom_call_target="tpu_custom_call" | custom-call | bytes 1310720 | tf_op jit(solution)/shard_map/pallas_call | solution.py:142
  10.3 0.1 collective-permute-start.6
  10.5 1.3 %collective-permute-start.5 = (bf16[3,64,640]{2,1,0:T(8,128)(2,1)S(1)}, bf16[3,64,640]{2,1,0:T(8,128)(2,1)S(1)}, u32[]{:S(2)}, u32[]{:S(2)}) collective-permute-start(bf16[3,64,640]{2,1,0:T(8,128)(2,1)S(1)} %collective-permute-done.1.refs_3_), channel_id=1, source_target_pairs={{0,10},{8,1},{10,4},{2,8},{4,14},{12,2},{14,7},{6,12},{7,13},{15,6... | collective-permute-start | bytes 737288 | tf_op jit(solution)/shard_map/ppermute | solution.py:39
  11.8 1.7 %shard_map.106 = (bf16[2,640,5120]{2,1,0:T(8,128)(2,1)}, bf16[2,128,5120]{2,1,0:T(8,128)(2,1)}, bf16[2,128,5120]{2,1,0:T(8,128)(2,1)}) custom-call(bf16[2,640,64]{2,1,0:T(8,128)(2,1)S(1)} %get-tuple-element.70.refs_0_, bf16[2,128,64]{2,1,0:T(8,128)(2,1)S(1)} %get-tuple-element.71.refs_1_, bf16[2,128,64]{2,1,0:T(8,128)(2,1)S(1)} %get-tuple-element.72.refs_2_, ...), custom_call_target="tpu_custom_call" | custom-call | flops 146800640 | bytes 4587520 | tf_op jit(solution)/shard_map/pallas_call | solution.py:190
  13.5 0.4 %collective-permute-start.11 = (bf16[3,64,640]{2,1,0:T(8,128)(2,1)S(1)}, bf16[3,64,640]{2,1,0:T(8,128)(2,1)S(1)}, u32[]{:S(2)}, u32[]{:S(2)}) collective-permute-start(bf16[3,64,640]{2,1,0:T(8,128)(2,1)S(1)} %collective-permute-done.7.refs_3_), channel_id=1, source_target_pairs={{0,8},{8,0},{1,9},{9,1},{2,10},{10,2},{3,11},{11,3},{4,12},{12,4},... | collective-permute-start | bytes 737288 | tf_op jit(solution)/shard_map/ppermute | solution.py:43
  13.9 1.3 %collective-permute-start.10 = (bf16[3,64,640]{2,1,0:T(8,128)(2,1)S(1)}, bf16[3,64,640]{2,1,0:T(8,128)(2,1)S(1)}, u32[]{:S(2)}, u32[]{:S(2)}) collective-permute-start(bf16[3,64,640]{2,1,0:T(8,128)(2,1)S(1)} %collective-permute-done.7.refs_3_), channel_id=1, source_target_pairs={{0,10},{8,1},{10,4},{2,8},{4,14},{12,2},{14,7},{6,12},{7,13},{15,6... | collective-permute-start | bytes 737288 | tf_op jit(solution)/shard_map/ppermute | solution.py:39
  15.3 1.7 %shard_map.107 = (bf16[2,640,5120]{2,1,0:T(8,128)(2,1)}, bf16[2,128,5120]{2,1,0:T(8,128)(2,1)}, bf16[2,128,5120]{2,1,0:T(8,128)(2,1)}) custom-call(bf16[2,640,64]{2,1,0:T(8,128)(2,1)S(1)} %get-tuple-element.70.refs_0_, bf16[2,128,64]{2,1,0:T(8,128)(2,1)S(1)} %get-tuple-element.71.refs_1_, ...), custom_call_target="tpu_custom_call", output_to_operand_aliasing={{0}: (8, {}), {1}: (9, {}), {2}: (10, {})} | custom-call | flops 146800640 | bytes 4587520 | tf_op jit(solution)/shard_map/pallas_call | solution.py:190
  17.0 0.1 collective-permute-start.9
  17.1 1.3 %collective-permute-start.8 = (bf16[3,64,640]{2,1,0:T(8,128)(2,1)S(1)}, bf16[3,64,640]{2,1,0:T(8,128)(2,1)S(1)}, u32[]{:S(2)}, u32[]{:S(2)}) collective-permute-start(bf16[3,64,640]{2,1,0:T(8,128)(2,1)S(1)} %collective-permute-done.5.refs_3_), channel_id=1, source_target_pairs={{0,10},{8,1},{10,4},{2,8},{4,14},{12,2},{14,7},{6,12},{7,13},{15,6... | collective-permute-start | bytes 737288 | tf_op jit(solution)/shard_map/ppermute | solution.py:39
  18.4 1.7 %shard_map.108 = (bf16[2,640,5120]{2,1,0:T(8,128)(2,1)}, bf16[2,128,5120]{2,1,0:T(8,128)(2,1)}, bf16[2,128,5120]{2,1,0:T(8,128)(2,1)}) custom-call(bf16[2,640,64]{2,1,0:T(8,128)(2,1)S(1)} %get-tuple-element.70.refs_0_, bf16[2,128,64]{2,1,0:T(8,128)(2,1)S(1)} %get-tuple-element.71.refs_1_, ...), custom_call_target="tpu_custom_call", output_to_operand_aliasing={{0}: (8, {}), {1}: (9, {}), {2}: (10, {})} | custom-call | flops 146800640 | bytes 4587520 | tf_op jit(solution)/shard_map/pallas_call | solution.py:190
  20.1 0.4 %collective-permute-start.15 = (bf16[3,64,640]{2,1,0:T(8,128)(2,1)S(1)}, bf16[3,64,640]{2,1,0:T(8,128)(2,1)S(1)}, u32[]{:S(2)}, u32[]{:S(2)}) collective-permute-start(bf16[3,64,640]{2,1,0:T(8,128)(2,1)S(1)} %collective-permute-done.10.refs_3_), channel_id=1, source_target_pairs={{0,8},{8,0},{1,9},{9,1},{2,10},{10,2},{3,11},{11,3},{4,12},{12,4},... | collective-permute-start | bytes 737288 | tf_op jit(solution)/shard_map/ppermute | solution.py:43
  20.6 1.2 %collective-permute-start.14 = (bf16[3,64,640]{2,1,0:T(8,128)(2,1)S(1)}, bf16[3,64,640]{2,1,0:T(8,128)(2,1)S(1)}, u32[]{:S(2)}, u32[]{:S(2)}) collective-permute-start(bf16[3,64,640]{2,1,0:T(8,128)(2,1)S(1)} %collective-permute-done.10.refs_3_), channel_id=1, source_target_pairs={{0,10},{8,1},{10,4},{2,8},{4,14},{12,2},{14,7},{6,12},{7,13},{15,6... | collective-permute-start | bytes 737288 | tf_op jit(solution)/shard_map/ppermute | solution.py:39
  21.8 1.7 %shard_map.109 = (bf16[2,640,5120]{2,1,0:T(8,128)(2,1)}, bf16[2,128,5120]{2,1,0:T(8,128)(2,1)}, bf16[2,128,5120]{2,1,0:T(8,128)(2,1)}) custom-call(bf16[2,640,64]{2,1,0:T(8,128)(2,1)S(1)} %get-tuple-element.70.refs_0_, bf16[2,128,64]{2,1,0:T(8,128)(2,1)S(1)} %get-tuple-element.71.refs_1_, ...), custom_call_target="tpu_custom_call", output_to_operand_aliasing={{0}: (8, {}), {1}: (9, {}), {2}: (10, {})} | custom-call | flops 146800640 | bytes 4587520 | tf_op jit(solution)/shard_map/pallas_call | solution.py:190
  23.5 0.1 collective-permute-start.13
  23.7 0.8 %collective-permute-start.12 = (bf16[3,64,640]{2,1,0:T(8,128)(2,1)S(1)}, bf16[3,64,640]{2,1,0:T(8,128)(2,1)S(1)}, u32[]{:S(2)}, u32[]{:S(2)}) collective-permute-start(bf16[3,64,640]{2,1,0:T(8,128)(2,1)S(1)} %collective-permute-done.8.refs_3_), channel_id=1, source_target_pairs={{0,10},{8,1},{10,4},{2,8},{4,14},{12,2},{14,7},{6,12},{7,13},{15,6... | collective-permute-start | bytes 737288 | tf_op jit(solution)/shard_map/ppermute | solution.py:39
  24.5 1.7 %shard_map.110 = (bf16[2,640,5120]{2,1,0:T(8,128)(2,1)}, bf16[2,128,5120]{2,1,0:T(8,128)(2,1)}, bf16[2,128,5120]{2,1,0:T(8,128)(2,1)}) custom-call(bf16[2,640,64]{2,1,0:T(8,128)(2,1)S(1)} %get-tuple-element.70.refs_0_, bf16[2,128,64]{2,1,0:T(8,128)(2,1)S(1)} %get-tuple-element.71.refs_1_, ...), custom_call_target="tpu_custom_call", output_to_operand_aliasing={{0}: (8, {}), {1}: (9, {}), {2}: (10, {})} | custom-call | flops 146800640 | bytes 4587520 | tf_op jit(solution)/shard_map/pallas_call | solution.py:190
  26.2 0.7 %collective-permute-start.17 = (bf16[3,64,640]{2,1,0:T(8,128)(2,1)S(1)}, bf16[3,64,640]{2,1,0:T(8,128)(2,1)S(1)}, u32[]{:S(2)}, u32[]{:S(2)}) collective-permute-start(bf16[3,64,640]{2,1,0:T(8,128)(2,1)S(1)} %collective-permute-done.14.refs_5_), channel_id=1, source_target_pairs={{0,8},{8,0},{1,9},{9,1},{2,10},{10,2},{3,11},{11,3},{4,12},{12,4},... | collective-permute-start | bytes 737288 | tf_op jit(solution)/shard_map/ppermute | solution.py:43
  26.9 2.1 %shard_map.111 = (bf16[2,640,5120]{2,1,0:T(8,128)(2,1)}, bf16[2,128,5120]{2,1,0:T(8,128)(2,1)}, bf16[2,128,5120]{2,1,0:T(8,128)(2,1)}) custom-call(bf16[2,640,64]{2,1,0:T(8,128)(2,1)S(1)} %get-tuple-element.70.refs_0_, bf16[2,128,64]{2,1,0:T(8,128)(2,1)S(1)} %get-tuple-element.71.refs_1_, ...), custom_call_target="tpu_custom_call", output_to_operand_aliasing={{0}: (9, {}), {1}: (10, {}), {2}: (11, {})} | custom-call | flops 220200960 | bytes 6881280 | tf_op jit(solution)/shard_map/pallas_call | solution.py:190
  29.1 0.2 collective-permute-done.12.refs_4_
  29.3 0.4 %collective-permute-start.16 = (bf16[3,64,640]{2,1,0:T(8,128)(2,1)S(1)}, bf16[3,64,640]{2,1,0:T(8,128)(2,1)S(1)}, u32[]{:S(2)}, u32[]{:S(2)}) collective-permute-start(bf16[3,64,640]{2,1,0:T(8,128)(2,1)S(1)} %collective-permute-done.12.refs_4_), channel_id=1, source_target_pairs={{0,8},{8,0},{1,9},{9,1},{2,10},{10,2},{3,11},{11,3},{4,12},{12,4},... | collective-permute-start | bytes 737288 | tf_op jit(solution)/shard_map/ppermute | solution.py:43
  29.7 1.7 %shard_map.112 = (bf16[2,640,5120]{2,1,0:T(8,128)(2,1)}, bf16[2,128,5120]{2,1,0:T(8,128)(2,1)}, bf16[2,128,5120]{2,1,0:T(8,128)(2,1)}) custom-call(bf16[2,640,64]{2,1,0:T(8,128)(2,1)S(1)} %get-tuple-element.70.refs_0_, bf16[2,128,64]{2,1,0:T(8,128)(2,1)S(1)} %get-tuple-element.71.refs_1_, ...), custom_call_target="tpu_custom_call", output_to_operand_aliasing={{0}: (8, {}), {1}: (9, {}), {2}: (10, {})} | custom-call | flops 146800640 | bytes 4587520 | tf_op jit(solution)/shard_map/pallas_call | solution.py:190
  31.4 1.2 %shard_map.113 = (bf16[2,640,5120]{2,1,0:T(8,128)(2,1)}, bf16[2,128,5120]{2,1,0:T(8,128)(2,1)}, bf16[2,128,5120]{2,1,0:T(8,128)(2,1)}) custom-call(bf16[2,640,64]{2,1,0:T(8,128)(2,1)S(1)} %get-tuple-element.70.refs_0_, bf16[2,128,64]{2,1,0:T(8,128)(2,1)S(1)} %get-tuple-element.71.refs_1_, ...), custom_call_target="tpu_custom_call", output_to_operand_aliasing={{0}: (7, {}), {1}: (8, {}), {2}: (9, {})} | custom-call | flops 73400320 | bytes 2293760 | tf_op jit(solution)/shard_map/pallas_call | solution.py:190
  (38 shorter events, 0.1 us)
Async XLA Ops:
  0.6 2.3 %copy-start.2 = (bf16[1,2,3,64,640]{4,3,2,1,0:T(8,128)(2,1)S(1)}, bf16[1,2,3,64,640]{4,3,2,1,0:T(8,128)(2,1)}, u32[]{:S(2)}) copy-start(bf16[1,2,3,64,640]{4,3,2,1,0:T(8,128)(2,1)} %param.12) | copy-start | bytes 1474564
  0.6 2.3 %copy-start.6 = (s32[2,3]{1,0:T(2,128)S(1)}, s32[2,3]{1,0:T(2,128)}, u32[]{:S(2)}) copy-start(s32[2,3]{1,0:T(2,128)} %owners.3) | copy-start | bytes 76
  0.7 5.2 %copy-start.3 = (bf16[1,2,640,64]{2,3,1,0:T(8,128)(2,1)S(1)}, bf16[1,2,640,64]{2,3,1,0:T(8,128)(2,1)}, u32[]{:S(2)}) copy-start(bf16[1,2,640,64]{2,3,1,0:T(8,128)(2,1)} %param.13) | copy-start | bytes 491524
  0.7 5.5 %copy-start.4 = (bf16[1,2,128,64]{2,3,1,0:T(8,128)(2,1)S(1)}, bf16[1,2,128,64]{2,3,1,0:T(8,128)(2,1)}, u32[]{:S(2)}) copy-start(bf16[1,2,128,64]{2,3,1,0:T(8,128)(2,1)} %param.14) | copy-start | bytes 98308
  0.7 5.6 %copy-start.5 = (bf16[1,2,128,64]{2,3,1,0:T(8,128)(2,1)S(1)}, bf16[1,2,128,64]{2,3,1,0:T(8,128)(2,1)}, u32[]{:S(2)}) copy-start(bf16[1,2,128,64]{2,3,1,0:T(8,128)(2,1)} %param.15) | copy-start | bytes 98308
  0.7 2.2 %collective-permute-start = (bf16[2,3,64,640]{3,2,1,0:T(8,128)(2,1)}, bf16[2,3,64,640]{3,2,1,0:T(8,128)(2,1)S(1)}, u32[]{:S(2)}, u32[]{:S(2)}) collective-permute-start(bf16[2,3,64,640]{3,2,1,0:T(8,128)(2,1)} %bitcast.12), channel_id=1, source_target_pairs={{0,8},{8,0},{1,9},{9,1},{2,10},{10,2},{3,11},{11,3},{4,12},{12,4},... | collective-permute-start | bytes 1474568 | tf_op jit(solution)/shard_map/ppermute | solution.py:43
  1.2 14.1 %slice-start = ((s8[13107200]{0:T(1024)(128)(4,1)}), s8[4194304]{0:T(1024)(128)(4,1)S(1)}, s32[]{:S(2)}) async-start(s8[13107200]{0:T(1024)(128)(4,1)} %bitcast.10), calls=%async_computation | async-start | bytes 8388608
  1.2 14.1 %slice-start.1 = ((s8[13107200]{0:T(1024)(128)(4,1)}), s8[4194304]{0:T(1024)(128)(4,1)S(1)}, s32[]{:S(2)}) async-start(s8[13107200]{0:T(1024)(128)(4,1)} %bitcast.10), calls=%async_computation.1 | async-start | bytes 8388608
  1.2 14.1 %slice-start.2 = ((s8[13107200]{0:T(1024)(128)(4,1)}), s8[4194304]{0:T(1024)(128)(4,1)S(1)}, s32[]{:S(2)}) async-start(s8[13107200]{0:T(1024)(128)(4,1)} %bitcast.10), calls=%async_computation.2 | async-start | bytes 8388608
  3.1 7.3 %collective-permute-start.1 = (bf16[3,64,640]{2,1,0:T(8,128)(2,1)S(1)}, bf16[3,64,640]{2,1,0:T(8,128)(2,1)S(1)}, u32[]{:S(2)}, u32[]{:S(2)}) collective-permute-start(bf16[3,64,640]{2,1,0:T(8,128)(2,1)S(1)} %get-tuple-element.64.refs_3_), channel_id=1, source_target_pairs={{0,10},{8,1},{10,4},{2,8},{4,14},{12,2},{14,7},{6,12},{7,13},{15,6... | collective-permute-start | bytes 737288 | tf_op jit(solution)/shard_map/ppermute | solution.py:39
  5.8 3.0 %collective-permute-start.2 = (bf16[2,64,640]{2,1,0:T(8,128)(2,1)S(1)}, bf16[2,64,640]{2,1,0:T(8,128)(2,1)S(1)}, u32[]{:S(2)}, u32[]{:S(2)}) collective-permute-start(bf16[2,64,640]{2,1,0:T(8,128)(2,1)S(1)} %bitcast.14), channel_id=1, source_target_pairs={{0,8},{8,0},{1,9},{9,1},{2,10},{10,2},{3,11},{11,3},{4,12},{12,4},... | collective-permute-start | bytes 491528 | tf_op jit(solution)/shard_map/ppermute | solution.py:43
  6.1 1.2 %collective-permute-start.3 = (bf16[2,64,128]{2,1,0:T(8,128)(2,1)S(1)}, bf16[2,64,128]{2,1,0:T(8,128)(2,1)S(1)}, u32[]{:S(2)}, u32[]{:S(2)}) collective-permute-start(bf16[2,64,128]{2,1,0:T(8,128)(2,1)S(1)} %bitcast.16), channel_id=1, source_target_pairs={{0,8},{8,0},{1,9},{9,1},{2,10},{10,2},{3,11},{11,3},{4,12},{12,4},... | collective-permute-start | bytes 98312 | tf_op jit(solution)/shard_map/ppermute | solution.py:43
  6.3 2.5 %collective-permute-start.4 = (bf16[2,64,128]{2,1,0:T(8,128)(2,1)S(1)}, bf16[2,64,128]{2,1,0:T(8,128)(2,1)S(1)}, u32[]{:S(2)}, u32[]{:S(2)}) collective-permute-start(bf16[2,64,128]{2,1,0:T(8,128)(2,1)S(1)} %bitcast.18), channel_id=1, source_target_pairs={{0,8},{8,0},{1,9},{9,1},{2,10},{10,2},{3,11},{11,3},{4,12},{12,4},... | collective-permute-start | bytes 98312 | tf_op jit(solution)/shard_map/ppermute | solution.py:43
  7.3 7.9 %slice-start.3 = ((s8[13107200]{0:T(1024)(128)(4,1)}), s8[524288]{0:T(1024)(128)(4,1)S(1)}, s32[]{:S(2)}) async-start(s8[13107200]{0:T(1024)(128)(4,1)} %bitcast.10), calls=%async_computation.3 | async-start | bytes 1048576
  7.3 6.2 %collective-permute-start.7 = (bf16[3,64,640]{2,1,0:T(8,128)(2,1)S(1)}, bf16[3,64,640]{2,1,0:T(8,128)(2,1)S(1)}, u32[]{:S(2)}, u32[]{:S(2)}) collective-permute-start(bf16[3,64,640]{2,1,0:T(8,128)(2,1)S(1)} %get-tuple-element.74.refs_4_), channel_id=1, source_target_pairs={{0,10},{8,1},{10,4},{2,8},{4,14},{12,2},{14,7},{6,12},{7,13},{15,6... | collective-permute-start | bytes 737288 | tf_op jit(solution)/shard_map/ppermute | solution.py:39
  8.8 6.5 %copy-start.1 = (bf16[2,128,5120]{2,1,0:T(8,128)(2,1)S(1)}, bf16[2,128,5120]{2,1,0:T(8,128)(2,1)}, u32[]{:S(2)}) copy-start(bf16[2,128,5120]{2,1,0:T(8,128)(2,1)} %refs_6_.15) | copy-start | bytes 7864324
  10.3 5.0 %copy-start = (bf16[2,128,5120]{2,1,0:T(8,128)(2,1)S(1)}, bf16[2,128,5120]{2,1,0:T(8,128)(2,1)}, u32[]{:S(2)}) copy-start(bf16[2,128,5120]{2,1,0:T(8,128)(2,1)} %refs_5_.11) | copy-start | bytes 7864324
  10.3 4.9 %collective-permute-start.6 = (bf16[3,64,640]{2,1,0:T(8,128)(2,1)S(1)}, bf16[3,64,640]{2,1,0:T(8,128)(2,1)S(1)}, u32[]{:S(2)}, u32[]{:S(2)}) collective-permute-start(bf16[3,64,640]{2,1,0:T(8,128)(2,1)S(1)} %collective-permute-done.1.refs_3_), channel_id=1, source_target_pairs={{0,8},{8,0},{1,9},{9,1},{2,10},{10,2},{3,11},{11,3},{4,12},{12,4},... | collective-permute-start | bytes 737288 | tf_op jit(solution)/shard_map/ppermute | solution.py:43
  10.5 6.5 %collective-permute-start.5 = (bf16[3,64,640]{2,1,0:T(8,128)(2,1)S(1)}, bf16[3,64,640]{2,1,0:T(8,128)(2,1)S(1)}, u32[]{:S(2)}, u32[]{:S(2)}) collective-permute-start(bf16[3,64,640]{2,1,0:T(8,128)(2,1)S(1)} %collective-permute-done.1.refs_3_), channel_id=1, source_target_pairs={{0,10},{8,1},{10,4},{2,8},{4,14},{12,2},{14,7},{6,12},{7,13},{15,6... | collective-permute-start | bytes 737288 | tf_op jit(solution)/shard_map/ppermute | solution.py:39
  13.5 4.9 %collective-permute-start.11 = (bf16[3,64,640]{2,1,0:T(8,128)(2,1)S(1)}, bf16[3,64,640]{2,1,0:T(8,128)(2,1)S(1)}, u32[]{:S(2)}, u32[]{:S(2)}) collective-permute-start(bf16[3,64,640]{2,1,0:T(8,128)(2,1)S(1)} %collective-permute-done.7.refs_3_), channel_id=1, source_target_pairs={{0,8},{8,0},{1,9},{9,1},{2,10},{10,2},{3,11},{11,3},{4,12},{12,4},... | collective-permute-start | bytes 737288 | tf_op jit(solution)/shard_map/ppermute | solution.py:43
  13.9 6.2 %collective-permute-start.10 = (bf16[3,64,640]{2,1,0:T(8,128)(2,1)S(1)}, bf16[3,64,640]{2,1,0:T(8,128)(2,1)S(1)}, u32[]{:S(2)}, u32[]{:S(2)}) collective-permute-start(bf16[3,64,640]{2,1,0:T(8,128)(2,1)S(1)} %collective-permute-done.7.refs_3_), channel_id=1, source_target_pairs={{0,10},{8,1},{10,4},{2,8},{4,14},{12,2},{14,7},{6,12},{7,13},{15,6... | collective-permute-start | bytes 737288 | tf_op jit(solution)/shard_map/ppermute | solution.py:39
  17.0 4.8 %collective-permute-start.9 = (bf16[3,64,640]{2,1,0:T(8,128)(2,1)S(1)}, bf16[3,64,640]{2,1,0:T(8,128)(2,1)S(1)}, u32[]{:S(2)}, u32[]{:S(2)}) collective-permute-start(bf16[3,64,640]{2,1,0:T(8,128)(2,1)S(1)} %collective-permute-done.5.refs_3_), channel_id=1, source_target_pairs={{0,8},{8,0},{1,9},{9,1},{2,10},{10,2},{3,11},{11,3},{4,12},{12,4},... | collective-permute-start | bytes 737288 | tf_op jit(solution)/shard_map/ppermute | solution.py:43
  17.1 6.4 %collective-permute-start.8 = (bf16[3,64,640]{2,1,0:T(8,128)(2,1)S(1)}, bf16[3,64,640]{2,1,0:T(8,128)(2,1)S(1)}, u32[]{:S(2)}, u32[]{:S(2)}) collective-permute-start(bf16[3,64,640]{2,1,0:T(8,128)(2,1)S(1)} %collective-permute-done.5.refs_3_), channel_id=1, source_target_pairs={{0,10},{8,1},{10,4},{2,8},{4,14},{12,2},{14,7},{6,12},{7,13},{15,6... | collective-permute-start | bytes 737288 | tf_op jit(solution)/shard_map/ppermute | solution.py:39
  20.1 4.4 %collective-permute-start.15 = (bf16[3,64,640]{2,1,0:T(8,128)(2,1)S(1)}, bf16[3,64,640]{2,1,0:T(8,128)(2,1)S(1)}, u32[]{:S(2)}, u32[]{:S(2)}) collective-permute-start(bf16[3,64,640]{2,1,0:T(8,128)(2,1)S(1)} %collective-permute-done.10.refs_3_), channel_id=1, source_target_pairs={{0,8},{8,0},{1,9},{9,1},{2,10},{10,2},{3,11},{11,3},{4,12},{12,4},... | collective-permute-start | bytes 737288 | tf_op jit(solution)/shard_map/ppermute | solution.py:43
  20.6 5.6 %collective-permute-start.14 = (bf16[3,64,640]{2,1,0:T(8,128)(2,1)S(1)}, bf16[3,64,640]{2,1,0:T(8,128)(2,1)S(1)}, u32[]{:S(2)}, u32[]{:S(2)}) collective-permute-start(bf16[3,64,640]{2,1,0:T(8,128)(2,1)S(1)} %collective-permute-done.10.refs_3_), channel_id=1, source_target_pairs={{0,10},{8,1},{10,4},{2,8},{4,14},{12,2},{14,7},{6,12},{7,13},{15,6... | collective-permute-start | bytes 737288 | tf_op jit(solution)/shard_map/ppermute | solution.py:39
  23.5 3.4 %collective-permute-start.13 = (bf16[3,64,640]{2,1,0:T(8,128)(2,1)S(1)}, bf16[3,64,640]{2,1,0:T(8,128)(2,1)S(1)}, u32[]{:S(2)}, u32[]{:S(2)}) collective-permute-start(bf16[3,64,640]{2,1,0:T(8,128)(2,1)S(1)} %collective-permute-done.8.refs_3_), channel_id=1, source_target_pairs={{0,8},{8,0},{1,9},{9,1},{2,10},{10,2},{3,11},{11,3},{4,12},{12,4},... | collective-permute-start | bytes 737288 | tf_op jit(solution)/shard_map/ppermute | solution.py:43
  23.7 5.6 %collective-permute-start.12 = (bf16[3,64,640]{2,1,0:T(8,128)(2,1)S(1)}, bf16[3,64,640]{2,1,0:T(8,128)(2,1)S(1)}, u32[]{:S(2)}, u32[]{:S(2)}) collective-permute-start(bf16[3,64,640]{2,1,0:T(8,128)(2,1)S(1)} %collective-permute-done.8.refs_3_), channel_id=1, source_target_pairs={{0,10},{8,1},{10,4},{2,8},{4,14},{12,2},{14,7},{6,12},{7,13},{15,6... | collective-permute-start | bytes 737288 | tf_op jit(solution)/shard_map/ppermute | solution.py:39
  26.2 3.5 %collective-permute-start.17 = (bf16[3,64,640]{2,1,0:T(8,128)(2,1)S(1)}, bf16[3,64,640]{2,1,0:T(8,128)(2,1)S(1)}, u32[]{:S(2)}, u32[]{:S(2)}) collective-permute-start(bf16[3,64,640]{2,1,0:T(8,128)(2,1)S(1)} %collective-permute-done.14.refs_5_), channel_id=1, source_target_pairs={{0,8},{8,0},{1,9},{9,1},{2,10},{10,2},{3,11},{11,3},{4,12},{12,4},... | collective-permute-start | bytes 737288 | tf_op jit(solution)/shard_map/ppermute | solution.py:43
  29.3 2.1 %collective-permute-start.16 = (bf16[3,64,640]{2,1,0:T(8,128)(2,1)S(1)}, bf16[3,64,640]{2,1,0:T(8,128)(2,1)S(1)}, u32[]{:S(2)}, u32[]{:S(2)}) collective-permute-start(bf16[3,64,640]{2,1,0:T(8,128)(2,1)S(1)} %collective-permute-done.12.refs_4_), channel_id=1, source_target_pairs={{0,8},{8,0},{1,9},{9,1},{2,10},{10,2},{3,11},{11,3},{4,12},{12,4},... | collective-permute-start | bytes 737288 | tf_op jit(solution)/shard_map/ppermute | solution.py:43

commit v13 on v12

--- a/solution.py
+++ b/solution.py
@@ -239,29 +239,29 @@
         first, b = tie((first, b))
         outs = merge(n, scale, b, held, [*query_block, *blocks], shapes, None, pieces)
 
-        def go(pieces, chunks, outs):
-            return merge(n, scale, b, chunks, bases, shapes, outs, pieces)
-
-        waiting = None
+        def go(outs, *named):
+            pieces = [(step, not swapped, ((step % 2 == 0) == (ring == "a")) != swapped) for step, ring, swapped, _ in named]
+            return merge(n, scale, b, [chunk for *_, chunk in named], bases, shapes, outs, pieces)
+
+        swapped_a = swapped_b = None
         for step in range(1, last):
+            a_here = (step, "a", False, first)
+            a_there = (step, "a", True, swap_cores(first))
+            first = ring_pass(first, n)
             if step > 1:
-                outs = go(*waiting, outs)
-            even = step % 2 == 0
-            pieces = [(step, True, even), (step, False, not even)]
-            chunks = [first, swap_cores(first)]
-            first = ring_pass(first, n)
+                outs = go(outs, a_here, swapped_a)
             second, outs = tie((second, outs))
-            waiting = [(step, True, not even), (step, False, even)], [second, swap_cores(second)]
-            if step == last - 1:
-                pieces, chunks = pieces + waiting[0][:1], chunks + waiting[1][:1]
-            outs = go(pieces, chunks, outs)
-            first, outs = tie((first, outs))
+            b_here = (step, "b", False, second)
+            b_there = (step, "b", True, swap_cores(second))
             if step < last - 1:
                 second = ring_pass(second, n)
-        swapped = swap_cores(first)
-        even = last % 2 == 0
-        outs = go([waiting[0][1], (last, True, even)], [waiting[1][1], first], outs)
-        return tuple(go([(last, False, not even)], [swapped], outs))
+            batch = [b_here, a_here if step == 1 else swapped_b]
+            outs = go(outs, *batch, *([a_there] if step == last - 1 else []))
+            first, outs = tie((first, outs))
+            swapped_a, swapped_b = a_there, b_there
+        a_there = (last, "a", True, swap_cores(first))
+        outs = go(outs, swapped_b, (last, "a", False, first))
+        return tuple(go(outs, a_there))
 
     core = lax.axis_index("rollout")
     tensor = lax.axis_index("tensor")

time: 32.8 us -> 32.7 us (level)
  starting transfers between devices: 14 us -> 13.1 us
  waiting for transfers between devices: 1.08 us -> 1.8 us
    ppermute x11, starting transfers between devices: 3.78 us -> 3.05 us  [swap_cores(): return lax.ppermute(array, 'rollout', [(0, 1), (1, 0)])]
    ppermute x7, waiting for transfers between devices: 0.24 us -> 0.96 us  [ring_pass(): return lax.ppermute(array, ('rollout', 'tensor'), pairs)]
where the time goes in v13:
time: 32.7 us; the launch traced here: 32.6 us
  Pallas kernels  16.7 us (51%)
  starting transfers between devices  13.1 us (40%)
  waiting for transfers between devices  1.8 us (6%)
  between operations  0.89 us (3%)
    pallas_call x8, Pallas kernels, merge(): pl.pallas_call(functools.partial(merge_kernel, n, pieces, scale, fresh),...  13.5 us
    ppermute x7, starting transfers between devices, ring_pass(): return lax.ppermute(array, ('rollout', 'tensor'), pairs)  10.1 us
    ppermute x11, starting transfers between devices, swap_cores(): return lax.ppermute(array, 'rollout', [(0, 1), (1, 0)])  3.05 us
    pallas_call x1, Pallas kernels, fetch_blocks(): pl.pallas_call(functools.partial(fetch_kernel, n, pieces), in_specs=[HBM]...  1.56 us
    pallas_call x1, Pallas kernels, choose_b(): pl.pallas_call(functools.partial(choose_b_kernel, n, pieces), in_specs=[V...  1.5 us
    ppermute x7, waiting for transfers between devices, ring_pass(): return lax.ppermute(array, ('rollout', 'tensor'), pairs)  0.96 us
    ppermute x11, waiting for transfers between devices, swap_cores(): return lax.ppermute(array, 'rollout', [(0, 1), (1, 0)])  0.84 us
  transfers between devices with their start and end apart: 18, of which 3 were waited for; matrix products, arithmetic and copies ran while one was open for 0% of the time, Pallas kernels for 47%

profile of v13, /device:TPU:0, one launch (start us, length us, event | category | flops | bytes accessed | tf_op | source)
XLA Modules:
  0.0 32.6 jit_solution(15820473366194400875)
XLA Ops:
  0.7 0.5 %collective-permute-start = (bf16[2,3,64,640]{3,2,1,0:T(8,128)(2,1)}, bf16[2,3,64,640]{3,2,1,0:T(8,128)(2,1)S(1)}, u32[]{:S(2)}, u32[]{:S(2)}) collective-permute-start(bf16[2,3,64,640]{3,2,1,0:T(8,128)(2,1)} %bitcast.12), channel_id=1, source_target_pairs={{0,8},{8,0},{1,9},{9,1},{2,10},{10,2},{3,11},{11,3},{4,12},{12,4},... | collective-permute-start | bytes 1474568 | tf_op jit(solution)/shard_map/ppermute | solution.py:43
  1.2 1.6 %shard_map.103.refs_5_ = bf16[2,640,640]{2,1,0:T(8,128)(2,1)S(1)} custom-call(bf16[2,640,5120]{2,1,0:T(8,128)(2,1)} %refs_4_.1), custom_call_target="tpu_custom_call" | custom-call | bytes 3276800 | tf_op jit(solution)/shard_map/pallas_call | solution.py:114
  2.8 0.1 collective-permute-done.other
  2.9 0.1 shard_map.104
  3.1 2.7 %collective-permute-start.1 = (bf16[3,64,640]{2,1,0:T(8,128)(2,1)S(1)}, bf16[3,64,640]{2,1,0:T(8,128)(2,1)S(1)}, u32[]{:S(2)}, u32[]{:S(2)}) collective-permute-start(bf16[3,64,640]{2,1,0:T(8,128)(2,1)S(1)} %get-tuple-element.64.refs_3_), channel_id=1, source_target_pairs={{0,10},{8,1},{10,4},{2,8},{4,14},{12,2},{14,7},{6,12},{7,13},{15,6... | collective-permute-start | bytes 737288 | tf_op jit(solution)/shard_map/ppermute | solution.py:39
  5.8 0.3 collective-permute-start.2
  6.1 0.2 collective-permute-start.3
  6.3 0.3 collective-permute-start.4
  6.6 0.7 %collective-permute-done.3.refs_4_ = bf16[2,64,128]{2,1,0:T(8,128)(2,1)S(1)} collective-permute-done((bf16[2,64,128]{2,1,0:T(8,128)(2,1)S(1)}, bf16[2,64,128]{2,1,0:T(8,128)(2,1)S(1)}, u32[]{:S(2)}, u32[]{:S(2)}) %collective-permute-start.3) | collective-permute-done | bytes 32800 | tf_op jit(solution)/shard_map/ppermute | solution.py:43
  7.3 1.5 %collective-permute-start.6 = (bf16[3,64,640]{2,1,0:T(8,128)(2,1)S(1)}, bf16[3,64,640]{2,1,0:T(8,128)(2,1)S(1)}, u32[]{:S(2)}, u32[]{:S(2)}) collective-permute-start(bf16[3,64,640]{2,1,0:T(8,128)(2,1)S(1)} %get-tuple-element.74.refs_4_), channel_id=1, source_target_pairs={{0,10},{8,1},{10,4},{2,8},{4,14},{12,2},{14,7},{6,12},{7,13},{15,6... | collective-permute-start | bytes 737288 | tf_op jit(solution)/shard_map/ppermute | solution.py:39
  8.8 1.5 %shard_map.105 = (bf16[2,640,64]{2,1,0:T(8,128)(2,1)S(1)}, bf16[2,128,64]{2,1,0:T(8,128)(2,1)S(1)}, bf16[2,128,64]{2,1,0:T(8,128)(2,1)S(1)}, bf16[2,128,640]{2,1,0:T(8,128)(2,1)S(1)}, bf16[2,128,640]{2,1,0:T(8,128)(2,1)S(1)}) custom-call(s32[2,3]{1,0:T(2,128)S(1)} %copy-done.6, bf16[2,64,640]{2,1,0:T(8,128)(2,1)S(1)} %bitcast.15, ...), custom_call_target="tpu_custom_call" | custom-call | bytes 1310720 | tf_op jit(solution)/shard_map/pallas_call | solution.py:142
  10.3 1.4 %collective-permute-start.5 = (bf16[3,64,640]{2,1,0:T(8,128)(2,1)S(1)}, bf16[3,64,640]{2,1,0:T(8,128)(2,1)S(1)}, u32[]{:S(2)}, u32[]{:S(2)}) collective-permute-start(bf16[3,64,640]{2,1,0:T(8,128)(2,1)S(1)} %collective-permute-done.1.refs_4_), channel_id=1, source_target_pairs={{0,10},{8,1},{10,4},{2,8},{4,14},{12,2},{14,7},{6,12},{7,13},{15,6... | collective-permute-start | bytes 737288 | tf_op jit(solution)/shard_map/ppermute | solution.py:39
  11.7 0.3 collective-permute-start.9
  12.0 1.7 %shard_map.106 = (bf16[2,640,5120]{2,1,0:T(8,128)(2,1)}, bf16[2,128,5120]{2,1,0:T(8,128)(2,1)}, bf16[2,128,5120]{2,1,0:T(8,128)(2,1)}) custom-call(bf16[2,640,64]{2,1,0:T(8,128)(2,1)S(1)} %get-tuple-element.70.refs_0_, bf16[2,128,64]{2,1,0:T(8,128)(2,1)S(1)} %get-tuple-element.71.refs_1_, bf16[2,128,64]{2,1,0:T(8,128)(2,1)S(1)} %get-tuple-element.72.refs_2_, ...), custom_call_target="tpu_custom_call" | custom-call | flops 146800640 | bytes 4587520 | tf_op jit(solution)/shard_map/pallas_call | solution.py:190
  13.7 1.2 %collective-permute-start.8 = (bf16[3,64,640]{2,1,0:T(8,128)(2,1)S(1)}, bf16[3,64,640]{2,1,0:T(8,128)(2,1)S(1)}, u32[]{:S(2)}, u32[]{:S(2)}) collective-permute-start(bf16[3,64,640]{2,1,0:T(8,128)(2,1)S(1)} %collective-permute-done.6.refs_3_), channel_id=1, source_target_pairs={{0,10},{8,1},{10,4},{2,8},{4,14},{12,2},{14,7},{6,12},{7,13},{15,6... | collective-permute-start | bytes 737288 | tf_op jit(solution)/shard_map/ppermute | solution.py:39
  15.0 0.1 collective-permute-start.10
  15.2 1.7 %shard_map.107 = (bf16[2,640,5120]{2,1,0:T(8,128)(2,1)}, bf16[2,128,5120]{2,1,0:T(8,128)(2,1)}, bf16[2,128,5120]{2,1,0:T(8,128)(2,1)}) custom-call(bf16[2,640,64]{2,1,0:T(8,128)(2,1)S(1)} %get-tuple-element.70.refs_0_, bf16[2,128,64]{2,1,0:T(8,128)(2,1)S(1)} %get-tuple-element.71.refs_1_, ...), custom_call_target="tpu_custom_call", output_to_operand_aliasing={{0}: (8, {}), {1}: (9, {}), {2}: (10, {})} | custom-call | flops 146800640 | bytes 4587520 | tf_op jit(solution)/shard_map/pallas_call | solution.py:190
  16.9 1.3 %collective-permute-start.7 = (bf16[3,64,640]{2,1,0:T(8,128)(2,1)S(1)}, bf16[3,64,640]{2,1,0:T(8,128)(2,1)S(1)}, u32[]{:S(2)}, u32[]{:S(2)}) collective-permute-start(bf16[3,64,640]{2,1,0:T(8,128)(2,1)S(1)} %collective-permute-done.5.refs_3_), channel_id=1, source_target_pairs={{0,10},{8,1},{10,4},{2,8},{4,14},{12,2},{14,7},{6,12},{7,13},{15,6... | collective-permute-start | bytes 737288 | tf_op jit(solution)/shard_map/ppermute | solution.py:39
  18.2 0.0 collective-permute-start.13
  18.2 1.7 %shard_map.108 = (bf16[2,640,5120]{2,1,0:T(8,128)(2,1)}, bf16[2,128,5120]{2,1,0:T(8,128)(2,1)}, bf16[2,128,5120]{2,1,0:T(8,128)(2,1)}) custom-call(bf16[2,640,64]{2,1,0:T(8,128)(2,1)S(1)} %get-tuple-element.70.refs_0_, bf16[2,128,64]{2,1,0:T(8,128)(2,1)S(1)} %get-tuple-element.71.refs_1_, ...), custom_call_target="tpu_custom_call", output_to_operand_aliasing={{0}: (8, {}), {1}: (9, {}), {2}: (10, {})} | custom-call | flops 146800640 | bytes 4587520 | tf_op jit(solution)/shard_map/pallas_call | solution.py:190
  19.9 0.5 %collective-permute-start.14 = (bf16[3,64,640]{2,1,0:T(8,128)(2,1)S(1)}, bf16[3,64,640]{2,1,0:T(8,128)(2,1)S(1)}, u32[]{:S(2)}, u32[]{:S(2)}) collective-permute-start(bf16[3,64,640]{2,1,0:T(8,128)(2,1)S(1)} %collective-permute-done.8.refs_3_), channel_id=1, source_target_pairs={{0,8},{8,0},{1,9},{9,1},{2,10},{10,2},{3,11},{11,3},{4,12},{12,4},... | collective-permute-start | bytes 737288 | tf_op jit(solution)/shard_map/ppermute | solution.py:43
  20.5 1.2 %collective-permute-start.12 = (bf16[3,64,640]{2,1,0:T(8,128)(2,1)S(1)}, bf16[3,64,640]{2,1,0:T(8,128)(2,1)S(1)}, u32[]{:S(2)}, u32[]{:S(2)}) collective-permute-start(bf16[3,64,640]{2,1,0:T(8,128)(2,1)S(1)} %collective-permute-done.8.refs_3_), channel_id=1, source_target_pairs={{0,10},{8,1},{10,4},{2,8},{4,14},{12,2},{14,7},{6,12},{7,13},{15,6... | collective-permute-start | bytes 737288 | tf_op jit(solution)/shard_map/ppermute | solution.py:39
  21.7 1.7 %shard_map.109 = (bf16[2,640,5120]{2,1,0:T(8,128)(2,1)}, bf16[2,128,5120]{2,1,0:T(8,128)(2,1)}, bf16[2,128,5120]{2,1,0:T(8,128)(2,1)}) custom-call(bf16[2,640,64]{2,1,0:T(8,128)(2,1)S(1)} %get-tuple-element.70.refs_0_, bf16[2,128,64]{2,1,0:T(8,128)(2,1)S(1)} %get-tuple-element.71.refs_1_, ...), custom_call_target="tpu_custom_call", output_to_operand_aliasing={{0}: (8, {}), {1}: (9, {}), {2}: (10, {})} | custom-call | flops 146800640 | bytes 4587520 | tf_op jit(solution)/shard_map/pallas_call | solution.py:190
  23.4 0.5 %collective-permute-start.15 = (bf16[3,64,640]{2,1,0:T(8,128)(2,1)S(1)}, bf16[3,64,640]{2,1,0:T(8,128)(2,1)S(1)}, u32[]{:S(2)}, u32[]{:S(2)}) collective-permute-start(bf16[3,64,640]{2,1,0:T(8,128)(2,1)S(1)} %collective-permute-done.7.refs_3_), channel_id=1, source_target_pairs={{0,8},{8,0},{1,9},{9,1},{2,10},{10,2},{3,11},{11,3},{4,12},{12,4},... | collective-permute-start | bytes 737288 | tf_op jit(solution)/shard_map/ppermute | solution.py:43
  23.9 0.7 %collective-permute-start.11 = (bf16[3,64,640]{2,1,0:T(8,128)(2,1)S(1)}, bf16[3,64,640]{2,1,0:T(8,128)(2,1)S(1)}, u32[]{:S(2)}, u32[]{:S(2)}) collective-permute-start(bf16[3,64,640]{2,1,0:T(8,128)(2,1)S(1)} %collective-permute-done.7.refs_3_), channel_id=1, source_target_pairs={{0,10},{8,1},{10,4},{2,8},{4,14},{12,2},{14,7},{6,12},{7,13},{15,6... | collective-permute-start | bytes 737288 | tf_op jit(solution)/shard_map/ppermute | solution.py:39
  24.6 1.7 %shard_map.110 = (bf16[2,640,5120]{2,1,0:T(8,128)(2,1)}, bf16[2,128,5120]{2,1,0:T(8,128)(2,1)}, bf16[2,128,5120]{2,1,0:T(8,128)(2,1)}) custom-call(bf16[2,640,64]{2,1,0:T(8,128)(2,1)S(1)} %get-tuple-element.70.refs_0_, bf16[2,128,64]{2,1,0:T(8,128)(2,1)S(1)} %get-tuple-element.71.refs_1_, ...), custom_call_target="tpu_custom_call", output_to_operand_aliasing={{0}: (8, {}), {1}: (9, {}), {2}: (10, {})} | custom-call | flops 146800640 | bytes 4587520 | tf_op jit(solution)/shard_map/pallas_call | solution.py:190
  26.3 0.1 collective-permute-start.17
  26.4 2.1 %shard_map.111 = (bf16[2,640,5120]{2,1,0:T(8,128)(2,1)}, bf16[2,128,5120]{2,1,0:T(8,128)(2,1)}, bf16[2,128,5120]{2,1,0:T(8,128)(2,1)}) custom-call(bf16[2,640,64]{2,1,0:T(8,128)(2,1)S(1)} %get-tuple-element.70.refs_0_, bf16[2,128,64]{2,1,0:T(8,128)(2,1)S(1)} %get-tuple-element.71.refs_1_, ...), custom_call_target="tpu_custom_call", output_to_operand_aliasing={{0}: (9, {}), {1}: (10, {}), {2}: (11, {})} | custom-call | flops 220200960 | bytes 6881280 | tf_op jit(solution)/shard_map/pallas_call | solution.py:190
  28.6 0.9 %collective-permute-done.11.refs_4_ = bf16[3,64,640]{2,1,0:T(8,128)(2,1)S(1)} collective-permute-done((bf16[3,64,640]{2,1,0:T(8,128)(2,1)S(1)}, bf16[3,64,640]{2,1,0:T(8,128)(2,1)S(1)}, u32[]{:S(2)}, u32[]{:S(2)}) %collective-permute-start.11) | collective-permute-done | bytes 245792 | tf_op jit(solution)/shard_map/ppermute | solution.py:39
  29.5 0.1 collective-permute-start.16
  29.6 1.7 %shard_map.112 = (bf16[2,640,5120]{2,1,0:T(8,128)(2,1)}, bf16[2,128,5120]{2,1,0:T(8,128)(2,1)}, bf16[2,128,5120]{2,1,0:T(8,128)(2,1)}) custom-call(bf16[2,640,64]{2,1,0:T(8,128)(2,1)S(1)} %get-tuple-element.70.refs_0_, bf16[2,128,64]{2,1,0:T(8,128)(2,1)S(1)} %get-tuple-element.71.refs_1_, ...), custom_call_target="tpu_custom_call", output_to_operand_aliasing={{0}: (8, {}), {1}: (9, {}), {2}: (10, {})} | custom-call | flops 146800640 | bytes 4587520 | tf_op jit(solution)/shard_map/pallas_call | solution.py:190
  31.3 1.2 %shard_map.113 = (bf16[2,640,5120]{2,1,0:T(8,128)(2,1)}, bf16[2,128,5120]{2,1,0:T(8,128)(2,1)}, bf16[2,128,5120]{2,1,0:T(8,128)(2,1)}) custom-call(bf16[2,640,64]{2,1,0:T(8,128)(2,1)S(1)} %get-tuple-element.70.refs_0_, bf16[2,128,64]{2,1,0:T(8,128)(2,1)S(1)} %get-tuple-element.71.refs_1_, ...), custom_call_target="tpu_custom_call", output_to_operand_aliasing={{0}: (7, {}), {1}: (8, {}), {2}: (9, {})} | custom-call | flops 73400320 | bytes 2293760 | tf_op jit(solution)/shard_map/pallas_call | solution.py:190
  (38 shorter events, 0.1 us)
Async XLA Ops:
  0.6 2.3 %copy-start.2 = (bf16[1,2,3,64,640]{4,3,2,1,0:T(8,128)(2,1)S(1)}, bf16[1,2,3,64,640]{4,3,2,1,0:T(8,128)(2,1)}, u32[]{:S(2)}) copy-start(bf16[1,2,3,64,640]{4,3,2,1,0:T(8,128)(2,1)} %param.12) | copy-start | bytes 1474564
  0.6 2.3 %copy-start.6 = (s32[2,3]{1,0:T(2,128)S(1)}, s32[2,3]{1,0:T(2,128)}, u32[]{:S(2)}) copy-start(s32[2,3]{1,0:T(2,128)} %owners.3) | copy-start | bytes 76
  0.7 5.2 %copy-start.3 = (bf16[1,2,640,64]{2,3,1,0:T(8,128)(2,1)S(1)}, bf16[1,2,640,64]{2,3,1,0:T(8,128)(2,1)}, u32[]{:S(2)}) copy-start(bf16[1,2,640,64]{2,3,1,0:T(8,128)(2,1)} %param.13) | copy-start | bytes 491524
  0.7 5.5 %copy-start.4 = (bf16[1,2,128,64]{2,3,1,0:T(8,128)(2,1)S(1)}, bf16[1,2,128,64]{2,3,1,0:T(8,128)(2,1)}, u32[]{:S(2)}) copy-start(bf16[1,2,128,64]{2,3,1,0:T(8,128)(2,1)} %param.14) | copy-start | bytes 98308
  0.7 5.6 %copy-start.5 = (bf16[1,2,128,64]{2,3,1,0:T(8,128)(2,1)S(1)}, bf16[1,2,128,64]{2,3,1,0:T(8,128)(2,1)}, u32[]{:S(2)}) copy-start(bf16[1,2,128,64]{2,3,1,0:T(8,128)(2,1)} %param.15) | copy-start | bytes 98308
  0.7 2.2 %collective-permute-start = (bf16[2,3,64,640]{3,2,1,0:T(8,128)(2,1)}, bf16[2,3,64,640]{3,2,1,0:T(8,128)(2,1)S(1)}, u32[]{:S(2)}, u32[]{:S(2)}) collective-permute-start(bf16[2,3,64,640]{3,2,1,0:T(8,128)(2,1)} %bitcast.12), channel_id=1, source_target_pairs={{0,8},{8,0},{1,9},{9,1},{2,10},{10,2},{3,11},{11,3},{4,12},{12,4},... | collective-permute-start | bytes 1474568 | tf_op jit(solution)/shard_map/ppermute | solution.py:43
  1.2 13.9 %slice-start = ((s8[13107200]{0:T(1024)(128)(4,1)}), s8[4194304]{0:T(1024)(128)(4,1)S(1)}, s32[]{:S(2)}) async-start(s8[13107200]{0:T(1024)(128)(4,1)} %bitcast.10), calls=%async_computation | async-start | bytes 8388608
  1.2 13.9 %slice-start.1 = ((s8[13107200]{0:T(1024)(128)(4,1)}), s8[4194304]{0:T(1024)(128)(4,1)S(1)}, s32[]{:S(2)}) async-start(s8[13107200]{0:T(1024)(128)(4,1)} %bitcast.10), calls=%async_computation.1 | async-start | bytes 8388608
  1.2 13.9 %slice-start.2 = ((s8[13107200]{0:T(1024)(128)(4,1)}), s8[4194304]{0:T(1024)(128)(4,1)S(1)}, s32[]{:S(2)}) async-start(s8[13107200]{0:T(1024)(128)(4,1)} %bitcast.10), calls=%async_computation.2 | async-start | bytes 8388608
  3.1 7.3 %collective-permute-start.1 = (bf16[3,64,640]{2,1,0:T(8,128)(2,1)S(1)}, bf16[3,64,640]{2,1,0:T(8,128)(2,1)S(1)}, u32[]{:S(2)}, u32[]{:S(2)}) collective-permute-start(bf16[3,64,640]{2,1,0:T(8,128)(2,1)S(1)} %get-tuple-element.64.refs_3_), channel_id=1, source_target_pairs={{0,10},{8,1},{10,4},{2,8},{4,14},{12,2},{14,7},{6,12},{7,13},{15,6... | collective-permute-start | bytes 737288 | tf_op jit(solution)/shard_map/ppermute | solution.py:39
  5.8 3.0 %collective-permute-start.2 = (bf16[2,64,640]{2,1,0:T(8,128)(2,1)S(1)}, bf16[2,64,640]{2,1,0:T(8,128)(2,1)S(1)}, u32[]{:S(2)}, u32[]{:S(2)}) collective-permute-start(bf16[2,64,640]{2,1,0:T(8,128)(2,1)S(1)} %bitcast.14), channel_id=1, source_target_pairs={{0,8},{8,0},{1,9},{9,1},{2,10},{10,2},{3,11},{11,3},{4,12},{12,4},... | collective-permute-start | bytes 491528 | tf_op jit(solution)/shard_map/ppermute | solution.py:43
  6.1 1.2 %collective-permute-start.3 = (bf16[2,64,128]{2,1,0:T(8,128)(2,1)S(1)}, bf16[2,64,128]{2,1,0:T(8,128)(2,1)S(1)}, u32[]{:S(2)}, u32[]{:S(2)}) collective-permute-start(bf16[2,64,128]{2,1,0:T(8,128)(2,1)S(1)} %bitcast.16), channel_id=1, source_target_pairs={{0,8},{8,0},{1,9},{9,1},{2,10},{10,2},{3,11},{11,3},{4,12},{12,4},... | collective-permute-start | bytes 98312 | tf_op jit(solution)/shard_map/ppermute | solution.py:43
  6.3 2.5 %collective-permute-start.4 = (bf16[2,64,128]{2,1,0:T(8,128)(2,1)S(1)}, bf16[2,64,128]{2,1,0:T(8,128)(2,1)S(1)}, u32[]{:S(2)}, u32[]{:S(2)}) collective-permute-start(bf16[2,64,128]{2,1,0:T(8,128)(2,1)S(1)} %bitcast.18), channel_id=1, source_target_pairs={{0,8},{8,0},{1,9},{9,1},{2,10},{10,2},{3,11},{11,3},{4,12},{12,4},... | collective-permute-start | bytes 98312 | tf_op jit(solution)/shard_map/ppermute | solution.py:43
  7.3 7.8 %slice-start.3 = ((s8[13107200]{0:T(1024)(128)(4,1)}), s8[524288]{0:T(1024)(128)(4,1)S(1)}, s32[]{:S(2)}) async-start(s8[13107200]{0:T(1024)(128)(4,1)} %bitcast.10), calls=%async_computation.3 | async-start | bytes 1048576
  7.3 6.4 %collective-permute-start.6 = (bf16[3,64,640]{2,1,0:T(8,128)(2,1)S(1)}, bf16[3,64,640]{2,1,0:T(8,128)(2,1)S(1)}, u32[]{:S(2)}, u32[]{:S(2)}) collective-permute-start(bf16[3,64,640]{2,1,0:T(8,128)(2,1)S(1)} %get-tuple-element.74.refs_4_), channel_id=1, source_target_pairs={{0,10},{8,1},{10,4},{2,8},{4,14},{12,2},{14,7},{6,12},{7,13},{15,6... | collective-permute-start | bytes 737288 | tf_op jit(solution)/shard_map/ppermute | solution.py:39
  8.8 6.3 %copy-start.1 = (bf16[2,128,5120]{2,1,0:T(8,128)(2,1)S(1)}, bf16[2,128,5120]{2,1,0:T(8,128)(2,1)}, u32[]{:S(2)}) copy-start(bf16[2,128,5120]{2,1,0:T(8,128)(2,1)} %refs_6_.15) | copy-start | bytes 7864324
  10.3 4.8 %copy-start = (bf16[2,128,5120]{2,1,0:T(8,128)(2,1)S(1)}, bf16[2,128,5120]{2,1,0:T(8,128)(2,1)}, u32[]{:S(2)}) copy-start(bf16[2,128,5120]{2,1,0:T(8,128)(2,1)} %refs_5_.11) | copy-start | bytes 7864324
  10.3 6.5 %collective-permute-start.5 = (bf16[3,64,640]{2,1,0:T(8,128)(2,1)S(1)}, bf16[3,64,640]{2,1,0:T(8,128)(2,1)S(1)}, u32[]{:S(2)}, u32[]{:S(2)}) collective-permute-start(bf16[3,64,640]{2,1,0:T(8,128)(2,1)S(1)} %collective-permute-done.1.refs_4_), channel_id=1, source_target_pairs={{0,10},{8,1},{10,4},{2,8},{4,14},{12,2},{14,7},{6,12},{7,13},{15,6... | collective-permute-start | bytes 737288 | tf_op jit(solution)/shard_map/ppermute | solution.py:39
  11.7 6.5 %collective-permute-start.9 = (bf16[3,64,640]{2,1,0:T(8,128)(2,1)S(1)}, bf16[3,64,640]{2,1,0:T(8,128)(2,1)S(1)}, u32[]{:S(2)}, u32[]{:S(2)}) collective-permute-start(bf16[3,64,640]{2,1,0:T(8,128)(2,1)S(1)} %collective-permute-done.1.refs_4_), channel_id=1, source_target_pairs={{0,8},{8,0},{1,9},{9,1},{2,10},{10,2},{3,11},{11,3},{4,12},{12,4},... | collective-permute-start | bytes 737288 | tf_op jit(solution)/shard_map/ppermute | solution.py:43
  13.7 6.2 %collective-permute-start.8 = (bf16[3,64,640]{2,1,0:T(8,128)(2,1)S(1)}, bf16[3,64,640]{2,1,0:T(8,128)(2,1)S(1)}, u32[]{:S(2)}, u32[]{:S(2)}) collective-permute-start(bf16[3,64,640]{2,1,0:T(8,128)(2,1)S(1)} %collective-permute-done.6.refs_3_), channel_id=1, source_target_pairs={{0,10},{8,1},{10,4},{2,8},{4,14},{12,2},{14,7},{6,12},{7,13},{15,6... | collective-permute-start | bytes 737288 | tf_op jit(solution)/shard_map/ppermute | solution.py:39
  15.0 6.7 %collective-permute-start.10 = (bf16[3,64,640]{2,1,0:T(8,128)(2,1)S(1)}, bf16[3,64,640]{2,1,0:T(8,128)(2,1)S(1)}, u32[]{:S(2)}, u32[]{:S(2)}) collective-permute-start(bf16[3,64,640]{2,1,0:T(8,128)(2,1)S(1)} %collective-permute-done.6.refs_3_), channel_id=1, source_target_pairs={{0,8},{8,0},{1,9},{9,1},{2,10},{10,2},{3,11},{11,3},{4,12},{12,4},... | collective-permute-start | bytes 737288 | tf_op jit(solution)/shard_map/ppermute | solution.py:43
  16.9 6.5 %collective-permute-start.7 = (bf16[3,64,640]{2,1,0:T(8,128)(2,1)S(1)}, bf16[3,64,640]{2,1,0:T(8,128)(2,1)S(1)}, u32[]{:S(2)}, u32[]{:S(2)}) collective-permute-start(bf16[3,64,640]{2,1,0:T(8,128)(2,1)S(1)} %collective-permute-done.5.refs_3_), channel_id=1, source_target_pairs={{0,10},{8,1},{10,4},{2,8},{4,14},{12,2},{14,7},{6,12},{7,13},{15,6... | collective-permute-start | bytes 737288 | tf_op jit(solution)/shard_map/ppermute | solution.py:39
  18.2 6.4 %collective-permute-start.13 = (bf16[3,64,640]{2,1,0:T(8,128)(2,1)S(1)}, bf16[3,64,640]{2,1,0:T(8,128)(2,1)S(1)}, u32[]{:S(2)}, u32[]{:S(2)}) collective-permute-start(bf16[3,64,640]{2,1,0:T(8,128)(2,1)S(1)} %collective-permute-done.5.refs_3_), channel_id=1, source_target_pairs={{0,8},{8,0},{1,9},{9,1},{2,10},{10,2},{3,11},{11,3},{4,12},{12,4},... | collective-permute-start | bytes 737288 | tf_op jit(solution)/shard_map/ppermute | solution.py:43
  19.9 6.5 %collective-permute-start.14 = (bf16[3,64,640]{2,1,0:T(8,128)(2,1)S(1)}, bf16[3,64,640]{2,1,0:T(8,128)(2,1)S(1)}, u32[]{:S(2)}, u32[]{:S(2)}) collective-permute-start(bf16[3,64,640]{2,1,0:T(8,128)(2,1)S(1)} %collective-permute-done.8.refs_3_), channel_id=1, source_target_pairs={{0,8},{8,0},{1,9},{9,1},{2,10},{10,2},{3,11},{11,3},{4,12},{12,4},... | collective-permute-start | bytes 737288 | tf_op jit(solution)/shard_map/ppermute | solution.py:43
  20.5 5.9 %collective-permute-start.12 = (bf16[3,64,640]{2,1,0:T(8,128)(2,1)S(1)}, bf16[3,64,640]{2,1,0:T(8,128)(2,1)S(1)}, u32[]{:S(2)}, u32[]{:S(2)}) collective-permute-start(bf16[3,64,640]{2,1,0:T(8,128)(2,1)S(1)} %collective-permute-done.8.refs_3_), channel_id=1, source_target_pairs={{0,10},{8,1},{10,4},{2,8},{4,14},{12,2},{14,7},{6,12},{7,13},{15,6... | collective-permute-start | bytes 737288 | tf_op jit(solution)/shard_map/ppermute | solution.py:39
  23.4 3.0 %collective-permute-start.15 = (bf16[3,64,640]{2,1,0:T(8,128)(2,1)S(1)}, bf16[3,64,640]{2,1,0:T(8,128)(2,1)S(1)}, u32[]{:S(2)}, u32[]{:S(2)}) collective-permute-start(bf16[3,64,640]{2,1,0:T(8,128)(2,1)S(1)} %collective-permute-done.7.refs_3_), channel_id=1, source_target_pairs={{0,8},{8,0},{1,9},{9,1},{2,10},{10,2},{3,11},{11,3},{4,12},{12,4},... | collective-permute-start | bytes 737288 | tf_op jit(solution)/shard_map/ppermute | solution.py:43
  23.9 5.6 %collective-permute-start.11 = (bf16[3,64,640]{2,1,0:T(8,128)(2,1)S(1)}, bf16[3,64,640]{2,1,0:T(8,128)(2,1)S(1)}, u32[]{:S(2)}, u32[]{:S(2)}) collective-permute-start(bf16[3,64,640]{2,1,0:T(8,128)(2,1)S(1)} %collective-permute-done.7.refs_3_), channel_id=1, source_target_pairs={{0,10},{8,1},{10,4},{2,8},{4,14},{12,2},{14,7},{6,12},{7,13},{15,6... | collective-permute-start | bytes 737288 | tf_op jit(solution)/shard_map/ppermute | solution.py:39
  26.3 3.3 %collective-permute-start.17 = (bf16[3,64,640]{2,1,0:T(8,128)(2,1)S(1)}, bf16[3,64,640]{2,1,0:T(8,128)(2,1)S(1)}, u32[]{:S(2)}, u32[]{:S(2)}) collective-permute-start(bf16[3,64,640]{2,1,0:T(8,128)(2,1)S(1)} %collective-permute-done.12.refs_3_), channel_id=1, source_target_pairs={{0,8},{8,0},{1,9},{9,1},{2,10},{10,2},{3,11},{11,3},{4,12},{12,4},... | collective-permute-start | bytes 737288 | tf_op jit(solution)/shard_map/ppermute | solution.py:43
  29.5 1.8 %collective-permute-start.16 = (bf16[3,64,640]{2,1,0:T(8,128)(2,1)S(1)}, bf16[3,64,640]{2,1,0:T(8,128)(2,1)S(1)}, u32[]{:S(2)}, u32[]{:S(2)}) collective-permute-start(bf16[3,64,640]{2,1,0:T(8,128)(2,1)S(1)} %collective-permute-done.11.refs_4_), channel_id=1, source_target_pairs={{0,8},{8,0},{1,9},{9,1},{2,10},{10,2},{3,11},{11,3},{4,12},{12,4},... | collective-permute-start | bytes 737288 | tf_op jit(solution)/shard_map/ppermute | solution.py:43

commit v14 on v13

--- a/solution.py
+++ b/solution.py
@@ -10,8 +10,9 @@
 numerator_gain = 16.0
 LANES = 128
 MIB = 1024 * 1024
-TILE_ROWS = 128
+TILE_ROWS = 160
 TILE_COLS = 256
+STORE_ROWS = 320
 VMEM = pl.BlockSpec(memory_space=pltpu.VMEM)
 HBM = pl.BlockSpec(memory_space=pltpu.HBM)
 ANY = pl.BlockSpec(memory_space=pl.ANY)
@@ -157,11 +158,11 @@
     at = 6 + count + (0 if fresh else 3)
     outs, bufs, sem = refs[at : at + 3], refs[at + 3 : at + 6], refs[at + 6]
     cols = a_refs[0].shape[-1]
-    stores = []
     for i, (layer, start) in enumerate(column_starts(n, pieces, cols)):
         for proj in (1, 2, 0):
-            for row in range(0, bufs[proj].shape[1], TILE_ROWS):
-                rows = pl.ds(row, min(TILE_ROWS, bufs[proj].shape[1] - row))
+            last_row = bufs[proj].shape[1]
+            for row in range(0, last_row, TILE_ROWS):
+                rows = pl.ds(row, min(TILE_ROWS, last_row - row))
                 for col in range(0, cols, TILE_COLS):
                     width = min(TILE_COLS, cols - col)
                     tile = pl.ds(col, width) if fresh else pl.ds(pl.multiple_of(start + col, LANES), width)
@@ -173,27 +174,27 @@
                     block = bases[proj][i if fresh else layer, rows, tile]
                     merged = block.astype(jnp.float32) + scale * delta
                     bufs[proj][i, rows, col : col + width] = merged.astype(jnp.bfloat16)
-                store = pltpu.make_async_copy(
-                    bufs[proj].at[i, rows], outs[proj].at[layer, rows, pl.ds(start, cols)], sem.at[len(stores)]
-                )
-                store.start()
-                stores.append(store)
-    for store in stores:
-        store.wait()
+                end = min(row + TILE_ROWS, last_row)
+                if end % STORE_ROWS == 0 or end == last_row:
+                    begin = (end - 1) // STORE_ROWS * STORE_ROWS
+                    done = pl.ds(begin, end - begin)
+                    target = outs[proj].at[layer, done, pl.ds(start, cols)]
+                    pltpu.make_async_copy(bufs[proj].at[i, done], target, sem.at[proj]).start()
+    for proj in range(3):
+        pltpu.make_async_copy(bufs[proj], bufs[proj], sem.at[proj]).wait()
 
 
 def merge(n, scale, b, a_list, bases, shapes, outs, pieces):
     fresh = outs is None
     rank, cols = a_list[0].shape[-2:]
     rows = sum(base.shape[1] for base in bases)
-    stores = len(pieces) * sum(-(-base.shape[1] // TILE_ROWS) for base in bases)
     return pl.pallas_call(
         functools.partial(merge_kernel, n, pieces, scale, fresh),
         in_specs=[VMEM] * (3 + len(a_list) + 3) + [HBM] * (0 if fresh else 3),
         out_specs=[HBM] * 3,
         out_shape=shapes,
         scratch_shapes=[pltpu.VMEM((len(pieces), base.shape[1], cols), base.dtype) for base in bases]
-        + [pltpu.SemaphoreType.DMA((stores,))],
+        + [pltpu.SemaphoreType.DMA((3,))],
         input_output_aliases={} if fresh else {6 + len(a_list) + i: i for i in range(3)},
         compiler_params=pltpu.CompilerParams(vmem_limit_bytes=16 * MIB),
         cost_estimate=pl.CostEstimate(
@@ -255,8 +256,10 @@
             b_there = (step, "b", True, swap_cores(second))
             if step < last - 1:
                 second = ring_pass(second, n)
-            batch = [b_here, a_here if step == 1 else swapped_b]
-            outs = go(outs, *batch, *([a_there] if step == last - 1 else []))
+            if step == 1:
+                outs, late = go(outs, a_here), b_here
+            else:
+                outs = go(outs, b_here, swapped_b, *([a_there, late] if step == last - 1 else []))
             first, outs = tie((first, outs))
             swapped_a, swapped_b = a_there, b_there
         a_there = (last, "a", True, swap_cores(first))

time: 32.7 us -> 32.3 us (0.988)
  waiting for transfers between devices: 1.8 us -> 1.09 us
  starting transfers between devices: 13.1 us -> 13.8 us
  Pallas kernels: 16.7 us -> 16.3 us
    ppermute x7, waiting for transfers between devices: 0.96 us -> 0.25 us  [ring_pass(): return lax.ppermute(array, ('rollout', 'tensor'), pairs)]
    ppermute x7, starting transfers between devices: 10.1 us -> 10.6 us  [ring_pass(): return lax.ppermute(array, ('rollout', 'tensor'), pairs)]
    pallas_call x8, Pallas kernels: 13.5 us -> 13.1 us  [merge(): pl.pallas_call(functools.partial(merge_kernel, n, pieces, scale, fresh),...]
  transfers between devices with their start and end apart: 18 -> 18, of which waited for: 3 -> 3; matrix products, arithmetic and copies ran while one was open for 0% -> 0% of each run, Pallas kernels for 47% -> 46%
where the time goes in v14:
time: 32.3 us; the launch traced here: 32.1 us
  Pallas kernels  16.3 us (50%)
  starting transfers between devices  13.8 us (43%)
  waiting for transfers between devices  1.09 us (3%)
  between operations  0.89 us (3%)
    pallas_call x8, Pallas kernels, merge(): pl.pallas_call(functools.partial(merge_kernel, n, pieces, scale, fresh),...  13.1 us
    ppermute x7, starting transfers between devices, ring_pass(): return lax.ppermute(array, ('rollout', 'tensor'), pairs)  10.6 us
    ppermute x11, starting transfers between devices, swap_cores(): return lax.ppermute(array, 'rollout', [(0, 1), (1, 0)])  3.2 us
    pallas_call x1, Pallas kernels, fetch_blocks(): pl.pallas_call(functools.partial(fetch_kernel, n, pieces), in_specs=[HBM]...  1.56 us
    pallas_call x1, Pallas kernels, choose_b(): pl.pallas_call(functools.partial(choose_b_kernel, n, pieces), in_specs=[V...  1.5 us
    ppermute x11, waiting for transfers between devices, swap_cores(): return lax.ppermute(array, 'rollout', [(0, 1), (1, 0)])  0.84 us
  transfers between devices with their start and end apart: 18, of which 3 were waited for; matrix products, arithmetic and copies ran while one was open for 0% of the time, Pallas kernels for 46%

profile of v14, /device:TPU:0, one launch (start us, length us, event | category | flops | bytes accessed | tf_op | source)
XLA Modules:
  0.0 32.1 jit_solution(8917642184230335905)
XLA Ops:
  0.7 0.5 %collective-permute-start = (bf16[2,3,64,640]{3,2,1,0:T(8,128)(2,1)}, bf16[2,3,64,640]{3,2,1,0:T(8,128)(2,1)S(1)}, u32[]{:S(2)}, u32[]{:S(2)}) collective-permute-start(bf16[2,3,64,640]{3,2,1,0:T(8,128)(2,1)} %bitcast.12), channel_id=1, source_target_pairs={{0,8},{8,0},{1,9},{9,1},{2,10},{10,2},{3,11},{11,3},{4,12},{12,4},... | collective-permute-start | bytes 1474568 | tf_op jit(solution)/shard_map/ppermute | solution.py:44
  1.2 1.6 %shard_map.103.refs_5_ = bf16[2,640,640]{2,1,0:T(8,128)(2,1)S(1)} custom-call(bf16[2,640,5120]{2,1,0:T(8,128)(2,1)} %refs_4_.3), custom_call_target="tpu_custom_call" | custom-call | bytes 3276800 | tf_op jit(solution)/shard_map/pallas_call | solution.py:115
  2.8 0.1 collective-permute-done.other
  2.9 0.1 shard_map.104
  3.1 2.7 %collective-permute-start.1 = (bf16[3,64,640]{2,1,0:T(8,128)(2,1)S(1)}, bf16[3,64,640]{2,1,0:T(8,128)(2,1)S(1)}, u32[]{:S(2)}, u32[]{:S(2)}) collective-permute-start(bf16[3,64,640]{2,1,0:T(8,128)(2,1)S(1)} %get-tuple-element.64.refs_3_), channel_id=1, source_target_pairs={{0,10},{8,1},{10,4},{2,8},{4,14},{12,2},{14,7},{6,12},{7,13},{15,6... | collective-permute-start | bytes 737288 | tf_op jit(solution)/shard_map/ppermute | solution.py:40
  5.8 0.3 collective-permute-start.2
  6.1 0.2 collective-permute-start.3
  6.3 0.3 collective-permute-start.4
  6.6 0.7 %collective-permute-done.3.refs_4_ = bf16[2,64,128]{2,1,0:T(8,128)(2,1)S(1)} collective-permute-done((bf16[2,64,128]{2,1,0:T(8,128)(2,1)S(1)}, bf16[2,64,128]{2,1,0:T(8,128)(2,1)S(1)}, u32[]{:S(2)}, u32[]{:S(2)}) %collective-permute-start.3) | collective-permute-done | bytes 32800 | tf_op jit(solution)/shard_map/ppermute | solution.py:44
  7.3 1.5 %collective-permute-start.6 = (bf16[3,64,640]{2,1,0:T(8,128)(2,1)S(1)}, bf16[3,64,640]{2,1,0:T(8,128)(2,1)S(1)}, u32[]{:S(2)}, u32[]{:S(2)}) collective-permute-start(bf16[3,64,640]{2,1,0:T(8,128)(2,1)S(1)} %get-tuple-element.74.refs_4_), channel_id=1, source_target_pairs={{0,10},{8,1},{10,4},{2,8},{4,14},{12,2},{14,7},{6,12},{7,13},{15,6... | collective-permute-start | bytes 737288 | tf_op jit(solution)/shard_map/ppermute | solution.py:40
  8.8 1.5 %shard_map.105 = (bf16[2,640,64]{2,1,0:T(8,128)(2,1)S(1)}, bf16[2,128,64]{2,1,0:T(8,128)(2,1)S(1)}, bf16[2,128,64]{2,1,0:T(8,128)(2,1)S(1)}, bf16[2,128,640]{2,1,0:T(8,128)(2,1)S(1)}, bf16[2,128,640]{2,1,0:T(8,128)(2,1)S(1)}) custom-call(s32[2,3]{1,0:T(2,128)S(1)} %copy-done.6, bf16[2,64,640]{2,1,0:T(8,128)(2,1)S(1)} %bitcast.15, ...), custom_call_target="tpu_custom_call" | custom-call | bytes 1310720 | tf_op jit(solution)/shard_map/pallas_call | solution.py:143
  10.3 1.4 %collective-permute-start.5 = (bf16[3,64,640]{2,1,0:T(8,128)(2,1)S(1)}, bf16[3,64,640]{2,1,0:T(8,128)(2,1)S(1)}, u32[]{:S(2)}, u32[]{:S(2)}) collective-permute-start(bf16[3,64,640]{2,1,0:T(8,128)(2,1)S(1)} %collective-permute-done.1.refs_3_), channel_id=1, source_target_pairs={{0,10},{8,1},{10,4},{2,8},{4,14},{12,2},{14,7},{6,12},{7,13},{15,6... | collective-permute-start | bytes 737288 | tf_op jit(solution)/shard_map/ppermute | solution.py:40
  11.7 0.3 collective-permute-start.9
  12.0 1.6 %shard_map.106 = (bf16[2,640,5120]{2,1,0:T(8,128)(2,1)}, bf16[2,128,5120]{2,1,0:T(8,128)(2,1)}, bf16[2,128,5120]{2,1,0:T(8,128)(2,1)}) custom-call(bf16[2,640,64]{2,1,0:T(8,128)(2,1)S(1)} %get-tuple-element.70.refs_0_, bf16[2,128,64]{2,1,0:T(8,128)(2,1)S(1)} %get-tuple-element.71.refs_1_, bf16[2,128,64]{2,1,0:T(8,128)(2,1)S(1)} %get-tuple-element.72.refs_2_, ...), custom_call_target="tpu_custom_call" | custom-call | flops 146800640 | bytes 4587520 | tf_op jit(solution)/shard_map/pallas_call | solution.py:191
  13.7 1.2 %collective-permute-start.8 = (bf16[3,64,640]{2,1,0:T(8,128)(2,1)S(1)}, bf16[3,64,640]{2,1,0:T(8,128)(2,1)S(1)}, u32[]{:S(2)}, u32[]{:S(2)}) collective-permute-start(bf16[3,64,640]{2,1,0:T(8,128)(2,1)S(1)} %collective-permute-done.6.refs_6_), channel_id=1, source_target_pairs={{0,10},{8,1},{10,4},{2,8},{4,14},{12,2},{14,7},{6,12},{7,13},{15,6... | collective-permute-start | bytes 737288 | tf_op jit(solution)/shard_map/ppermute | solution.py:40
  14.9 0.1 collective-permute-start.10
  15.1 1.3 %shard_map.107 = (bf16[2,640,5120]{2,1,0:T(8,128)(2,1)}, bf16[2,128,5120]{2,1,0:T(8,128)(2,1)}, bf16[2,128,5120]{2,1,0:T(8,128)(2,1)}) custom-call(bf16[2,640,64]{2,1,0:T(8,128)(2,1)S(1)} %get-tuple-element.70.refs_0_, bf16[2,128,64]{2,1,0:T(8,128)(2,1)S(1)} %get-tuple-element.71.refs_1_, ...), custom_call_target="tpu_custom_call", output_to_operand_aliasing={{0}: (7, {}), {1}: (8, {}), {2}: (9, {})} | custom-call | flops 73400320 | bytes 2293760 | tf_op jit(solution)/shard_map/pallas_call | solution.py:191
  16.4 1.3 %collective-permute-start.7 = (bf16[3,64,640]{2,1,0:T(8,128)(2,1)S(1)}, bf16[3,64,640]{2,1,0:T(8,128)(2,1)S(1)}, u32[]{:S(2)}, u32[]{:S(2)}) collective-permute-start(bf16[3,64,640]{2,1,0:T(8,128)(2,1)S(1)} %collective-permute-done.5.refs_3_), channel_id=1, source_target_pairs={{0,10},{8,1},{10,4},{2,8},{4,14},{12,2},{14,7},{6,12},{7,13},{15,6... | collective-permute-start | bytes 737288 | tf_op jit(solution)/shard_map/ppermute | solution.py:40
  17.7 0.1 collective-permute-start.13
  17.8 1.6 %shard_map.108 = (bf16[2,640,5120]{2,1,0:T(8,128)(2,1)}, bf16[2,128,5120]{2,1,0:T(8,128)(2,1)}, bf16[2,128,5120]{2,1,0:T(8,128)(2,1)}) custom-call(bf16[2,640,64]{2,1,0:T(8,128)(2,1)S(1)} %get-tuple-element.70.refs_0_, bf16[2,128,64]{2,1,0:T(8,128)(2,1)S(1)} %get-tuple-element.71.refs_1_, ...), custom_call_target="tpu_custom_call", output_to_operand_aliasing={{0}: (8, {}), {1}: (9, {}), {2}: (10, {})} | custom-call | flops 146800640 | bytes 4587520 | tf_op jit(solution)/shard_map/pallas_call | solution.py:191
  19.4 0.5 %collective-permute-start.14 = (bf16[3,64,640]{2,1,0:T(8,128)(2,1)S(1)}, bf16[3,64,640]{2,1,0:T(8,128)(2,1)S(1)}, u32[]{:S(2)}, u32[]{:S(2)}) collective-permute-start(bf16[3,64,640]{2,1,0:T(8,128)(2,1)S(1)} %collective-permute-done.8.refs_3_), channel_id=1, source_target_pairs={{0,8},{8,0},{1,9},{9,1},{2,10},{10,2},{3,11},{11,3},{4,12},{12,4},... | collective-permute-start | bytes 737288 | tf_op jit(solution)/shard_map/ppermute | solution.py:44
  19.9 1.2 %collective-permute-start.12 = (bf16[3,64,640]{2,1,0:T(8,128)(2,1)S(1)}, bf16[3,64,640]{2,1,0:T(8,128)(2,1)S(1)}, u32[]{:S(2)}, u32[]{:S(2)}) collective-permute-start(bf16[3,64,640]{2,1,0:T(8,128)(2,1)S(1)} %collective-permute-done.8.refs_3_), channel_id=1, source_target_pairs={{0,10},{8,1},{10,4},{2,8},{4,14},{12,2},{14,7},{6,12},{7,13},{15,6... | collective-permute-start | bytes 737288 | tf_op jit(solution)/shard_map/ppermute | solution.py:40
  21.2 1.6 %shard_map.109 = (bf16[2,640,5120]{2,1,0:T(8,128)(2,1)}, bf16[2,128,5120]{2,1,0:T(8,128)(2,1)}, bf16[2,128,5120]{2,1,0:T(8,128)(2,1)}) custom-call(bf16[2,640,64]{2,1,0:T(8,128)(2,1)S(1)} %get-tuple-element.70.refs_0_, bf16[2,128,64]{2,1,0:T(8,128)(2,1)S(1)} %get-tuple-element.71.refs_1_, ...), custom_call_target="tpu_custom_call", output_to_operand_aliasing={{0}: (8, {}), {1}: (9, {}), {2}: (10, {})} | custom-call | flops 146800640 | bytes 4587520 | tf_op jit(solution)/shard_map/pallas_call | solution.py:191
  22.8 0.4 %collective-permute-start.15 = (bf16[3,64,640]{2,1,0:T(8,128)(2,1)S(1)}, bf16[3,64,640]{2,1,0:T(8,128)(2,1)S(1)}, u32[]{:S(2)}, u32[]{:S(2)}) collective-permute-start(bf16[3,64,640]{2,1,0:T(8,128)(2,1)S(1)} %collective-permute-done.7.refs_3_), channel_id=1, source_target_pairs={{0,8},{8,0},{1,9},{9,1},{2,10},{10,2},{3,11},{11,3},{4,12},{12,4},... | collective-permute-start | bytes 737288 | tf_op jit(solution)/shard_map/ppermute | solution.py:44
  23.3 1.2 %collective-permute-start.11 = (bf16[3,64,640]{2,1,0:T(8,128)(2,1)S(1)}, bf16[3,64,640]{2,1,0:T(8,128)(2,1)S(1)}, u32[]{:S(2)}, u32[]{:S(2)}) collective-permute-start(bf16[3,64,640]{2,1,0:T(8,128)(2,1)S(1)} %collective-permute-done.7.refs_3_), channel_id=1, source_target_pairs={{0,10},{8,1},{10,4},{2,8},{4,14},{12,2},{14,7},{6,12},{7,13},{15,6... | collective-permute-start | bytes 737288 | tf_op jit(solution)/shard_map/ppermute | solution.py:40
  24.5 1.6 %shard_map.110 = (bf16[2,640,5120]{2,1,0:T(8,128)(2,1)}, bf16[2,128,5120]{2,1,0:T(8,128)(2,1)}, bf16[2,128,5120]{2,1,0:T(8,128)(2,1)}) custom-call(bf16[2,640,64]{2,1,0:T(8,128)(2,1)S(1)} %get-tuple-element.70.refs_0_, bf16[2,128,64]{2,1,0:T(8,128)(2,1)S(1)} %get-tuple-element.71.refs_1_, ...), custom_call_target="tpu_custom_call", output_to_operand_aliasing={{0}: (8, {}), {1}: (9, {}), {2}: (10, {})} | custom-call | flops 146800640 | bytes 4587520 | tf_op jit(solution)/shard_map/pallas_call | solution.py:191
  26.2 0.1 collective-permute-start.17
  26.3 2.4 %shard_map.111 = (bf16[2,640,5120]{2,1,0:T(8,128)(2,1)}, bf16[2,128,5120]{2,1,0:T(8,128)(2,1)}, bf16[2,128,5120]{2,1,0:T(8,128)(2,1)}) custom-call(bf16[2,640,64]{2,1,0:T(8,128)(2,1)S(1)} %get-tuple-element.70.refs_0_, bf16[2,128,64]{2,1,0:T(8,128)(2,1)S(1)} %get-tuple-element.71.refs_1_, ...), custom_call_target="tpu_custom_call", output_to_operand_aliasing={{0}: (10, {}), {1}: (11, {}), {2}: (12, {})} | custom-call | flops 293601280 | bytes 9175040 | tf_op jit(solution)/shard_map/pallas_call | solution.py:191
  28.7 0.2 collective-permute-done.11.refs_4_
  28.9 0.3 collective-permute-start.16
  29.2 1.6 %shard_map.112 = (bf16[2,640,5120]{2,1,0:T(8,128)(2,1)}, bf16[2,128,5120]{2,1,0:T(8,128)(2,1)}, bf16[2,128,5120]{2,1,0:T(8,128)(2,1)}) custom-call(bf16[2,640,64]{2,1,0:T(8,128)(2,1)S(1)} %get-tuple-element.70.refs_0_, bf16[2,128,64]{2,1,0:T(8,128)(2,1)S(1)} %get-tuple-element.71.refs_1_, ...), custom_call_target="tpu_custom_call", output_to_operand_aliasing={{0}: (8, {}), {1}: (9, {}), {2}: (10, {})} | custom-call | flops 146800640 | bytes 4587520 | tf_op jit(solution)/shard_map/pallas_call | solution.py:191
  30.9 1.3 %shard_map.113 = (bf16[2,640,5120]{2,1,0:T(8,128)(2,1)}, bf16[2,128,5120]{2,1,0:T(8,128)(2,1)}, bf16[2,128,5120]{2,1,0:T(8,128)(2,1)}) custom-call(bf16[2,640,64]{2,1,0:T(8,128)(2,1)S(1)} %get-tuple-element.70.refs_0_, bf16[2,128,64]{2,1,0:T(8,128)(2,1)S(1)} %get-tuple-element.71.refs_1_, ...), custom_call_target="tpu_custom_call", output_to_operand_aliasing={{0}: (7, {}), {1}: (8, {}), {2}: (9, {})} | custom-call | flops 73400320 | bytes 2293760 | tf_op jit(solution)/shard_map/pallas_call | solution.py:191
  (38 shorter events, 0.1 us)
Async XLA Ops:
  0.6 2.3 %copy-start.2 = (bf16[1,2,3,64,640]{4,3,2,1,0:T(8,128)(2,1)S(1)}, bf16[1,2,3,64,640]{4,3,2,1,0:T(8,128)(2,1)}, u32[]{:S(2)}) copy-start(bf16[1,2,3,64,640]{4,3,2,1,0:T(8,128)(2,1)} %param.12) | copy-start | bytes 1474564
  0.6 2.3 %copy-start.6 = (s32[2,3]{1,0:T(2,128)S(1)}, s32[2,3]{1,0:T(2,128)}, u32[]{:S(2)}) copy-start(s32[2,3]{1,0:T(2,128)} %owners.3) | copy-start | bytes 76
  0.7 5.2 %copy-start.3 = (bf16[1,2,640,64]{2,3,1,0:T(8,128)(2,1)S(1)}, bf16[1,2,640,64]{2,3,1,0:T(8,128)(2,1)}, u32[]{:S(2)}) copy-start(bf16[1,2,640,64]{2,3,1,0:T(8,128)(2,1)} %param.13) | copy-start | bytes 491524
  0.7 5.5 %copy-start.4 = (bf16[1,2,128,64]{2,3,1,0:T(8,128)(2,1)S(1)}, bf16[1,2,128,64]{2,3,1,0:T(8,128)(2,1)}, u32[]{:S(2)}) copy-start(bf16[1,2,128,64]{2,3,1,0:T(8,128)(2,1)} %param.14) | copy-start | bytes 98308
  0.7 5.6 %copy-start.5 = (bf16[1,2,128,64]{2,3,1,0:T(8,128)(2,1)S(1)}, bf16[1,2,128,64]{2,3,1,0:T(8,128)(2,1)}, u32[]{:S(2)}) copy-start(bf16[1,2,128,64]{2,3,1,0:T(8,128)(2,1)} %param.15) | copy-start | bytes 98308
  0.7 2.2 %collective-permute-start = (bf16[2,3,64,640]{3,2,1,0:T(8,128)(2,1)}, bf16[2,3,64,640]{3,2,1,0:T(8,128)(2,1)S(1)}, u32[]{:S(2)}, u32[]{:S(2)}) collective-permute-start(bf16[2,3,64,640]{3,2,1,0:T(8,128)(2,1)} %bitcast.12), channel_id=1, source_target_pairs={{0,8},{8,0},{1,9},{9,1},{2,10},{10,2},{3,11},{11,3},{4,12},{12,4},... | collective-permute-start | bytes 1474568 | tf_op jit(solution)/shard_map/ppermute | solution.py:44
  1.2 13.9 %slice-start = ((s8[13107200]{0:T(1024)(128)(4,1)}), s8[4194304]{0:T(1024)(128)(4,1)S(1)}, s32[]{:S(2)}) async-start(s8[13107200]{0:T(1024)(128)(4,1)} %bitcast.10), calls=%async_computation | async-start | bytes 8388608
  1.2 13.9 %slice-start.1 = ((s8[13107200]{0:T(1024)(128)(4,1)}), s8[4194304]{0:T(1024)(128)(4,1)S(1)}, s32[]{:S(2)}) async-start(s8[13107200]{0:T(1024)(128)(4,1)} %bitcast.10), calls=%async_computation.1 | async-start | bytes 8388608
  1.2 13.9 %slice-start.2 = ((s8[13107200]{0:T(1024)(128)(4,1)}), s8[4194304]{0:T(1024)(128)(4,1)S(1)}, s32[]{:S(2)}) async-start(s8[13107200]{0:T(1024)(128)(4,1)} %bitcast.10), calls=%async_computation.2 | async-start | bytes 8388608
  3.1 7.3 %collective-permute-start.1 = (bf16[3,64,640]{2,1,0:T(8,128)(2,1)S(1)}, bf16[3,64,640]{2,1,0:T(8,128)(2,1)S(1)}, u32[]{:S(2)}, u32[]{:S(2)}) collective-permute-start(bf16[3,64,640]{2,1,0:T(8,128)(2,1)S(1)} %get-tuple-element.64.refs_3_), channel_id=1, source_target_pairs={{0,10},{8,1},{10,4},{2,8},{4,14},{12,2},{14,7},{6,12},{7,13},{15,6... | collective-permute-start | bytes 737288 | tf_op jit(solution)/shard_map/ppermute | solution.py:40
  5.8 3.0 %collective-permute-start.2 = (bf16[2,64,640]{2,1,0:T(8,128)(2,1)S(1)}, bf16[2,64,640]{2,1,0:T(8,128)(2,1)S(1)}, u32[]{:S(2)}, u32[]{:S(2)}) collective-permute-start(bf16[2,64,640]{2,1,0:T(8,128)(2,1)S(1)} %bitcast.14), channel_id=1, source_target_pairs={{0,8},{8,0},{1,9},{9,1},{2,10},{10,2},{3,11},{11,3},{4,12},{12,4},... | collective-permute-start | bytes 491528 | tf_op jit(solution)/shard_map/ppermute | solution.py:44
  6.1 1.2 %collective-permute-start.3 = (bf16[2,64,128]{2,1,0:T(8,128)(2,1)S(1)}, bf16[2,64,128]{2,1,0:T(8,128)(2,1)S(1)}, u32[]{:S(2)}, u32[]{:S(2)}) collective-permute-start(bf16[2,64,128]{2,1,0:T(8,128)(2,1)S(1)} %bitcast.16), channel_id=1, source_target_pairs={{0,8},{8,0},{1,9},{9,1},{2,10},{10,2},{3,11},{11,3},{4,12},{12,4},... | collective-permute-start | bytes 98312 | tf_op jit(solution)/shard_map/ppermute | solution.py:44
  6.3 2.5 %collective-permute-start.4 = (bf16[2,64,128]{2,1,0:T(8,128)(2,1)S(1)}, bf16[2,64,128]{2,1,0:T(8,128)(2,1)S(1)}, u32[]{:S(2)}, u32[]{:S(2)}) collective-permute-start(bf16[2,64,128]{2,1,0:T(8,128)(2,1)S(1)} %bitcast.18), channel_id=1, source_target_pairs={{0,8},{8,0},{1,9},{9,1},{2,10},{10,2},{3,11},{11,3},{4,12},{12,4},... | collective-permute-start | bytes 98312 | tf_op jit(solution)/shard_map/ppermute | solution.py:44
  7.3 7.7 %slice-start.3 = ((s8[13107200]{0:T(1024)(128)(4,1)}), s8[524288]{0:T(1024)(128)(4,1)S(1)}, s32[]{:S(2)}) async-start(s8[13107200]{0:T(1024)(128)(4,1)} %bitcast.10), calls=%async_computation.3 | async-start | bytes 1048576
  7.3 6.3 %collective-permute-start.6 = (bf16[3,64,640]{2,1,0:T(8,128)(2,1)S(1)}, bf16[3,64,640]{2,1,0:T(8,128)(2,1)S(1)}, u32[]{:S(2)}, u32[]{:S(2)}) collective-permute-start(bf16[3,64,640]{2,1,0:T(8,128)(2,1)S(1)} %get-tuple-element.74.refs_4_), channel_id=1, source_target_pairs={{0,10},{8,1},{10,4},{2,8},{4,14},{12,2},{14,7},{6,12},{7,13},{15,6... | collective-permute-start | bytes 737288 | tf_op jit(solution)/shard_map/ppermute | solution.py:40
  8.8 6.3 %copy-start.1 = (bf16[2,128,5120]{2,1,0:T(8,128)(2,1)S(1)}, bf16[2,128,5120]{2,1,0:T(8,128)(2,1)}, u32[]{:S(2)}) copy-start(bf16[2,128,5120]{2,1,0:T(8,128)(2,1)} %refs_6_.13) | copy-start | bytes 7864324
  10.3 4.8 %copy-start = (bf16[2,128,5120]{2,1,0:T(8,128)(2,1)S(1)}, bf16[2,128,5120]{2,1,0:T(8,128)(2,1)}, u32[]{:S(2)}) copy-start(bf16[2,128,5120]{2,1,0:T(8,128)(2,1)} %refs_5_.11) | copy-start | bytes 7864324
  10.3 6.0 %collective-permute-start.5 = (bf16[3,64,640]{2,1,0:T(8,128)(2,1)S(1)}, bf16[3,64,640]{2,1,0:T(8,128)(2,1)S(1)}, u32[]{:S(2)}, u32[]{:S(2)}) collective-permute-start(bf16[3,64,640]{2,1,0:T(8,128)(2,1)S(1)} %collective-permute-done.1.refs_3_), channel_id=1, source_target_pairs={{0,10},{8,1},{10,4},{2,8},{4,14},{12,2},{14,7},{6,12},{7,13},{15,6... | collective-permute-start | bytes 737288 | tf_op jit(solution)/shard_map/ppermute | solution.py:40
  11.7 6.0 %collective-permute-start.9 = (bf16[3,64,640]{2,1,0:T(8,128)(2,1)S(1)}, bf16[3,64,640]{2,1,0:T(8,128)(2,1)S(1)}, u32[]{:S(2)}, u32[]{:S(2)}) collective-permute-start(bf16[3,64,640]{2,1,0:T(8,128)(2,1)S(1)} %collective-permute-done.1.refs_3_), channel_id=1, source_target_pairs={{0,8},{8,0},{1,9},{9,1},{2,10},{10,2},{3,11},{11,3},{4,12},{12,4},... | collective-permute-start | bytes 737288 | tf_op jit(solution)/shard_map/ppermute | solution.py:44
  13.7 5.7 %collective-permute-start.8 = (bf16[3,64,640]{2,1,0:T(8,128)(2,1)S(1)}, bf16[3,64,640]{2,1,0:T(8,128)(2,1)S(1)}, u32[]{:S(2)}, u32[]{:S(2)}) collective-permute-start(bf16[3,64,640]{2,1,0:T(8,128)(2,1)S(1)} %collective-permute-done.6.refs_6_), channel_id=1, source_target_pairs={{0,10},{8,1},{10,4},{2,8},{4,14},{12,2},{14,7},{6,12},{7,13},{15,6... | collective-permute-start | bytes 737288 | tf_op jit(solution)/shard_map/ppermute | solution.py:40
  14.9 6.2 %collective-permute-start.10 = (bf16[3,64,640]{2,1,0:T(8,128)(2,1)S(1)}, bf16[3,64,640]{2,1,0:T(8,128)(2,1)S(1)}, u32[]{:S(2)}, u32[]{:S(2)}) collective-permute-start(bf16[3,64,640]{2,1,0:T(8,128)(2,1)S(1)} %collective-permute-done.6.refs_6_), channel_id=1, source_target_pairs={{0,8},{8,0},{1,9},{9,1},{2,10},{10,2},{3,11},{11,3},{4,12},{12,4},... | collective-permute-start | bytes 737288 | tf_op jit(solution)/shard_map/ppermute | solution.py:44
  16.4 6.4 %collective-permute-start.7 = (bf16[3,64,640]{2,1,0:T(8,128)(2,1)S(1)}, bf16[3,64,640]{2,1,0:T(8,128)(2,1)S(1)}, u32[]{:S(2)}, u32[]{:S(2)}) collective-permute-start(bf16[3,64,640]{2,1,0:T(8,128)(2,1)S(1)} %collective-permute-done.5.refs_3_), channel_id=1, source_target_pairs={{0,10},{8,1},{10,4},{2,8},{4,14},{12,2},{14,7},{6,12},{7,13},{15,6... | collective-permute-start | bytes 737288 | tf_op jit(solution)/shard_map/ppermute | solution.py:40
  17.7 6.8 %collective-permute-start.13 = (bf16[3,64,640]{2,1,0:T(8,128)(2,1)S(1)}, bf16[3,64,640]{2,1,0:T(8,128)(2,1)S(1)}, u32[]{:S(2)}, u32[]{:S(2)}) collective-permute-start(bf16[3,64,640]{2,1,0:T(8,128)(2,1)S(1)} %collective-permute-done.5.refs_3_), channel_id=1, source_target_pairs={{0,8},{8,0},{1,9},{9,1},{2,10},{10,2},{3,11},{11,3},{4,12},{12,4},... | collective-permute-start | bytes 737288 | tf_op jit(solution)/shard_map/ppermute | solution.py:44
  19.4 6.8 %collective-permute-start.14 = (bf16[3,64,640]{2,1,0:T(8,128)(2,1)S(1)}, bf16[3,64,640]{2,1,0:T(8,128)(2,1)S(1)}, u32[]{:S(2)}, u32[]{:S(2)}) collective-permute-start(bf16[3,64,640]{2,1,0:T(8,128)(2,1)S(1)} %collective-permute-done.8.refs_3_), channel_id=1, source_target_pairs={{0,8},{8,0},{1,9},{9,1},{2,10},{10,2},{3,11},{11,3},{4,12},{12,4},... | collective-permute-start | bytes 737288 | tf_op jit(solution)/shard_map/ppermute | solution.py:44
  19.9 6.2 %collective-permute-start.12 = (bf16[3,64,640]{2,1,0:T(8,128)(2,1)S(1)}, bf16[3,64,640]{2,1,0:T(8,128)(2,1)S(1)}, u32[]{:S(2)}, u32[]{:S(2)}) collective-permute-start(bf16[3,64,640]{2,1,0:T(8,128)(2,1)S(1)} %collective-permute-done.8.refs_3_), channel_id=1, source_target_pairs={{0,10},{8,1},{10,4},{2,8},{4,14},{12,2},{14,7},{6,12},{7,13},{15,6... | collective-permute-start | bytes 737288 | tf_op jit(solution)/shard_map/ppermute | solution.py:40
  22.8 3.4 %collective-permute-start.15 = (bf16[3,64,640]{2,1,0:T(8,128)(2,1)S(1)}, bf16[3,64,640]{2,1,0:T(8,128)(2,1)S(1)}, u32[]{:S(2)}, u32[]{:S(2)}) collective-permute-start(bf16[3,64,640]{2,1,0:T(8,128)(2,1)S(1)} %collective-permute-done.7.refs_3_), channel_id=1, source_target_pairs={{0,8},{8,0},{1,9},{9,1},{2,10},{10,2},{3,11},{11,3},{4,12},{12,4},... | collective-permute-start | bytes 737288 | tf_op jit(solution)/shard_map/ppermute | solution.py:44
  23.3 5.6 %collective-permute-start.11 = (bf16[3,64,640]{2,1,0:T(8,128)(2,1)S(1)}, bf16[3,64,640]{2,1,0:T(8,128)(2,1)S(1)}, u32[]{:S(2)}, u32[]{:S(2)}) collective-permute-start(bf16[3,64,640]{2,1,0:T(8,128)(2,1)S(1)} %collective-permute-done.7.refs_3_), channel_id=1, source_target_pairs={{0,10},{8,1},{10,4},{2,8},{4,14},{12,2},{14,7},{6,12},{7,13},{15,6... | collective-permute-start | bytes 737288 | tf_op jit(solution)/shard_map/ppermute | solution.py:40
  26.2 3.1 %collective-permute-start.17 = (bf16[3,64,640]{2,1,0:T(8,128)(2,1)S(1)}, bf16[3,64,640]{2,1,0:T(8,128)(2,1)S(1)}, u32[]{:S(2)}, u32[]{:S(2)}) collective-permute-start(bf16[3,64,640]{2,1,0:T(8,128)(2,1)S(1)} %collective-permute-done.12.refs_3_), channel_id=1, source_target_pairs={{0,8},{8,0},{1,9},{9,1},{2,10},{10,2},{3,11},{11,3},{4,12},{12,4},... | collective-permute-start | bytes 737288 | tf_op jit(solution)/shard_map/ppermute | solution.py:44
  28.9 2.0 %collective-permute-start.16 = (bf16[3,64,640]{2,1,0:T(8,128)(2,1)S(1)}, bf16[3,64,640]{2,1,0:T(8,128)(2,1)S(1)}, u32[]{:S(2)}, u32[]{:S(2)}) collective-permute-start(bf16[3,64,640]{2,1,0:T(8,128)(2,1)S(1)} %collective-permute-done.11.refs_4_), channel_id=1, source_target_pairs={{0,8},{8,0},{1,9},{9,1},{2,10},{10,2},{3,11},{11,3},{4,12},{12,4},... | collective-permute-start | bytes 737288 | tf_op jit(solution)/shard_map/ppermute | solution.py:44

commit v15 on v14

--- a/solution.py
+++ b/solution.py
@@ -244,24 +244,21 @@
             pieces = [(step, not swapped, ((step % 2 == 0) == (ring == "a")) != swapped) for step, ring, swapped, _ in named]
             return merge(n, scale, b, [chunk for *_, chunk in named], bases, shapes, outs, pieces)
 
-        swapped_a = swapped_b = None
+        before = []
         for step in range(1, last):
             a_here = (step, "a", False, first)
             a_there = (step, "a", True, swap_cores(first))
             first = ring_pass(first, n)
             if step > 1:
-                outs = go(outs, a_here, swapped_a)
+                outs = go(outs, *before)
             second, outs = tie((second, outs))
             b_here = (step, "b", False, second)
-            b_there = (step, "b", True, swap_cores(second))
+            swapped_b = (step, "b", True, swap_cores(second))
+            before = [a_there, b_here, swapped_b]
             if step < last - 1:
                 second = ring_pass(second, n)
-            if step == 1:
-                outs, late = go(outs, a_here), b_here
-            else:
-                outs = go(outs, b_here, swapped_b, *([a_there, late] if step == last - 1 else []))
+            outs = go(outs, a_here, *(before[:2] if step == last - 1 else []))
             first, outs = tie((first, outs))
-            swapped_a, swapped_b = a_there, b_there
         a_there = (last, "a", True, swap_cores(first))
         outs = go(outs, swapped_b, (last, "a", False, first))
         return tuple(go(outs, a_there))

time: 32.3 us -> 33.6 us (1.040)
  waiting for transfers between devices: 1.09 us -> 2.75 us
    ppermute x11, waiting for transfers between devices: 0.84 us -> 2.29 us  [swap_cores(): return lax.ppermute(array, 'rollout', [(0, 1), (1, 0)])]
    ppermute x7, starting transfers between devices: 10.6 us -> 9.9 us  [ring_pass(): return lax.ppermute(array, ('rollout', 'tensor'), pairs)]
    ppermute x11, starting transfers between devices: 3.2 us -> 3.62 us  [swap_cores(): return lax.ppermute(array, 'rollout', [(0, 1), (1, 0)])]
  transfers between devices with their start and end apart: 18 -> 18, of which waited for: 3 -> 5; matrix products, arithmetic and copies ran while one was open for 0% -> 0% of each run, Pallas kernels for 46% -> 45%
where the time goes in v15:
time: 33.6 us; the launch traced here: 33.4 us
  Pallas kernels  16.3 us (49%)
  starting transfers between devices  13.5 us (40%)
  waiting for transfers between devices  2.75 us (8%)
  between operations  0.85 us (3%)
    pallas_call x8, Pallas kernels, merge(): pl.pallas_call(functools.partial(merge_kernel, n, pieces, scale, fresh),...  13.1 us
    ppermute x7, starting transfers between devices, ring_pass(): return lax.ppermute(array, ('rollout', 'tensor'), pairs)  9.9 us
    ppermute x11, starting transfers between devices, swap_cores(): return lax.ppermute(array, 'rollout', [(0, 1), (1, 0)])  3.62 us
    ppermute x11, waiting for transfers between devices, swap_cores(): return lax.ppermute(array, 'rollout', [(0, 1), (1, 0)])  2.29 us
    pallas_call x1, Pallas kernels, fetch_blocks(): pl.pallas_call(functools.partial(fetch_kernel, n, pieces), in_specs=[HBM]...  1.56 us
    pallas_call x1, Pallas kernels, choose_b(): pl.pallas_call(functools.partial(choose_b_kernel, n, pieces), in_specs=[V...  1.5 us
  transfers between devices with their start and end apart: 18, of which 5 were waited for; matrix products, arithmetic and copies ran while one was open for 0% of the time, Pallas kernels for 45%

profile of v15, /device:TPU:0, one launch (start us, length us, event | category | flops | bytes accessed | tf_op | source)
XLA Modules:
  0.0 33.4 jit_solution(10863500320084480763)
XLA Ops:
  0.7 0.5 %collective-permute-start = (bf16[2,3,64,640]{3,2,1,0:T(8,128)(2,1)}, bf16[2,3,64,640]{3,2,1,0:T(8,128)(2,1)S(1)}, u32[]{:S(2)}, u32[]{:S(2)}) collective-permute-start(bf16[2,3,64,640]{3,2,1,0:T(8,128)(2,1)} %bitcast.12), channel_id=1, source_target_pairs={{0,8},{8,0},{1,9},{9,1},{2,10},{10,2},{3,11},{11,3},{4,12},{12,4},... | collective-permute-start | bytes 1474568 | tf_op jit(solution)/shard_map/ppermute | solution.py:44
  1.2 1.6 %shard_map.103.refs_5_ = bf16[2,640,640]{2,1,0:T(8,128)(2,1)S(1)} custom-call(bf16[2,640,5120]{2,1,0:T(8,128)(2,1)} %refs_4_.5), custom_call_target="tpu_custom_call" | custom-call | bytes 3276800 | tf_op jit(solution)/shard_map/pallas_call | solution.py:115
  2.8 0.1 collective-permute-done.other
  2.9 0.1 shard_map.104
  3.1 2.7 %collective-permute-start.1 = (bf16[3,64,640]{2,1,0:T(8,128)(2,1)S(1)}, bf16[3,64,640]{2,1,0:T(8,128)(2,1)S(1)}, u32[]{:S(2)}, u32[]{:S(2)}) collective-permute-start(bf16[3,64,640]{2,1,0:T(8,128)(2,1)S(1)} %get-tuple-element.64.refs_3_), channel_id=1, source_target_pairs={{0,10},{8,1},{10,4},{2,8},{4,14},{12,2},{14,7},{6,12},{7,13},{15,6... | collective-permute-start | bytes 737288 | tf_op jit(solution)/shard_map/ppermute | solution.py:40
  5.8 0.3 collective-permute-start.2
  6.1 0.2 collective-permute-start.3
  6.3 1.0 %collective-permute-done.3.refs_4_ = bf16[2,64,128]{2,1,0:T(8,128)(2,1)S(1)} collective-permute-done((bf16[2,64,128]{2,1,0:T(8,128)(2,1)S(1)}, bf16[2,64,128]{2,1,0:T(8,128)(2,1)S(1)}, u32[]{:S(2)}, u32[]{:S(2)}) %collective-permute-start.3) | collective-permute-done | bytes 32800 | tf_op jit(solution)/shard_map/ppermute | solution.py:44
  7.3 1.5 %collective-permute-start.6 = (bf16[3,64,640]{2,1,0:T(8,128)(2,1)S(1)}, bf16[3,64,640]{2,1,0:T(8,128)(2,1)S(1)}, u32[]{:S(2)}, u32[]{:S(2)}) collective-permute-start(bf16[3,64,640]{2,1,0:T(8,128)(2,1)S(1)} %get-tuple-element.74.refs_4_), channel_id=1, source_target_pairs={{0,10},{8,1},{10,4},{2,8},{4,14},{12,2},{14,7},{6,12},{7,13},{15,6... | collective-permute-start | bytes 737288 | tf_op jit(solution)/shard_map/ppermute | solution.py:40
  8.9 1.1 %collective-permute-done.4.refs_5_ = bf16[2,64,128]{2,1,0:T(8,128)(2,1)S(1)} collective-permute-done((bf16[2,64,128]{2,1,0:T(8,128)(2,1)S(1)}, bf16[2,64,128]{2,1,0:T(8,128)(2,1)S(1)}, u32[]{:S(2)}, u32[]{:S(2)}) %collective-permute-start.4) | collective-permute-done | bytes 32800 | tf_op jit(solution)/shard_map/ppermute | solution.py:44
  10.0 1.5 %shard_map.105 = (bf16[2,640,64]{2,1,0:T(8,128)(2,1)S(1)}, bf16[2,128,64]{2,1,0:T(8,128)(2,1)S(1)}, bf16[2,128,64]{2,1,0:T(8,128)(2,1)S(1)}, bf16[2,128,640]{2,1,0:T(8,128)(2,1)S(1)}, bf16[2,128,640]{2,1,0:T(8,128)(2,1)S(1)}) custom-call(s32[2,3]{1,0:T(2,128)S(1)} %copy-done.6, bf16[2,64,640]{2,1,0:T(8,128)(2,1)S(1)} %bitcast.15, ...), custom_call_target="tpu_custom_call" | custom-call | bytes 1310720 | tf_op jit(solution)/shard_map/pallas_call | solution.py:143
  11.6 1.4 %collective-permute-start.5 = (bf16[3,64,640]{2,1,0:T(8,128)(2,1)S(1)}, bf16[3,64,640]{2,1,0:T(8,128)(2,1)S(1)}, u32[]{:S(2)}, u32[]{:S(2)}) collective-permute-start(bf16[3,64,640]{2,1,0:T(8,128)(2,1)S(1)} %collective-permute-done.1.refs_3_), channel_id=1, source_target_pairs={{0,10},{8,1},{10,4},{2,8},{4,14},{12,2},{14,7},{6,12},{7,13},{15,6... | collective-permute-start | bytes 737288 | tf_op jit(solution)/shard_map/ppermute | solution.py:40
  12.9 1.6 %shard_map.106 = (bf16[2,640,5120]{2,1,0:T(8,128)(2,1)}, bf16[2,128,5120]{2,1,0:T(8,128)(2,1)}, bf16[2,128,5120]{2,1,0:T(8,128)(2,1)}) custom-call(bf16[2,640,64]{2,1,0:T(8,128)(2,1)S(1)} %get-tuple-element.70.refs_0_, bf16[2,128,64]{2,1,0:T(8,128)(2,1)S(1)} %get-tuple-element.71.refs_1_, bf16[2,128,64]{2,1,0:T(8,128)(2,1)S(1)} %get-tuple-element.72.refs_2_, ...), custom_call_target="tpu_custom_call" | custom-call | flops 146800640 | bytes 4587520 | tf_op jit(solution)/shard_map/pallas_call | solution.py:191
  14.6 0.4 %collective-permute-start.10 = (bf16[3,64,640]{2,1,0:T(8,128)(2,1)S(1)}, bf16[3,64,640]{2,1,0:T(8,128)(2,1)S(1)}, u32[]{:S(2)}, u32[]{:S(2)}) collective-permute-start(bf16[3,64,640]{2,1,0:T(8,128)(2,1)S(1)} %collective-permute-done.6.refs_4_), channel_id=1, source_target_pairs={{0,8},{8,0},{1,9},{9,1},{2,10},{10,2},{3,11},{11,3},{4,12},{12,4},... | collective-permute-start | bytes 737288 | tf_op jit(solution)/shard_map/ppermute | solution.py:44
  14.9 0.2 collective-permute-start.9
  15.1 1.5 %collective-permute-start.8 = (bf16[3,64,640]{2,1,0:T(8,128)(2,1)S(1)}, bf16[3,64,640]{2,1,0:T(8,128)(2,1)S(1)}, u32[]{:S(2)}, u32[]{:S(2)}) collective-permute-start(bf16[3,64,640]{2,1,0:T(8,128)(2,1)S(1)} %collective-permute-done.6.refs_4_), channel_id=1, source_target_pairs={{0,10},{8,1},{10,4},{2,8},{4,14},{12,2},{14,7},{6,12},{7,13},{15,6... | collective-permute-start | bytes 737288 | tf_op jit(solution)/shard_map/ppermute | solution.py:40
  16.7 1.3 %shard_map.107 = (bf16[2,640,5120]{2,1,0:T(8,128)(2,1)}, bf16[2,128,5120]{2,1,0:T(8,128)(2,1)}, bf16[2,128,5120]{2,1,0:T(8,128)(2,1)}) custom-call(bf16[2,640,64]{2,1,0:T(8,128)(2,1)S(1)} %get-tuple-element.70.refs_0_, bf16[2,128,64]{2,1,0:T(8,128)(2,1)S(1)} %get-tuple-element.71.refs_1_, ...), custom_call_target="tpu_custom_call", output_to_operand_aliasing={{0}: (7, {}), {1}: (8, {}), {2}: (9, {})} | custom-call | flops 73400320 | bytes 2293760 | tf_op jit(solution)/shard_map/pallas_call | solution.py:191
  18.0 0.6 %collective-permute-start.7 = (bf16[3,64,640]{2,1,0:T(8,128)(2,1)S(1)}, bf16[3,64,640]{2,1,0:T(8,128)(2,1)S(1)}, u32[]{:S(2)}, u32[]{:S(2)}) collective-permute-start(bf16[3,64,640]{2,1,0:T(8,128)(2,1)S(1)} %collective-permute-done.5.refs_3_), channel_id=1, source_target_pairs={{0,10},{8,1},{10,4},{2,8},{4,14},{12,2},{14,7},{6,12},{7,13},{15,6... | collective-permute-start | bytes 737288 | tf_op jit(solution)/shard_map/ppermute | solution.py:40
  18.6 2.0 %shard_map.108 = (bf16[2,640,5120]{2,1,0:T(8,128)(2,1)}, bf16[2,128,5120]{2,1,0:T(8,128)(2,1)}, bf16[2,128,5120]{2,1,0:T(8,128)(2,1)}) custom-call(bf16[2,640,64]{2,1,0:T(8,128)(2,1)S(1)} %get-tuple-element.70.refs_0_, bf16[2,128,64]{2,1,0:T(8,128)(2,1)S(1)} %get-tuple-element.71.refs_1_, ...), custom_call_target="tpu_custom_call", output_to_operand_aliasing={{0}: (9, {}), {1}: (10, {}), {2}: (11, {})} | custom-call | flops 220200960 | bytes 6881280 | tf_op jit(solution)/shard_map/pallas_call | solution.py:191
  20.6 0.2 collective-permute-done.8.refs_4_
  20.8 0.6 %collective-permute-start.15 = (bf16[3,64,640]{2,1,0:T(8,128)(2,1)S(1)}, bf16[3,64,640]{2,1,0:T(8,128)(2,1)S(1)}, u32[]{:S(2)}, u32[]{:S(2)}) collective-permute-start(bf16[3,64,640]{2,1,0:T(8,128)(2,1)S(1)} %collective-permute-done.8.refs_4_), channel_id=1, source_target_pairs={{0,8},{8,0},{1,9},{9,1},{2,10},{10,2},{3,11},{11,3},{4,12},{12,4},... | collective-permute-start | bytes 737288 | tf_op jit(solution)/shard_map/ppermute | solution.py:44
  21.4 1.7 %collective-permute-start.13 = (bf16[3,64,640]{2,1,0:T(8,128)(2,1)S(1)}, bf16[3,64,640]{2,1,0:T(8,128)(2,1)S(1)}, u32[]{:S(2)}, u32[]{:S(2)}) collective-permute-start(bf16[3,64,640]{2,1,0:T(8,128)(2,1)S(1)} %collective-permute-done.8.refs_4_), channel_id=1, source_target_pairs={{0,10},{8,1},{10,4},{2,8},{4,14},{12,2},{14,7},{6,12},{7,13},{15,6... | collective-permute-start | bytes 737288 | tf_op jit(solution)/shard_map/ppermute | solution.py:40
  23.1 1.2 %shard_map.109 = (bf16[2,640,5120]{2,1,0:T(8,128)(2,1)}, bf16[2,128,5120]{2,1,0:T(8,128)(2,1)}, bf16[2,128,5120]{2,1,0:T(8,128)(2,1)}) custom-call(bf16[2,640,64]{2,1,0:T(8,128)(2,1)S(1)} %get-tuple-element.70.refs_0_, bf16[2,128,64]{2,1,0:T(8,128)(2,1)S(1)} %get-tuple-element.71.refs_1_, ...), custom_call_target="tpu_custom_call", output_to_operand_aliasing={{0}: (7, {}), {1}: (8, {}), {2}: (9, {})} | custom-call | flops 73400320 | bytes 2293760 | tf_op jit(solution)/shard_map/pallas_call | solution.py:191
  24.3 0.1 collective-permute-start.12
  24.4 0.6 %collective-permute-start.11 = (bf16[3,64,640]{2,1,0:T(8,128)(2,1)S(1)}, bf16[3,64,640]{2,1,0:T(8,128)(2,1)S(1)}, u32[]{:S(2)}, u32[]{:S(2)}) collective-permute-start(bf16[3,64,640]{2,1,0:T(8,128)(2,1)S(1)} %collective-permute-done.7.refs_3_), channel_id=1, source_target_pairs={{0,10},{8,1},{10,4},{2,8},{4,14},{12,2},{14,7},{6,12},{7,13},{15,6... | collective-permute-start | bytes 737288 | tf_op jit(solution)/shard_map/ppermute | solution.py:40
  25.0 2.0 %shard_map.110 = (bf16[2,640,5120]{2,1,0:T(8,128)(2,1)}, bf16[2,128,5120]{2,1,0:T(8,128)(2,1)}, bf16[2,128,5120]{2,1,0:T(8,128)(2,1)}) custom-call(bf16[2,640,64]{2,1,0:T(8,128)(2,1)S(1)} %get-tuple-element.70.refs_0_, bf16[2,128,64]{2,1,0:T(8,128)(2,1)S(1)} %get-tuple-element.71.refs_1_, ...), custom_call_target="tpu_custom_call", output_to_operand_aliasing={{0}: (9, {}), {1}: (10, {}), {2}: (11, {})} | custom-call | flops 220200960 | bytes 6881280 | tf_op jit(solution)/shard_map/pallas_call | solution.py:191
  27.0 0.8 %collective-permute-start.17 = (bf16[3,64,640]{2,1,0:T(8,128)(2,1)S(1)}, bf16[3,64,640]{2,1,0:T(8,128)(2,1)S(1)}, u32[]{:S(2)}, u32[]{:S(2)}) collective-permute-start(bf16[3,64,640]{2,1,0:T(8,128)(2,1)S(1)} %collective-permute-done.13.refs_5_), channel_id=1, source_target_pairs={{0,8},{8,0},{1,9},{9,1},{2,10},{10,2},{3,11},{11,3},{4,12},{12,4},... | collective-permute-start | bytes 737288 | tf_op jit(solution)/shard_map/ppermute | solution.py:44
  27.8 2.0 %shard_map.111 = (bf16[2,640,5120]{2,1,0:T(8,128)(2,1)}, bf16[2,128,5120]{2,1,0:T(8,128)(2,1)}, bf16[2,128,5120]{2,1,0:T(8,128)(2,1)}) custom-call(bf16[2,640,64]{2,1,0:T(8,128)(2,1)S(1)} %get-tuple-element.70.refs_0_, bf16[2,128,64]{2,1,0:T(8,128)(2,1)S(1)} %get-tuple-element.71.refs_1_, ...), custom_call_target="tpu_custom_call", output_to_operand_aliasing={{0}: (9, {}), {1}: (10, {}), {2}: (11, {})} | custom-call | flops 220200960 | bytes 6881280 | tf_op jit(solution)/shard_map/pallas_call | solution.py:191
  29.8 0.3 collective-permute-done.11.refs_4_
  30.1 0.4 %collective-permute-start.16 = (bf16[3,64,640]{2,1,0:T(8,128)(2,1)S(1)}, bf16[3,64,640]{2,1,0:T(8,128)(2,1)S(1)}, u32[]{:S(2)}, u32[]{:S(2)}) collective-permute-start(bf16[3,64,640]{2,1,0:T(8,128)(2,1)S(1)} %collective-permute-done.11.refs_4_), channel_id=1, source_target_pairs={{0,8},{8,0},{1,9},{9,1},{2,10},{10,2},{3,11},{11,3},{4,12},{12,4},... | collective-permute-start | bytes 737288 | tf_op jit(solution)/shard_map/ppermute | solution.py:44
  30.5 1.6 %shard_map.112 = (bf16[2,640,5120]{2,1,0:T(8,128)(2,1)}, bf16[2,128,5120]{2,1,0:T(8,128)(2,1)}, bf16[2,128,5120]{2,1,0:T(8,128)(2,1)}) custom-call(bf16[2,640,64]{2,1,0:T(8,128)(2,1)S(1)} %get-tuple-element.70.refs_0_, bf16[2,128,64]{2,1,0:T(8,128)(2,1)S(1)} %get-tuple-element.71.refs_1_, ...), custom_call_target="tpu_custom_call", output_to_operand_aliasing={{0}: (8, {}), {1}: (9, {}), {2}: (10, {})} | custom-call | flops 146800640 | bytes 4587520 | tf_op jit(solution)/shard_map/pallas_call | solution.py:191
  32.2 1.3 %shard_map.113 = (bf16[2,640,5120]{2,1,0:T(8,128)(2,1)}, bf16[2,128,5120]{2,1,0:T(8,128)(2,1)}, bf16[2,128,5120]{2,1,0:T(8,128)(2,1)}) custom-call(bf16[2,640,64]{2,1,0:T(8,128)(2,1)S(1)} %get-tuple-element.70.refs_0_, bf16[2,128,64]{2,1,0:T(8,128)(2,1)S(1)} %get-tuple-element.71.refs_1_, ...), custom_call_target="tpu_custom_call", output_to_operand_aliasing={{0}: (7, {}), {1}: (8, {}), {2}: (9, {})} | custom-call | flops 73400320 | bytes 2293760 | tf_op jit(solution)/shard_map/pallas_call | solution.py:191
  (38 shorter events, 0.2 us)
Async XLA Ops:
  0.6 2.3 %copy-start.2 = (bf16[1,2,3,64,640]{4,3,2,1,0:T(8,128)(2,1)S(1)}, bf16[1,2,3,64,640]{4,3,2,1,0:T(8,128)(2,1)}, u32[]{:S(2)}) copy-start(bf16[1,2,3,64,640]{4,3,2,1,0:T(8,128)(2,1)} %param.12) | copy-start | bytes 1474564
  0.6 2.3 %copy-start.6 = (s32[2,3]{1,0:T(2,128)S(1)}, s32[2,3]{1,0:T(2,128)}, u32[]{:S(2)}) copy-start(s32[2,3]{1,0:T(2,128)} %owners.3) | copy-start | bytes 76
  0.7 5.2 %copy-start.3 = (bf16[1,2,640,64]{2,3,1,0:T(8,128)(2,1)S(1)}, bf16[1,2,640,64]{2,3,1,0:T(8,128)(2,1)}, u32[]{:S(2)}) copy-start(bf16[1,2,640,64]{2,3,1,0:T(8,128)(2,1)} %param.13) | copy-start | bytes 491524
  0.7 5.5 %copy-start.4 = (bf16[1,2,128,64]{2,3,1,0:T(8,128)(2,1)S(1)}, bf16[1,2,128,64]{2,3,1,0:T(8,128)(2,1)}, u32[]{:S(2)}) copy-start(bf16[1,2,128,64]{2,3,1,0:T(8,128)(2,1)} %param.14) | copy-start | bytes 98308
  0.7 8.1 %copy-start.5 = (bf16[1,2,128,64]{2,3,1,0:T(8,128)(2,1)S(1)}, bf16[1,2,128,64]{2,3,1,0:T(8,128)(2,1)}, u32[]{:S(2)}) copy-start(bf16[1,2,128,64]{2,3,1,0:T(8,128)(2,1)} %param.15) | copy-start | bytes 98308
  0.7 2.2 %collective-permute-start = (bf16[2,3,64,640]{3,2,1,0:T(8,128)(2,1)}, bf16[2,3,64,640]{3,2,1,0:T(8,128)(2,1)S(1)}, u32[]{:S(2)}, u32[]{:S(2)}) collective-permute-start(bf16[2,3,64,640]{3,2,1,0:T(8,128)(2,1)} %bitcast.12), channel_id=1, source_target_pairs={{0,8},{8,0},{1,9},{9,1},{2,10},{10,2},{3,11},{11,3},{4,12},{12,4},... | collective-permute-start | bytes 1474568 | tf_op jit(solution)/shard_map/ppermute | solution.py:44
  1.2 15.4 %slice-start = ((s8[13107200]{0:T(1024)(128)(4,1)}), s8[4194304]{0:T(1024)(128)(4,1)S(1)}, s32[]{:S(2)}) async-start(s8[13107200]{0:T(1024)(128)(4,1)} %bitcast.10), calls=%async_computation | async-start | bytes 8388608
  1.2 15.4 %slice-start.1 = ((s8[13107200]{0:T(1024)(128)(4,1)}), s8[4194304]{0:T(1024)(128)(4,1)S(1)}, s32[]{:S(2)}) async-start(s8[13107200]{0:T(1024)(128)(4,1)} %bitcast.10), calls=%async_computation.1 | async-start | bytes 8388608
  1.2 15.4 %slice-start.2 = ((s8[13107200]{0:T(1024)(128)(4,1)}), s8[4194304]{0:T(1024)(128)(4,1)S(1)}, s32[]{:S(2)}) async-start(s8[13107200]{0:T(1024)(128)(4,1)} %bitcast.10), calls=%async_computation.2 | async-start | bytes 8388608
  3.1 8.5 %collective-permute-start.1 = (bf16[3,64,640]{2,1,0:T(8,128)(2,1)S(1)}, bf16[3,64,640]{2,1,0:T(8,128)(2,1)S(1)}, u32[]{:S(2)}, u32[]{:S(2)}) collective-permute-start(bf16[3,64,640]{2,1,0:T(8,128)(2,1)S(1)} %get-tuple-element.64.refs_3_), channel_id=1, source_target_pairs={{0,10},{8,1},{10,4},{2,8},{4,14},{12,2},{14,7},{6,12},{7,13},{15,6... | collective-permute-start | bytes 737288 | tf_op jit(solution)/shard_map/ppermute | solution.py:40
  5.8 4.2 %collective-permute-start.2 = (bf16[2,64,640]{2,1,0:T(8,128)(2,1)S(1)}, bf16[2,64,640]{2,1,0:T(8,128)(2,1)S(1)}, u32[]{:S(2)}, u32[]{:S(2)}) collective-permute-start(bf16[2,64,640]{2,1,0:T(8,128)(2,1)S(1)} %bitcast.14), channel_id=1, source_target_pairs={{0,8},{8,0},{1,9},{9,1},{2,10},{10,2},{3,11},{11,3},{4,12},{12,4},... | collective-permute-start | bytes 491528 | tf_op jit(solution)/shard_map/ppermute | solution.py:44
  6.1 1.2 %collective-permute-start.3 = (bf16[2,64,128]{2,1,0:T(8,128)(2,1)S(1)}, bf16[2,64,128]{2,1,0:T(8,128)(2,1)S(1)}, u32[]{:S(2)}, u32[]{:S(2)}) collective-permute-start(bf16[2,64,128]{2,1,0:T(8,128)(2,1)S(1)} %bitcast.16), channel_id=1, source_target_pairs={{0,8},{8,0},{1,9},{9,1},{2,10},{10,2},{3,11},{11,3},{4,12},{12,4},... | collective-permute-start | bytes 98312 | tf_op jit(solution)/shard_map/ppermute | solution.py:44
  7.3 7.2 %collective-permute-start.6 = (bf16[3,64,640]{2,1,0:T(8,128)(2,1)S(1)}, bf16[3,64,640]{2,1,0:T(8,128)(2,1)S(1)}, u32[]{:S(2)}, u32[]{:S(2)}) collective-permute-start(bf16[3,64,640]{2,1,0:T(8,128)(2,1)S(1)} %get-tuple-element.74.refs_4_), channel_id=1, source_target_pairs={{0,10},{8,1},{10,4},{2,8},{4,14},{12,2},{14,7},{6,12},{7,13},{15,6... | collective-permute-start | bytes 737288 | tf_op jit(solution)/shard_map/ppermute | solution.py:40
  8.8 7.8 %slice-start.3 = ((s8[13107200]{0:T(1024)(128)(4,1)}), s8[524288]{0:T(1024)(128)(4,1)S(1)}, s32[]{:S(2)}) async-start(s8[13107200]{0:T(1024)(128)(4,1)} %bitcast.10), calls=%async_computation.3 | async-start | bytes 1048576
  8.8 1.2 %collective-permute-start.4 = (bf16[2,64,128]{2,1,0:T(8,128)(2,1)S(1)}, bf16[2,64,128]{2,1,0:T(8,128)(2,1)S(1)}, u32[]{:S(2)}, u32[]{:S(2)}) collective-permute-start(bf16[2,64,128]{2,1,0:T(8,128)(2,1)S(1)} %bitcast.18), channel_id=1, source_target_pairs={{0,8},{8,0},{1,9},{9,1},{2,10},{10,2},{3,11},{11,3},{4,12},{12,4},... | collective-permute-start | bytes 98312 | tf_op jit(solution)/shard_map/ppermute | solution.py:44
  10.0 6.6 %copy-start.1 = (bf16[2,128,5120]{2,1,0:T(8,128)(2,1)S(1)}, bf16[2,128,5120]{2,1,0:T(8,128)(2,1)}, u32[]{:S(2)}) copy-start(bf16[2,128,5120]{2,1,0:T(8,128)(2,1)} %refs_6_.15) | copy-start | bytes 7864324
  11.5 5.1 %copy-start = (bf16[2,128,5120]{2,1,0:T(8,128)(2,1)S(1)}, bf16[2,128,5120]{2,1,0:T(8,128)(2,1)}, u32[]{:S(2)}) copy-start(bf16[2,128,5120]{2,1,0:T(8,128)(2,1)} %refs_5_.7) | copy-start | bytes 7864324
  11.6 6.4 %collective-permute-start.5 = (bf16[3,64,640]{2,1,0:T(8,128)(2,1)S(1)}, bf16[3,64,640]{2,1,0:T(8,128)(2,1)S(1)}, u32[]{:S(2)}, u32[]{:S(2)}) collective-permute-start(bf16[3,64,640]{2,1,0:T(8,128)(2,1)S(1)} %collective-permute-done.1.refs_3_), channel_id=1, source_target_pairs={{0,10},{8,1},{10,4},{2,8},{4,14},{12,2},{14,7},{6,12},{7,13},{15,6... | collective-permute-start | bytes 737288 | tf_op jit(solution)/shard_map/ppermute | solution.py:40
  14.6 4.0 %collective-permute-start.10 = (bf16[3,64,640]{2,1,0:T(8,128)(2,1)S(1)}, bf16[3,64,640]{2,1,0:T(8,128)(2,1)S(1)}, u32[]{:S(2)}, u32[]{:S(2)}) collective-permute-start(bf16[3,64,640]{2,1,0:T(8,128)(2,1)S(1)} %collective-permute-done.6.refs_4_), channel_id=1, source_target_pairs={{0,8},{8,0},{1,9},{9,1},{2,10},{10,2},{3,11},{11,3},{4,12},{12,4},... | collective-permute-start | bytes 737288 | tf_op jit(solution)/shard_map/ppermute | solution.py:44
  14.9 3.6 %collective-permute-start.9 = (bf16[3,64,640]{2,1,0:T(8,128)(2,1)S(1)}, bf16[3,64,640]{2,1,0:T(8,128)(2,1)S(1)}, u32[]{:S(2)}, u32[]{:S(2)}) collective-permute-start(bf16[3,64,640]{2,1,0:T(8,128)(2,1)S(1)} %collective-permute-done.1.refs_3_), channel_id=1, source_target_pairs={{0,8},{8,0},{1,9},{9,1},{2,10},{10,2},{3,11},{11,3},{4,12},{12,4},... | collective-permute-start | bytes 737288 | tf_op jit(solution)/shard_map/ppermute | solution.py:44
  15.1 5.6 %collective-permute-start.8 = (bf16[3,64,640]{2,1,0:T(8,128)(2,1)S(1)}, bf16[3,64,640]{2,1,0:T(8,128)(2,1)S(1)}, u32[]{:S(2)}, u32[]{:S(2)}) collective-permute-start(bf16[3,64,640]{2,1,0:T(8,128)(2,1)S(1)} %collective-permute-done.6.refs_4_), channel_id=1, source_target_pairs={{0,10},{8,1},{10,4},{2,8},{4,14},{12,2},{14,7},{6,12},{7,13},{15,6... | collective-permute-start | bytes 737288 | tf_op jit(solution)/shard_map/ppermute | solution.py:40
  18.0 6.4 %collective-permute-start.7 = (bf16[3,64,640]{2,1,0:T(8,128)(2,1)S(1)}, bf16[3,64,640]{2,1,0:T(8,128)(2,1)S(1)}, u32[]{:S(2)}, u32[]{:S(2)}) collective-permute-start(bf16[3,64,640]{2,1,0:T(8,128)(2,1)S(1)} %collective-permute-done.5.refs_3_), channel_id=1, source_target_pairs={{0,10},{8,1},{10,4},{2,8},{4,14},{12,2},{14,7},{6,12},{7,13},{15,6... | collective-permute-start | bytes 737288 | tf_op jit(solution)/shard_map/ppermute | solution.py:40
  20.8 4.2 %collective-permute-start.15 = (bf16[3,64,640]{2,1,0:T(8,128)(2,1)S(1)}, bf16[3,64,640]{2,1,0:T(8,128)(2,1)S(1)}, u32[]{:S(2)}, u32[]{:S(2)}) collective-permute-start(bf16[3,64,640]{2,1,0:T(8,128)(2,1)S(1)} %collective-permute-done.8.refs_4_), channel_id=1, source_target_pairs={{0,8},{8,0},{1,9},{9,1},{2,10},{10,2},{3,11},{11,3},{4,12},{12,4},... | collective-permute-start | bytes 737288 | tf_op jit(solution)/shard_map/ppermute | solution.py:44
  21.4 3.6 %collective-permute-start.14 = (bf16[3,64,640]{2,1,0:T(8,128)(2,1)S(1)}, bf16[3,64,640]{2,1,0:T(8,128)(2,1)S(1)}, u32[]{:S(2)}, u32[]{:S(2)}) collective-permute-start(bf16[3,64,640]{2,1,0:T(8,128)(2,1)S(1)} %collective-permute-done.5.refs_3_), channel_id=1, source_target_pairs={{0,8},{8,0},{1,9},{9,1},{2,10},{10,2},{3,11},{11,3},{4,12},{12,4},... | collective-permute-start | bytes 737288 | tf_op jit(solution)/shard_map/ppermute | solution.py:44
  21.4 5.6 %collective-permute-start.13 = (bf16[3,64,640]{2,1,0:T(8,128)(2,1)S(1)}, bf16[3,64,640]{2,1,0:T(8,128)(2,1)S(1)}, u32[]{:S(2)}, u32[]{:S(2)}) collective-permute-start(bf16[3,64,640]{2,1,0:T(8,128)(2,1)S(1)} %collective-permute-done.8.refs_4_), channel_id=1, source_target_pairs={{0,10},{8,1},{10,4},{2,8},{4,14},{12,2},{14,7},{6,12},{7,13},{15,6... | collective-permute-start | bytes 737288 | tf_op jit(solution)/shard_map/ppermute | solution.py:40
  24.3 3.5 %collective-permute-start.12 = (bf16[3,64,640]{2,1,0:T(8,128)(2,1)S(1)}, bf16[3,64,640]{2,1,0:T(8,128)(2,1)S(1)}, u32[]{:S(2)}, u32[]{:S(2)}) collective-permute-start(bf16[3,64,640]{2,1,0:T(8,128)(2,1)S(1)} %collective-permute-done.7.refs_3_), channel_id=1, source_target_pairs={{0,8},{8,0},{1,9},{9,1},{2,10},{10,2},{3,11},{11,3},{4,12},{12,4},... | collective-permute-start | bytes 737288 | tf_op jit(solution)/shard_map/ppermute | solution.py:44
  24.4 5.7 %collective-permute-start.11 = (bf16[3,64,640]{2,1,0:T(8,128)(2,1)S(1)}, bf16[3,64,640]{2,1,0:T(8,128)(2,1)S(1)}, u32[]{:S(2)}, u32[]{:S(2)}) collective-permute-start(bf16[3,64,640]{2,1,0:T(8,128)(2,1)S(1)} %collective-permute-done.7.refs_3_), channel_id=1, source_target_pairs={{0,10},{8,1},{10,4},{2,8},{4,14},{12,2},{14,7},{6,12},{7,13},{15,6... | collective-permute-start | bytes 737288 | tf_op jit(solution)/shard_map/ppermute | solution.py:40
  27.0 3.5 %collective-permute-start.17 = (bf16[3,64,640]{2,1,0:T(8,128)(2,1)S(1)}, bf16[3,64,640]{2,1,0:T(8,128)(2,1)S(1)}, u32[]{:S(2)}, u32[]{:S(2)}) collective-permute-start(bf16[3,64,640]{2,1,0:T(8,128)(2,1)S(1)} %collective-permute-done.13.refs_5_), channel_id=1, source_target_pairs={{0,8},{8,0},{1,9},{9,1},{2,10},{10,2},{3,11},{11,3},{4,12},{12,4},... | collective-permute-start | bytes 737288 | tf_op jit(solution)/shard_map/ppermute | solution.py:44
  30.1 2.1 %collective-permute-start.16 = (bf16[3,64,640]{2,1,0:T(8,128)(2,1)S(1)}, bf16[3,64,640]{2,1,0:T(8,128)(2,1)S(1)}, u32[]{:S(2)}, u32[]{:S(2)}) collective-permute-start(bf16[3,64,640]{2,1,0:T(8,128)(2,1)S(1)} %collective-permute-done.11.refs_4_), channel_id=1, source_target_pairs={{0,8},{8,0},{1,9},{9,1},{2,10},{10,2},{3,11},{11,3},{4,12},{12,4},... | collective-permute-start | bytes 737288 | tf_op jit(solution)/shard_map/ppermute | solution.py:44

commit v16 on v15

--- a/solution.py
+++ b/solution.py
@@ -123,40 +123,7 @@
     )(*[in_hbm(base) for base in bases])
 
 
-def choose_b_kernel(n, pieces, owners, *refs):
-    core = lax.axis_index("rollout")
-    own, other, refs, sems = refs[0:3], refs[3:6], refs[6:-1], refs[-1]
-    count = (len(refs) - 3) // 2
-    bases, outs, blocks = refs[:count], refs[count : count + 3], refs[count + 3 :]
-    fetches = start_fetches(n, pieces, bases, blocks, sems)
-    for proj in range(3):
-        for layer in range(own[proj].shape[0]):
-            mine = owned(owners, layer, proj, core, own[proj].shape[1:])
-            outs[proj][layer] = jnp.where(mine, own[proj][layer], other[proj][layer]).T
-    for fetch in fetches:
-        fetch.wait()
-
-
-def choose_b(n, cols, owners, own, other, bases, pieces):
-    chosen = [jax.ShapeDtypeStruct((x.shape[0], x.shape[2], x.shape[1]), x.dtype) for x in own]
-    blocks = block_shapes(bases, pieces, cols)
-    out = pl.pallas_call(
-        functools.partial(choose_b_kernel, n, pieces),
-        in_specs=[VMEM] * 7 + [HBM] * len(bases),
-        out_specs=[VMEM] * (3 + len(blocks)),
-        out_shape=chosen + blocks,
-        scratch_shapes=[pltpu.SemaphoreType.DMA((len(bases) * len(pieces),))],
-        compiler_params=pltpu.CompilerParams(vmem_limit_bytes=4 * MIB),
-        cost_estimate=moved(blocks),
-    )(in_vmem(owners), *[in_vmem(x) for x in own], *other, *[in_hbm(base) for base in bases])
-    return out[:3], out[3:]
-
-
-def merge_kernel(n, pieces, scale, fresh, *refs):
-    count = len(pieces)
-    b_refs, a_refs, bases = refs[0:3], refs[3 : 3 + count], refs[3 + count : 6 + count]
-    at = 6 + count + (0 if fresh else 3)
-    outs, bufs, sem = refs[at : at + 3], refs[at + 3 : at + 6], refs[at + 6]
+def merge_pieces(n, pieces, scale, b_refs, a_refs, base_of, outs, bufs, sem):
     cols = a_refs[0].shape[-1]
     for i, (layer, start) in enumerate(column_starts(n, pieces, cols)):
         for proj in (1, 2, 0):
@@ -165,13 +132,12 @@
                 rows = pl.ds(row, min(TILE_ROWS, last_row - row))
                 for col in range(0, cols, TILE_COLS):
                     width = min(TILE_COLS, cols - col)
-                    tile = pl.ds(col, width) if fresh else pl.ds(pl.multiple_of(start + col, LANES), width)
                     delta = jnp.dot(
                         b_refs[proj][layer, rows],
                         a_refs[i][proj, :, col : col + width],
                         preferred_element_type=jnp.float32,
                     )
-                    block = bases[proj][i if fresh else layer, rows, tile]
+                    block = base_of(proj, i, layer, rows, start, col, width)
                     merged = block.astype(jnp.float32) + scale * delta
                     bufs[proj][i, rows, col : col + width] = merged.astype(jnp.bfloat16)
                 end = min(row + TILE_ROWS, last_row)
@@ -184,25 +150,84 @@
         pltpu.make_async_copy(bufs[proj], bufs[proj], sem.at[proj]).wait()
 
 
-def merge(n, scale, b, a_list, bases, shapes, outs, pieces):
-    fresh = outs is None
+def merge_own_kernel(n, pieces, scale, owners, *refs):
+    own, other, small_bases, query_block = refs[0:3], refs[3:6], refs[6:8], refs[8]
+    a_refs, outs, b_refs = refs[9:11], refs[11:14], refs[14:17]
+    small_blocks, bufs, load_sems, sem = refs[17:19], refs[19:22], refs[22], refs[23]
+    core = lax.axis_index("rollout")
+    fetches = start_fetches(n, pieces, small_bases, small_blocks, load_sems)
+    for proj in range(3):
+        for layer in range(own[proj].shape[0]):
+            mine = owned(owners, layer, proj, core, own[proj].shape[1:])
+            b_refs[proj][layer] = jnp.where(mine, own[proj][layer], other[proj][layer]).T
+    for fetch in fetches:
+        fetch.wait()
+    blocks = (query_block, *small_blocks)
+
+    def base_of(proj, i, layer, rows, start, col, width):
+        return blocks[proj][i, rows, col : col + width]
+
+    merge_pieces(n, pieces, scale, b_refs, a_refs, base_of, outs, bufs, sem)
+
+
+def merge_kernel(n, pieces, scale, *refs):
+    count = len(pieces)
+    b_refs, a_refs, bases = refs[0:3], refs[3 : 3 + count], refs[3 + count : 6 + count]
+    outs, bufs, sem = refs[9 + count : 12 + count], refs[12 + count : 15 + count], refs[15 + count]
+
+    def base_of(proj, i, layer, rows, start, col, width):
+        return bases[proj][layer, rows, pl.ds(pl.multiple_of(start + col, LANES), width)]
+
+    merge_pieces(n, pieces, scale, b_refs, a_refs, base_of, outs, bufs, sem)
+
+
+def merge_cost(bases, a_list):
     rank, cols = a_list[0].shape[-2:]
-    rows = sum(base.shape[1] for base in bases)
+    cells = len(a_list) * sum(base.shape[1] for base in bases) * cols
+    return pl.CostEstimate(flops=2 * cells * rank, bytes_accessed=4 * cells, transcendentals=0)
+
+
+def buffers(bases, a_list):
+    cols = a_list[0].shape[-1]
+    return [pltpu.VMEM((len(a_list), base.shape[1], cols), base.dtype) for base in bases]
+
+
+def merge_own(n, scale, owners, own, other, query_block, a_list, bases, pieces):
+    chosen = [jax.ShapeDtypeStruct((x.shape[0], x.shape[2], x.shape[1]), x.dtype) for x in own]
+    bufs = buffers(bases, a_list)
+    out = pl.pallas_call(
+        functools.partial(merge_own_kernel, n, pieces, scale),
+        in_specs=[VMEM] * 7 + [HBM] * 2 + [VMEM] * (1 + len(a_list)),
+        out_specs=[HBM] * 3 + [VMEM] * 3,
+        out_shape=[jax.ShapeDtypeStruct(base.shape, base.dtype) for base in bases] + chosen,
+        scratch_shapes=bufs[1:]
+        + bufs
+        + [pltpu.SemaphoreType.DMA((2 * len(pieces),)), pltpu.SemaphoreType.DMA((3,))],
+        compiler_params=pltpu.CompilerParams(vmem_limit_bytes=16 * MIB),
+        cost_estimate=merge_cost(bases, a_list),
+    )(
+        in_vmem(owners),
+        *[in_vmem(x) for x in own],
+        *other,
+        *[in_hbm(base) for base in bases[1:]],
+        query_block,
+        *a_list,
+    )
+    return out[:3], out[3:]
+
+
+def merge(n, scale, b, a_list, bases, outs, pieces):
     return pl.pallas_call(
-        functools.partial(merge_kernel, n, pieces, scale, fresh),
-        in_specs=[VMEM] * (3 + len(a_list) + 3) + [HBM] * (0 if fresh else 3),
+        functools.partial(merge_kernel, n, pieces, scale),
+        in_specs=[VMEM] * (3 + len(a_list) + 3) + [HBM] * 3,
         out_specs=[HBM] * 3,
-        out_shape=shapes,
-        scratch_shapes=[pltpu.VMEM((len(pieces), base.shape[1], cols), base.dtype) for base in bases]
-        + [pltpu.SemaphoreType.DMA((3,))],
-        input_output_aliases={} if fresh else {6 + len(a_list) + i: i for i in range(3)},
+        out_shape=[jax.ShapeDtypeStruct(base.shape, base.dtype) for base in bases],
+        scratch_shapes=buffers(bases, a_list) + [pltpu.SemaphoreType.DMA((3,))],
+        input_output_aliases={6 + len(a_list) + i: i for i in range(3)},
         compiler_params=pltpu.CompilerParams(vmem_limit_bytes=16 * MIB),
-        cost_estimate=pl.CostEstimate(
-            flops=2 * len(pieces) * rows * cols * rank,
-            bytes_accessed=4 * len(pieces) * rows * cols,
-            transcendentals=0,
-        ),
-    )(*b, *a_list, *(bases if fresh else [in_vmem(base) for base in bases]), *([] if fresh else outs))
+        cost_estimate=merge_cost(bases, a_list),
+    )(*b, *a_list, *[in_vmem(base) for base in bases], *outs)
+
 
 def per_device(
     n,
@@ -226,41 +251,37 @@
 
     if cols % LANES == 0:
         tie = lax.optimization_barrier
-        shapes = [jax.ShapeDtypeStruct(base.shape, base.dtype) for base in bases]
         pieces = [(0, True, True), (0, True, False)]
         query_block = fetch_blocks(n, cols, [base_query], pieces)
         other_a, query_block = tie((swap_cores(own_a), query_block))
         first, second = choose_a(owners, own_a, other_a)
         other_b = [swap_cores(x) for x in own_b]
-        second, other_b[1] = tie((second, other_b[1]))
         held = [first, second]
         first = ring_pass(first, n)
         second = ring_pass(second, n)
-        b, blocks = choose_b(n, cols, owners, own_b, other_b, [base_key, base_value], pieces)
-        first, b = tie((first, b))
-        outs = merge(n, scale, b, held, [*query_block, *blocks], shapes, None, pieces)
+        outs, b = merge_own(n, scale, owners, own_b, other_b, *query_block, held, bases, pieces)
+        first, outs = tie((first, outs))
 
         def go(outs, *named):
             pieces = [(step, not swapped, ((step % 2 == 0) == (ring == "a")) != swapped) for step, ring, swapped, _ in named]
-            return merge(n, scale, b, [chunk for *_, chunk in named], bases, shapes, outs, pieces)
-
-        before = []
+            return merge(n, scale, b, [chunk for *_, chunk in named], bases, outs, pieces)
+
+        swapped_a = swapped_b = ()
         for step in range(1, last):
             a_here = (step, "a", False, first)
             a_there = (step, "a", True, swap_cores(first))
             first = ring_pass(first, n)
-            if step > 1:
-                outs = go(outs, *before)
+            outs = go(outs, a_here, *swapped_a)
             second, outs = tie((second, outs))
             b_here = (step, "b", False, second)
-            swapped_b = (step, "b", True, swap_cores(second))
-            before = [a_there, b_here, swapped_b]
+            b_there = (step, "b", True, swap_cores(second))
             if step < last - 1:
                 second = ring_pass(second, n)
-            outs = go(outs, a_here, *(before[:2] if step == last - 1 else []))
+            outs = go(outs, b_here, *swapped_b, *([a_there] if step == last - 1 else []))
             first, outs = tie((first, outs))
+            swapped_a, swapped_b = (a_there,), (b_there,)
         a_there = (last, "a", True, swap_cores(first))
-        outs = go(outs, swapped_b, (last, "a", False, first))
+        outs = go(outs, *swapped_b, (last, "a", False, first))
         return tuple(go(outs, a_there))
 
     core = lax.axis_index("rollout")

time: 33.6 us -> 32.7 us (0.973)
  waiting for transfers between devices: 2.75 us -> 0.33 us
  Pallas kernels: 16.3 us -> 17.1 us
  starting transfers between devices: 13.5 us -> 14.2 us
    ppermute x11, waiting for transfers between devices: 2.29 us -> 0.15 us  [swap_cores(): return lax.ppermute(array, 'rollout', [(0, 1), (1, 0)])]
    ppermute x7, starting transfers between devices: 9.9 us -> 11.3 us  [ring_pass(): return lax.ppermute(array, ('rollout', 'tensor'), pairs)]
    pallas_call x9, Pallas kernels: 14.6 us -> 15.4 us  [the longest x8 12.3 us: merge(): pl.pallas_call(functools.partial(merge_kernel, n, pieces, scale), in_spec...]
    ppermute x11, starting transfers between devices: 3.62 us -> 2.9 us  [swap_cores(): return lax.ppermute(array, 'rollout', [(0, 1), (1, 0)])]
  transfers between devices with their start and end apart: 18 -> 18, of which waited for: 5 -> 2; matrix products, arithmetic and copies ran while one was open for 0% -> 0% of each run, Pallas kernels for 45% -> 48%
where the time goes in v16:
time: 32.7 us; the launch traced here: 32.5 us
  Pallas kernels  17.1 us (52%)
  starting transfers between devices  14.2 us (43%)
  between operations  0.86 us (3%)
  waiting for transfers between devices  0.33 us (1%)
    pallas_call x8, Pallas kernels, merge(): pl.pallas_call(functools.partial(merge_kernel, n, pieces, scale), in_spec...  12.3 us
    ppermute x7, starting transfers between devices, ring_pass(): return lax.ppermute(array, ('rollout', 'tensor'), pairs)  11.3 us
    pallas_call x1, Pallas kernels, merge_own(): pl.pallas_call(functools.partial(merge_own_kernel, n, pieces, scale), in_...  3.05 us
    ppermute x11, starting transfers between devices, swap_cores(): return lax.ppermute(array, 'rollout', [(0, 1), (1, 0)])  2.9 us
    pallas_call x1, Pallas kernels, fetch_blocks(): pl.pallas_call(functools.partial(fetch_kernel, n, pieces), in_specs=[HBM]...  1.56 us
  transfers between devices with their start and end apart: 18, of which 2 were waited for; matrix products, arithmetic and copies ran while one was open for 0% of the time, Pallas kernels for 48%

profile of v16, /device:TPU:0, one launch (start us, length us, event | category | flops | bytes accessed | tf_op | source)
XLA Modules:
  0.0 32.5 jit_solution(1064929859202595164)
XLA Ops:
  0.7 0.5 %collective-permute-start.3 = (bf16[2,3,64,640]{3,2,1,0:T(8,128)(2,1)}, bf16[2,3,64,640]{3,2,1,0:T(8,128)(2,1)S(1)}, u32[]{:S(2)}, u32[]{:S(2)}) collective-permute-start(bf16[2,3,64,640]{3,2,1,0:T(8,128)(2,1)} %bitcast.10), channel_id=1, source_target_pairs={{0,8},{8,0},{1,9},{9,1},{2,10},{10,2},{3,11},{11,3},{4,12},{12,4},... | collective-permute-start | bytes 1474568 | tf_op jit(solution)/shard_map/ppermute | solution.py:44
  1.2 1.6 %shard_map.103.refs_8_ = bf16[2,640,640]{2,1,0:T(8,128)(2,1)S(1)} custom-call(bf16[2,640,5120]{2,1,0:T(8,128)(2,1)} %refs_4_.5), custom_call_target="tpu_custom_call" | custom-call | bytes 3276800 | tf_op jit(solution)/shard_map/pallas_call | solution.py:115
  2.8 0.1 collective-permute-done.3.other
  2.9 0.1 shard_map.104
  3.1 2.7 %collective-permute-start.4 = (bf16[3,64,640]{2,1,0:T(8,128)(2,1)S(1)}, bf16[3,64,640]{2,1,0:T(8,128)(2,1)S(1)}, u32[]{:S(2)}, u32[]{:S(2)}) collective-permute-start(bf16[3,64,640]{2,1,0:T(8,128)(2,1)S(1)} %get-tuple-element.64.refs_9_), channel_id=1, source_target_pairs={{0,10},{8,1},{10,4},{2,8},{4,14},{12,2},{14,7},{6,12},{7,13},{15,6... | collective-permute-start | bytes 737288 | tf_op jit(solution)/shard_map/ppermute | solution.py:40
  5.8 0.3 collective-permute-start
  6.1 0.2 collective-permute-start.1
  6.3 0.3 collective-permute-start.2
  6.6 1.3 %collective-permute-start.6 = (bf16[3,64,640]{2,1,0:T(8,128)(2,1)S(1)}, bf16[3,64,640]{2,1,0:T(8,128)(2,1)S(1)}, u32[]{:S(2)}, u32[]{:S(2)}) collective-permute-start(bf16[3,64,640]{2,1,0:T(8,128)(2,1)S(1)} %get-tuple-element.65.refs_10_), channel_id=1, source_target_pairs={{0,10},{8,1},{10,4},{2,8},{4,14},{12,2},{14,7},{6,12},{7,13},{15,6... | collective-permute-start | bytes 737288 | tf_op jit(solution)/shard_map/ppermute | solution.py:40
  8.0 3.0 %shard_map.105 = (bf16[2,640,5120]{2,1,0:T(8,128)(2,1)}, bf16[2,128,5120]{2,1,0:T(8,128)(2,1)}, bf16[2,128,5120]{2,1,0:T(8,128)(2,1)}, bf16[2,640,64]{2,1,0:T(8,...) custom-call(s32[2,3]{1,0:T(2,128)S(1)} %copy-done.7, bf16[2,64,640]{2,1,0:T(8,128)(2,1)S(1)} %bitcast.13, ...), custom_call_target="tpu_custom_call" | custom-call | flops 146800640 | bytes 4587520 | tf_op jit(solution)/shard_map/pallas_call | solution.py:198
  11.0 1.5 %collective-permute-start.5 = (bf16[3,64,640]{2,1,0:T(8,128)(2,1)S(1)}, bf16[3,64,640]{2,1,0:T(8,128)(2,1)S(1)}, u32[]{:S(2)}, u32[]{:S(2)}) collective-permute-start(bf16[3,64,640]{2,1,0:T(8,128)(2,1)S(1)} %collective-permute-done.4.refs_3_), channel_id=1, source_target_pairs={{0,10},{8,1},{10,4},{2,8},{4,14},{12,2},{14,7},{6,12},{7,13},{15,6... | collective-permute-start | bytes 737288 | tf_op jit(solution)/shard_map/ppermute | solution.py:40
  12.5 0.1 collective-permute-start.9
  12.7 1.3 %shard_map.106 = (bf16[2,640,5120]{2,1,0:T(8,128)(2,1)}, bf16[2,128,5120]{2,1,0:T(8,128)(2,1)}, bf16[2,128,5120]{2,1,0:T(8,128)(2,1)}) custom-call(bf16[2,640,64]{2,1,0:T(8,128)(2,1)S(1)} %get-tuple-element.66.refs_0_, bf16[2,128,64]{2,1,0:T(8,128)(2,1)S(1)} %get-tuple-element.67.refs_1_, ...), custom_call_target="tpu_custom_call", output_to_operand_aliasing={{0}: (7, {}), {1}: (8, {}), {2}: (9, {})} | custom-call | flops 73400320 | bytes 2293760 | tf_op jit(solution)/shard_map/pallas_call | solution.py:220
  13.9 1.3 %collective-permute-start.8 = (bf16[3,64,640]{2,1,0:T(8,128)(2,1)S(1)}, bf16[3,64,640]{2,1,0:T(8,128)(2,1)S(1)}, u32[]{:S(2)}, u32[]{:S(2)}) collective-permute-start(bf16[3,64,640]{2,1,0:T(8,128)(2,1)S(1)} %collective-permute-done.6.refs_3_), channel_id=1, source_target_pairs={{0,10},{8,1},{10,4},{2,8},{4,14},{12,2},{14,7},{6,12},{7,13},{15,6... | collective-permute-start | bytes 737288 | tf_op jit(solution)/shard_map/ppermute | solution.py:40
  15.2 0.3 collective-permute-start.10
  15.5 1.3 %shard_map.107 = (bf16[2,640,5120]{2,1,0:T(8,128)(2,1)}, bf16[2,128,5120]{2,1,0:T(8,128)(2,1)}, bf16[2,128,5120]{2,1,0:T(8,128)(2,1)}) custom-call(bf16[2,640,64]{2,1,0:T(8,128)(2,1)S(1)} %get-tuple-element.66.refs_0_, bf16[2,128,64]{2,1,0:T(8,128)(2,1)S(1)} %get-tuple-element.67.refs_1_, ...), custom_call_target="tpu_custom_call", output_to_operand_aliasing={{0}: (7, {}), {1}: (8, {}), {2}: (9, {})} | custom-call | flops 73400320 | bytes 2293760 | tf_op jit(solution)/shard_map/pallas_call | solution.py:220
  16.7 0.0 collective-permute-done.5.refs_3_
  16.7 1.7 %collective-permute-start.7 = (bf16[3,64,640]{2,1,0:T(8,128)(2,1)S(1)}, bf16[3,64,640]{2,1,0:T(8,128)(2,1)S(1)}, u32[]{:S(2)}, u32[]{:S(2)}) collective-permute-start(bf16[3,64,640]{2,1,0:T(8,128)(2,1)S(1)} %collective-permute-done.5.refs_3_), channel_id=1, source_target_pairs={{0,10},{8,1},{10,4},{2,8},{4,14},{12,2},{14,7},{6,12},{7,13},{15,6... | collective-permute-start | bytes 737288 | tf_op jit(solution)/shard_map/ppermute | solution.py:40
  18.4 1.6 %shard_map.108 = (bf16[2,640,5120]{2,1,0:T(8,128)(2,1)}, bf16[2,128,5120]{2,1,0:T(8,128)(2,1)}, bf16[2,128,5120]{2,1,0:T(8,128)(2,1)}) custom-call(bf16[2,640,64]{2,1,0:T(8,128)(2,1)S(1)} %get-tuple-element.66.refs_0_, bf16[2,128,64]{2,1,0:T(8,128)(2,1)S(1)} %get-tuple-element.67.refs_1_, ...), custom_call_target="tpu_custom_call", output_to_operand_aliasing={{0}: (8, {}), {1}: (9, {}), {2}: (10, {})} | custom-call | flops 146800640 | bytes 4587520 | tf_op jit(solution)/shard_map/pallas_call | solution.py:220
  20.1 1.1 %collective-permute-start.12 = (bf16[3,64,640]{2,1,0:T(8,128)(2,1)S(1)}, bf16[3,64,640]{2,1,0:T(8,128)(2,1)S(1)}, u32[]{:S(2)}, u32[]{:S(2)}) collective-permute-start(bf16[3,64,640]{2,1,0:T(8,128)(2,1)S(1)} %collective-permute-done.8.refs_3_), channel_id=1, source_target_pairs={{0,10},{8,1},{10,4},{2,8},{4,14},{12,2},{14,7},{6,12},{7,13},{15,6... | collective-permute-start | bytes 737288 | tf_op jit(solution)/shard_map/ppermute | solution.py:40
  21.2 0.6 %collective-permute-start.14 = (bf16[3,64,640]{2,1,0:T(8,128)(2,1)S(1)}, bf16[3,64,640]{2,1,0:T(8,128)(2,1)S(1)}, u32[]{:S(2)}, u32[]{:S(2)}) collective-permute-start(bf16[3,64,640]{2,1,0:T(8,128)(2,1)S(1)} %collective-permute-done.8.refs_3_), channel_id=1, source_target_pairs={{0,8},{8,0},{1,9},{9,1},{2,10},{10,2},{3,11},{11,3},{4,12},{12,4},... | collective-permute-start | bytes 737288 | tf_op jit(solution)/shard_map/ppermute | solution.py:44
  21.8 0.0 collective-permute-done.10.refs_4_
  21.8 1.6 %shard_map.109 = (bf16[2,640,5120]{2,1,0:T(8,128)(2,1)}, bf16[2,128,5120]{2,1,0:T(8,128)(2,1)}, bf16[2,128,5120]{2,1,0:T(8,128)(2,1)}) custom-call(bf16[2,640,64]{2,1,0:T(8,128)(2,1)S(1)} %get-tuple-element.66.refs_0_, bf16[2,128,64]{2,1,0:T(8,128)(2,1)S(1)} %get-tuple-element.67.refs_1_, ...), custom_call_target="tpu_custom_call", output_to_operand_aliasing={{0}: (8, {}), {1}: (9, {}), {2}: (10, {})} | custom-call | flops 146800640 | bytes 4587520 | tf_op jit(solution)/shard_map/pallas_call | solution.py:220
  23.4 0.1 collective-permute-start.15
  23.5 1.7 %collective-permute-start.11 = (bf16[3,64,640]{2,1,0:T(8,128)(2,1)S(1)}, bf16[3,64,640]{2,1,0:T(8,128)(2,1)S(1)}, u32[]{:S(2)}, u32[]{:S(2)}) collective-permute-start(bf16[3,64,640]{2,1,0:T(8,128)(2,1)S(1)} %collective-permute-done.7.refs_3_), channel_id=1, source_target_pairs={{0,10},{8,1},{10,4},{2,8},{4,14},{12,2},{14,7},{6,12},{7,13},{15,6... | collective-permute-start | bytes 737288 | tf_op jit(solution)/shard_map/ppermute | solution.py:40
  25.2 1.6 %shard_map.110 = (bf16[2,640,5120]{2,1,0:T(8,128)(2,1)}, bf16[2,128,5120]{2,1,0:T(8,128)(2,1)}, bf16[2,128,5120]{2,1,0:T(8,128)(2,1)}) custom-call(bf16[2,640,64]{2,1,0:T(8,128)(2,1)S(1)} %get-tuple-element.66.refs_0_, bf16[2,128,64]{2,1,0:T(8,128)(2,1)S(1)} %get-tuple-element.67.refs_1_, ...), custom_call_target="tpu_custom_call", output_to_operand_aliasing={{0}: (8, {}), {1}: (9, {}), {2}: (10, {})} | custom-call | flops 146800640 | bytes 4587520 | tf_op jit(solution)/shard_map/pallas_call | solution.py:220
  26.9 0.1 collective-permute-start.17
  27.0 2.0 %shard_map.111 = (bf16[2,640,5120]{2,1,0:T(8,128)(2,1)}, bf16[2,128,5120]{2,1,0:T(8,128)(2,1)}, bf16[2,128,5120]{2,1,0:T(8,128)(2,1)}) custom-call(bf16[2,640,64]{2,1,0:T(8,128)(2,1)S(1)} %get-tuple-element.66.refs_0_, bf16[2,128,64]{2,1,0:T(8,128)(2,1)S(1)} %get-tuple-element.67.refs_1_, ...), custom_call_target="tpu_custom_call", output_to_operand_aliasing={{0}: (9, {}), {1}: (10, {}), {2}: (11, {})} | custom-call | flops 220200960 | bytes 6881280 | tf_op jit(solution)/shard_map/pallas_call | solution.py:220
  29.0 0.2 collective-permute-done.11.refs_4_
  29.2 0.4 %collective-permute-start.16 = (bf16[3,64,640]{2,1,0:T(8,128)(2,1)S(1)}, bf16[3,64,640]{2,1,0:T(8,128)(2,1)S(1)}, u32[]{:S(2)}, u32[]{:S(2)}) collective-permute-start(bf16[3,64,640]{2,1,0:T(8,128)(2,1)S(1)} %collective-permute-done.11.refs_4_), channel_id=1, source_target_pairs={{0,8},{8,0},{1,9},{9,1},{2,10},{10,2},{3,11},{11,3},{4,12},{12,4},... | collective-permute-start | bytes 737288 | tf_op jit(solution)/shard_map/ppermute | solution.py:44
  29.6 1.6 %shard_map.112 = (bf16[2,640,5120]{2,1,0:T(8,128)(2,1)}, bf16[2,128,5120]{2,1,0:T(8,128)(2,1)}, bf16[2,128,5120]{2,1,0:T(8,128)(2,1)}) custom-call(bf16[2,640,64]{2,1,0:T(8,128)(2,1)S(1)} %get-tuple-element.66.refs_0_, bf16[2,128,64]{2,1,0:T(8,128)(2,1)S(1)} %get-tuple-element.67.refs_1_, ...), custom_call_target="tpu_custom_call", output_to_operand_aliasing={{0}: (8, {}), {1}: (9, {}), {2}: (10, {})} | custom-call | flops 146800640 | bytes 4587520 | tf_op jit(solution)/shard_map/pallas_call | solution.py:220
  31.3 1.3 %shard_map.113 = (bf16[2,640,5120]{2,1,0:T(8,128)(2,1)}, bf16[2,128,5120]{2,1,0:T(8,128)(2,1)}, bf16[2,128,5120]{2,1,0:T(8,128)(2,1)}) custom-call(bf16[2,640,64]{2,1,0:T(8,128)(2,1)S(1)} %get-tuple-element.66.refs_0_, bf16[2,128,64]{2,1,0:T(8,128)(2,1)S(1)} %get-tuple-element.67.refs_1_, ...), custom_call_target="tpu_custom_call", output_to_operand_aliasing={{0}: (7, {}), {1}: (8, {}), {2}: (9, {})} | custom-call | flops 73400320 | bytes 2293760 | tf_op jit(solution)/shard_map/pallas_call | solution.py:220
  (31 shorter events, 0.1 us)
Async XLA Ops:
  0.6 2.3 %copy-start.3 = (bf16[1,2,3,64,640]{4,3,2,1,0:T(8,128)(2,1)S(1)}, bf16[1,2,3,64,640]{4,3,2,1,0:T(8,128)(2,1)}, u32[]{:S(2)}) copy-start(bf16[1,2,3,64,640]{4,3,2,1,0:T(8,128)(2,1)} %param.12) | copy-start | bytes 1474564
  0.6 2.3 %copy-start.7 = (s32[2,3]{1,0:T(2,128)S(1)}, s32[2,3]{1,0:T(2,128)}, u32[]{:S(2)}) copy-start(s32[2,3]{1,0:T(2,128)} %owners.3) | copy-start | bytes 76
  0.7 5.2 %copy-start.4 = (bf16[1,2,640,64]{2,3,1,0:T(8,128)(2,1)S(1)}, bf16[1,2,640,64]{2,3,1,0:T(8,128)(2,1)}, u32[]{:S(2)}) copy-start(bf16[1,2,640,64]{2,3,1,0:T(8,128)(2,1)} %param.13) | copy-start | bytes 491524
  0.7 5.5 %copy-start.5 = (bf16[1,2,128,64]{2,3,1,0:T(8,128)(2,1)S(1)}, bf16[1,2,128,64]{2,3,1,0:T(8,128)(2,1)}, u32[]{:S(2)}) copy-start(bf16[1,2,128,64]{2,3,1,0:T(8,128)(2,1)} %param.14) | copy-start | bytes 98308
  0.7 5.6 %copy-start.6 = (bf16[1,2,128,64]{2,3,1,0:T(8,128)(2,1)S(1)}, bf16[1,2,128,64]{2,3,1,0:T(8,128)(2,1)}, u32[]{:S(2)}) copy-start(bf16[1,2,128,64]{2,3,1,0:T(8,128)(2,1)} %param.15) | copy-start | bytes 98308
  0.7 2.2 %collective-permute-start.3 = (bf16[2,3,64,640]{3,2,1,0:T(8,128)(2,1)}, bf16[2,3,64,640]{3,2,1,0:T(8,128)(2,1)S(1)}, u32[]{:S(2)}, u32[]{:S(2)}) collective-permute-start(bf16[2,3,64,640]{3,2,1,0:T(8,128)(2,1)} %bitcast.10), channel_id=1, source_target_pairs={{0,8},{8,0},{1,9},{9,1},{2,10},{10,2},{3,11},{11,3},{4,12},{12,4},... | collective-permute-start | bytes 1474568 | tf_op jit(solution)/shard_map/ppermute | solution.py:44
  1.2 11.5 %copy-start = (bf16[2,640,5120]{2,1,0:T(8,128)(2,1)S(1)}, bf16[2,640,5120]{2,1,0:T(8,128)(2,1)}, u32[]{:S(2)}) copy-start(bf16[2,640,5120]{2,1,0:T(8,128)(2,1)} %refs_4_.5) | copy-start | bytes 39321604
  3.1 8.0 %collective-permute-start.4 = (bf16[3,64,640]{2,1,0:T(8,128)(2,1)S(1)}, bf16[3,64,640]{2,1,0:T(8,128)(2,1)S(1)}, u32[]{:S(2)}, u32[]{:S(2)}) collective-permute-start(bf16[3,64,640]{2,1,0:T(8,128)(2,1)S(1)} %get-tuple-element.64.refs_9_), channel_id=1, source_target_pairs={{0,10},{8,1},{10,4},{2,8},{4,14},{12,2},{14,7},{6,12},{7,13},{15,6... | collective-permute-start | bytes 737288 | tf_op jit(solution)/shard_map/ppermute | solution.py:40
  5.8 2.2 %collective-permute-start = (bf16[2,64,640]{2,1,0:T(8,128)(2,1)S(1)}, bf16[2,64,640]{2,1,0:T(8,128)(2,1)S(1)}, u32[]{:S(2)}, u32[]{:S(2)}) collective-permute-start(bf16[2,64,640]{2,1,0:T(8,128)(2,1)S(1)} %bitcast.12), channel_id=1, source_target_pairs={{0,8},{8,0},{1,9},{9,1},{2,10},{10,2},{3,11},{11,3},{4,12},{12,4},... | collective-permute-start | bytes 491528 | tf_op jit(solution)/shard_map/ppermute | solution.py:44
  6.1 1.8 %collective-permute-start.1 = (bf16[2,64,128]{2,1,0:T(8,128)(2,1)S(1)}, bf16[2,64,128]{2,1,0:T(8,128)(2,1)S(1)}, u32[]{:S(2)}, u32[]{:S(2)}) collective-permute-start(bf16[2,64,128]{2,1,0:T(8,128)(2,1)S(1)} %bitcast.14), channel_id=1, source_target_pairs={{0,8},{8,0},{1,9},{9,1},{2,10},{10,2},{3,11},{11,3},{4,12},{12,4},... | collective-permute-start | bytes 98312 | tf_op jit(solution)/shard_map/ppermute | solution.py:44
  6.3 1.6 %collective-permute-start.2 = (bf16[2,64,128]{2,1,0:T(8,128)(2,1)S(1)}, bf16[2,64,128]{2,1,0:T(8,128)(2,1)S(1)}, u32[]{:S(2)}, u32[]{:S(2)}) collective-permute-start(bf16[2,64,128]{2,1,0:T(8,128)(2,1)S(1)} %bitcast.16), channel_id=1, source_target_pairs={{0,8},{8,0},{1,9},{9,1},{2,10},{10,2},{3,11},{11,3},{4,12},{12,4},... | collective-permute-start | bytes 98312 | tf_op jit(solution)/shard_map/ppermute | solution.py:44
  6.6 6.0 %copy-start.1 = (bf16[2,128,5120]{2,1,0:T(8,128)(2,1)S(1)}, bf16[2,128,5120]{2,1,0:T(8,128)(2,1)}, u32[]{:S(2)}) copy-start(bf16[2,128,5120]{2,1,0:T(8,128)(2,1)} %refs_5_.13) | copy-start | bytes 7864324
  6.6 6.0 %copy-start.2 = (bf16[2,128,5120]{2,1,0:T(8,128)(2,1)S(1)}, bf16[2,128,5120]{2,1,0:T(8,128)(2,1)}, u32[]{:S(2)}) copy-start(bf16[2,128,5120]{2,1,0:T(8,128)(2,1)} %refs_6_.17) | copy-start | bytes 7864324
  6.6 7.3 %collective-permute-start.6 = (bf16[3,64,640]{2,1,0:T(8,128)(2,1)S(1)}, bf16[3,64,640]{2,1,0:T(8,128)(2,1)S(1)}, u32[]{:S(2)}, u32[]{:S(2)}) collective-permute-start(bf16[3,64,640]{2,1,0:T(8,128)(2,1)S(1)} %get-tuple-element.65.refs_10_), channel_id=1, source_target_pairs={{0,10},{8,1},{10,4},{2,8},{4,14},{12,2},{14,7},{6,12},{7,13},{15,6... | collective-permute-start | bytes 737288 | tf_op jit(solution)/shard_map/ppermute | solution.py:40
  11.0 5.7 %collective-permute-start.5 = (bf16[3,64,640]{2,1,0:T(8,128)(2,1)S(1)}, bf16[3,64,640]{2,1,0:T(8,128)(2,1)S(1)}, u32[]{:S(2)}, u32[]{:S(2)}) collective-permute-start(bf16[3,64,640]{2,1,0:T(8,128)(2,1)S(1)} %collective-permute-done.4.refs_3_), channel_id=1, source_target_pairs={{0,10},{8,1},{10,4},{2,8},{4,14},{12,2},{14,7},{6,12},{7,13},{15,6... | collective-permute-start | bytes 737288 | tf_op jit(solution)/shard_map/ppermute | solution.py:40
  12.5 5.9 %collective-permute-start.9 = (bf16[3,64,640]{2,1,0:T(8,128)(2,1)S(1)}, bf16[3,64,640]{2,1,0:T(8,128)(2,1)S(1)}, u32[]{:S(2)}, u32[]{:S(2)}) collective-permute-start(bf16[3,64,640]{2,1,0:T(8,128)(2,1)S(1)} %collective-permute-done.4.refs_3_), channel_id=1, source_target_pairs={{0,8},{8,0},{1,9},{9,1},{2,10},{10,2},{3,11},{11,3},{4,12},{12,4},... | collective-permute-start | bytes 737288 | tf_op jit(solution)/shard_map/ppermute | solution.py:44
  13.9 6.1 %collective-permute-start.8 = (bf16[3,64,640]{2,1,0:T(8,128)(2,1)S(1)}, bf16[3,64,640]{2,1,0:T(8,128)(2,1)S(1)}, u32[]{:S(2)}, u32[]{:S(2)}) collective-permute-start(bf16[3,64,640]{2,1,0:T(8,128)(2,1)S(1)} %collective-permute-done.6.refs_3_), channel_id=1, source_target_pairs={{0,10},{8,1},{10,4},{2,8},{4,14},{12,2},{14,7},{6,12},{7,13},{15,6... | collective-permute-start | bytes 737288 | tf_op jit(solution)/shard_map/ppermute | solution.py:40
  15.2 6.6 %collective-permute-start.10 = (bf16[3,64,640]{2,1,0:T(8,128)(2,1)S(1)}, bf16[3,64,640]{2,1,0:T(8,128)(2,1)S(1)}, u32[]{:S(2)}, u32[]{:S(2)}) collective-permute-start(bf16[3,64,640]{2,1,0:T(8,128)(2,1)S(1)} %collective-permute-done.6.refs_3_), channel_id=1, source_target_pairs={{0,8},{8,0},{1,9},{9,1},{2,10},{10,2},{3,11},{11,3},{4,12},{12,4},... | collective-permute-start | bytes 737288 | tf_op jit(solution)/shard_map/ppermute | solution.py:44
  16.7 6.7 %collective-permute-start.7 = (bf16[3,64,640]{2,1,0:T(8,128)(2,1)S(1)}, bf16[3,64,640]{2,1,0:T(8,128)(2,1)S(1)}, u32[]{:S(2)}, u32[]{:S(2)}) collective-permute-start(bf16[3,64,640]{2,1,0:T(8,128)(2,1)S(1)} %collective-permute-done.5.refs_3_), channel_id=1, source_target_pairs={{0,10},{8,1},{10,4},{2,8},{4,14},{12,2},{14,7},{6,12},{7,13},{15,6... | collective-permute-start | bytes 737288 | tf_op jit(solution)/shard_map/ppermute | solution.py:40
  18.4 6.8 %collective-permute-start.13 = (bf16[3,64,640]{2,1,0:T(8,128)(2,1)S(1)}, bf16[3,64,640]{2,1,0:T(8,128)(2,1)S(1)}, u32[]{:S(2)}, u32[]{:S(2)}) collective-permute-start(bf16[3,64,640]{2,1,0:T(8,128)(2,1)S(1)} %collective-permute-done.5.refs_3_), channel_id=1, source_target_pairs={{0,8},{8,0},{1,9},{9,1},{2,10},{10,2},{3,11},{11,3},{4,12},{12,4},... | collective-permute-start | bytes 737288 | tf_op jit(solution)/shard_map/ppermute | solution.py:44
  20.1 6.8 %collective-permute-start.12 = (bf16[3,64,640]{2,1,0:T(8,128)(2,1)S(1)}, bf16[3,64,640]{2,1,0:T(8,128)(2,1)S(1)}, u32[]{:S(2)}, u32[]{:S(2)}) collective-permute-start(bf16[3,64,640]{2,1,0:T(8,128)(2,1)S(1)} %collective-permute-done.8.refs_3_), channel_id=1, source_target_pairs={{0,10},{8,1},{10,4},{2,8},{4,14},{12,2},{14,7},{6,12},{7,13},{15,6... | collective-permute-start | bytes 737288 | tf_op jit(solution)/shard_map/ppermute | solution.py:40
  21.2 5.8 %collective-permute-start.14 = (bf16[3,64,640]{2,1,0:T(8,128)(2,1)S(1)}, bf16[3,64,640]{2,1,0:T(8,128)(2,1)S(1)}, u32[]{:S(2)}, u32[]{:S(2)}) collective-permute-start(bf16[3,64,640]{2,1,0:T(8,128)(2,1)S(1)} %collective-permute-done.8.refs_3_), channel_id=1, source_target_pairs={{0,8},{8,0},{1,9},{9,1},{2,10},{10,2},{3,11},{11,3},{4,12},{12,4},... | collective-permute-start | bytes 737288 | tf_op jit(solution)/shard_map/ppermute | solution.py:44
  23.4 3.6 %collective-permute-start.15 = (bf16[3,64,640]{2,1,0:T(8,128)(2,1)S(1)}, bf16[3,64,640]{2,1,0:T(8,128)(2,1)S(1)}, u32[]{:S(2)}, u32[]{:S(2)}) collective-permute-start(bf16[3,64,640]{2,1,0:T(8,128)(2,1)S(1)} %collective-permute-done.7.refs_3_), channel_id=1, source_target_pairs={{0,8},{8,0},{1,9},{9,1},{2,10},{10,2},{3,11},{11,3},{4,12},{12,4},... | collective-permute-start | bytes 737288 | tf_op jit(solution)/shard_map/ppermute | solution.py:44
  23.5 5.7 %collective-permute-start.11 = (bf16[3,64,640]{2,1,0:T(8,128)(2,1)S(1)}, bf16[3,64,640]{2,1,0:T(8,128)(2,1)S(1)}, u32[]{:S(2)}, u32[]{:S(2)}) collective-permute-start(bf16[3,64,640]{2,1,0:T(8,128)(2,1)S(1)} %collective-permute-done.7.refs_3_), channel_id=1, source_target_pairs={{0,10},{8,1},{10,4},{2,8},{4,14},{12,2},{14,7},{6,12},{7,13},{15,6... | collective-permute-start | bytes 737288 | tf_op jit(solution)/shard_map/ppermute | solution.py:40
  26.9 2.7 %collective-permute-start.17 = (bf16[3,64,640]{2,1,0:T(8,128)(2,1)S(1)}, bf16[3,64,640]{2,1,0:T(8,128)(2,1)S(1)}, u32[]{:S(2)}, u32[]{:S(2)}) collective-permute-start(bf16[3,64,640]{2,1,0:T(8,128)(2,1)S(1)} %collective-permute-done.12.refs_3_), channel_id=1, source_target_pairs={{0,8},{8,0},{1,9},{9,1},{2,10},{10,2},{3,11},{11,3},{4,12},{12,4},... | collective-permute-start | bytes 737288 | tf_op jit(solution)/shard_map/ppermute | solution.py:44
  29.2 2.1 %collective-permute-start.16 = (bf16[3,64,640]{2,1,0:T(8,128)(2,1)S(1)}, bf16[3,64,640]{2,1,0:T(8,128)(2,1)S(1)}, u32[]{:S(2)}, u32[]{:S(2)}) collective-permute-start(bf16[3,64,640]{2,1,0:T(8,128)(2,1)S(1)} %collective-permute-done.11.refs_4_), channel_id=1, source_target_pairs={{0,8},{8,0},{1,9},{9,1},{2,10},{10,2},{3,11},{11,3},{4,12},{12,4},... | collective-permute-start | bytes 737288 | tf_op jit(solution)/shard_map/ppermute | solution.py:44

commit v17 on v16

--- a/solution.py
+++ b/solution.py
@@ -151,18 +151,13 @@
 
 
 def merge_own_kernel(n, pieces, scale, owners, *refs):
-    own, other, small_bases, query_block = refs[0:3], refs[3:6], refs[6:8], refs[8]
-    a_refs, outs, b_refs = refs[9:11], refs[11:14], refs[14:17]
-    small_blocks, bufs, load_sems, sem = refs[17:19], refs[19:22], refs[22], refs[23]
+    own, other, blocks, a_refs = refs[0:3], refs[3:6], refs[6:9], refs[9:11]
+    outs, b_refs, bufs, sem = refs[11:14], refs[14:17], refs[17:20], refs[20]
     core = lax.axis_index("rollout")
-    fetches = start_fetches(n, pieces, small_bases, small_blocks, load_sems)
     for proj in range(3):
         for layer in range(own[proj].shape[0]):
             mine = owned(owners, layer, proj, core, own[proj].shape[1:])
             b_refs[proj][layer] = jnp.where(mine, own[proj][layer], other[proj][layer]).T
-    for fetch in fetches:
-        fetch.wait()
-    blocks = (query_block, *small_blocks)
 
     def base_of(proj, i, layer, rows, start, col, width):
         return blocks[proj][i, rows, col : col + width]
@@ -192,27 +187,17 @@
     return [pltpu.VMEM((len(a_list), base.shape[1], cols), base.dtype) for base in bases]
 
 
-def merge_own(n, scale, owners, own, other, query_block, a_list, bases, pieces):
+def merge_own(n, scale, owners, own, other, blocks, a_list, bases, pieces):
     chosen = [jax.ShapeDtypeStruct((x.shape[0], x.shape[2], x.shape[1]), x.dtype) for x in own]
-    bufs = buffers(bases, a_list)
     out = pl.pallas_call(
         functools.partial(merge_own_kernel, n, pieces, scale),
-        in_specs=[VMEM] * 7 + [HBM] * 2 + [VMEM] * (1 + len(a_list)),
+        in_specs=[VMEM] * (10 + len(a_list)),
         out_specs=[HBM] * 3 + [VMEM] * 3,
         out_shape=[jax.ShapeDtypeStruct(base.shape, base.dtype) for base in bases] + chosen,
-        scratch_shapes=bufs[1:]
-        + bufs
-        + [pltpu.SemaphoreType.DMA((2 * len(pieces),)), pltpu.SemaphoreType.DMA((3,))],
+        scratch_shapes=buffers(bases, a_list) + [pltpu.SemaphoreType.DMA((3,))],
         compiler_params=pltpu.CompilerParams(vmem_limit_bytes=16 * MIB),
         cost_estimate=merge_cost(bases, a_list),
-    )(
-        in_vmem(owners),
-        *[in_vmem(x) for x in own],
-        *other,
-        *[in_hbm(base) for base in bases[1:]],
-        query_block,
-        *a_list,
-    )
+    )(in_vmem(owners), *[in_vmem(x) for x in own], *other, *blocks, *a_list)
     return out[:3], out[3:]
 
 
@@ -252,14 +237,14 @@
     if cols % LANES == 0:
         tie = lax.optimization_barrier
         pieces = [(0, True, True), (0, True, False)]
-        query_block = fetch_blocks(n, cols, [base_query], pieces)
-        other_a, query_block = tie((swap_cores(own_a), query_block))
+        blocks = fetch_blocks(n, cols, bases, pieces)
+        other_a, blocks = tie((swap_cores(own_a), blocks))
         first, second = choose_a(owners, own_a, other_a)
         other_b = [swap_cores(x) for x in own_b]
         held = [first, second]
         first = ring_pass(first, n)
         second = ring_pass(second, n)
-        outs, b = merge_own(n, scale, owners, own_b, other_b, *query_block, held, bases, pieces)
+        outs, b = merge_own(n, scale, owners, own_b, other_b, blocks, held, bases, pieces)
         first, outs = tie((first, outs))
 
         def go(outs, *named):

time: 32.7 us -> 32 us (0.979)
  Pallas kernels: 17.1 us -> 16.1 us
  starting transfers between devices: 14.2 us -> 14.7 us
    pallas_call x1, Pallas kernels: 3.05 us -> 1.85 us  [merge_own(): pl.pallas_call(functools.partial(merge_own_kernel, n, pieces, scale), in_...]
    ppermute x7, starting transfers between devices: 11.3 us -> 11.8 us  [ring_pass(): return lax.ppermute(array, ('rollout', 'tensor'), pairs)]
  transfers between devices with their start and end apart: 18 -> 18, of which waited for: 2 -> 1; matrix products, arithmetic and copies ran while one was open for 0% -> 0% of each run, Pallas kernels for 48% -> 46%
where the time goes in v17:
time: 32 us; the launch traced here: 31.9 us
  Pallas kernels  16.1 us (50%)
  starting transfers between devices  14.7 us (46%)
  between operations  0.9 us (3%)
    pallas_call x8, Pallas kernels, merge(): pl.pallas_call(functools.partial(merge_kernel, n, pieces, scale), in_spec...  12.3 us
    ppermute x7, starting transfers between devices, ring_pass(): return lax.ppermute(array, ('rollout', 'tensor'), pairs)  11.8 us
    ppermute x11, starting transfers between devices, swap_cores(): return lax.ppermute(array, 'rollout', [(0, 1), (1, 0)])  2.87 us
    pallas_call x1, Pallas kernels, merge_own(): pl.pallas_call(functools.partial(merge_own_kernel, n, pieces, scale), in_...  1.85 us
    pallas_call x1, Pallas kernels, fetch_blocks(): pl.pallas_call(functools.partial(fetch_kernel, n, pieces), in_specs=[HBM]...  1.77 us
  transfers between devices with their start and end apart: 18, of which 1 were waited for; matrix products, arithmetic and copies ran while one was open for 0% of the time, Pallas kernels for 46%

profile of v17, /device:TPU:0, one launch (start us, length us, event | category | flops | bytes accessed | tf_op | source)
XLA Modules:
  0.0 31.9 jit_solution(14608288897018440595)
XLA Ops:
  0.7 0.5 %collective-permute-start.3 = (bf16[2,3,64,640]{3,2,1,0:T(8,128)(2,1)}, bf16[2,3,64,640]{3,2,1,0:T(8,128)(2,1)S(1)}, u32[]{:S(2)}, u32[]{:S(2)}) collective-permute-start(bf16[2,3,64,640]{3,2,1,0:T(8,128)(2,1)} %bitcast.10), channel_id=1, source_target_pairs={{0,8},{8,0},{1,9},{9,1},{2,10},{10,2},{3,11},{11,3},{4,12},{12,4},... | collective-permute-start | bytes 1474568 | tf_op jit(solution)/shard_map/ppermute | solution.py:44
  1.2 1.8 %shard_map.103 = (bf16[2,640,640]{2,1,0:T(8,128)(2,1)S(1)}, bf16[2,128,640]{2,1,0:T(8,128)(2,1)S(1)}, bf16[2,128,640]{2,1,0:T(8,128)(2,1)S(1)}) custom-call(bf16[2,640,5120]{2,1,0:T(8,128)(2,1)} %refs_4_.5, bf16[2,128,5120]{2,1,0:T(8,128)(2,1)} %refs_5_.13, bf16[2,128,5120]{2,1,0:T(8,128)(2,1)} %refs_6_.15), custom_call_target="tpu_custom_call" | custom-call | bytes 4587520 | tf_op jit(solution)/shard_map/pallas_call | solution.py:115
  3.0 0.0 copy-start.1
  3.0 0.0 collective-permute-done.3.other
  3.0 0.2 shard_map.104
  3.2 2.7 %collective-permute-start.4 = (bf16[3,64,640]{2,1,0:T(8,128)(2,1)S(1)}, bf16[3,64,640]{2,1,0:T(8,128)(2,1)S(1)}, u32[]{:S(2)}, u32[]{:S(2)}) collective-permute-start(bf16[3,64,640]{2,1,0:T(8,128)(2,1)S(1)} %get-tuple-element.74.refs_9_), channel_id=1, source_target_pairs={{0,10},{8,1},{10,4},{2,8},{4,14},{12,2},{14,7},{6,12},{7,13},{15,6... | collective-permute-start | bytes 737288 | tf_op jit(solution)/shard_map/ppermute | solution.py:40
  5.9 0.2 collective-permute-start
  6.1 0.3 %collective-permute-start.1 = (bf16[2,64,128]{2,1,0:T(8,128)(2,1)S(1)}, bf16[2,64,128]{2,1,0:T(8,128)(2,1)S(1)}, u32[]{:S(2)}, u32[]{:S(2)}) collective-permute-start(bf16[2,64,128]{2,1,0:T(8,128)(2,1)S(1)} %bitcast.14), channel_id=1, source_target_pairs={{0,8},{8,0},{1,9},{9,1},{2,10},{10,2},{3,11},{11,3},{4,12},{12,4},... | collective-permute-start | bytes 98312 | tf_op jit(solution)/shard_map/ppermute | solution.py:44
  6.5 0.2 collective-permute-start.2
  6.6 1.3 %collective-permute-start.6 = (bf16[3,64,640]{2,1,0:T(8,128)(2,1)S(1)}, bf16[3,64,640]{2,1,0:T(8,128)(2,1)S(1)}, u32[]{:S(2)}, u32[]{:S(2)}) collective-permute-start(bf16[3,64,640]{2,1,0:T(8,128)(2,1)S(1)} %get-tuple-element.75.refs_10_), channel_id=1, source_target_pairs={{0,10},{8,1},{10,4},{2,8},{4,14},{12,2},{14,7},{6,12},{7,13},{15,6... | collective-permute-start | bytes 737288 | tf_op jit(solution)/shard_map/ppermute | solution.py:40
  8.0 0.0 collective-permute-done.1.refs_4_
  8.0 1.8 %shard_map.105 = (bf16[2,640,5120]{2,1,0:T(8,128)(2,1)}, bf16[2,128,5120]{2,1,0:T(8,128)(2,1)}, bf16[2,128,5120]{2,1,0:T(8,128)(2,1)}, bf16[2,640,64]{2,1,0:T(8,...) custom-call(s32[2,3]{1,0:T(2,128)S(1)} %copy-done.7, bf16[2,64,640]{2,1,0:T(8,128)(2,1)S(1)} %bitcast.13, ...), custom_call_target="tpu_custom_call" | custom-call | flops 146800640 | bytes 4587520 | tf_op jit(solution)/shard_map/pallas_call | solution.py:192
  9.8 0.0 collective-permute-done.4.refs_3_
  9.8 2.0 %collective-permute-start.5 = (bf16[3,64,640]{2,1,0:T(8,128)(2,1)S(1)}, bf16[3,64,640]{2,1,0:T(8,128)(2,1)S(1)}, u32[]{:S(2)}, u32[]{:S(2)}) collective-permute-start(bf16[3,64,640]{2,1,0:T(8,128)(2,1)S(1)} %collective-permute-done.4.refs_3_), channel_id=1, source_target_pairs={{0,10},{8,1},{10,4},{2,8},{4,14},{12,2},{14,7},{6,12},{7,13},{15,6... | collective-permute-start | bytes 737288 | tf_op jit(solution)/shard_map/ppermute | solution.py:40
  11.9 1.3 %shard_map.106 = (bf16[2,640,5120]{2,1,0:T(8,128)(2,1)}, bf16[2,128,5120]{2,1,0:T(8,128)(2,1)}, bf16[2,128,5120]{2,1,0:T(8,128)(2,1)}) custom-call(bf16[2,640,64]{2,1,0:T(8,128)(2,1)S(1)} %get-tuple-element.76.refs_0_, bf16[2,128,64]{2,1,0:T(8,128)(2,1)S(1)} %get-tuple-element.77.refs_1_, ...), custom_call_target="tpu_custom_call", output_to_operand_aliasing={{0}: (7, {}), {1}: (8, {}), {2}: (9, {})} | custom-call | flops 73400320 | bytes 2293760 | tf_op jit(solution)/shard_map/pallas_call | solution.py:205
  13.1 1.3 %collective-permute-start.8 = (bf16[3,64,640]{2,1,0:T(8,128)(2,1)S(1)}, bf16[3,64,640]{2,1,0:T(8,128)(2,1)S(1)}, u32[]{:S(2)}, u32[]{:S(2)}) collective-permute-start(bf16[3,64,640]{2,1,0:T(8,128)(2,1)S(1)} %collective-permute-done.6.refs_3_), channel_id=1, source_target_pairs={{0,10},{8,1},{10,4},{2,8},{4,14},{12,2},{14,7},{6,12},{7,13},{15,6... | collective-permute-start | bytes 737288 | tf_op jit(solution)/shard_map/ppermute | solution.py:40
  14.5 0.3 %collective-permute-start.10 = (bf16[3,64,640]{2,1,0:T(8,128)(2,1)S(1)}, bf16[3,64,640]{2,1,0:T(8,128)(2,1)S(1)}, u32[]{:S(2)}, u32[]{:S(2)}) collective-permute-start(bf16[3,64,640]{2,1,0:T(8,128)(2,1)S(1)} %collective-permute-done.6.refs_3_), channel_id=1, source_target_pairs={{0,8},{8,0},{1,9},{9,1},{2,10},{10,2},{3,11},{11,3},{4,12},{12,4},... | collective-permute-start | bytes 737288 | tf_op jit(solution)/shard_map/ppermute | solution.py:44
  14.8 1.3 %shard_map.107 = (bf16[2,640,5120]{2,1,0:T(8,128)(2,1)}, bf16[2,128,5120]{2,1,0:T(8,128)(2,1)}, bf16[2,128,5120]{2,1,0:T(8,128)(2,1)}) custom-call(bf16[2,640,64]{2,1,0:T(8,128)(2,1)S(1)} %get-tuple-element.76.refs_0_, bf16[2,128,64]{2,1,0:T(8,128)(2,1)S(1)} %get-tuple-element.77.refs_1_, ...), custom_call_target="tpu_custom_call", output_to_operand_aliasing={{0}: (7, {}), {1}: (8, {}), {2}: (9, {})} | custom-call | flops 73400320 | bytes 2293760 | tf_op jit(solution)/shard_map/pallas_call | solution.py:205
  16.1 1.7 %collective-permute-start.7 = (bf16[3,64,640]{2,1,0:T(8,128)(2,1)S(1)}, bf16[3,64,640]{2,1,0:T(8,128)(2,1)S(1)}, u32[]{:S(2)}, u32[]{:S(2)}) collective-permute-start(bf16[3,64,640]{2,1,0:T(8,128)(2,1)S(1)} %collective-permute-done.5.refs_3_), channel_id=1, source_target_pairs={{0,10},{8,1},{10,4},{2,8},{4,14},{12,2},{14,7},{6,12},{7,13},{15,6... | collective-permute-start | bytes 737288 | tf_op jit(solution)/shard_map/ppermute | solution.py:40
  17.8 1.6 %shard_map.108 = (bf16[2,640,5120]{2,1,0:T(8,128)(2,1)}, bf16[2,128,5120]{2,1,0:T(8,128)(2,1)}, bf16[2,128,5120]{2,1,0:T(8,128)(2,1)}) custom-call(bf16[2,640,64]{2,1,0:T(8,128)(2,1)S(1)} %get-tuple-element.76.refs_0_, bf16[2,128,64]{2,1,0:T(8,128)(2,1)S(1)} %get-tuple-element.77.refs_1_, ...), custom_call_target="tpu_custom_call", output_to_operand_aliasing={{0}: (8, {}), {1}: (9, {}), {2}: (10, {})} | custom-call | flops 146800640 | bytes 4587520 | tf_op jit(solution)/shard_map/pallas_call | solution.py:205
  19.4 1.0 %collective-permute-start.12 = (bf16[3,64,640]{2,1,0:T(8,128)(2,1)S(1)}, bf16[3,64,640]{2,1,0:T(8,128)(2,1)S(1)}, u32[]{:S(2)}, u32[]{:S(2)}) collective-permute-start(bf16[3,64,640]{2,1,0:T(8,128)(2,1)S(1)} %collective-permute-done.8.refs_3_), channel_id=1, source_target_pairs={{0,10},{8,1},{10,4},{2,8},{4,14},{12,2},{14,7},{6,12},{7,13},{15,6... | collective-permute-start | bytes 737288 | tf_op jit(solution)/shard_map/ppermute | solution.py:40
  20.4 0.7 %collective-permute-start.14 = (bf16[3,64,640]{2,1,0:T(8,128)(2,1)S(1)}, bf16[3,64,640]{2,1,0:T(8,128)(2,1)S(1)}, u32[]{:S(2)}, u32[]{:S(2)}) collective-permute-start(bf16[3,64,640]{2,1,0:T(8,128)(2,1)S(1)} %collective-permute-done.8.refs_3_), channel_id=1, source_target_pairs={{0,8},{8,0},{1,9},{9,1},{2,10},{10,2},{3,11},{11,3},{4,12},{12,4},... | collective-permute-start | bytes 737288 | tf_op jit(solution)/shard_map/ppermute | solution.py:44
  21.1 1.6 %shard_map.109 = (bf16[2,640,5120]{2,1,0:T(8,128)(2,1)}, bf16[2,128,5120]{2,1,0:T(8,128)(2,1)}, bf16[2,128,5120]{2,1,0:T(8,128)(2,1)}) custom-call(bf16[2,640,64]{2,1,0:T(8,128)(2,1)S(1)} %get-tuple-element.76.refs_0_, bf16[2,128,64]{2,1,0:T(8,128)(2,1)S(1)} %get-tuple-element.77.refs_1_, ...), custom_call_target="tpu_custom_call", output_to_operand_aliasing={{0}: (8, {}), {1}: (9, {}), {2}: (10, {})} | custom-call | flops 146800640 | bytes 4587520 | tf_op jit(solution)/shard_map/pallas_call | solution.py:205
  22.8 0.1 collective-permute-start.15
  22.9 1.7 %collective-permute-start.11 = (bf16[3,64,640]{2,1,0:T(8,128)(2,1)S(1)}, bf16[3,64,640]{2,1,0:T(8,128)(2,1)S(1)}, u32[]{:S(2)}, u32[]{:S(2)}) collective-permute-start(bf16[3,64,640]{2,1,0:T(8,128)(2,1)S(1)} %collective-permute-done.7.refs_3_), channel_id=1, source_target_pairs={{0,10},{8,1},{10,4},{2,8},{4,14},{12,2},{14,7},{6,12},{7,13},{15,6... | collective-permute-start | bytes 737288 | tf_op jit(solution)/shard_map/ppermute | solution.py:40
  24.6 1.6 %shard_map.110 = (bf16[2,640,5120]{2,1,0:T(8,128)(2,1)}, bf16[2,128,5120]{2,1,0:T(8,128)(2,1)}, bf16[2,128,5120]{2,1,0:T(8,128)(2,1)}) custom-call(bf16[2,640,64]{2,1,0:T(8,128)(2,1)S(1)} %get-tuple-element.76.refs_0_, bf16[2,128,64]{2,1,0:T(8,128)(2,1)S(1)} %get-tuple-element.77.refs_1_, ...), custom_call_target="tpu_custom_call", output_to_operand_aliasing={{0}: (8, {}), {1}: (9, {}), {2}: (10, {})} | custom-call | flops 146800640 | bytes 4587520 | tf_op jit(solution)/shard_map/pallas_call | solution.py:205
  26.2 0.1 collective-permute-start.17
  26.3 2.0 %shard_map.111 = (bf16[2,640,5120]{2,1,0:T(8,128)(2,1)}, bf16[2,128,5120]{2,1,0:T(8,128)(2,1)}, bf16[2,128,5120]{2,1,0:T(8,128)(2,1)}) custom-call(bf16[2,640,64]{2,1,0:T(8,128)(2,1)S(1)} %get-tuple-element.76.refs_0_, bf16[2,128,64]{2,1,0:T(8,128)(2,1)S(1)} %get-tuple-element.77.refs_1_, ...), custom_call_target="tpu_custom_call", output_to_operand_aliasing={{0}: (9, {}), {1}: (10, {}), {2}: (11, {})} | custom-call | flops 220200960 | bytes 6881280 | tf_op jit(solution)/shard_map/pallas_call | solution.py:205
  28.4 0.2 collective-permute-done.11.refs_4_
  28.5 0.4 %collective-permute-start.16 = (bf16[3,64,640]{2,1,0:T(8,128)(2,1)S(1)}, bf16[3,64,640]{2,1,0:T(8,128)(2,1)S(1)}, u32[]{:S(2)}, u32[]{:S(2)}) collective-permute-start(bf16[3,64,640]{2,1,0:T(8,128)(2,1)S(1)} %collective-permute-done.11.refs_4_), channel_id=1, source_target_pairs={{0,8},{8,0},{1,9},{9,1},{2,10},{10,2},{3,11},{11,3},{4,12},{12,4},... | collective-permute-start | bytes 737288 | tf_op jit(solution)/shard_map/ppermute | solution.py:44
  29.0 1.6 %shard_map.112 = (bf16[2,640,5120]{2,1,0:T(8,128)(2,1)}, bf16[2,128,5120]{2,1,0:T(8,128)(2,1)}, bf16[2,128,5120]{2,1,0:T(8,128)(2,1)}) custom-call(bf16[2,640,64]{2,1,0:T(8,128)(2,1)S(1)} %get-tuple-element.76.refs_0_, bf16[2,128,64]{2,1,0:T(8,128)(2,1)S(1)} %get-tuple-element.77.refs_1_, ...), custom_call_target="tpu_custom_call", output_to_operand_aliasing={{0}: (8, {}), {1}: (9, {}), {2}: (10, {})} | custom-call | flops 146800640 | bytes 4587520 | tf_op jit(solution)/shard_map/pallas_call | solution.py:205
  30.6 1.3 %shard_map.113 = (bf16[2,640,5120]{2,1,0:T(8,128)(2,1)}, bf16[2,128,5120]{2,1,0:T(8,128)(2,1)}, bf16[2,128,5120]{2,1,0:T(8,128)(2,1)}) custom-call(bf16[2,640,64]{2,1,0:T(8,128)(2,1)S(1)} %get-tuple-element.76.refs_0_, bf16[2,128,64]{2,1,0:T(8,128)(2,1)S(1)} %get-tuple-element.77.refs_1_, ...), custom_call_target="tpu_custom_call", output_to_operand_aliasing={{0}: (7, {}), {1}: (8, {}), {2}: (9, {})} | custom-call | flops 73400320 | bytes 2293760 | tf_op jit(solution)/shard_map/pallas_call | solution.py:205
  (31 shorter events, 0.1 us)
Async XLA Ops:
  0.6 2.4 %copy-start.3 = (bf16[1,2,3,64,640]{4,3,2,1,0:T(8,128)(2,1)S(1)}, bf16[1,2,3,64,640]{4,3,2,1,0:T(8,128)(2,1)}, u32[]{:S(2)}) copy-start(bf16[1,2,3,64,640]{4,3,2,1,0:T(8,128)(2,1)} %param.12) | copy-start | bytes 1474564
  0.6 2.4 %copy-start.7 = (s32[2,3]{1,0:T(2,128)S(1)}, s32[2,3]{1,0:T(2,128)}, u32[]{:S(2)}) copy-start(s32[2,3]{1,0:T(2,128)} %owners.3) | copy-start | bytes 76
  0.7 5.3 %copy-start.4 = (bf16[1,2,640,64]{2,3,1,0:T(8,128)(2,1)S(1)}, bf16[1,2,640,64]{2,3,1,0:T(8,128)(2,1)}, u32[]{:S(2)}) copy-start(bf16[1,2,640,64]{2,3,1,0:T(8,128)(2,1)} %param.13) | copy-start | bytes 491524
  0.7 5.5 %copy-start.5 = (bf16[1,2,128,64]{2,3,1,0:T(8,128)(2,1)S(1)}, bf16[1,2,128,64]{2,3,1,0:T(8,128)(2,1)}, u32[]{:S(2)}) copy-start(bf16[1,2,128,64]{2,3,1,0:T(8,128)(2,1)} %param.14) | copy-start | bytes 98308
  0.7 5.8 %copy-start.6 = (bf16[1,2,128,64]{2,3,1,0:T(8,128)(2,1)S(1)}, bf16[1,2,128,64]{2,3,1,0:T(8,128)(2,1)}, u32[]{:S(2)}) copy-start(bf16[1,2,128,64]{2,3,1,0:T(8,128)(2,1)} %param.15) | copy-start | bytes 98308
  0.7 2.3 %collective-permute-start.3 = (bf16[2,3,64,640]{3,2,1,0:T(8,128)(2,1)}, bf16[2,3,64,640]{3,2,1,0:T(8,128)(2,1)S(1)}, u32[]{:S(2)}, u32[]{:S(2)}) collective-permute-start(bf16[2,3,64,640]{3,2,1,0:T(8,128)(2,1)} %bitcast.10), channel_id=1, source_target_pairs={{0,8},{8,0},{1,9},{9,1},{2,10},{10,2},{3,11},{11,3},{4,12},{12,4},... | collective-permute-start | bytes 1474568 | tf_op jit(solution)/shard_map/ppermute | solution.py:44
  1.2 10.7 %copy-start = (bf16[2,640,5120]{2,1,0:T(8,128)(2,1)S(1)}, bf16[2,640,5120]{2,1,0:T(8,128)(2,1)}, u32[]{:S(2)}) copy-start(bf16[2,640,5120]{2,1,0:T(8,128)(2,1)} %refs_4_.5) | copy-start | bytes 39321604
  1.2 10.7 %copy-start.2 = (bf16[2,128,5120]{2,1,0:T(8,128)(2,1)S(1)}, bf16[2,128,5120]{2,1,0:T(8,128)(2,1)}, u32[]{:S(2)}) copy-start(bf16[2,128,5120]{2,1,0:T(8,128)(2,1)} %refs_6_.15) | copy-start | bytes 7864324
  3.0 8.9 %copy-start.1 = (bf16[2,128,5120]{2,1,0:T(8,128)(2,1)S(1)}, bf16[2,128,5120]{2,1,0:T(8,128)(2,1)}, u32[]{:S(2)}) copy-start(bf16[2,128,5120]{2,1,0:T(8,128)(2,1)} %refs_5_.13) | copy-start | bytes 7864324
  3.2 6.6 %collective-permute-start.4 = (bf16[3,64,640]{2,1,0:T(8,128)(2,1)S(1)}, bf16[3,64,640]{2,1,0:T(8,128)(2,1)S(1)}, u32[]{:S(2)}, u32[]{:S(2)}) collective-permute-start(bf16[3,64,640]{2,1,0:T(8,128)(2,1)S(1)} %get-tuple-element.74.refs_9_), channel_id=1, source_target_pairs={{0,10},{8,1},{10,4},{2,8},{4,14},{12,2},{14,7},{6,12},{7,13},{15,6... | collective-permute-start | bytes 737288 | tf_op jit(solution)/shard_map/ppermute | solution.py:40
  5.9 2.0 %collective-permute-start = (bf16[2,64,640]{2,1,0:T(8,128)(2,1)S(1)}, bf16[2,64,640]{2,1,0:T(8,128)(2,1)S(1)}, u32[]{:S(2)}, u32[]{:S(2)}) collective-permute-start(bf16[2,64,640]{2,1,0:T(8,128)(2,1)S(1)} %bitcast.12), channel_id=1, source_target_pairs={{0,8},{8,0},{1,9},{9,1},{2,10},{10,2},{3,11},{11,3},{4,12},{12,4},... | collective-permute-start | bytes 491528 | tf_op jit(solution)/shard_map/ppermute | solution.py:44
  6.1 1.8 %collective-permute-start.1 = (bf16[2,64,128]{2,1,0:T(8,128)(2,1)S(1)}, bf16[2,64,128]{2,1,0:T(8,128)(2,1)S(1)}, u32[]{:S(2)}, u32[]{:S(2)}) collective-permute-start(bf16[2,64,128]{2,1,0:T(8,128)(2,1)S(1)} %bitcast.14), channel_id=1, source_target_pairs={{0,8},{8,0},{1,9},{9,1},{2,10},{10,2},{3,11},{11,3},{4,12},{12,4},... | collective-permute-start | bytes 98312 | tf_op jit(solution)/shard_map/ppermute | solution.py:44
  6.5 1.5 %collective-permute-start.2 = (bf16[2,64,128]{2,1,0:T(8,128)(2,1)S(1)}, bf16[2,64,128]{2,1,0:T(8,128)(2,1)S(1)}, u32[]{:S(2)}, u32[]{:S(2)}) collective-permute-start(bf16[2,64,128]{2,1,0:T(8,128)(2,1)S(1)} %bitcast.16), channel_id=1, source_target_pairs={{0,8},{8,0},{1,9},{9,1},{2,10},{10,2},{3,11},{11,3},{4,12},{12,4},... | collective-permute-start | bytes 98312 | tf_op jit(solution)/shard_map/ppermute | solution.py:44
  6.6 6.5 %collective-permute-start.6 = (bf16[3,64,640]{2,1,0:T(8,128)(2,1)S(1)}, bf16[3,64,640]{2,1,0:T(8,128)(2,1)S(1)}, u32[]{:S(2)}, u32[]{:S(2)}) collective-permute-start(bf16[3,64,640]{2,1,0:T(8,128)(2,1)S(1)} %get-tuple-element.75.refs_10_), channel_id=1, source_target_pairs={{0,10},{8,1},{10,4},{2,8},{4,14},{12,2},{14,7},{6,12},{7,13},{15,6... | collective-permute-start | bytes 737288 | tf_op jit(solution)/shard_map/ppermute | solution.py:40
  9.8 6.3 %collective-permute-start.5 = (bf16[3,64,640]{2,1,0:T(8,128)(2,1)S(1)}, bf16[3,64,640]{2,1,0:T(8,128)(2,1)S(1)}, u32[]{:S(2)}, u32[]{:S(2)}) collective-permute-start(bf16[3,64,640]{2,1,0:T(8,128)(2,1)S(1)} %collective-permute-done.4.refs_3_), channel_id=1, source_target_pairs={{0,10},{8,1},{10,4},{2,8},{4,14},{12,2},{14,7},{6,12},{7,13},{15,6... | collective-permute-start | bytes 737288 | tf_op jit(solution)/shard_map/ppermute | solution.py:40
  11.9 5.9 %collective-permute-start.9 = (bf16[3,64,640]{2,1,0:T(8,128)(2,1)S(1)}, bf16[3,64,640]{2,1,0:T(8,128)(2,1)S(1)}, u32[]{:S(2)}, u32[]{:S(2)}) collective-permute-start(bf16[3,64,640]{2,1,0:T(8,128)(2,1)S(1)} %collective-permute-done.4.refs_3_), channel_id=1, source_target_pairs={{0,8},{8,0},{1,9},{9,1},{2,10},{10,2},{3,11},{11,3},{4,12},{12,4},... | collective-permute-start | bytes 737288 | tf_op jit(solution)/shard_map/ppermute | solution.py:44
  13.1 6.3 %collective-permute-start.8 = (bf16[3,64,640]{2,1,0:T(8,128)(2,1)S(1)}, bf16[3,64,640]{2,1,0:T(8,128)(2,1)S(1)}, u32[]{:S(2)}, u32[]{:S(2)}) collective-permute-start(bf16[3,64,640]{2,1,0:T(8,128)(2,1)S(1)} %collective-permute-done.6.refs_3_), channel_id=1, source_target_pairs={{0,10},{8,1},{10,4},{2,8},{4,14},{12,2},{14,7},{6,12},{7,13},{15,6... | collective-permute-start | bytes 737288 | tf_op jit(solution)/shard_map/ppermute | solution.py:40
  14.5 6.6 %collective-permute-start.10 = (bf16[3,64,640]{2,1,0:T(8,128)(2,1)S(1)}, bf16[3,64,640]{2,1,0:T(8,128)(2,1)S(1)}, u32[]{:S(2)}, u32[]{:S(2)}) collective-permute-start(bf16[3,64,640]{2,1,0:T(8,128)(2,1)S(1)} %collective-permute-done.6.refs_3_), channel_id=1, source_target_pairs={{0,8},{8,0},{1,9},{9,1},{2,10},{10,2},{3,11},{11,3},{4,12},{12,4},... | collective-permute-start | bytes 737288 | tf_op jit(solution)/shard_map/ppermute | solution.py:44
  16.1 6.7 %collective-permute-start.7 = (bf16[3,64,640]{2,1,0:T(8,128)(2,1)S(1)}, bf16[3,64,640]{2,1,0:T(8,128)(2,1)S(1)}, u32[]{:S(2)}, u32[]{:S(2)}) collective-permute-start(bf16[3,64,640]{2,1,0:T(8,128)(2,1)S(1)} %collective-permute-done.5.refs_3_), channel_id=1, source_target_pairs={{0,10},{8,1},{10,4},{2,8},{4,14},{12,2},{14,7},{6,12},{7,13},{15,6... | collective-permute-start | bytes 737288 | tf_op jit(solution)/shard_map/ppermute | solution.py:40
  17.8 6.8 %collective-permute-start.13 = (bf16[3,64,640]{2,1,0:T(8,128)(2,1)S(1)}, bf16[3,64,640]{2,1,0:T(8,128)(2,1)S(1)}, u32[]{:S(2)}, u32[]{:S(2)}) collective-permute-start(bf16[3,64,640]{2,1,0:T(8,128)(2,1)S(1)} %collective-permute-done.5.refs_3_), channel_id=1, source_target_pairs={{0,8},{8,0},{1,9},{9,1},{2,10},{10,2},{3,11},{11,3},{4,12},{12,4},... | collective-permute-start | bytes 737288 | tf_op jit(solution)/shard_map/ppermute | solution.py:44
  19.4 6.8 %collective-permute-start.12 = (bf16[3,64,640]{2,1,0:T(8,128)(2,1)S(1)}, bf16[3,64,640]{2,1,0:T(8,128)(2,1)S(1)}, u32[]{:S(2)}, u32[]{:S(2)}) collective-permute-start(bf16[3,64,640]{2,1,0:T(8,128)(2,1)S(1)} %collective-permute-done.8.refs_3_), channel_id=1, source_target_pairs={{0,10},{8,1},{10,4},{2,8},{4,14},{12,2},{14,7},{6,12},{7,13},{15,6... | collective-permute-start | bytes 737288 | tf_op jit(solution)/shard_map/ppermute | solution.py:40
  20.4 5.9 %collective-permute-start.14 = (bf16[3,64,640]{2,1,0:T(8,128)(2,1)S(1)}, bf16[3,64,640]{2,1,0:T(8,128)(2,1)S(1)}, u32[]{:S(2)}, u32[]{:S(2)}) collective-permute-start(bf16[3,64,640]{2,1,0:T(8,128)(2,1)S(1)} %collective-permute-done.8.refs_3_), channel_id=1, source_target_pairs={{0,8},{8,0},{1,9},{9,1},{2,10},{10,2},{3,11},{11,3},{4,12},{12,4},... | collective-permute-start | bytes 737288 | tf_op jit(solution)/shard_map/ppermute | solution.py:44
  22.8 3.6 %collective-permute-start.15 = (bf16[3,64,640]{2,1,0:T(8,128)(2,1)S(1)}, bf16[3,64,640]{2,1,0:T(8,128)(2,1)S(1)}, u32[]{:S(2)}, u32[]{:S(2)}) collective-permute-start(bf16[3,64,640]{2,1,0:T(8,128)(2,1)S(1)} %collective-permute-done.7.refs_3_), channel_id=1, source_target_pairs={{0,8},{8,0},{1,9},{9,1},{2,10},{10,2},{3,11},{11,3},{4,12},{12,4},... | collective-permute-start | bytes 737288 | tf_op jit(solution)/shard_map/ppermute | solution.py:44
  22.9 5.7 %collective-permute-start.11 = (bf16[3,64,640]{2,1,0:T(8,128)(2,1)S(1)}, bf16[3,64,640]{2,1,0:T(8,128)(2,1)S(1)}, u32[]{:S(2)}, u32[]{:S(2)}) collective-permute-start(bf16[3,64,640]{2,1,0:T(8,128)(2,1)S(1)} %collective-permute-done.7.refs_3_), channel_id=1, source_target_pairs={{0,10},{8,1},{10,4},{2,8},{4,14},{12,2},{14,7},{6,12},{7,13},{15,6... | collective-permute-start | bytes 737288 | tf_op jit(solution)/shard_map/ppermute | solution.py:40
  26.2 2.7 %collective-permute-start.17 = (bf16[3,64,640]{2,1,0:T(8,128)(2,1)S(1)}, bf16[3,64,640]{2,1,0:T(8,128)(2,1)S(1)}, u32[]{:S(2)}, u32[]{:S(2)}) collective-permute-start(bf16[3,64,640]{2,1,0:T(8,128)(2,1)S(1)} %collective-permute-done.12.refs_3_), channel_id=1, source_target_pairs={{0,8},{8,0},{1,9},{9,1},{2,10},{10,2},{3,11},{11,3},{4,12},{12,4},... | collective-permute-start | bytes 737288 | tf_op jit(solution)/shard_map/ppermute | solution.py:44
  28.5 2.1 %collective-permute-start.16 = (bf16[3,64,640]{2,1,0:T(8,128)(2,1)S(1)}, bf16[3,64,640]{2,1,0:T(8,128)(2,1)S(1)}, u32[]{:S(2)}, u32[]{:S(2)}) collective-permute-start(bf16[3,64,640]{2,1,0:T(8,128)(2,1)S(1)} %collective-permute-done.11.refs_4_), channel_id=1, source_target_pairs={{0,8},{8,0},{1,9},{9,1},{2,10},{10,2},{3,11},{11,3},{4,12},{12,4},... | collective-permute-start | bytes 737288 | tf_op jit(solution)/shard_map/ppermute | solution.py:44

commit v18 on v17

--- a/solution.py
+++ b/solution.py
@@ -251,20 +251,20 @@
             pieces = [(step, not swapped, ((step % 2 == 0) == (ring == "a")) != swapped) for step, ring, swapped, _ in named]
             return merge(n, scale, b, [chunk for *_, chunk in named], bases, outs, pieces)
 
-        swapped_a = swapped_b = ()
+        swapped_a = swapped_b = late = ()
         for step in range(1, last):
             a_here = (step, "a", False, first)
             a_there = (step, "a", True, swap_cores(first))
             first = ring_pass(first, n)
-            outs = go(outs, a_here, *swapped_a)
+            outs = go(outs, a_here, *swapped_a, *late)
             second, outs = tie((second, outs))
             b_here = (step, "b", False, second)
             b_there = (step, "b", True, swap_cores(second))
             if step < last - 1:
                 second = ring_pass(second, n)
-            outs = go(outs, b_here, *swapped_b, *([a_there] if step == last - 1 else []))
+            outs = go(outs, b_here, *((*swapped_b, a_there) if step == last - 1 else ()))
             first, outs = tie((first, outs))
-            swapped_a, swapped_b = (a_there,), (b_there,)
+            swapped_a, swapped_b, late = (a_there,), (b_there,), swapped_b
         a_there = (last, "a", True, swap_cores(first))
         outs = go(outs, *swapped_b, (last, "a", False, first))
         return tuple(go(outs, a_there))

time: 32 us -> 32.5 us (1.016)
  starting transfers between devices: 14.7 us -> 15.2 us
  transfers between devices with their start and end apart: 18 -> 18, of which waited for: 1 -> 0; matrix products, arithmetic and copies ran while one was open for 0% -> 0% of each run, Pallas kernels for 46% -> 45%
where the time goes in v18:
time: 32.5 us; the launch traced here: 32.3 us
  Pallas kernels  16.1 us (50%)
  starting transfers between devices  15.2 us (47%)
  between operations  0.91 us (3%)
    pallas_call x8, Pallas kernels, merge(): pl.pallas_call(functools.partial(merge_kernel, n, pieces, scale), in_spec...  12.3 us
    ppermute x7, starting transfers between devices, ring_pass(): return lax.ppermute(array, ('rollout', 'tensor'), pairs)  12.1 us
    ppermute x11, starting transfers between devices, swap_cores(): return lax.ppermute(array, 'rollout', [(0, 1), (1, 0)])  3.15 us
    pallas_call x1, Pallas kernels, merge_own(): pl.pallas_call(functools.partial(merge_own_kernel, n, pieces, scale), in_...  1.85 us
    pallas_call x1, Pallas kernels, fetch_blocks(): pl.pallas_call(functools.partial(fetch_kernel, n, pieces), in_specs=[HBM]...  1.77 us
  transfers between devices with their start and end apart: 18, of which 0 were waited for; matrix products, arithmetic and copies ran while one was open for 0% of the time, Pallas kernels for 45%

profile of v18, /device:TPU:0, one launch (start us, length us, event | category | flops | bytes accessed | tf_op | source)
XLA Modules:
  0.0 32.3 jit_solution(5266766382739235295)
XLA Ops:
  0.7 0.5 %collective-permute-start.3 = (bf16[2,3,64,640]{3,2,1,0:T(8,128)(2,1)}, bf16[2,3,64,640]{3,2,1,0:T(8,128)(2,1)S(1)}, u32[]{:S(2)}, u32[]{:S(2)}) collective-permute-start(bf16[2,3,64,640]{3,2,1,0:T(8,128)(2,1)} %bitcast.10), channel_id=1, source_target_pairs={{0,8},{8,0},{1,9},{9,1},{2,10},{10,2},{3,11},{11,3},{4,12},{12,4},... | collective-permute-start | bytes 1474568 | tf_op jit(solution)/shard_map/ppermute | solution.py:44
  1.2 1.8 %shard_map.103 = (bf16[2,640,640]{2,1,0:T(8,128)(2,1)S(1)}, bf16[2,128,640]{2,1,0:T(8,128)(2,1)S(1)}, bf16[2,128,640]{2,1,0:T(8,128)(2,1)S(1)}) custom-call(bf16[2,640,5120]{2,1,0:T(8,128)(2,1)} %refs_4_.7, bf16[2,128,5120]{2,1,0:T(8,128)(2,1)} %refs_5_.11, bf16[2,128,5120]{2,1,0:T(8,128)(2,1)} %refs_6_.15), custom_call_target="tpu_custom_call" | custom-call | bytes 4587520 | tf_op jit(solution)/shard_map/pallas_call | solution.py:115
  3.0 0.0 copy-start.1
  3.0 0.2 shard_map.104
  3.2 2.7 %collective-permute-start.4 = (bf16[3,64,640]{2,1,0:T(8,128)(2,1)S(1)}, bf16[3,64,640]{2,1,0:T(8,128)(2,1)S(1)}, u32[]{:S(2)}, u32[]{:S(2)}) collective-permute-start(bf16[3,64,640]{2,1,0:T(8,128)(2,1)S(1)} %get-tuple-element.74.refs_9_), channel_id=1, source_target_pairs={{0,10},{8,1},{10,4},{2,8},{4,14},{12,2},{14,7},{6,12},{7,13},{15,6... | collective-permute-start | bytes 737288 | tf_op jit(solution)/shard_map/ppermute | solution.py:40
  5.9 0.2 collective-permute-start
  6.1 0.3 collective-permute-start.1
  6.5 0.2 collective-permute-start.2
  6.6 1.3 %collective-permute-start.6 = (bf16[3,64,640]{2,1,0:T(8,128)(2,1)S(1)}, bf16[3,64,640]{2,1,0:T(8,128)(2,1)S(1)}, u32[]{:S(2)}, u32[]{:S(2)}) collective-permute-start(bf16[3,64,640]{2,1,0:T(8,128)(2,1)S(1)} %get-tuple-element.75.refs_10_), channel_id=1, source_target_pairs={{0,10},{8,1},{10,4},{2,8},{4,14},{12,2},{14,7},{6,12},{7,13},{15,6... | collective-permute-start | bytes 737288 | tf_op jit(solution)/shard_map/ppermute | solution.py:40
  8.0 0.0 collective-permute-done.1.refs_4_
  8.0 0.0 collective-permute-done.2.refs_5_
  8.0 0.0 collective-permute-done.refs_3_
  8.0 1.8 %shard_map.105 = (bf16[2,640,5120]{2,1,0:T(8,128)(2,1)}, bf16[2,128,5120]{2,1,0:T(8,128)(2,1)}, bf16[2,128,5120]{2,1,0:T(8,128)(2,1)}, bf16[2,640,64]{2,1,0:T(8,...) custom-call(s32[2,3]{1,0:T(2,128)S(1)} %copy-done.7, bf16[2,64,640]{2,1,0:T(8,128)(2,1)S(1)} %bitcast.13, ...), custom_call_target="tpu_custom_call" | custom-call | flops 146800640 | bytes 4587520 | tf_op jit(solution)/shard_map/pallas_call | solution.py:192
  9.8 2.0 %collective-permute-start.5 = (bf16[3,64,640]{2,1,0:T(8,128)(2,1)S(1)}, bf16[3,64,640]{2,1,0:T(8,128)(2,1)S(1)}, u32[]{:S(2)}, u32[]{:S(2)}) collective-permute-start(bf16[3,64,640]{2,1,0:T(8,128)(2,1)S(1)} %collective-permute-done.4.refs_3_), channel_id=1, source_target_pairs={{0,10},{8,1},{10,4},{2,8},{4,14},{12,2},{14,7},{6,12},{7,13},{15,6... | collective-permute-start | bytes 737288 | tf_op jit(solution)/shard_map/ppermute | solution.py:40
  11.9 1.3 %shard_map.106 = (bf16[2,640,5120]{2,1,0:T(8,128)(2,1)}, bf16[2,128,5120]{2,1,0:T(8,128)(2,1)}, bf16[2,128,5120]{2,1,0:T(8,128)(2,1)}) custom-call(bf16[2,640,64]{2,1,0:T(8,128)(2,1)S(1)} %get-tuple-element.76.refs_0_, bf16[2,128,64]{2,1,0:T(8,128)(2,1)S(1)} %get-tuple-element.77.refs_1_, ...), custom_call_target="tpu_custom_call", output_to_operand_aliasing={{0}: (7, {}), {1}: (8, {}), {2}: (9, {})} | custom-call | flops 73400320 | bytes 2293760 | tf_op jit(solution)/shard_map/pallas_call | solution.py:205
  13.1 1.3 %collective-permute-start.8 = (bf16[3,64,640]{2,1,0:T(8,128)(2,1)S(1)}, bf16[3,64,640]{2,1,0:T(8,128)(2,1)S(1)}, u32[]{:S(2)}, u32[]{:S(2)}) collective-permute-start(bf16[3,64,640]{2,1,0:T(8,128)(2,1)S(1)} %collective-permute-done.6.refs_3_), channel_id=1, source_target_pairs={{0,10},{8,1},{10,4},{2,8},{4,14},{12,2},{14,7},{6,12},{7,13},{15,6... | collective-permute-start | bytes 737288 | tf_op jit(solution)/shard_map/ppermute | solution.py:40
  14.5 1.3 %shard_map.107 = (bf16[2,640,5120]{2,1,0:T(8,128)(2,1)}, bf16[2,128,5120]{2,1,0:T(8,128)(2,1)}, bf16[2,128,5120]{2,1,0:T(8,128)(2,1)}) custom-call(bf16[2,640,64]{2,1,0:T(8,128)(2,1)S(1)} %get-tuple-element.76.refs_0_, bf16[2,128,64]{2,1,0:T(8,128)(2,1)S(1)} %get-tuple-element.77.refs_1_, ...), custom_call_target="tpu_custom_call", output_to_operand_aliasing={{0}: (7, {}), {1}: (8, {}), {2}: (9, {})} | custom-call | flops 73400320 | bytes 2293760 | tf_op jit(solution)/shard_map/pallas_call | solution.py:205
  15.8 2.0 %collective-permute-start.7 = (bf16[3,64,640]{2,1,0:T(8,128)(2,1)S(1)}, bf16[3,64,640]{2,1,0:T(8,128)(2,1)S(1)}, u32[]{:S(2)}, u32[]{:S(2)}) collective-permute-start(bf16[3,64,640]{2,1,0:T(8,128)(2,1)S(1)} %collective-permute-done.5.refs_3_), channel_id=1, source_target_pairs={{0,10},{8,1},{10,4},{2,8},{4,14},{12,2},{14,7},{6,12},{7,13},{15,6... | collective-permute-start | bytes 737288 | tf_op jit(solution)/shard_map/ppermute | solution.py:40
  17.8 0.0 collective-permute-start.13
  17.8 0.5 %collective-permute-start.12 = (bf16[3,64,640]{2,1,0:T(8,128)(2,1)S(1)}, bf16[3,64,640]{2,1,0:T(8,128)(2,1)S(1)}, u32[]{:S(2)}, u32[]{:S(2)}) collective-permute-start(bf16[3,64,640]{2,1,0:T(8,128)(2,1)S(1)} %collective-permute-done.5.refs_3_), channel_id=1, source_target_pairs={{0,8},{8,0},{1,9},{9,1},{2,10},{10,2},{3,11},{11,3},{4,12},{12,4},... | collective-permute-start | bytes 737288 | tf_op jit(solution)/shard_map/ppermute | solution.py:44
  18.3 1.6 %shard_map.108 = (bf16[2,640,5120]{2,1,0:T(8,128)(2,1)}, bf16[2,128,5120]{2,1,0:T(8,128)(2,1)}, bf16[2,128,5120]{2,1,0:T(8,128)(2,1)}) custom-call(bf16[2,640,64]{2,1,0:T(8,128)(2,1)S(1)} %get-tuple-element.76.refs_0_, bf16[2,128,64]{2,1,0:T(8,128)(2,1)S(1)} %get-tuple-element.77.refs_1_, ...), custom_call_target="tpu_custom_call", output_to_operand_aliasing={{0}: (8, {}), {1}: (9, {}), {2}: (10, {})} | custom-call | flops 146800640 | bytes 4587520 | tf_op jit(solution)/shard_map/pallas_call | solution.py:205
  19.9 1.0 %collective-permute-start.11 = (bf16[3,64,640]{2,1,0:T(8,128)(2,1)S(1)}, bf16[3,64,640]{2,1,0:T(8,128)(2,1)S(1)}, u32[]{:S(2)}, u32[]{:S(2)}) collective-permute-start(bf16[3,64,640]{2,1,0:T(8,128)(2,1)S(1)} %collective-permute-done.8.refs_3_), channel_id=1, source_target_pairs={{0,10},{8,1},{10,4},{2,8},{4,14},{12,2},{14,7},{6,12},{7,13},{15,6... | collective-permute-start | bytes 737288 | tf_op jit(solution)/shard_map/ppermute | solution.py:40
  20.9 0.7 %collective-permute-start.14 = (bf16[3,64,640]{2,1,0:T(8,128)(2,1)S(1)}, bf16[3,64,640]{2,1,0:T(8,128)(2,1)S(1)}, u32[]{:S(2)}, u32[]{:S(2)}) collective-permute-start(bf16[3,64,640]{2,1,0:T(8,128)(2,1)S(1)} %collective-permute-done.8.refs_3_), channel_id=1, source_target_pairs={{0,8},{8,0},{1,9},{9,1},{2,10},{10,2},{3,11},{11,3},{4,12},{12,4},... | collective-permute-start | bytes 737288 | tf_op jit(solution)/shard_map/ppermute | solution.py:44
  21.6 1.3 %shard_map.109 = (bf16[2,640,5120]{2,1,0:T(8,128)(2,1)}, bf16[2,128,5120]{2,1,0:T(8,128)(2,1)}, bf16[2,128,5120]{2,1,0:T(8,128)(2,1)}) custom-call(bf16[2,640,64]{2,1,0:T(8,128)(2,1)S(1)} %get-tuple-element.76.refs_0_, bf16[2,128,64]{2,1,0:T(8,128)(2,1)S(1)} %get-tuple-element.77.refs_1_, ...), custom_call_target="tpu_custom_call", output_to_operand_aliasing={{0}: (7, {}), {1}: (8, {}), {2}: (9, {})} | custom-call | flops 73400320 | bytes 2293760 | tf_op jit(solution)/shard_map/pallas_call | solution.py:205
  22.9 0.1 collective-permute-start.15
  23.0 1.7 %collective-permute-start.10 = (bf16[3,64,640]{2,1,0:T(8,128)(2,1)S(1)}, bf16[3,64,640]{2,1,0:T(8,128)(2,1)S(1)}, u32[]{:S(2)}, u32[]{:S(2)}) collective-permute-start(bf16[3,64,640]{2,1,0:T(8,128)(2,1)S(1)} %collective-permute-done.7.refs_3_), channel_id=1, source_target_pairs={{0,10},{8,1},{10,4},{2,8},{4,14},{12,2},{14,7},{6,12},{7,13},{15,6... | collective-permute-start | bytes 737288 | tf_op jit(solution)/shard_map/ppermute | solution.py:40
  24.7 2.0 %shard_map.110 = (bf16[2,640,5120]{2,1,0:T(8,128)(2,1)}, bf16[2,128,5120]{2,1,0:T(8,128)(2,1)}, bf16[2,128,5120]{2,1,0:T(8,128)(2,1)}) custom-call(bf16[2,640,64]{2,1,0:T(8,128)(2,1)S(1)} %get-tuple-element.76.refs_0_, bf16[2,128,64]{2,1,0:T(8,128)(2,1)S(1)} %get-tuple-element.77.refs_1_, ...), custom_call_target="tpu_custom_call", output_to_operand_aliasing={{0}: (9, {}), {1}: (10, {}), {2}: (11, {})} | custom-call | flops 220200960 | bytes 6881280 | tf_op jit(solution)/shard_map/pallas_call | solution.py:205
  26.7 0.1 collective-permute-start.17
  26.8 2.0 %shard_map.111 = (bf16[2,640,5120]{2,1,0:T(8,128)(2,1)}, bf16[2,128,5120]{2,1,0:T(8,128)(2,1)}, bf16[2,128,5120]{2,1,0:T(8,128)(2,1)}) custom-call(bf16[2,640,64]{2,1,0:T(8,128)(2,1)S(1)} %get-tuple-element.76.refs_0_, bf16[2,128,64]{2,1,0:T(8,128)(2,1)S(1)} %get-tuple-element.77.refs_1_, ...), custom_call_target="tpu_custom_call", output_to_operand_aliasing={{0}: (9, {}), {1}: (10, {}), {2}: (11, {})} | custom-call | flops 220200960 | bytes 6881280 | tf_op jit(solution)/shard_map/pallas_call | solution.py:205
  28.9 0.5 %collective-permute-start.16 = (bf16[3,64,640]{2,1,0:T(8,128)(2,1)S(1)}, bf16[3,64,640]{2,1,0:T(8,128)(2,1)S(1)}, u32[]{:S(2)}, u32[]{:S(2)}) collective-permute-start(bf16[3,64,640]{2,1,0:T(8,128)(2,1)S(1)} %collective-permute-done.10.refs_4_), channel_id=1, source_target_pairs={{0,8},{8,0},{1,9},{9,1},{2,10},{10,2},{3,11},{11,3},{4,12},{12,4},... | collective-permute-start | bytes 737288 | tf_op jit(solution)/shard_map/ppermute | solution.py:44
  29.4 1.6 %shard_map.112 = (bf16[2,640,5120]{2,1,0:T(8,128)(2,1)}, bf16[2,128,5120]{2,1,0:T(8,128)(2,1)}, bf16[2,128,5120]{2,1,0:T(8,128)(2,1)}) custom-call(bf16[2,640,64]{2,1,0:T(8,128)(2,1)S(1)} %get-tuple-element.76.refs_0_, bf16[2,128,64]{2,1,0:T(8,128)(2,1)S(1)} %get-tuple-element.77.refs_1_, ...), custom_call_target="tpu_custom_call", output_to_operand_aliasing={{0}: (8, {}), {1}: (9, {}), {2}: (10, {})} | custom-call | flops 146800640 | bytes 4587520 | tf_op jit(solution)/shard_map/pallas_call | solution.py:205
  31.1 1.3 %shard_map.113 = (bf16[2,640,5120]{2,1,0:T(8,128)(2,1)}, bf16[2,128,5120]{2,1,0:T(8,128)(2,1)}, bf16[2,128,5120]{2,1,0:T(8,128)(2,1)}) custom-call(bf16[2,640,64]{2,1,0:T(8,128)(2,1)S(1)} %get-tuple-element.76.refs_0_, bf16[2,128,64]{2,1,0:T(8,128)(2,1)S(1)} %get-tuple-element.77.refs_1_, ...), custom_call_target="tpu_custom_call", output_to_operand_aliasing={{0}: (7, {}), {1}: (8, {}), {2}: (9, {})} | custom-call | flops 73400320 | bytes 2293760 | tf_op jit(solution)/shard_map/pallas_call | solution.py:205
  (31 shorter events, 0.1 us)
Async XLA Ops:
  0.6 2.4 %copy-start.3 = (bf16[1,2,3,64,640]{4,3,2,1,0:T(8,128)(2,1)S(1)}, bf16[1,2,3,64,640]{4,3,2,1,0:T(8,128)(2,1)}, u32[]{:S(2)}) copy-start(bf16[1,2,3,64,640]{4,3,2,1,0:T(8,128)(2,1)} %param.12) | copy-start | bytes 1474564
  0.6 2.4 %copy-start.7 = (s32[2,3]{1,0:T(2,128)S(1)}, s32[2,3]{1,0:T(2,128)}, u32[]{:S(2)}) copy-start(s32[2,3]{1,0:T(2,128)} %owners.3) | copy-start | bytes 76
  0.7 5.3 %copy-start.4 = (bf16[1,2,640,64]{2,3,1,0:T(8,128)(2,1)S(1)}, bf16[1,2,640,64]{2,3,1,0:T(8,128)(2,1)}, u32[]{:S(2)}) copy-start(bf16[1,2,640,64]{2,3,1,0:T(8,128)(2,1)} %param.13) | copy-start | bytes 491524
  0.7 5.5 %copy-start.5 = (bf16[1,2,128,64]{2,3,1,0:T(8,128)(2,1)S(1)}, bf16[1,2,128,64]{2,3,1,0:T(8,128)(2,1)}, u32[]{:S(2)}) copy-start(bf16[1,2,128,64]{2,3,1,0:T(8,128)(2,1)} %param.14) | copy-start | bytes 98308
  0.7 5.8 %copy-start.6 = (bf16[1,2,128,64]{2,3,1,0:T(8,128)(2,1)S(1)}, bf16[1,2,128,64]{2,3,1,0:T(8,128)(2,1)}, u32[]{:S(2)}) copy-start(bf16[1,2,128,64]{2,3,1,0:T(8,128)(2,1)} %param.15) | copy-start | bytes 98308
  0.7 2.3 %collective-permute-start.3 = (bf16[2,3,64,640]{3,2,1,0:T(8,128)(2,1)}, bf16[2,3,64,640]{3,2,1,0:T(8,128)(2,1)S(1)}, u32[]{:S(2)}, u32[]{:S(2)}) collective-permute-start(bf16[2,3,64,640]{3,2,1,0:T(8,128)(2,1)} %bitcast.10), channel_id=1, source_target_pairs={{0,8},{8,0},{1,9},{9,1},{2,10},{10,2},{3,11},{11,3},{4,12},{12,4},... | collective-permute-start | bytes 1474568 | tf_op jit(solution)/shard_map/ppermute | solution.py:44
  1.2 10.7 %copy-start = (bf16[2,640,5120]{2,1,0:T(8,128)(2,1)S(1)}, bf16[2,640,5120]{2,1,0:T(8,128)(2,1)}, u32[]{:S(2)}) copy-start(bf16[2,640,5120]{2,1,0:T(8,128)(2,1)} %refs_4_.7) | copy-start | bytes 39321604
  1.2 10.7 %copy-start.2 = (bf16[2,128,5120]{2,1,0:T(8,128)(2,1)S(1)}, bf16[2,128,5120]{2,1,0:T(8,128)(2,1)}, u32[]{:S(2)}) copy-start(bf16[2,128,5120]{2,1,0:T(8,128)(2,1)} %refs_6_.15) | copy-start | bytes 7864324
  3.0 8.9 %copy-start.1 = (bf16[2,128,5120]{2,1,0:T(8,128)(2,1)S(1)}, bf16[2,128,5120]{2,1,0:T(8,128)(2,1)}, u32[]{:S(2)}) copy-start(bf16[2,128,5120]{2,1,0:T(8,128)(2,1)} %refs_5_.11) | copy-start | bytes 7864324
  3.2 6.6 %collective-permute-start.4 = (bf16[3,64,640]{2,1,0:T(8,128)(2,1)S(1)}, bf16[3,64,640]{2,1,0:T(8,128)(2,1)S(1)}, u32[]{:S(2)}, u32[]{:S(2)}) collective-permute-start(bf16[3,64,640]{2,1,0:T(8,128)(2,1)S(1)} %get-tuple-element.74.refs_9_), channel_id=1, source_target_pairs={{0,10},{8,1},{10,4},{2,8},{4,14},{12,2},{14,7},{6,12},{7,13},{15,6... | collective-permute-start | bytes 737288 | tf_op jit(solution)/shard_map/ppermute | solution.py:40
  5.9 2.0 %collective-permute-start = (bf16[2,64,640]{2,1,0:T(8,128)(2,1)S(1)}, bf16[2,64,640]{2,1,0:T(8,128)(2,1)S(1)}, u32[]{:S(2)}, u32[]{:S(2)}) collective-permute-start(bf16[2,64,640]{2,1,0:T(8,128)(2,1)S(1)} %bitcast.12), channel_id=1, source_target_pairs={{0,8},{8,0},{1,9},{9,1},{2,10},{10,2},{3,11},{11,3},{4,12},{12,4},... | collective-permute-start | bytes 491528 | tf_op jit(solution)/shard_map/ppermute | solution.py:44
  6.1 1.8 %collective-permute-start.1 = (bf16[2,64,128]{2,1,0:T(8,128)(2,1)S(1)}, bf16[2,64,128]{2,1,0:T(8,128)(2,1)S(1)}, u32[]{:S(2)}, u32[]{:S(2)}) collective-permute-start(bf16[2,64,128]{2,1,0:T(8,128)(2,1)S(1)} %bitcast.14), channel_id=1, source_target_pairs={{0,8},{8,0},{1,9},{9,1},{2,10},{10,2},{3,11},{11,3},{4,12},{12,4},... | collective-permute-start | bytes 98312 | tf_op jit(solution)/shard_map/ppermute | solution.py:44
  6.5 1.5 %collective-permute-start.2 = (bf16[2,64,128]{2,1,0:T(8,128)(2,1)S(1)}, bf16[2,64,128]{2,1,0:T(8,128)(2,1)S(1)}, u32[]{:S(2)}, u32[]{:S(2)}) collective-permute-start(bf16[2,64,128]{2,1,0:T(8,128)(2,1)S(1)} %bitcast.16), channel_id=1, source_target_pairs={{0,8},{8,0},{1,9},{9,1},{2,10},{10,2},{3,11},{11,3},{4,12},{12,4},... | collective-permute-start | bytes 98312 | tf_op jit(solution)/shard_map/ppermute | solution.py:44
  6.6 6.5 %collective-permute-start.6 = (bf16[3,64,640]{2,1,0:T(8,128)(2,1)S(1)}, bf16[3,64,640]{2,1,0:T(8,128)(2,1)S(1)}, u32[]{:S(2)}, u32[]{:S(2)}) collective-permute-start(bf16[3,64,640]{2,1,0:T(8,128)(2,1)S(1)} %get-tuple-element.75.refs_10_), channel_id=1, source_target_pairs={{0,10},{8,1},{10,4},{2,8},{4,14},{12,2},{14,7},{6,12},{7,13},{15,6... | collective-permute-start | bytes 737288 | tf_op jit(solution)/shard_map/ppermute | solution.py:40
  9.8 5.9 %collective-permute-start.5 = (bf16[3,64,640]{2,1,0:T(8,128)(2,1)S(1)}, bf16[3,64,640]{2,1,0:T(8,128)(2,1)S(1)}, u32[]{:S(2)}, u32[]{:S(2)}) collective-permute-start(bf16[3,64,640]{2,1,0:T(8,128)(2,1)S(1)} %collective-permute-done.4.refs_3_), channel_id=1, source_target_pairs={{0,10},{8,1},{10,4},{2,8},{4,14},{12,2},{14,7},{6,12},{7,13},{15,6... | collective-permute-start | bytes 737288 | tf_op jit(solution)/shard_map/ppermute | solution.py:40
  11.9 6.4 %collective-permute-start.9 = (bf16[3,64,640]{2,1,0:T(8,128)(2,1)S(1)}, bf16[3,64,640]{2,1,0:T(8,128)(2,1)S(1)}, u32[]{:S(2)}, u32[]{:S(2)}) collective-permute-start(bf16[3,64,640]{2,1,0:T(8,128)(2,1)S(1)} %collective-permute-done.4.refs_3_), channel_id=1, source_target_pairs={{0,8},{8,0},{1,9},{9,1},{2,10},{10,2},{3,11},{11,3},{4,12},{12,4},... | collective-permute-start | bytes 737288 | tf_op jit(solution)/shard_map/ppermute | solution.py:44
  13.1 6.8 %collective-permute-start.8 = (bf16[3,64,640]{2,1,0:T(8,128)(2,1)S(1)}, bf16[3,64,640]{2,1,0:T(8,128)(2,1)S(1)}, u32[]{:S(2)}, u32[]{:S(2)}) collective-permute-start(bf16[3,64,640]{2,1,0:T(8,128)(2,1)S(1)} %collective-permute-done.6.refs_3_), channel_id=1, source_target_pairs={{0,10},{8,1},{10,4},{2,8},{4,14},{12,2},{14,7},{6,12},{7,13},{15,6... | collective-permute-start | bytes 737288 | tf_op jit(solution)/shard_map/ppermute | solution.py:40
  15.8 7.1 %collective-permute-start.7 = (bf16[3,64,640]{2,1,0:T(8,128)(2,1)S(1)}, bf16[3,64,640]{2,1,0:T(8,128)(2,1)S(1)}, u32[]{:S(2)}, u32[]{:S(2)}) collective-permute-start(bf16[3,64,640]{2,1,0:T(8,128)(2,1)S(1)} %collective-permute-done.5.refs_3_), channel_id=1, source_target_pairs={{0,10},{8,1},{10,4},{2,8},{4,14},{12,2},{14,7},{6,12},{7,13},{15,6... | collective-permute-start | bytes 737288 | tf_op jit(solution)/shard_map/ppermute | solution.py:40
  17.8 5.2 %collective-permute-start.13 = (bf16[3,64,640]{2,1,0:T(8,128)(2,1)S(1)}, bf16[3,64,640]{2,1,0:T(8,128)(2,1)S(1)}, u32[]{:S(2)}, u32[]{:S(2)}) collective-permute-start(bf16[3,64,640]{2,1,0:T(8,128)(2,1)S(1)} %collective-permute-done.6.refs_3_), channel_id=1, source_target_pairs={{0,8},{8,0},{1,9},{9,1},{2,10},{10,2},{3,11},{11,3},{4,12},{12,4},... | collective-permute-start | bytes 737288 | tf_op jit(solution)/shard_map/ppermute | solution.py:44
  17.8 6.9 %collective-permute-start.12 = (bf16[3,64,640]{2,1,0:T(8,128)(2,1)S(1)}, bf16[3,64,640]{2,1,0:T(8,128)(2,1)S(1)}, u32[]{:S(2)}, u32[]{:S(2)}) collective-permute-start(bf16[3,64,640]{2,1,0:T(8,128)(2,1)S(1)} %collective-permute-done.5.refs_3_), channel_id=1, source_target_pairs={{0,8},{8,0},{1,9},{9,1},{2,10},{10,2},{3,11},{11,3},{4,12},{12,4},... | collective-permute-start | bytes 737288 | tf_op jit(solution)/shard_map/ppermute | solution.py:44
  19.9 6.8 %collective-permute-start.11 = (bf16[3,64,640]{2,1,0:T(8,128)(2,1)S(1)}, bf16[3,64,640]{2,1,0:T(8,128)(2,1)S(1)}, u32[]{:S(2)}, u32[]{:S(2)}) collective-permute-start(bf16[3,64,640]{2,1,0:T(8,128)(2,1)S(1)} %collective-permute-done.8.refs_3_), channel_id=1, source_target_pairs={{0,10},{8,1},{10,4},{2,8},{4,14},{12,2},{14,7},{6,12},{7,13},{15,6... | collective-permute-start | bytes 737288 | tf_op jit(solution)/shard_map/ppermute | solution.py:40
  20.9 5.9 %collective-permute-start.14 = (bf16[3,64,640]{2,1,0:T(8,128)(2,1)S(1)}, bf16[3,64,640]{2,1,0:T(8,128)(2,1)S(1)}, u32[]{:S(2)}, u32[]{:S(2)}) collective-permute-start(bf16[3,64,640]{2,1,0:T(8,128)(2,1)S(1)} %collective-permute-done.8.refs_3_), channel_id=1, source_target_pairs={{0,8},{8,0},{1,9},{9,1},{2,10},{10,2},{3,11},{11,3},{4,12},{12,4},... | collective-permute-start | bytes 737288 | tf_op jit(solution)/shard_map/ppermute | solution.py:44
  22.9 3.9 %collective-permute-start.15 = (bf16[3,64,640]{2,1,0:T(8,128)(2,1)S(1)}, bf16[3,64,640]{2,1,0:T(8,128)(2,1)S(1)}, u32[]{:S(2)}, u32[]{:S(2)}) collective-permute-start(bf16[3,64,640]{2,1,0:T(8,128)(2,1)S(1)} %collective-permute-done.7.refs_3_), channel_id=1, source_target_pairs={{0,8},{8,0},{1,9},{9,1},{2,10},{10,2},{3,11},{11,3},{4,12},{12,4},... | collective-permute-start | bytes 737288 | tf_op jit(solution)/shard_map/ppermute | solution.py:44
  23.0 5.9 %collective-permute-start.10 = (bf16[3,64,640]{2,1,0:T(8,128)(2,1)S(1)}, bf16[3,64,640]{2,1,0:T(8,128)(2,1)S(1)}, u32[]{:S(2)}, u32[]{:S(2)}) collective-permute-start(bf16[3,64,640]{2,1,0:T(8,128)(2,1)S(1)} %collective-permute-done.7.refs_3_), channel_id=1, source_target_pairs={{0,10},{8,1},{10,4},{2,8},{4,14},{12,2},{14,7},{6,12},{7,13},{15,6... | collective-permute-start | bytes 737288 | tf_op jit(solution)/shard_map/ppermute | solution.py:40
  26.7 2.7 %collective-permute-start.17 = (bf16[3,64,640]{2,1,0:T(8,128)(2,1)S(1)}, bf16[3,64,640]{2,1,0:T(8,128)(2,1)S(1)}, u32[]{:S(2)}, u32[]{:S(2)}) collective-permute-start(bf16[3,64,640]{2,1,0:T(8,128)(2,1)S(1)} %collective-permute-done.11.refs_3_), channel_id=1, source_target_pairs={{0,8},{8,0},{1,9},{9,1},{2,10},{10,2},{3,11},{11,3},{4,12},{12,4},... | collective-permute-start | bytes 737288 | tf_op jit(solution)/shard_map/ppermute | solution.py:44
  28.9 2.2 %collective-permute-start.16 = (bf16[3,64,640]{2,1,0:T(8,128)(2,1)S(1)}, bf16[3,64,640]{2,1,0:T(8,128)(2,1)S(1)}, u32[]{:S(2)}, u32[]{:S(2)}) collective-permute-start(bf16[3,64,640]{2,1,0:T(8,128)(2,1)S(1)} %collective-permute-done.10.refs_4_), channel_id=1, source_target_pairs={{0,8},{8,0},{1,9},{9,1},{2,10},{10,2},{3,11},{11,3},{4,12},{12,4},... | collective-permute-start | bytes 737288 | tf_op jit(solution)/shard_map/ppermute | solution.py:44

commit v19 on v18

--- a/solution.py
+++ b/solution.py
@@ -251,22 +251,23 @@
             pieces = [(step, not swapped, ((step % 2 == 0) == (ring == "a")) != swapped) for step, ring, swapped, _ in named]
             return merge(n, scale, b, [chunk for *_, chunk in named], bases, outs, pieces)
 
-        swapped_a = swapped_b = late = ()
+        swapped = ()
         for step in range(1, last):
             a_here = (step, "a", False, first)
             a_there = (step, "a", True, swap_cores(first))
             first = ring_pass(first, n)
-            outs = go(outs, a_here, *swapped_a, *late)
+            if step == last - 1 and swapped:
+                outs, swapped = go(outs, *swapped), ()
             second, outs = tie((second, outs))
             b_here = (step, "b", False, second)
             b_there = (step, "b", True, swap_cores(second))
             if step < last - 1:
                 second = ring_pass(second, n)
-            outs = go(outs, b_here, *((*swapped_b, a_there) if step == last - 1 else ()))
+            outs = go(outs, a_here, b_here, *swapped, *([a_there] if step == last - 1 else []))
             first, outs = tie((first, outs))
-            swapped_a, swapped_b, late = (a_there,), (b_there,), swapped_b
+            swapped = (a_there, b_there)
         a_there = (last, "a", True, swap_cores(first))
-        outs = go(outs, *swapped_b, (last, "a", False, first))
+        outs = go(outs, b_there, (last, "a", False, first))
         return tuple(go(outs, a_there))
 
     core = lax.axis_index("rollout")

time: 32.5 us -> 32.2 us (level)
  Pallas kernels: 16.1 us -> 14.4 us
  waiting for transfers between devices: 0.05 us -> 1.21 us
  starting transfers between devices: 15.2 us -> 15.6 us
    pallas_call x8 -> x6, Pallas kernels: 12.3 us -> 10.6 us  [merge(): pl.pallas_call(functools.partial(merge_kernel, n, pieces, scale), in_spec...]
    ppermute x7, waiting for transfers between devices: 0.02 us -> 1.18 us  [ring_pass(): return lax.ppermute(array, ('rollout', 'tensor'), pairs)]
    ppermute x7, starting transfers between devices: 12.1 us -> 12.5 us  [ring_pass(): return lax.ppermute(array, ('rollout', 'tensor'), pairs)]
  transfers between devices with their start and end apart: 18 -> 18, of which waited for: 0 -> 3; matrix products, arithmetic and copies ran while one was open for 0% -> 0% of each run, Pallas kernels for 45% -> 40%
where the time goes in v19:
time: 32.2 us; the launch traced here: 32.1 us
  starting transfers between devices  15.6 us (48%)
  Pallas kernels  14.4 us (45%)
  waiting for transfers between devices  1.21 us (4%)
  between operations  0.84 us (3%)
    ppermute x7, starting transfers between devices, ring_pass(): return lax.ppermute(array, ('rollout', 'tensor'), pairs)  12.5 us
    pallas_call x6, Pallas kernels, merge(): pl.pallas_call(functools.partial(merge_kernel, n, pieces, scale), in_spec...  10.6 us
    ppermute x11, starting transfers between devices, swap_cores(): return lax.ppermute(array, 'rollout', [(0, 1), (1, 0)])  3.12 us
    pallas_call x1, Pallas kernels, merge_own(): pl.pallas_call(functools.partial(merge_own_kernel, n, pieces, scale), in_...  1.85 us
    pallas_call x1, Pallas kernels, fetch_blocks(): pl.pallas_call(functools.partial(fetch_kernel, n, pieces), in_specs=[HBM]...  1.77 us
    ppermute x7, waiting for transfers between devices, ring_pass(): return lax.ppermute(array, ('rollout', 'tensor'), pairs)  1.18 us
  transfers between devices with their start and end apart: 18, of which 3 were waited for; matrix products, arithmetic and copies ran while one was open for 0% of the time, Pallas kernels for 40%

profile of v19, /device:TPU:0, one launch (start us, length us, event | category | flops | bytes accessed | tf_op | source)
XLA Modules:
  0.0 32.1 jit_solution(5786622693415296992)
XLA Ops:
  0.7 0.5 %collective-permute-start.3 = (bf16[2,3,64,640]{3,2,1,0:T(8,128)(2,1)}, bf16[2,3,64,640]{3,2,1,0:T(8,128)(2,1)S(1)}, u32[]{:S(2)}, u32[]{:S(2)}) collective-permute-start(bf16[2,3,64,640]{3,2,1,0:T(8,128)(2,1)} %bitcast.10), channel_id=1, source_target_pairs={{0,8},{8,0},{1,9},{9,1},{2,10},{10,2},{3,11},{11,3},{4,12},{12,4},... | collective-permute-start | bytes 1474568 | tf_op jit(solution)/shard_map/ppermute | solution.py:44
  1.2 1.8 %shard_map.103 = (bf16[2,640,640]{2,1,0:T(8,128)(2,1)S(1)}, bf16[2,128,640]{2,1,0:T(8,128)(2,1)S(1)}, bf16[2,128,640]{2,1,0:T(8,128)(2,1)S(1)}) custom-call(bf16[2,640,5120]{2,1,0:T(8,128)(2,1)} %refs_4_.1, bf16[2,128,5120]{2,1,0:T(8,128)(2,1)} %refs_5_.7, bf16[2,128,5120]{2,1,0:T(8,128)(2,1)} %refs_6_.9), custom_call_target="tpu_custom_call" | custom-call | bytes 4587520 | tf_op jit(solution)/shard_map/pallas_call | solution.py:115
  3.0 0.0 copy-start.1
  3.0 0.2 shard_map.104
  3.2 2.7 %collective-permute-start.4 = (bf16[3,64,640]{2,1,0:T(8,128)(2,1)S(1)}, bf16[3,64,640]{2,1,0:T(8,128)(2,1)S(1)}, u32[]{:S(2)}, u32[]{:S(2)}) collective-permute-start(bf16[3,64,640]{2,1,0:T(8,128)(2,1)S(1)} %get-tuple-element.68.refs_9_), channel_id=1, source_target_pairs={{0,10},{8,1},{10,4},{2,8},{4,14},{12,2},{14,7},{6,12},{7,13},{15,6... | collective-permute-start | bytes 737288 | tf_op jit(solution)/shard_map/ppermute | solution.py:40
  5.9 0.2 collective-permute-start
  6.1 0.3 %collective-permute-start.1 = (bf16[2,64,128]{2,1,0:T(8,128)(2,1)S(1)}, bf16[2,64,128]{2,1,0:T(8,128)(2,1)S(1)}, u32[]{:S(2)}, u32[]{:S(2)}) collective-permute-start(bf16[2,64,128]{2,1,0:T(8,128)(2,1)S(1)} %bitcast.14), channel_id=1, source_target_pairs={{0,8},{8,0},{1,9},{9,1},{2,10},{10,2},{3,11},{11,3},{4,12},{12,4},... | collective-permute-start | bytes 98312 | tf_op jit(solution)/shard_map/ppermute | solution.py:44
  6.5 0.2 collective-permute-start.2
  6.6 1.3 %collective-permute-start.6 = (bf16[3,64,640]{2,1,0:T(8,128)(2,1)S(1)}, bf16[3,64,640]{2,1,0:T(8,128)(2,1)S(1)}, u32[]{:S(2)}, u32[]{:S(2)}) collective-permute-start(bf16[3,64,640]{2,1,0:T(8,128)(2,1)S(1)} %get-tuple-element.69.refs_10_), channel_id=1, source_target_pairs={{0,10},{8,1},{10,4},{2,8},{4,14},{12,2},{14,7},{6,12},{7,13},{15,6... | collective-permute-start | bytes 737288 | tf_op jit(solution)/shard_map/ppermute | solution.py:40
  8.0 0.0 collective-permute-done.1.refs_4_
  8.0 0.0 collective-permute-done.2.refs_5_
  8.0 1.8 %shard_map.105 = (bf16[2,640,5120]{2,1,0:T(8,128)(2,1)}, bf16[2,128,5120]{2,1,0:T(8,128)(2,1)}, bf16[2,128,5120]{2,1,0:T(8,128)(2,1)}, bf16[2,640,64]{2,1,0:T(8,...) custom-call(s32[2,3]{1,0:T(2,128)S(1)} %copy-done.7, bf16[2,64,640]{2,1,0:T(8,128)(2,1)S(1)} %bitcast.13, ...), custom_call_target="tpu_custom_call" | custom-call | flops 146800640 | bytes 4587520 | tf_op jit(solution)/shard_map/pallas_call | solution.py:192
  9.8 2.0 %collective-permute-start.5 = (bf16[3,64,640]{2,1,0:T(8,128)(2,1)S(1)}, bf16[3,64,640]{2,1,0:T(8,128)(2,1)S(1)}, u32[]{:S(2)}, u32[]{:S(2)}) collective-permute-start(bf16[3,64,640]{2,1,0:T(8,128)(2,1)S(1)} %collective-permute-done.4.refs_3_), channel_id=1, source_target_pairs={{0,10},{8,1},{10,4},{2,8},{4,14},{12,2},{14,7},{6,12},{7,13},{15,6... | collective-permute-start | bytes 737288 | tf_op jit(solution)/shard_map/ppermute | solution.py:40
  11.9 0.5 %collective-permute-done.6.refs_4_ = bf16[3,64,640]{2,1,0:T(8,128)(2,1)S(1)} collective-permute-done((bf16[3,64,640]{2,1,0:T(8,128)(2,1)S(1)}, bf16[3,64,640]{2,1,0:T(8,128)(2,1)S(1)}, u32[]{:S(2)}, u32[]{:S(2)}) %collective-permute-start.6) | collective-permute-done | bytes 245792 | tf_op jit(solution)/shard_map/ppermute | solution.py:40
  12.4 2.1 %collective-permute-start.8 = (bf16[3,64,640]{2,1,0:T(8,128)(2,1)S(1)}, bf16[3,64,640]{2,1,0:T(8,128)(2,1)S(1)}, u32[]{:S(2)}, u32[]{:S(2)}) collective-permute-start(bf16[3,64,640]{2,1,0:T(8,128)(2,1)S(1)} %collective-permute-done.6.refs_4_), channel_id=1, source_target_pairs={{0,10},{8,1},{10,4},{2,8},{4,14},{12,2},{14,7},{6,12},{7,13},{15,6... | collective-permute-start | bytes 737288 | tf_op jit(solution)/shard_map/ppermute | solution.py:40
  14.5 0.5 %collective-permute-start.9 = (bf16[3,64,640]{2,1,0:T(8,128)(2,1)S(1)}, bf16[3,64,640]{2,1,0:T(8,128)(2,1)S(1)}, u32[]{:S(2)}, u32[]{:S(2)}) collective-permute-start(bf16[3,64,640]{2,1,0:T(8,128)(2,1)S(1)} %collective-permute-done.4.refs_3_), channel_id=1, source_target_pairs={{0,8},{8,0},{1,9},{9,1},{2,10},{10,2},{3,11},{11,3},{4,12},{12,4},... | collective-permute-start | bytes 737288 | tf_op jit(solution)/shard_map/ppermute | solution.py:44
  15.0 1.6 %shard_map.106 = (bf16[2,640,5120]{2,1,0:T(8,128)(2,1)}, bf16[2,128,5120]{2,1,0:T(8,128)(2,1)}, bf16[2,128,5120]{2,1,0:T(8,128)(2,1)}) custom-call(bf16[2,640,64]{2,1,0:T(8,128)(2,1)S(1)} %get-tuple-element.70.refs_0_, bf16[2,128,64]{2,1,0:T(8,128)(2,1)S(1)} %get-tuple-element.71.refs_1_, ...), custom_call_target="tpu_custom_call", output_to_operand_aliasing={{0}: (8, {}), {1}: (9, {}), {2}: (10, {})} | custom-call | flops 146800640 | bytes 4587520 | tf_op jit(solution)/shard_map/pallas_call | solution.py:205
  16.7 1.2 %collective-permute-start.7 = (bf16[3,64,640]{2,1,0:T(8,128)(2,1)S(1)}, bf16[3,64,640]{2,1,0:T(8,128)(2,1)S(1)}, u32[]{:S(2)}, u32[]{:S(2)}) collective-permute-start(bf16[3,64,640]{2,1,0:T(8,128)(2,1)S(1)} %collective-permute-done.5.refs_3_), channel_id=1, source_target_pairs={{0,10},{8,1},{10,4},{2,8},{4,14},{12,2},{14,7},{6,12},{7,13},{15,6... | collective-permute-start | bytes 737288 | tf_op jit(solution)/shard_map/ppermute | solution.py:40
  17.8 0.5 %collective-permute-done.8.refs_4_ = bf16[3,64,640]{2,1,0:T(8,128)(2,1)S(1)} collective-permute-done((bf16[3,64,640]{2,1,0:T(8,128)(2,1)S(1)}, bf16[3,64,640]{2,1,0:T(8,128)(2,1)S(1)}, u32[]{:S(2)}, u32[]{:S(2)}) %collective-permute-start.8) | collective-permute-done | bytes 245792 | tf_op jit(solution)/shard_map/ppermute | solution.py:40
  18.3 0.3 collective-permute-start.14
  18.6 1.5 %collective-permute-start.12 = (bf16[3,64,640]{2,1,0:T(8,128)(2,1)S(1)}, bf16[3,64,640]{2,1,0:T(8,128)(2,1)S(1)}, u32[]{:S(2)}, u32[]{:S(2)}) collective-permute-start(bf16[3,64,640]{2,1,0:T(8,128)(2,1)S(1)} %collective-permute-done.8.refs_4_), channel_id=1, source_target_pairs={{0,10},{8,1},{10,4},{2,8},{4,14},{12,2},{14,7},{6,12},{7,13},{15,6... | collective-permute-start | bytes 737288 | tf_op jit(solution)/shard_map/ppermute | solution.py:40
  20.1 0.5 %collective-permute-start.13 = (bf16[3,64,640]{2,1,0:T(8,128)(2,1)S(1)}, bf16[3,64,640]{2,1,0:T(8,128)(2,1)S(1)}, u32[]{:S(2)}, u32[]{:S(2)}) collective-permute-start(bf16[3,64,640]{2,1,0:T(8,128)(2,1)S(1)} %collective-permute-done.5.refs_3_), channel_id=1, source_target_pairs={{0,8},{8,0},{1,9},{9,1},{2,10},{10,2},{3,11},{11,3},{4,12},{12,4},... | collective-permute-start | bytes 737288 | tf_op jit(solution)/shard_map/ppermute | solution.py:44
  20.6 2.4 %shard_map.107 = (bf16[2,640,5120]{2,1,0:T(8,128)(2,1)}, bf16[2,128,5120]{2,1,0:T(8,128)(2,1)}, bf16[2,128,5120]{2,1,0:T(8,128)(2,1)}) custom-call(bf16[2,640,64]{2,1,0:T(8,128)(2,1)S(1)} %get-tuple-element.70.refs_0_, bf16[2,128,64]{2,1,0:T(8,128)(2,1)S(1)} %get-tuple-element.71.refs_1_, ...), custom_call_target="tpu_custom_call", output_to_operand_aliasing={{0}: (10, {}), {1}: (11, {}), {2}: (12, {})} | custom-call | flops 293601280 | bytes 9175040 | tf_op jit(solution)/shard_map/pallas_call | solution.py:205
  23.0 0.1 collective-permute-start.15
  23.1 1.7 %collective-permute-start.11 = (bf16[3,64,640]{2,1,0:T(8,128)(2,1)S(1)}, bf16[3,64,640]{2,1,0:T(8,128)(2,1)S(1)}, u32[]{:S(2)}, u32[]{:S(2)}) collective-permute-start(bf16[3,64,640]{2,1,0:T(8,128)(2,1)S(1)} %collective-permute-done.7.refs_3_), channel_id=1, source_target_pairs={{0,10},{8,1},{10,4},{2,8},{4,14},{12,2},{14,7},{6,12},{7,13},{15,6... | collective-permute-start | bytes 737288 | tf_op jit(solution)/shard_map/ppermute | solution.py:40
  24.8 1.6 %shard_map.108 = (bf16[2,640,5120]{2,1,0:T(8,128)(2,1)}, bf16[2,128,5120]{2,1,0:T(8,128)(2,1)}, bf16[2,128,5120]{2,1,0:T(8,128)(2,1)}) custom-call(bf16[2,640,64]{2,1,0:T(8,128)(2,1)S(1)} %get-tuple-element.70.refs_0_, bf16[2,128,64]{2,1,0:T(8,128)(2,1)S(1)} %get-tuple-element.71.refs_1_, ...), custom_call_target="tpu_custom_call", output_to_operand_aliasing={{0}: (8, {}), {1}: (9, {}), {2}: (10, {})} | custom-call | flops 146800640 | bytes 4587520 | tf_op jit(solution)/shard_map/pallas_call | solution.py:205
  26.4 0.1 collective-permute-start.17
  26.5 2.0 %shard_map.109 = (bf16[2,640,5120]{2,1,0:T(8,128)(2,1)}, bf16[2,128,5120]{2,1,0:T(8,128)(2,1)}, bf16[2,128,5120]{2,1,0:T(8,128)(2,1)}) custom-call(bf16[2,640,64]{2,1,0:T(8,128)(2,1)S(1)} %get-tuple-element.70.refs_0_, bf16[2,128,64]{2,1,0:T(8,128)(2,1)S(1)} %get-tuple-element.71.refs_1_, ...), custom_call_target="tpu_custom_call", output_to_operand_aliasing={{0}: (9, {}), {1}: (10, {}), {2}: (11, {})} | custom-call | flops 220200960 | bytes 6881280 | tf_op jit(solution)/shard_map/pallas_call | solution.py:205
  28.6 0.2 collective-permute-done.11.refs_4_
  28.7 0.4 %collective-permute-start.16 = (bf16[3,64,640]{2,1,0:T(8,128)(2,1)S(1)}, bf16[3,64,640]{2,1,0:T(8,128)(2,1)S(1)}, u32[]{:S(2)}, u32[]{:S(2)}) collective-permute-start(bf16[3,64,640]{2,1,0:T(8,128)(2,1)S(1)} %collective-permute-done.11.refs_4_), channel_id=1, source_target_pairs={{0,8},{8,0},{1,9},{9,1},{2,10},{10,2},{3,11},{11,3},{4,12},{12,4},... | collective-permute-start | bytes 737288 | tf_op jit(solution)/shard_map/ppermute | solution.py:44
  29.2 1.6 %shard_map.110 = (bf16[2,640,5120]{2,1,0:T(8,128)(2,1)}, bf16[2,128,5120]{2,1,0:T(8,128)(2,1)}, bf16[2,128,5120]{2,1,0:T(8,128)(2,1)}) custom-call(bf16[2,640,64]{2,1,0:T(8,128)(2,1)S(1)} %get-tuple-element.70.refs_0_, bf16[2,128,64]{2,1,0:T(8,128)(2,1)S(1)} %get-tuple-element.71.refs_1_, ...), custom_call_target="tpu_custom_call", output_to_operand_aliasing={{0}: (8, {}), {1}: (9, {}), {2}: (10, {})} | custom-call | flops 146800640 | bytes 4587520 | tf_op jit(solution)/shard_map/pallas_call | solution.py:205
  30.8 1.3 %shard_map.111 = (bf16[2,640,5120]{2,1,0:T(8,128)(2,1)}, bf16[2,128,5120]{2,1,0:T(8,128)(2,1)}, bf16[2,128,5120]{2,1,0:T(8,128)(2,1)}) custom-call(bf16[2,640,64]{2,1,0:T(8,128)(2,1)S(1)} %get-tuple-element.70.refs_0_, bf16[2,128,64]{2,1,0:T(8,128)(2,1)S(1)} %get-tuple-element.71.refs_1_, ...), custom_call_target="tpu_custom_call", output_to_operand_aliasing={{0}: (7, {}), {1}: (8, {}), {2}: (9, {})} | custom-call | flops 73400320 | bytes 2293760 | tf_op jit(solution)/shard_map/pallas_call | solution.py:205
  (29 shorter events, 0.1 us)
Async XLA Ops:
  0.6 2.4 %copy-start.3 = (bf16[1,2,3,64,640]{4,3,2,1,0:T(8,128)(2,1)S(1)}, bf16[1,2,3,64,640]{4,3,2,1,0:T(8,128)(2,1)}, u32[]{:S(2)}) copy-start(bf16[1,2,3,64,640]{4,3,2,1,0:T(8,128)(2,1)} %param.12) | copy-start | bytes 1474564
  0.6 2.4 %copy-start.7 = (s32[2,3]{1,0:T(2,128)S(1)}, s32[2,3]{1,0:T(2,128)}, u32[]{:S(2)}) copy-start(s32[2,3]{1,0:T(2,128)} %owners.3) | copy-start | bytes 76
  0.7 5.3 %copy-start.4 = (bf16[1,2,640,64]{2,3,1,0:T(8,128)(2,1)S(1)}, bf16[1,2,640,64]{2,3,1,0:T(8,128)(2,1)}, u32[]{:S(2)}) copy-start(bf16[1,2,640,64]{2,3,1,0:T(8,128)(2,1)} %param.13) | copy-start | bytes 491524
  0.7 5.5 %copy-start.5 = (bf16[1,2,128,64]{2,3,1,0:T(8,128)(2,1)S(1)}, bf16[1,2,128,64]{2,3,1,0:T(8,128)(2,1)}, u32[]{:S(2)}) copy-start(bf16[1,2,128,64]{2,3,1,0:T(8,128)(2,1)} %param.14) | copy-start | bytes 98308
  0.7 5.8 %copy-start.6 = (bf16[1,2,128,64]{2,3,1,0:T(8,128)(2,1)S(1)}, bf16[1,2,128,64]{2,3,1,0:T(8,128)(2,1)}, u32[]{:S(2)}) copy-start(bf16[1,2,128,64]{2,3,1,0:T(8,128)(2,1)} %param.15) | copy-start | bytes 98308
  0.7 2.3 %collective-permute-start.3 = (bf16[2,3,64,640]{3,2,1,0:T(8,128)(2,1)}, bf16[2,3,64,640]{3,2,1,0:T(8,128)(2,1)S(1)}, u32[]{:S(2)}, u32[]{:S(2)}) collective-permute-start(bf16[2,3,64,640]{3,2,1,0:T(8,128)(2,1)} %bitcast.10), channel_id=1, source_target_pairs={{0,8},{8,0},{1,9},{9,1},{2,10},{10,2},{3,11},{11,3},{4,12},{12,4},... | collective-permute-start | bytes 1474568 | tf_op jit(solution)/shard_map/ppermute | solution.py:44
  1.2 13.8 %copy-start = (bf16[2,640,5120]{2,1,0:T(8,128)(2,1)S(1)}, bf16[2,640,5120]{2,1,0:T(8,128)(2,1)}, u32[]{:S(2)}) copy-start(bf16[2,640,5120]{2,1,0:T(8,128)(2,1)} %refs_4_.1) | copy-start | bytes 39321604
  1.2 13.8 %copy-start.2 = (bf16[2,128,5120]{2,1,0:T(8,128)(2,1)S(1)}, bf16[2,128,5120]{2,1,0:T(8,128)(2,1)}, u32[]{:S(2)}) copy-start(bf16[2,128,5120]{2,1,0:T(8,128)(2,1)} %refs_6_.9) | copy-start | bytes 7864324
  3.0 12.0 %copy-start.1 = (bf16[2,128,5120]{2,1,0:T(8,128)(2,1)S(1)}, bf16[2,128,5120]{2,1,0:T(8,128)(2,1)}, u32[]{:S(2)}) copy-start(bf16[2,128,5120]{2,1,0:T(8,128)(2,1)} %refs_5_.7) | copy-start | bytes 7864324
  3.2 6.6 %collective-permute-start.4 = (bf16[3,64,640]{2,1,0:T(8,128)(2,1)S(1)}, bf16[3,64,640]{2,1,0:T(8,128)(2,1)S(1)}, u32[]{:S(2)}, u32[]{:S(2)}) collective-permute-start(bf16[3,64,640]{2,1,0:T(8,128)(2,1)S(1)} %get-tuple-element.68.refs_9_), channel_id=1, source_target_pairs={{0,10},{8,1},{10,4},{2,8},{4,14},{12,2},{14,7},{6,12},{7,13},{15,6... | collective-permute-start | bytes 737288 | tf_op jit(solution)/shard_map/ppermute | solution.py:40
  5.9 2.0 %collective-permute-start = (bf16[2,64,640]{2,1,0:T(8,128)(2,1)S(1)}, bf16[2,64,640]{2,1,0:T(8,128)(2,1)S(1)}, u32[]{:S(2)}, u32[]{:S(2)}) collective-permute-start(bf16[2,64,640]{2,1,0:T(8,128)(2,1)S(1)} %bitcast.12), channel_id=1, source_target_pairs={{0,8},{8,0},{1,9},{9,1},{2,10},{10,2},{3,11},{11,3},{4,12},{12,4},... | collective-permute-start | bytes 491528 | tf_op jit(solution)/shard_map/ppermute | solution.py:44
  6.1 1.8 %collective-permute-start.1 = (bf16[2,64,128]{2,1,0:T(8,128)(2,1)S(1)}, bf16[2,64,128]{2,1,0:T(8,128)(2,1)S(1)}, u32[]{:S(2)}, u32[]{:S(2)}) collective-permute-start(bf16[2,64,128]{2,1,0:T(8,128)(2,1)S(1)} %bitcast.14), channel_id=1, source_target_pairs={{0,8},{8,0},{1,9},{9,1},{2,10},{10,2},{3,11},{11,3},{4,12},{12,4},... | collective-permute-start | bytes 98312 | tf_op jit(solution)/shard_map/ppermute | solution.py:44
  6.5 1.5 %collective-permute-start.2 = (bf16[2,64,128]{2,1,0:T(8,128)(2,1)S(1)}, bf16[2,64,128]{2,1,0:T(8,128)(2,1)S(1)}, u32[]{:S(2)}, u32[]{:S(2)}) collective-permute-start(bf16[2,64,128]{2,1,0:T(8,128)(2,1)S(1)} %bitcast.16), channel_id=1, source_target_pairs={{0,8},{8,0},{1,9},{9,1},{2,10},{10,2},{3,11},{11,3},{4,12},{12,4},... | collective-permute-start | bytes 98312 | tf_op jit(solution)/shard_map/ppermute | solution.py:44
  6.6 5.8 %collective-permute-start.6 = (bf16[3,64,640]{2,1,0:T(8,128)(2,1)S(1)}, bf16[3,64,640]{2,1,0:T(8,128)(2,1)S(1)}, u32[]{:S(2)}, u32[]{:S(2)}) collective-permute-start(bf16[3,64,640]{2,1,0:T(8,128)(2,1)S(1)} %get-tuple-element.69.refs_10_), channel_id=1, source_target_pairs={{0,10},{8,1},{10,4},{2,8},{4,14},{12,2},{14,7},{6,12},{7,13},{15,6... | collective-permute-start | bytes 737288 | tf_op jit(solution)/shard_map/ppermute | solution.py:40
  9.8 6.8 %collective-permute-start.5 = (bf16[3,64,640]{2,1,0:T(8,128)(2,1)S(1)}, bf16[3,64,640]{2,1,0:T(8,128)(2,1)S(1)}, u32[]{:S(2)}, u32[]{:S(2)}) collective-permute-start(bf16[3,64,640]{2,1,0:T(8,128)(2,1)S(1)} %collective-permute-done.4.refs_3_), channel_id=1, source_target_pairs={{0,10},{8,1},{10,4},{2,8},{4,14},{12,2},{14,7},{6,12},{7,13},{15,6... | collective-permute-start | bytes 737288 | tf_op jit(solution)/shard_map/ppermute | solution.py:40
  12.4 5.9 %collective-permute-start.8 = (bf16[3,64,640]{2,1,0:T(8,128)(2,1)S(1)}, bf16[3,64,640]{2,1,0:T(8,128)(2,1)S(1)}, u32[]{:S(2)}, u32[]{:S(2)}) collective-permute-start(bf16[3,64,640]{2,1,0:T(8,128)(2,1)S(1)} %collective-permute-done.6.refs_4_), channel_id=1, source_target_pairs={{0,10},{8,1},{10,4},{2,8},{4,14},{12,2},{14,7},{6,12},{7,13},{15,6... | collective-permute-start | bytes 737288 | tf_op jit(solution)/shard_map/ppermute | solution.py:40
  14.5 5.6 %collective-permute-start.10 = (bf16[3,64,640]{2,1,0:T(8,128)(2,1)S(1)}, bf16[3,64,640]{2,1,0:T(8,128)(2,1)S(1)}, u32[]{:S(2)}, u32[]{:S(2)}) collective-permute-start(bf16[3,64,640]{2,1,0:T(8,128)(2,1)S(1)} %collective-permute-done.6.refs_4_), channel_id=1, source_target_pairs={{0,8},{8,0},{1,9},{9,1},{2,10},{10,2},{3,11},{11,3},{4,12},{12,4},... | collective-permute-start | bytes 737288 | tf_op jit(solution)/shard_map/ppermute | solution.py:44
  14.5 6.1 %collective-permute-start.9 = (bf16[3,64,640]{2,1,0:T(8,128)(2,1)S(1)}, bf16[3,64,640]{2,1,0:T(8,128)(2,1)S(1)}, u32[]{:S(2)}, u32[]{:S(2)}) collective-permute-start(bf16[3,64,640]{2,1,0:T(8,128)(2,1)S(1)} %collective-permute-done.4.refs_3_), channel_id=1, source_target_pairs={{0,8},{8,0},{1,9},{9,1},{2,10},{10,2},{3,11},{11,3},{4,12},{12,4},... | collective-permute-start | bytes 737288 | tf_op jit(solution)/shard_map/ppermute | solution.py:44
  16.7 6.3 %collective-permute-start.7 = (bf16[3,64,640]{2,1,0:T(8,128)(2,1)S(1)}, bf16[3,64,640]{2,1,0:T(8,128)(2,1)S(1)}, u32[]{:S(2)}, u32[]{:S(2)}) collective-permute-start(bf16[3,64,640]{2,1,0:T(8,128)(2,1)S(1)} %collective-permute-done.5.refs_3_), channel_id=1, source_target_pairs={{0,10},{8,1},{10,4},{2,8},{4,14},{12,2},{14,7},{6,12},{7,13},{15,6... | collective-permute-start | bytes 737288 | tf_op jit(solution)/shard_map/ppermute | solution.py:40
  18.3 6.5 %collective-permute-start.14 = (bf16[3,64,640]{2,1,0:T(8,128)(2,1)S(1)}, bf16[3,64,640]{2,1,0:T(8,128)(2,1)S(1)}, u32[]{:S(2)}, u32[]{:S(2)}) collective-permute-start(bf16[3,64,640]{2,1,0:T(8,128)(2,1)S(1)} %collective-permute-done.8.refs_4_), channel_id=1, source_target_pairs={{0,8},{8,0},{1,9},{9,1},{2,10},{10,2},{3,11},{11,3},{4,12},{12,4},... | collective-permute-start | bytes 737288 | tf_op jit(solution)/shard_map/ppermute | solution.py:44
  18.6 7.8 %collective-permute-start.12 = (bf16[3,64,640]{2,1,0:T(8,128)(2,1)S(1)}, bf16[3,64,640]{2,1,0:T(8,128)(2,1)S(1)}, u32[]{:S(2)}, u32[]{:S(2)}) collective-permute-start(bf16[3,64,640]{2,1,0:T(8,128)(2,1)S(1)} %collective-permute-done.8.refs_4_), channel_id=1, source_target_pairs={{0,10},{8,1},{10,4},{2,8},{4,14},{12,2},{14,7},{6,12},{7,13},{15,6... | collective-permute-start | bytes 737288 | tf_op jit(solution)/shard_map/ppermute | solution.py:40
  20.1 4.7 %collective-permute-start.13 = (bf16[3,64,640]{2,1,0:T(8,128)(2,1)S(1)}, bf16[3,64,640]{2,1,0:T(8,128)(2,1)S(1)}, u32[]{:S(2)}, u32[]{:S(2)}) collective-permute-start(bf16[3,64,640]{2,1,0:T(8,128)(2,1)S(1)} %collective-permute-done.5.refs_3_), channel_id=1, source_target_pairs={{0,8},{8,0},{1,9},{9,1},{2,10},{10,2},{3,11},{11,3},{4,12},{12,4},... | collective-permute-start | bytes 737288 | tf_op jit(solution)/shard_map/ppermute | solution.py:44
  23.0 3.6 %collective-permute-start.15 = (bf16[3,64,640]{2,1,0:T(8,128)(2,1)S(1)}, bf16[3,64,640]{2,1,0:T(8,128)(2,1)S(1)}, u32[]{:S(2)}, u32[]{:S(2)}) collective-permute-start(bf16[3,64,640]{2,1,0:T(8,128)(2,1)S(1)} %collective-permute-done.7.refs_3_), channel_id=1, source_target_pairs={{0,8},{8,0},{1,9},{9,1},{2,10},{10,2},{3,11},{11,3},{4,12},{12,4},... | collective-permute-start | bytes 737288 | tf_op jit(solution)/shard_map/ppermute | solution.py:44
  23.1 5.6 %collective-permute-start.11 = (bf16[3,64,640]{2,1,0:T(8,128)(2,1)S(1)}, bf16[3,64,640]{2,1,0:T(8,128)(2,1)S(1)}, u32[]{:S(2)}, u32[]{:S(2)}) collective-permute-start(bf16[3,64,640]{2,1,0:T(8,128)(2,1)S(1)} %collective-permute-done.7.refs_3_), channel_id=1, source_target_pairs={{0,10},{8,1},{10,4},{2,8},{4,14},{12,2},{14,7},{6,12},{7,13},{15,6... | collective-permute-start | bytes 737288 | tf_op jit(solution)/shard_map/ppermute | solution.py:40
  26.4 2.7 %collective-permute-start.17 = (bf16[3,64,640]{2,1,0:T(8,128)(2,1)S(1)}, bf16[3,64,640]{2,1,0:T(8,128)(2,1)S(1)}, u32[]{:S(2)}, u32[]{:S(2)}) collective-permute-start(bf16[3,64,640]{2,1,0:T(8,128)(2,1)S(1)} %collective-permute-done.12.refs_4_), channel_id=1, source_target_pairs={{0,8},{8,0},{1,9},{9,1},{2,10},{10,2},{3,11},{11,3},{4,12},{12,4},... | collective-permute-start | bytes 737288 | tf_op jit(solution)/shard_map/ppermute | solution.py:44
  28.7 2.1 %collective-permute-start.16 = (bf16[3,64,640]{2,1,0:T(8,128)(2,1)S(1)}, bf16[3,64,640]{2,1,0:T(8,128)(2,1)S(1)}, u32[]{:S(2)}, u32[]{:S(2)}) collective-permute-start(bf16[3,64,640]{2,1,0:T(8,128)(2,1)S(1)} %collective-permute-done.11.refs_4_), channel_id=1, source_target_pairs={{0,8},{8,0},{1,9},{9,1},{2,10},{10,2},{3,11},{11,3},{4,12},{12,4},... | collective-permute-start | bytes 737288 | tf_op jit(solution)/shard_map/ppermute | solution.py:44

commit v20 on v19

--- a/solution.py
+++ b/solution.py
@@ -256,14 +256,16 @@
             a_here = (step, "a", False, first)
             a_there = (step, "a", True, swap_cores(first))
             first = ring_pass(first, n)
-            if step == last - 1 and swapped:
+            if step < last - 1:
+                outs = go(outs, a_here)
+            elif swapped:
                 outs, swapped = go(outs, *swapped), ()
             second, outs = tie((second, outs))
             b_here = (step, "b", False, second)
             b_there = (step, "b", True, swap_cores(second))
             if step < last - 1:
                 second = ring_pass(second, n)
-            outs = go(outs, a_here, b_here, *swapped, *([a_there] if step == last - 1 else []))
+            outs = go(outs, b_here, *swapped, *([a_here, a_there] if step == last - 1 else []))
             first, outs = tie((first, outs))
             swapped = (a_there, b_there)
         a_there = (last, "a", True, swap_cores(first))

time: 32.2 us -> 32.2 us (level)
  Pallas kernels: 14.4 us -> 16.1 us
  waiting for transfers between devices: 1.21 us -> 0.22 us
  starting transfers between devices: 15.6 us -> 14.8 us
    pallas_call x6 -> x8, Pallas kernels: 10.6 us -> 12.4 us  [merge(): pl.pallas_call(functools.partial(merge_kernel, n, pieces, scale), in_spec...]
    ppermute x7, waiting for transfers between devices: 1.18 us -> 0.19 us  [ring_pass(): return lax.ppermute(array, ('rollout', 'tensor'), pairs)]
    ppermute x7, starting transfers between devices: 12.5 us -> 11.8 us  [ring_pass(): return lax.ppermute(array, ('rollout', 'tensor'), pairs)]
  transfers between devices with their start and end apart: 18 -> 18, of which waited for: 3 -> 1; matrix products, arithmetic and copies ran while one was open for 0% -> 0% of each run, Pallas kernels for 40% -> 46%
where the time goes in v20:
time: 32.2 us; the launch traced here: 32.1 us
  Pallas kernels  16.1 us (50%)
  starting transfers between devices  14.8 us (46%)
  between operations  0.86 us (3%)
    pallas_call x8, Pallas kernels, merge(): pl.pallas_call(functools.partial(merge_kernel, n, pieces, scale), in_spec...  12.4 us
    ppermute x7, starting transfers between devices, ring_pass(): return lax.ppermute(array, ('rollout', 'tensor'), pairs)  11.8 us
    ppermute x11, starting transfers between devices, swap_cores(): return lax.ppermute(array, 'rollout', [(0, 1), (1, 0)])  3.02 us
    pallas_call x1, Pallas kernels, merge_own(): pl.pallas_call(functools.partial(merge_own_kernel, n, pieces, scale), in_...  1.85 us
    pallas_call x1, Pallas kernels, fetch_blocks(): pl.pallas_call(functools.partial(fetch_kernel, n, pieces), in_specs=[HBM]...  1.77 us
  transfers between devices with their start and end apart: 18, of which 1 were waited for; matrix products, arithmetic and copies ran while one was open for 0% of the time, Pallas kernels for 46%

profile of v20, /device:TPU:0, one launch (start us, length us, event | category | flops | bytes accessed | tf_op | source)
XLA Modules:
  0.0 32.1 jit_solution(16247930267751242477)
XLA Ops:
  0.7 0.5 %collective-permute-start.3 = (bf16[2,3,64,640]{3,2,1,0:T(8,128)(2,1)}, bf16[2,3,64,640]{3,2,1,0:T(8,128)(2,1)S(1)}, u32[]{:S(2)}, u32[]{:S(2)}) collective-permute-start(bf16[2,3,64,640]{3,2,1,0:T(8,128)(2,1)} %bitcast.10), channel_id=1, source_target_pairs={{0,8},{8,0},{1,9},{9,1},{2,10},{10,2},{3,11},{11,3},{4,12},{12,4},... | collective-permute-start | bytes 1474568 | tf_op jit(solution)/shard_map/ppermute | solution.py:44
  1.2 1.8 %shard_map.103 = (bf16[2,640,640]{2,1,0:T(8,128)(2,1)S(1)}, bf16[2,128,640]{2,1,0:T(8,128)(2,1)S(1)}, bf16[2,128,640]{2,1,0:T(8,128)(2,1)S(1)}) custom-call(bf16[2,640,5120]{2,1,0:T(8,128)(2,1)} %refs_4_.7, bf16[2,128,5120]{2,1,0:T(8,128)(2,1)} %refs_5_.11, bf16[2,128,5120]{2,1,0:T(8,128)(2,1)} %refs_6_.15), custom_call_target="tpu_custom_call" | custom-call | bytes 4587520 | tf_op jit(solution)/shard_map/pallas_call | solution.py:115
  3.0 0.0 copy-start.1
  3.0 0.0 collective-permute-done.3.other
  3.0 0.2 shard_map.104
  3.2 2.7 %collective-permute-start.4 = (bf16[3,64,640]{2,1,0:T(8,128)(2,1)S(1)}, bf16[3,64,640]{2,1,0:T(8,128)(2,1)S(1)}, u32[]{:S(2)}, u32[]{:S(2)}) collective-permute-start(bf16[3,64,640]{2,1,0:T(8,128)(2,1)S(1)} %get-tuple-element.74.refs_9_), channel_id=1, source_target_pairs={{0,10},{8,1},{10,4},{2,8},{4,14},{12,2},{14,7},{6,12},{7,13},{15,6... | collective-permute-start | bytes 737288 | tf_op jit(solution)/shard_map/ppermute | solution.py:40
  5.9 0.2 collective-permute-start
  6.1 0.3 %collective-permute-start.1 = (bf16[2,64,128]{2,1,0:T(8,128)(2,1)S(1)}, bf16[2,64,128]{2,1,0:T(8,128)(2,1)S(1)}, u32[]{:S(2)}, u32[]{:S(2)}) collective-permute-start(bf16[2,64,128]{2,1,0:T(8,128)(2,1)S(1)} %bitcast.14), channel_id=1, source_target_pairs={{0,8},{8,0},{1,9},{9,1},{2,10},{10,2},{3,11},{11,3},{4,12},{12,4},... | collective-permute-start | bytes 98312 | tf_op jit(solution)/shard_map/ppermute | solution.py:44
  6.5 0.2 collective-permute-start.2
  6.6 1.3 %collective-permute-start.6 = (bf16[3,64,640]{2,1,0:T(8,128)(2,1)S(1)}, bf16[3,64,640]{2,1,0:T(8,128)(2,1)S(1)}, u32[]{:S(2)}, u32[]{:S(2)}) collective-permute-start(bf16[3,64,640]{2,1,0:T(8,128)(2,1)S(1)} %get-tuple-element.75.refs_10_), channel_id=1, source_target_pairs={{0,10},{8,1},{10,4},{2,8},{4,14},{12,2},{14,7},{6,12},{7,13},{15,6... | collective-permute-start | bytes 737288 | tf_op jit(solution)/shard_map/ppermute | solution.py:40
  8.0 1.8 %shard_map.105 = (bf16[2,640,5120]{2,1,0:T(8,128)(2,1)}, bf16[2,128,5120]{2,1,0:T(8,128)(2,1)}, bf16[2,128,5120]{2,1,0:T(8,128)(2,1)}, bf16[2,640,64]{2,1,0:T(8,...) custom-call(s32[2,3]{1,0:T(2,128)S(1)} %copy-done.7, bf16[2,64,640]{2,1,0:T(8,128)(2,1)S(1)} %bitcast.13, ...), custom_call_target="tpu_custom_call" | custom-call | flops 146800640 | bytes 4587520 | tf_op jit(solution)/shard_map/pallas_call | solution.py:192
  9.8 2.0 %collective-permute-start.5 = (bf16[3,64,640]{2,1,0:T(8,128)(2,1)S(1)}, bf16[3,64,640]{2,1,0:T(8,128)(2,1)S(1)}, u32[]{:S(2)}, u32[]{:S(2)}) collective-permute-start(bf16[3,64,640]{2,1,0:T(8,128)(2,1)S(1)} %collective-permute-done.4.refs_3_), channel_id=1, source_target_pairs={{0,10},{8,1},{10,4},{2,8},{4,14},{12,2},{14,7},{6,12},{7,13},{15,6... | collective-permute-start | bytes 737288 | tf_op jit(solution)/shard_map/ppermute | solution.py:40
  11.9 1.2 %shard_map.106 = (bf16[2,640,5120]{2,1,0:T(8,128)(2,1)}, bf16[2,128,5120]{2,1,0:T(8,128)(2,1)}, bf16[2,128,5120]{2,1,0:T(8,128)(2,1)}) custom-call(bf16[2,640,64]{2,1,0:T(8,128)(2,1)S(1)} %get-tuple-element.76.refs_0_, bf16[2,128,64]{2,1,0:T(8,128)(2,1)S(1)} %get-tuple-element.77.refs_1_, ...), custom_call_target="tpu_custom_call", output_to_operand_aliasing={{0}: (7, {}), {1}: (8, {}), {2}: (9, {})} | custom-call | flops 73400320 | bytes 2293760 | tf_op jit(solution)/shard_map/pallas_call | solution.py:205
  13.1 1.4 %collective-permute-start.8 = (bf16[3,64,640]{2,1,0:T(8,128)(2,1)S(1)}, bf16[3,64,640]{2,1,0:T(8,128)(2,1)S(1)}, u32[]{:S(2)}, u32[]{:S(2)}) collective-permute-start(bf16[3,64,640]{2,1,0:T(8,128)(2,1)S(1)} %collective-permute-done.6.refs_3_), channel_id=1, source_target_pairs={{0,10},{8,1},{10,4},{2,8},{4,14},{12,2},{14,7},{6,12},{7,13},{15,6... | collective-permute-start | bytes 737288 | tf_op jit(solution)/shard_map/ppermute | solution.py:40
  14.5 0.3 %collective-permute-start.10 = (bf16[3,64,640]{2,1,0:T(8,128)(2,1)S(1)}, bf16[3,64,640]{2,1,0:T(8,128)(2,1)S(1)}, u32[]{:S(2)}, u32[]{:S(2)}) collective-permute-start(bf16[3,64,640]{2,1,0:T(8,128)(2,1)S(1)} %collective-permute-done.6.refs_3_), channel_id=1, source_target_pairs={{0,8},{8,0},{1,9},{9,1},{2,10},{10,2},{3,11},{11,3},{4,12},{12,4},... | collective-permute-start | bytes 737288 | tf_op jit(solution)/shard_map/ppermute | solution.py:44
  14.8 0.2 collective-permute-start.9
  15.0 1.2 %shard_map.107 = (bf16[2,640,5120]{2,1,0:T(8,128)(2,1)}, bf16[2,128,5120]{2,1,0:T(8,128)(2,1)}, bf16[2,128,5120]{2,1,0:T(8,128)(2,1)}) custom-call(bf16[2,640,64]{2,1,0:T(8,128)(2,1)S(1)} %get-tuple-element.76.refs_0_, bf16[2,128,64]{2,1,0:T(8,128)(2,1)S(1)} %get-tuple-element.77.refs_1_, ...), custom_call_target="tpu_custom_call", output_to_operand_aliasing={{0}: (7, {}), {1}: (8, {}), {2}: (9, {})} | custom-call | flops 73400320 | bytes 2293760 | tf_op jit(solution)/shard_map/pallas_call | solution.py:205
  16.3 1.6 %collective-permute-start.7 = (bf16[3,64,640]{2,1,0:T(8,128)(2,1)S(1)}, bf16[3,64,640]{2,1,0:T(8,128)(2,1)S(1)}, u32[]{:S(2)}, u32[]{:S(2)}) collective-permute-start(bf16[3,64,640]{2,1,0:T(8,128)(2,1)S(1)} %collective-permute-done.5.refs_3_), channel_id=1, source_target_pairs={{0,10},{8,1},{10,4},{2,8},{4,14},{12,2},{14,7},{6,12},{7,13},{15,6... | collective-permute-start | bytes 737288 | tf_op jit(solution)/shard_map/ppermute | solution.py:40
  17.9 1.2 %shard_map.108 = (bf16[2,640,5120]{2,1,0:T(8,128)(2,1)}, bf16[2,128,5120]{2,1,0:T(8,128)(2,1)}, bf16[2,128,5120]{2,1,0:T(8,128)(2,1)}) custom-call(bf16[2,640,64]{2,1,0:T(8,128)(2,1)S(1)} %get-tuple-element.76.refs_0_, bf16[2,128,64]{2,1,0:T(8,128)(2,1)S(1)} %get-tuple-element.77.refs_1_, ...), custom_call_target="tpu_custom_call", output_to_operand_aliasing={{0}: (7, {}), {1}: (8, {}), {2}: (9, {})} | custom-call | flops 73400320 | bytes 2293760 | tf_op jit(solution)/shard_map/pallas_call | solution.py:205
  19.2 0.1 collective-permute-start.14
  19.3 1.3 %collective-permute-start.12 = (bf16[3,64,640]{2,1,0:T(8,128)(2,1)S(1)}, bf16[3,64,640]{2,1,0:T(8,128)(2,1)S(1)}, u32[]{:S(2)}, u32[]{:S(2)}) collective-permute-start(bf16[3,64,640]{2,1,0:T(8,128)(2,1)S(1)} %collective-permute-done.8.refs_3_), channel_id=1, source_target_pairs={{0,10},{8,1},{10,4},{2,8},{4,14},{12,2},{14,7},{6,12},{7,13},{15,6... | collective-permute-start | bytes 737288 | tf_op jit(solution)/shard_map/ppermute | solution.py:40
  20.6 0.3 %collective-permute-start.13 = (bf16[3,64,640]{2,1,0:T(8,128)(2,1)S(1)}, bf16[3,64,640]{2,1,0:T(8,128)(2,1)S(1)}, u32[]{:S(2)}, u32[]{:S(2)}) collective-permute-start(bf16[3,64,640]{2,1,0:T(8,128)(2,1)S(1)} %collective-permute-done.5.refs_3_), channel_id=1, source_target_pairs={{0,8},{8,0},{1,9},{9,1},{2,10},{10,2},{3,11},{11,3},{4,12},{12,4},... | collective-permute-start | bytes 737288 | tf_op jit(solution)/shard_map/ppermute | solution.py:44
  20.9 2.0 %shard_map.109 = (bf16[2,640,5120]{2,1,0:T(8,128)(2,1)}, bf16[2,128,5120]{2,1,0:T(8,128)(2,1)}, bf16[2,128,5120]{2,1,0:T(8,128)(2,1)}) custom-call(bf16[2,640,64]{2,1,0:T(8,128)(2,1)S(1)} %get-tuple-element.76.refs_0_, bf16[2,128,64]{2,1,0:T(8,128)(2,1)S(1)} %get-tuple-element.77.refs_1_, ...), custom_call_target="tpu_custom_call", output_to_operand_aliasing={{0}: (9, {}), {1}: (10, {}), {2}: (11, {})} | custom-call | flops 220200960 | bytes 6881280 | tf_op jit(solution)/shard_map/pallas_call | solution.py:205
  23.0 0.2 collective-permute-start.15
  23.2 1.5 %collective-permute-start.11 = (bf16[3,64,640]{2,1,0:T(8,128)(2,1)S(1)}, bf16[3,64,640]{2,1,0:T(8,128)(2,1)S(1)}, u32[]{:S(2)}, u32[]{:S(2)}) collective-permute-start(bf16[3,64,640]{2,1,0:T(8,128)(2,1)S(1)} %collective-permute-done.7.refs_4_), channel_id=1, source_target_pairs={{0,10},{8,1},{10,4},{2,8},{4,14},{12,2},{14,7},{6,12},{7,13},{15,6... | collective-permute-start | bytes 737288 | tf_op jit(solution)/shard_map/ppermute | solution.py:40
  24.7 1.6 %shard_map.110 = (bf16[2,640,5120]{2,1,0:T(8,128)(2,1)}, bf16[2,128,5120]{2,1,0:T(8,128)(2,1)}, bf16[2,128,5120]{2,1,0:T(8,128)(2,1)}) custom-call(bf16[2,640,64]{2,1,0:T(8,128)(2,1)S(1)} %get-tuple-element.76.refs_0_, bf16[2,128,64]{2,1,0:T(8,128)(2,1)S(1)} %get-tuple-element.77.refs_1_, ...), custom_call_target="tpu_custom_call", output_to_operand_aliasing={{0}: (8, {}), {1}: (9, {}), {2}: (10, {})} | custom-call | flops 146800640 | bytes 4587520 | tf_op jit(solution)/shard_map/pallas_call | solution.py:205
  26.3 0.3 collective-permute-start.17
  26.6 2.1 %shard_map.111 = (bf16[2,640,5120]{2,1,0:T(8,128)(2,1)}, bf16[2,128,5120]{2,1,0:T(8,128)(2,1)}, bf16[2,128,5120]{2,1,0:T(8,128)(2,1)}) custom-call(bf16[2,640,64]{2,1,0:T(8,128)(2,1)S(1)} %get-tuple-element.76.refs_0_, bf16[2,128,64]{2,1,0:T(8,128)(2,1)S(1)} %get-tuple-element.77.refs_1_, ...), custom_call_target="tpu_custom_call", output_to_operand_aliasing={{0}: (9, {}), {1}: (10, {}), {2}: (11, {})} | custom-call | flops 220200960 | bytes 6881280 | tf_op jit(solution)/shard_map/pallas_call | solution.py:205
  28.6 0.2 collective-permute-done.11.refs_4_
  28.8 0.4 %collective-permute-start.16 = (bf16[3,64,640]{2,1,0:T(8,128)(2,1)S(1)}, bf16[3,64,640]{2,1,0:T(8,128)(2,1)S(1)}, u32[]{:S(2)}, u32[]{:S(2)}) collective-permute-start(bf16[3,64,640]{2,1,0:T(8,128)(2,1)S(1)} %collective-permute-done.11.refs_4_), channel_id=1, source_target_pairs={{0,8},{8,0},{1,9},{9,1},{2,10},{10,2},{3,11},{11,3},{4,12},{12,4},... | collective-permute-start | bytes 737288 | tf_op jit(solution)/shard_map/ppermute | solution.py:44
  29.2 1.6 %shard_map.112 = (bf16[2,640,5120]{2,1,0:T(8,128)(2,1)}, bf16[2,128,5120]{2,1,0:T(8,128)(2,1)}, bf16[2,128,5120]{2,1,0:T(8,128)(2,1)}) custom-call(bf16[2,640,64]{2,1,0:T(8,128)(2,1)S(1)} %get-tuple-element.76.refs_0_, bf16[2,128,64]{2,1,0:T(8,128)(2,1)S(1)} %get-tuple-element.77.refs_1_, ...), custom_call_target="tpu_custom_call", output_to_operand_aliasing={{0}: (8, {}), {1}: (9, {}), {2}: (10, {})} | custom-call | flops 146800640 | bytes 4587520 | tf_op jit(solution)/shard_map/pallas_call | solution.py:205
  30.8 1.3 %shard_map.113 = (bf16[2,640,5120]{2,1,0:T(8,128)(2,1)}, bf16[2,128,5120]{2,1,0:T(8,128)(2,1)}, bf16[2,128,5120]{2,1,0:T(8,128)(2,1)}) custom-call(bf16[2,640,64]{2,1,0:T(8,128)(2,1)S(1)} %get-tuple-element.76.refs_0_, bf16[2,128,64]{2,1,0:T(8,128)(2,1)S(1)} %get-tuple-element.77.refs_1_, ...), custom_call_target="tpu_custom_call", output_to_operand_aliasing={{0}: (7, {}), {1}: (8, {}), {2}: (9, {})} | custom-call | flops 73400320 | bytes 2293760 | tf_op jit(solution)/shard_map/pallas_call | solution.py:205
  (31 shorter events, 0.1 us)
Async XLA Ops:
  0.6 2.4 %copy-start.3 = (bf16[1,2,3,64,640]{4,3,2,1,0:T(8,128)(2,1)S(1)}, bf16[1,2,3,64,640]{4,3,2,1,0:T(8,128)(2,1)}, u32[]{:S(2)}) copy-start(bf16[1,2,3,64,640]{4,3,2,1,0:T(8,128)(2,1)} %param.12) | copy-start | bytes 1474564
  0.6 2.4 %copy-start.7 = (s32[2,3]{1,0:T(2,128)S(1)}, s32[2,3]{1,0:T(2,128)}, u32[]{:S(2)}) copy-start(s32[2,3]{1,0:T(2,128)} %owners.3) | copy-start | bytes 76
  0.7 5.3 %copy-start.4 = (bf16[1,2,640,64]{2,3,1,0:T(8,128)(2,1)S(1)}, bf16[1,2,640,64]{2,3,1,0:T(8,128)(2,1)}, u32[]{:S(2)}) copy-start(bf16[1,2,640,64]{2,3,1,0:T(8,128)(2,1)} %param.13) | copy-start | bytes 491524
  0.7 5.5 %copy-start.5 = (bf16[1,2,128,64]{2,3,1,0:T(8,128)(2,1)S(1)}, bf16[1,2,128,64]{2,3,1,0:T(8,128)(2,1)}, u32[]{:S(2)}) copy-start(bf16[1,2,128,64]{2,3,1,0:T(8,128)(2,1)} %param.14) | copy-start | bytes 98308
  0.7 5.8 %copy-start.6 = (bf16[1,2,128,64]{2,3,1,0:T(8,128)(2,1)S(1)}, bf16[1,2,128,64]{2,3,1,0:T(8,128)(2,1)}, u32[]{:S(2)}) copy-start(bf16[1,2,128,64]{2,3,1,0:T(8,128)(2,1)} %param.15) | copy-start | bytes 98308
  0.7 2.3 %collective-permute-start.3 = (bf16[2,3,64,640]{3,2,1,0:T(8,128)(2,1)}, bf16[2,3,64,640]{3,2,1,0:T(8,128)(2,1)S(1)}, u32[]{:S(2)}, u32[]{:S(2)}) collective-permute-start(bf16[2,3,64,640]{3,2,1,0:T(8,128)(2,1)} %bitcast.10), channel_id=1, source_target_pairs={{0,8},{8,0},{1,9},{9,1},{2,10},{10,2},{3,11},{11,3},{4,12},{12,4},... | collective-permute-start | bytes 1474568 | tf_op jit(solution)/shard_map/ppermute | solution.py:44
  1.2 10.7 %copy-start = (bf16[2,640,5120]{2,1,0:T(8,128)(2,1)S(1)}, bf16[2,640,5120]{2,1,0:T(8,128)(2,1)}, u32[]{:S(2)}) copy-start(bf16[2,640,5120]{2,1,0:T(8,128)(2,1)} %refs_4_.7) | copy-start | bytes 39321604
  1.2 10.7 %copy-start.2 = (bf16[2,128,5120]{2,1,0:T(8,128)(2,1)S(1)}, bf16[2,128,5120]{2,1,0:T(8,128)(2,1)}, u32[]{:S(2)}) copy-start(bf16[2,128,5120]{2,1,0:T(8,128)(2,1)} %refs_6_.15) | copy-start | bytes 7864324
  3.0 8.9 %copy-start.1 = (bf16[2,128,5120]{2,1,0:T(8,128)(2,1)S(1)}, bf16[2,128,5120]{2,1,0:T(8,128)(2,1)}, u32[]{:S(2)}) copy-start(bf16[2,128,5120]{2,1,0:T(8,128)(2,1)} %refs_5_.11) | copy-start | bytes 7864324
  3.2 6.6 %collective-permute-start.4 = (bf16[3,64,640]{2,1,0:T(8,128)(2,1)S(1)}, bf16[3,64,640]{2,1,0:T(8,128)(2,1)S(1)}, u32[]{:S(2)}, u32[]{:S(2)}) collective-permute-start(bf16[3,64,640]{2,1,0:T(8,128)(2,1)S(1)} %get-tuple-element.74.refs_9_), channel_id=1, source_target_pairs={{0,10},{8,1},{10,4},{2,8},{4,14},{12,2},{14,7},{6,12},{7,13},{15,6... | collective-permute-start | bytes 737288 | tf_op jit(solution)/shard_map/ppermute | solution.py:40
  5.9 2.0 %collective-permute-start = (bf16[2,64,640]{2,1,0:T(8,128)(2,1)S(1)}, bf16[2,64,640]{2,1,0:T(8,128)(2,1)S(1)}, u32[]{:S(2)}, u32[]{:S(2)}) collective-permute-start(bf16[2,64,640]{2,1,0:T(8,128)(2,1)S(1)} %bitcast.12), channel_id=1, source_target_pairs={{0,8},{8,0},{1,9},{9,1},{2,10},{10,2},{3,11},{11,3},{4,12},{12,4},... | collective-permute-start | bytes 491528 | tf_op jit(solution)/shard_map/ppermute | solution.py:44
  6.1 1.8 %collective-permute-start.1 = (bf16[2,64,128]{2,1,0:T(8,128)(2,1)S(1)}, bf16[2,64,128]{2,1,0:T(8,128)(2,1)S(1)}, u32[]{:S(2)}, u32[]{:S(2)}) collective-permute-start(bf16[2,64,128]{2,1,0:T(8,128)(2,1)S(1)} %bitcast.14), channel_id=1, source_target_pairs={{0,8},{8,0},{1,9},{9,1},{2,10},{10,2},{3,11},{11,3},{4,12},{12,4},... | collective-permute-start | bytes 98312 | tf_op jit(solution)/shard_map/ppermute | solution.py:44
  6.5 1.5 %collective-permute-start.2 = (bf16[2,64,128]{2,1,0:T(8,128)(2,1)S(1)}, bf16[2,64,128]{2,1,0:T(8,128)(2,1)S(1)}, u32[]{:S(2)}, u32[]{:S(2)}) collective-permute-start(bf16[2,64,128]{2,1,0:T(8,128)(2,1)S(1)} %bitcast.16), channel_id=1, source_target_pairs={{0,8},{8,0},{1,9},{9,1},{2,10},{10,2},{3,11},{11,3},{4,12},{12,4},... | collective-permute-start | bytes 98312 | tf_op jit(solution)/shard_map/ppermute | solution.py:44
  6.6 6.5 %collective-permute-start.6 = (bf16[3,64,640]{2,1,0:T(8,128)(2,1)S(1)}, bf16[3,64,640]{2,1,0:T(8,128)(2,1)S(1)}, u32[]{:S(2)}, u32[]{:S(2)}) collective-permute-start(bf16[3,64,640]{2,1,0:T(8,128)(2,1)S(1)} %get-tuple-element.75.refs_10_), channel_id=1, source_target_pairs={{0,10},{8,1},{10,4},{2,8},{4,14},{12,2},{14,7},{6,12},{7,13},{15,6... | collective-permute-start | bytes 737288 | tf_op jit(solution)/shard_map/ppermute | solution.py:40
  9.8 6.4 %collective-permute-start.5 = (bf16[3,64,640]{2,1,0:T(8,128)(2,1)S(1)}, bf16[3,64,640]{2,1,0:T(8,128)(2,1)S(1)}, u32[]{:S(2)}, u32[]{:S(2)}) collective-permute-start(bf16[3,64,640]{2,1,0:T(8,128)(2,1)S(1)} %collective-permute-done.4.refs_3_), channel_id=1, source_target_pairs={{0,10},{8,1},{10,4},{2,8},{4,14},{12,2},{14,7},{6,12},{7,13},{15,6... | collective-permute-start | bytes 737288 | tf_op jit(solution)/shard_map/ppermute | solution.py:40
  13.1 6.0 %collective-permute-start.8 = (bf16[3,64,640]{2,1,0:T(8,128)(2,1)S(1)}, bf16[3,64,640]{2,1,0:T(8,128)(2,1)S(1)}, u32[]{:S(2)}, u32[]{:S(2)}) collective-permute-start(bf16[3,64,640]{2,1,0:T(8,128)(2,1)S(1)} %collective-permute-done.6.refs_3_), channel_id=1, source_target_pairs={{0,10},{8,1},{10,4},{2,8},{4,14},{12,2},{14,7},{6,12},{7,13},{15,6... | collective-permute-start | bytes 737288 | tf_op jit(solution)/shard_map/ppermute | solution.py:40
  14.5 6.1 %collective-permute-start.10 = (bf16[3,64,640]{2,1,0:T(8,128)(2,1)S(1)}, bf16[3,64,640]{2,1,0:T(8,128)(2,1)S(1)}, u32[]{:S(2)}, u32[]{:S(2)}) collective-permute-start(bf16[3,64,640]{2,1,0:T(8,128)(2,1)S(1)} %collective-permute-done.6.refs_3_), channel_id=1, source_target_pairs={{0,8},{8,0},{1,9},{9,1},{2,10},{10,2},{3,11},{11,3},{4,12},{12,4},... | collective-permute-start | bytes 737288 | tf_op jit(solution)/shard_map/ppermute | solution.py:44
  14.8 6.1 %collective-permute-start.9 = (bf16[3,64,640]{2,1,0:T(8,128)(2,1)S(1)}, bf16[3,64,640]{2,1,0:T(8,128)(2,1)S(1)}, u32[]{:S(2)}, u32[]{:S(2)}) collective-permute-start(bf16[3,64,640]{2,1,0:T(8,128)(2,1)S(1)} %collective-permute-done.4.refs_3_), channel_id=1, source_target_pairs={{0,8},{8,0},{1,9},{9,1},{2,10},{10,2},{3,11},{11,3},{4,12},{12,4},... | collective-permute-start | bytes 737288 | tf_op jit(solution)/shard_map/ppermute | solution.py:44
  16.3 6.7 %collective-permute-start.7 = (bf16[3,64,640]{2,1,0:T(8,128)(2,1)S(1)}, bf16[3,64,640]{2,1,0:T(8,128)(2,1)S(1)}, u32[]{:S(2)}, u32[]{:S(2)}) collective-permute-start(bf16[3,64,640]{2,1,0:T(8,128)(2,1)S(1)} %collective-permute-done.5.refs_3_), channel_id=1, source_target_pairs={{0,10},{8,1},{10,4},{2,8},{4,14},{12,2},{14,7},{6,12},{7,13},{15,6... | collective-permute-start | bytes 737288 | tf_op jit(solution)/shard_map/ppermute | solution.py:40
  19.2 5.5 %collective-permute-start.14 = (bf16[3,64,640]{2,1,0:T(8,128)(2,1)S(1)}, bf16[3,64,640]{2,1,0:T(8,128)(2,1)S(1)}, u32[]{:S(2)}, u32[]{:S(2)}) collective-permute-start(bf16[3,64,640]{2,1,0:T(8,128)(2,1)S(1)} %collective-permute-done.8.refs_3_), channel_id=1, source_target_pairs={{0,8},{8,0},{1,9},{9,1},{2,10},{10,2},{3,11},{11,3},{4,12},{12,4},... | collective-permute-start | bytes 737288 | tf_op jit(solution)/shard_map/ppermute | solution.py:44
  19.3 7.0 %collective-permute-start.12 = (bf16[3,64,640]{2,1,0:T(8,128)(2,1)S(1)}, bf16[3,64,640]{2,1,0:T(8,128)(2,1)S(1)}, u32[]{:S(2)}, u32[]{:S(2)}) collective-permute-start(bf16[3,64,640]{2,1,0:T(8,128)(2,1)S(1)} %collective-permute-done.8.refs_3_), channel_id=1, source_target_pairs={{0,10},{8,1},{10,4},{2,8},{4,14},{12,2},{14,7},{6,12},{7,13},{15,6... | collective-permute-start | bytes 737288 | tf_op jit(solution)/shard_map/ppermute | solution.py:40
  20.6 4.1 %collective-permute-start.13 = (bf16[3,64,640]{2,1,0:T(8,128)(2,1)S(1)}, bf16[3,64,640]{2,1,0:T(8,128)(2,1)S(1)}, u32[]{:S(2)}, u32[]{:S(2)}) collective-permute-start(bf16[3,64,640]{2,1,0:T(8,128)(2,1)S(1)} %collective-permute-done.5.refs_3_), channel_id=1, source_target_pairs={{0,8},{8,0},{1,9},{9,1},{2,10},{10,2},{3,11},{11,3},{4,12},{12,4},... | collective-permute-start | bytes 737288 | tf_op jit(solution)/shard_map/ppermute | solution.py:44
  23.0 3.6 %collective-permute-start.15 = (bf16[3,64,640]{2,1,0:T(8,128)(2,1)S(1)}, bf16[3,64,640]{2,1,0:T(8,128)(2,1)S(1)}, u32[]{:S(2)}, u32[]{:S(2)}) collective-permute-start(bf16[3,64,640]{2,1,0:T(8,128)(2,1)S(1)} %collective-permute-done.7.refs_4_), channel_id=1, source_target_pairs={{0,8},{8,0},{1,9},{9,1},{2,10},{10,2},{3,11},{11,3},{4,12},{12,4},... | collective-permute-start | bytes 737288 | tf_op jit(solution)/shard_map/ppermute | solution.py:44
  23.2 5.6 %collective-permute-start.11 = (bf16[3,64,640]{2,1,0:T(8,128)(2,1)S(1)}, bf16[3,64,640]{2,1,0:T(8,128)(2,1)S(1)}, u32[]{:S(2)}, u32[]{:S(2)}) collective-permute-start(bf16[3,64,640]{2,1,0:T(8,128)(2,1)S(1)} %collective-permute-done.7.refs_4_), channel_id=1, source_target_pairs={{0,10},{8,1},{10,4},{2,8},{4,14},{12,2},{14,7},{6,12},{7,13},{15,6... | collective-permute-start | bytes 737288 | tf_op jit(solution)/shard_map/ppermute | solution.py:40
  26.3 2.9 %collective-permute-start.17 = (bf16[3,64,640]{2,1,0:T(8,128)(2,1)S(1)}, bf16[3,64,640]{2,1,0:T(8,128)(2,1)S(1)}, u32[]{:S(2)}, u32[]{:S(2)}) collective-permute-start(bf16[3,64,640]{2,1,0:T(8,128)(2,1)S(1)} %collective-permute-done.12.refs_3_), channel_id=1, source_target_pairs={{0,8},{8,0},{1,9},{9,1},{2,10},{10,2},{3,11},{11,3},{4,12},{12,4},... | collective-permute-start | bytes 737288 | tf_op jit(solution)/shard_map/ppermute | solution.py:44
  28.8 2.0 %collective-permute-start.16 = (bf16[3,64,640]{2,1,0:T(8,128)(2,1)S(1)}, bf16[3,64,640]{2,1,0:T(8,128)(2,1)S(1)}, u32[]{:S(2)}, u32[]{:S(2)}) collective-permute-start(bf16[3,64,640]{2,1,0:T(8,128)(2,1)S(1)} %collective-permute-done.11.refs_4_), channel_id=1, source_target_pairs={{0,8},{8,0},{1,9},{9,1},{2,10},{10,2},{3,11},{11,3},{4,12},{12,4},... | collective-permute-start | bytes 737288 | tf_op jit(solution)/shard_map/ppermute | solution.py:44
